TPU v7x, 512 devices: a whole 4x8x8 slice. The times are simulated.
512 devices in a mesh: lon: 16 (over z, y_hi), lat: 8 (over y_lo, core), lev: 4 (over x).
Axes of the slice: x: 4, y: 8 (y_hi: 2, y_lo: 4; y = y_hi * 4 + y_lo), z: 8, core: 2. Of those that a mesh axis runs over, the one named last changes fastest.
Arguments:
- fields: bfloat16 [8, 48, 192, 192], P('lev', 'lat', 'lon'), may hold values from -7 to 7
- w_qkv: bfloat16 [4, 192, 576], replicated, may hold values from -7 to 7
- w_out: bfloat16 [4, 192, 192], replicated, may hold values from -0.4375 to 0.4375
- w_up: bfloat16 [4, 192, 768], replicated, may hold values from -0.4375 to 0.4375
- w_down: bfloat16 [4, 768, 192], replicated, may hold values from -0.21875 to 0.21875
- gains: float32 [4, 2, 192], replicated, may hold values from 0.25 to 1.75
- bias_table: bfloat16 [4, 4, 8, 6, 3312], P(None, None, 'lat'), may hold values from -4 to 4
- labels: int32 [8, 48, 192], P(None, 'lat', 'lon'), may hold values from 0 to 7, as said below
Outputs:
- fields_out: bfloat16 [8, 48, 192, 192], P('lev', 'lat', 'lon')
Inputs may be any that keep to these rules, and one draw needn't show every extreme that they name: labels[z, y, x] = e + 2 f + 4 g, the same for every x, where e is 1 when z >= 7, f is 1 when y >= 45, and g is 1 when the row (y + 3) mod 48 is one of the first n or the last s padding rows of the grid, with n and s between 1 and 3.
All inputs are finite; a program needn't handle non-finite values.
Results may differ from a plain program's by a relative error of at most 0.025.
Values may be sent and summed in bfloat16 or wider, within the bound.
No kernel may reach another device: no remote copies, remote signals or barrier semaphores. Data moves between devices by JAX's collectives and lax.ppermute only.
A program may use at most 64 MiB of HBM per device.

v0:
```python
import jax
import jax.numpy as jnp
from jax import lax
from jax.sharding import PartitionSpec as P

HEADS = 6
WZ = 2
WY = 6
WX = 12
BLOCKS = 4


def shifted_2(value, axis, steps):
    count = lax.axis_size(axis)
    pairs = [(source, (source + steps) % count) for source in range(count)]
    return lax.ppermute(value, axis, pairs)


def layer_norm(values, gain_row):
    floats = values.astype(jnp.float32)
    center = floats - jnp.mean(floats, axis=-1, keepdims=True)
    spread = jnp.mean(center * center, axis=-1, keepdims=True)
    return center * lax.rsqrt(spread + 1e-05) * gain_row


def expand_bias(bias_rows):
    row_count = bias_rows.shape[0]
    shaped = bias_rows.astype(jnp.float32).reshape(row_count, HEADS, WZ, WZ, WY, WY, 2 * WX - 1)
    offset = (
        jnp.arange(WX, dtype=jnp.int32)[:, None]
        - jnp.arange(WX, dtype=jnp.int32)[None, :]
        + (WX - 1)
    )
    selector = (
        offset[:, :, None] == jnp.arange(2 * WX - 1, dtype=jnp.int32)[None, None, :]
    ).astype(jnp.float32)
    spread_out = jnp.einsum(
        "nhpqrsd,abd->nhpraqsb", shaped, selector, precision=lax.Precision.HIGHEST
    )
    size_window = WZ * WY * WX
    return spread_out.reshape(row_count, HEADS, size_window, size_window)


def head_weights(weight):
    return weight.reshape(weight.shape[0], 3, HEADS, weight.shape[1] // (3 * HEADS))


def out_projection(mixed_heads, weight):
    shaped = weight.reshape(HEADS, weight.shape[0] // HEADS, weight.shape[1])
    return jnp.einsum(
        "whae,hef->waf", mixed_heads, shaped, preferred_element_type=jnp.float32
    ).astype(jnp.bfloat16)


def attend(queries, key_part, val_part, bias_full, query_labels, key_labels):
    head_size = queries.shape[-1]
    scores = jnp.einsum("whae,whbe->whab", queries, key_part, preferred_element_type=jnp.float32)
    scores = scores * head_size ** (-0.5)
    groups = bias_full.shape[0]
    scores = (scores.reshape((groups, -1) + scores.shape[1:]) + bias_full[:, None]).reshape(
        scores.shape
    )
    if query_labels is None:
        allowed = jnp.ones(scores.shape, dtype=bool)
    else:
        allowed = query_labels[:, None, :, None] == key_labels[:, None, None, :]
    masked = jnp.where(allowed, scores, -1e30)
    row_max = jnp.max(masked, axis=-1, keepdims=True)
    exp_terms = jnp.where(allowed, jnp.exp(masked - row_max), 0.0)
    weights = (exp_terms / jnp.sum(exp_terms, axis=-1, keepdims=True)).astype(jnp.bfloat16)
    mixed_heads = jnp.einsum(
        "whab,whbe->whae", weights, val_part, preferred_element_type=jnp.float32
    )
    return mixed_heads.astype(jnp.bfloat16)


def per_device(fields, w_qkv, w_out, w_up, w_down, gains, bias_table, labels):
    levels, lat_rows, lon_cols, model_width = fields.shape
    row_windows = lat_rows // WY
    col_windows = lon_cols // WX
    size_window = WZ * WY * WX
    half_z = WZ // 2
    half_y = WY // 2
    half_x = WX // 2
    level_pos = lax.axis_index("lev")

    def window_bias(block_idx, level_window):
        table = lax.dynamic_index_in_dim(bias_table[block_idx], level_window, 0, keepdims=False)
        return expand_bias(table)

    def whole_windows(frame_tile, block_idx, use_labels):
        windows = frame_tile.reshape(WZ, row_windows, WY, col_windows, WX, model_width).transpose(
            1, 3, 0, 2, 4, 5
        )
        windows = windows.reshape(row_windows * col_windows, size_window, model_width)
        proj_qkv = jnp.einsum(
            "wtd,dkhe->kwhte",
            windows,
            head_weights(w_qkv[block_idx]),
            preferred_element_type=jnp.float32,
        ).astype(jnp.bfloat16)
        bias_full = window_bias(block_idx, level_pos)
        if use_labels:
            label_rows = lax.dynamic_slice_in_dim(labels, level_pos * WZ, WZ, 0)
            label_rows = label_rows.reshape(WZ, row_windows, WY, col_windows, WX).transpose(
                1, 3, 0, 2, 4
            )
            label_rows = label_rows.reshape(row_windows * col_windows, size_window)
            mixed_heads = attend(
                proj_qkv[0], proj_qkv[1], proj_qkv[2], bias_full, label_rows, label_rows
            )
        else:
            mixed_heads = attend(proj_qkv[0], proj_qkv[1], proj_qkv[2], bias_full, None, None)
        projected = out_projection(mixed_heads, w_out[block_idx])
        projected = projected.reshape(row_windows, col_windows, WZ, WY, WX, model_width).transpose(
            2, 0, 3, 1, 4, 5
        )
        return projected.reshape(WZ, lat_rows, lon_cols, model_width)

    stream = fields
    for block_idx in range(BLOCKS):
        shifted = block_idx % 2 == 1
        normed = layer_norm(stream, gains[block_idx, 0]).astype(jnp.bfloat16)
        if shifted:
            roll_block_tile = normed
            roll_edge_slab = shifted_2(roll_block_tile[:, :, :half_x], "lon", -1)
            roll_block_tile = jnp.concatenate(
                [roll_block_tile[:, :, half_x:], roll_edge_slab], axis=2
            )
            roll_edge_slab = shifted_2(roll_block_tile[:, :half_y], "lat", -1)
            roll_block_tile = jnp.concatenate([roll_block_tile[:, half_y:], roll_edge_slab], axis=1)
            roll_edge_slab = shifted_2(roll_block_tile[:half_z], "lev", -1)
            roll_block_tile = jnp.concatenate([roll_block_tile[half_z:], roll_edge_slab], axis=0)
            frame_tile = roll_block_tile
            attended = whole_windows(frame_tile, block_idx, True)
            block_tile = attended
            edge_slab = shifted_2(block_tile[-half_z:], "lev", 1)
            block_tile = jnp.concatenate([edge_slab, block_tile[:-half_z]], axis=0)
            edge_slab = shifted_2(block_tile[:, -half_y:], "lat", 1)
            block_tile = jnp.concatenate([edge_slab, block_tile[:, :-half_y]], axis=1)
            edge_slab = shifted_2(block_tile[:, :, -half_x:], "lon", 1)
            block_tile = jnp.concatenate([edge_slab, block_tile[:, :, :-half_x]], axis=2)
            attended = block_tile
        else:
            attended = whole_windows(normed, block_idx, False)
        middle = (stream.astype(jnp.float32) + attended.astype(jnp.float32)).astype(jnp.bfloat16)
        normed_two = layer_norm(middle, gains[block_idx, 1]).astype(jnp.bfloat16)
        hidden = jax.nn.gelu(
            jnp.dot(
                normed_two.reshape(-1, model_width),
                w_up[block_idx],
                preferred_element_type=jnp.float32,
            ),
            approximate=False,
        ).astype(jnp.bfloat16)
        down_rows = jnp.dot(hidden, w_down[block_idx], preferred_element_type=jnp.float32).reshape(
            levels, lat_rows, lon_cols, model_width
        )
        stream = (middle.astype(jnp.float32) + down_rows).astype(jnp.bfloat16)
    return stream


def solution(mesh):
    in_specs = (
        P("lev", "lat", "lon", None),
        P(),
        P(),
        P(),
        P(),
        P(),
        P(None, None, "lat", None, None),
        P(None, "lat", "lon"),
    )
    out_specs = P("lev", "lat", "lon", None)
    return jax.shard_map(
        per_device, mesh=mesh, in_specs=in_specs, out_specs=out_specs, check_vma=False
    )
```

profile of v0, /device:TPU:6, one launch (start us, length us, event | category | flops | bytes accessed | tf_op | source)
XLA Modules:
  0.0 197.9 jit_solution(2467292229687901241)
XLA Ops:
  3.6 4.1 %convolution_bitcast_fusion.3 = f32[1,6,2,6,12,2,6,12]{7,6,3,5,2,1,4,0:T(8,128)} fusion(bf16[6,2,2,6,6,23,1]{5,4,3,2,1,0,6:T(8,128)(2,1)S(1)} %reshape.484, s32[12,12]{1,0:T(8,128)S(1)} %subtract_add_fusion), kind=kOutput, calls=%fused_computation.7 | convolution fusion | flops 5726448 | bytes 537984 | tf_op jit(solution)/shard_map/nhpqrsd,abd->nhpraqsb/dot_general | solution.py:37
  7.7 11.3 %copy.39 = f32[1,6,2,6,12,2,6,12]{4,3,2,7,6,5,1,0:T(8,128)} copy(f32[1,6,2,6,12,2,6,12]{7,6,3,5,2,1,4,0:T(8,128)} %convolution_bitcast_fusion.3) | data formatting | bytes 995328 | tf_op jit(solution)/shard_map/broadcast_in_dim;reshape | solution.py:60
  19.0 5.0 %reshape.503 = f32[6,144,144]{1,2,0:T(8,128)S(1)} reshape(f32[1,6,2,6,12,2,6,12]{4,3,2,7,6,5,1,0:T(8,128)} %copy.39) | data formatting | bytes 995328 | tf_op jit(solution)/shard_map/broadcast_in_dim;reshape | solution.py:60
  30.6 16.2 %collective-permute-start = (bf16[2,6,6,192]{3,2,1,0:T(8,128)(2,1)S(1)}, bf16[2,6,6,192]{3,2,1,0:T(8,128)(2,1)S(1)}, u32[]{:S(2)}, u32[]{:S(2)}) collective-permute-start(bf16[2,6,6,192]{3,2,1,0:T(8,128)(2,1)S(1)} %get-tuple-element.36), channel_id=1, source_target_pairs={{0,480},{32,0},{64,32},{96,64},{128,96},{160,128},{192,160},{224,1... | collective-permute-start | bytes 82952 | tf_op jit(solution)/shard_map/ppermute | solution.py:16
  52.3 2.7 %collective-permute-start.2 = (bf16[1,6,12,192]{3,2,1,0:T(8,128)(2,1)S(1)}, bf16[1,6,12,192]{3,2,1,0:T(8,128)(2,1)S(1)}, u32[]{:S(2)}, u32[]{:S(2)}) collective-permute-start(bf16[1,6,12,192]{3,2,1,0:T(8,128)(2,1)S(1)} %get-tuple-element.32), channel_id=1, source_target_pairs={{0,3},{1,0},{2,1},{3,2},{4,7},{5,4},{6,5},{7,6},{8,11},{9,8},{10,9... | collective-permute-start | bytes 82952 | tf_op jit(solution)/shard_map/ppermute | solution.py:16
  55.0 4.1 %convolution_bitcast_fusion.2 = f32[1,6,2,6,12,2,6,12]{7,6,3,5,2,1,4,0:T(8,128)} fusion(bf16[6,2,2,6,6,23,1]{5,4,3,2,1,0,6:T(8,128)(2,1)S(1)} %reshape.489, s32[12,12]{1,0:T(8,128)S(1)} %subtract_add_fusion), kind=kOutput, calls=%fused_computation.6 | convolution fusion | flops 5726448 | bytes 537984 | tf_op jit(solution)/shard_map/nhpqrsd,abd->nhpraqsb/dot_general | solution.py:37
  59.1 11.3 %copy.40 = f32[1,6,2,6,12,2,6,12]{4,3,2,7,6,5,1,0:T(8,128)} copy(f32[1,6,2,6,12,2,6,12]{7,6,3,5,2,1,4,0:T(8,128)} %convolution_bitcast_fusion.2) | data formatting | bytes 995328 | tf_op jit(solution)/shard_map/broadcast_in_dim;reshape | solution.py:60
  70.4 4.9 %reshape.505 = f32[6,144,144]{1,2,0:T(8,128)S(1)} reshape(f32[1,6,2,6,12,2,6,12]{4,3,2,7,6,5,1,0:T(8,128)} %copy.40) | data formatting | bytes 995328 | tf_op jit(solution)/shard_map/broadcast_in_dim;reshape | solution.py:60
  79.0 4.5 %collective-permute-start.3 = (bf16[1,6,12,192]{3,2,1,0:T(8,128)(2,1)S(1)}, bf16[1,6,12,192]{3,2,1,0:T(8,128)(2,1)S(1)}, u32[]{:S(2)}, u32[]{:S(2)}) collective-permute-start(bf16[1,6,12,192]{3,2,1,0:T(8,128)(2,1)S(1)} %slice.228), channel_id=1, source_target_pairs={{0,1},{1,2},{2,3},{3,0},{4,5},{5,6},{6,7},{7,4},{8,9},{9,10},{10,1... | collective-permute-start | bytes 82952 | tf_op jit(solution)/shard_map/ppermute | solution.py:16
  83.5 2.1 %collective-permute-done.3 = bf16[1,6,12,192]{3,2,1,0:T(8,128)(2,1)S(1)} collective-permute-done((bf16[1,6,12,192]{3,2,1,0:T(8,128)(2,1)S(1)}, bf16[1,6,12,192]{3,2,1,0:T(8,128)(2,1)S(1)}, u32[]{:S(2)}, u32[]{:S(2)}) %collective-permute-start.3) | collective-permute-done | bytes 27680 | tf_op jit(solution)/shard_map/ppermute | solution.py:16
  88.6 4.4 %collective-permute-done.4 = bf16[2,3,12,192]{3,2,1,0:T(8,128)(2,1)S(1)} collective-permute-done((bf16[2,3,12,192]{3,2,1,0:T(8,128)(2,1)S(1)}, bf16[2,3,12,192]{3,2,1,0:T(8,128)(2,1)S(1)}, u32[]{:S(2)}, u32[]{:S(2)}) %collective-permute-start.4) | collective-permute-done | bytes 27680 | tf_op jit(solution)/shard_map/ppermute | solution.py:16
  94.9 4.1 %convolution_bitcast_fusion.1 = f32[1,6,2,6,12,2,6,12]{7,6,3,5,2,1,4,0:T(8,128)} fusion(bf16[6,2,2,6,6,23,1]{5,4,3,2,1,0,6:T(8,128)(2,1)S(1)} %reshape.494, s32[12,12]{1,0:T(8,128)S(1)} %subtract_add_fusion), kind=kOutput, calls=%fused_computation.5 | convolution fusion | flops 5726448 | bytes 537984 | tf_op jit(solution)/shard_map/nhpqrsd,abd->nhpraqsb/dot_general | solution.py:37
  99.0 11.3 %copy.41 = f32[1,6,2,6,12,2,6,12]{4,3,2,7,6,5,1,0:T(8,128)} copy(f32[1,6,2,6,12,2,6,12]{7,6,3,5,2,1,4,0:T(8,128)} %convolution_bitcast_fusion.1) | data formatting | bytes 995328 | tf_op jit(solution)/shard_map/broadcast_in_dim;reshape | solution.py:60
  110.3 4.9 %reshape.507 = f32[6,144,144]{1,2,0:T(8,128)S(1)} reshape(f32[1,6,2,6,12,2,6,12]{4,3,2,7,6,5,1,0:T(8,128)} %copy.41) | data formatting | bytes 995328 | tf_op jit(solution)/shard_map/broadcast_in_dim;reshape | solution.py:60
  122.4 2.0 %fusion.43 = bf16[144,768]{1,0:T(8,128)(2,1)S(1)} fusion(bf16[144,192]{1,0:T(8,128)(2,1)S(1)} %reshape.472, bf16[4,192,768]{2,1,0:T(8,128)(2,1)} %param.11), kind=kOutput, calls=%fused_computation.71 | convolution fusion | flops 49655808 | bytes 571392 | tf_op jit(solution)/shard_map/dot_general | solution.py:149
  126.2 10.2 %collective-permute-start.6 = (bf16[2,6,6,192]{3,2,1,0:T(8,128)(2,1)S(1)}, bf16[2,6,6,192]{3,2,1,0:T(8,128)(2,1)S(1)}, u32[]{:S(2)}, u32[]{:S(2)}) collective-permute-start(bf16[2,6,6,192]{3,2,1,0:T(8,128)(2,1)S(1)} %get-tuple-element.28), channel_id=1, source_target_pairs={{0,480},{32,0},{64,32},{96,64},{128,96},{160,128},{192,160},{224,1... | collective-permute-start | bytes 82952 | tf_op jit(solution)/shard_map/ppermute | solution.py:16
  141.8 2.7 %collective-permute-start.8 = (bf16[1,6,12,192]{3,2,1,0:T(8,128)(2,1)S(1)}, bf16[1,6,12,192]{3,2,1,0:T(8,128)(2,1)S(1)}, u32[]{:S(2)}, u32[]{:S(2)}) collective-permute-start(bf16[1,6,12,192]{3,2,1,0:T(8,128)(2,1)S(1)} %get-tuple-element.24), channel_id=1, source_target_pairs={{0,3},{1,0},{2,1},{3,2},{4,7},{5,4},{6,5},{7,6},{8,11},{9,8},{10,9... | collective-permute-start | bytes 82952 | tf_op jit(solution)/shard_map/ppermute | solution.py:16
  144.5 4.1 %convolution_bitcast_fusion = f32[1,6,2,6,12,2,6,12]{7,6,3,5,2,1,4,0:T(8,128)} fusion(bf16[6,2,2,6,6,23,1]{5,4,3,2,1,0,6:T(8,128)(2,1)S(1)} %reshape.499, s32[12,12]{1,0:T(8,128)S(1)} %subtract_add_fusion), kind=kOutput, calls=%fused_computation.4 | convolution fusion | flops 5726448 | bytes 537984 | tf_op jit(solution)/shard_map/nhpqrsd,abd->nhpraqsb/dot_general | solution.py:37
  148.5 11.3 %copy.42 = f32[1,6,2,6,12,2,6,12]{4,3,2,7,6,5,1,0:T(8,128)} copy(f32[1,6,2,6,12,2,6,12]{7,6,3,5,2,1,4,0:T(8,128)} %convolution_bitcast_fusion) | data formatting | bytes 995328 | tf_op jit(solution)/shard_map/broadcast_in_dim;reshape | solution.py:60
  159.9 4.9 %reshape.509 = f32[6,144,144]{1,2,0:T(8,128)S(1)} reshape(f32[1,6,2,6,12,2,6,12]{4,3,2,7,6,5,1,0:T(8,128)} %copy.42) | data formatting | bytes 995328 | tf_op jit(solution)/shard_map/broadcast_in_dim;reshape | solution.py:60
  166.6 5.0 %collective-permute-start.9 = (bf16[1,6,12,192]{3,2,1,0:T(8,128)(2,1)S(1)}, bf16[1,6,12,192]{3,2,1,0:T(8,128)(2,1)S(1)}, u32[]{:S(2)}, u32[]{:S(2)}) collective-permute-start(bf16[1,6,12,192]{3,2,1,0:T(8,128)(2,1)S(1)} %slice.262), channel_id=1, source_target_pairs={{0,1},{1,2},{2,3},{3,0},{4,5},{5,6},{6,7},{7,4},{8,9},{9,10},{10,1... | collective-permute-start | bytes 82952 | tf_op jit(solution)/shard_map/ppermute | solution.py:16
  175.3 5.3 %collective-permute-done.10 = bf16[2,3,12,192]{3,2,1,0:T(8,128)(2,1)S(1)} collective-permute-done((bf16[2,3,12,192]{3,2,1,0:T(8,128)(2,1)S(1)}, bf16[2,3,12,192]{3,2,1,0:T(8,128)(2,1)S(1)}, u32[]{:S(2)}, u32[]{:S(2)}) %collective-permute-start.10) | collective-permute-done | bytes 27680 | tf_op jit(solution)/shard_map/ppermute | solution.py:16
  182.5 10.8 %collective-permute-done.11 = bf16[2,6,6,192]{3,2,1,0:T(8,128)(2,1)S(1)} collective-permute-done((bf16[2,6,6,192]{3,2,1,0:T(8,128)(2,1)S(1)}, bf16[2,6,6,192]{3,2,1,0:T(8,128)(2,1)S(1)}, u32[]{:S(2)}, u32[]{:S(2)}) %collective-permute-start.11) | collective-permute-done | bytes 27680 | tf_op jit(solution)/shard_map/ppermute | solution.py:16
  193.8 2.0 %fusion.46 = bf16[144,768]{1,0:T(8,128)(2,1)S(1)} fusion(bf16[144,192]{1,0:T(8,128)(2,1)S(1)} %reshape.478, bf16[4,192,768]{2,1,0:T(8,128)(2,1)} %param.11), kind=kOutput, calls=%fused_computation.74 | convolution fusion | flops 49655808 | bytes 571392 | tf_op jit(solution)/shard_map/dot_general | solution.py:149
  (146 shorter events, 47.6 us)
Async XLA Ops:
  0.0 46.8 %copy-start = (s32[8,6,12]{2,0,1:T(8,128)S(1)}, s32[8,6,12]{2,0,1:T(8,128)}, u32[]{:S(2)}) copy-start(s32[8,6,12]{2,0,1:T(8,128)} %param.15) | copy-start | bytes 6916
  0.0 1.9 copy-start.4
  19.0 5.1 %copy-start.9 = (f32[4,2,192]{2,1,0:T(2,128)S(1)}, f32[4,2,192]{2,1,0:T(2,128)}, u32[]{:S(2)}) copy-start(f32[4,2,192]{2,1,0:T(2,128)} %param.13) | copy-start | bytes 18436
  19.0 5.1 %copy-start.2 = (bf16[2,6,12,192]{3,0,2,1:T(2,128)(2,1)S(1)}, bf16[2,6,12,192]{3,0,2,1:T(2,128)(2,1)}, u32[]{:S(2)}) copy-start(bf16[2,6,12,192]{3,0,2,1:T(2,128)(2,1)} %param.8) | copy-start | bytes 165892
  19.0 5.6 %copy-start.3 = (bf16[4,192,576]{2,1,0:T(8,128)(2,1)S(1)}, bf16[4,192,576]{2,1,0:T(8,128)(2,1)}, u32[]{:S(2)}) copy-start(bf16[4,192,576]{2,1,0:T(8,128)(2,1)} %param.9) | copy-start | bytes 2654212
  24.9 0.9 copy-start.8
  30.6 17.9 %collective-permute-start = (bf16[2,6,6,192]{3,2,1,0:T(8,128)(2,1)S(1)}, bf16[2,6,6,192]{3,2,1,0:T(8,128)(2,1)S(1)}, u32[]{:S(2)}, u32[]{:S(2)}) collective-permute-start(bf16[2,6,6,192]{3,2,1,0:T(8,128)(2,1)S(1)} %get-tuple-element.36), channel_id=1, source_target_pairs={{0,480},{32,0},{64,32},{96,64},{128,96},{160,128},{192,160},{224,1... | collective-permute-start | bytes 82952 | tf_op jit(solution)/shard_map/ppermute | solution.py:16
  48.6 3.7 %collective-permute-start.1 = (bf16[2,3,12,192]{3,2,1,0:T(8,128)(2,1)S(1)}, bf16[2,3,12,192]{3,2,1,0:T(8,128)(2,1)S(1)}, u32[]{:S(2)}, u32[]{:S(2)}) collective-permute-start(bf16[2,3,12,192]{3,2,1,0:T(8,128)(2,1)S(1)} %get-tuple-element.34), channel_id=1, source_target_pairs={{0,28},{4,0},{8,4},{12,8},{16,12},{20,16},{24,20},{28,24},{1,29},{... | collective-permute-start | bytes 82952 | tf_op jit(solution)/shard_map/ppermute | solution.py:16
  52.3 23.1 %collective-permute-start.2 = (bf16[1,6,12,192]{3,2,1,0:T(8,128)(2,1)S(1)}, bf16[1,6,12,192]{3,2,1,0:T(8,128)(2,1)S(1)}, u32[]{:S(2)}, u32[]{:S(2)}) collective-permute-start(bf16[1,6,12,192]{3,2,1,0:T(8,128)(2,1)S(1)} %get-tuple-element.32), channel_id=1, source_target_pairs={{0,3},{1,0},{2,1},{3,2},{4,7},{5,4},{6,5},{7,6},{8,11},{9,8},{10,9... | collective-permute-start | bytes 82952 | tf_op jit(solution)/shard_map/ppermute | solution.py:16
  75.8 1.5 copy-start.7
  77.3 10.4 %copy-start.5 = (bf16[1,4,1,6,3312]{4,1,3,2,0:T(4,128)(2,1)S(1)}, bf16[1,4,1,6,3312]{4,1,3,2,0:T(4,128)(2,1)}, u32[]{:S(2)}) copy-start(bf16[1,4,1,6,3312]{4,1,3,2,0:T(4,128)(2,1)} %get-tuple-element.16) | copy-start | bytes 476932
  79.0 6.7 %collective-permute-start.3 = (bf16[1,6,12,192]{3,2,1,0:T(8,128)(2,1)S(1)}, bf16[1,6,12,192]{3,2,1,0:T(8,128)(2,1)S(1)}, u32[]{:S(2)}, u32[]{:S(2)}) collective-permute-start(bf16[1,6,12,192]{3,2,1,0:T(8,128)(2,1)S(1)} %slice.228), channel_id=1, source_target_pairs={{0,1},{1,2},{2,3},{3,0},{4,5},{5,6},{6,7},{7,4},{8,9},{9,10},{10,1... | collective-permute-start | bytes 82952 | tf_op jit(solution)/shard_map/ppermute | solution.py:16
  85.7 7.2 %collective-permute-start.4 = (bf16[2,3,12,192]{3,2,1,0:T(8,128)(2,1)S(1)}, bf16[2,3,12,192]{3,2,1,0:T(8,128)(2,1)S(1)}, u32[]{:S(2)}, u32[]{:S(2)}) collective-permute-start(bf16[2,3,12,192]{3,2,1,0:T(8,128)(2,1)S(1)} %get-tuple-element.29), channel_id=1, source_target_pairs={{0,4},{4,8},{8,12},{12,16},{16,20},{20,24},{24,28},{28,0},{1,5},{5... | collective-permute-start | bytes 82952 | tf_op jit(solution)/shard_map/ppermute | solution.py:16
  93.0 22.3 %collective-permute-start.5 = (bf16[2,6,6,192]{3,2,1,0:T(8,128)(2,1)S(1)}, bf16[2,6,6,192]{3,2,1,0:T(8,128)(2,1)S(1)}, u32[]{:S(2)}, u32[]{:S(2)}) collective-permute-start(bf16[2,6,6,192]{3,2,1,0:T(8,128)(2,1)S(1)} %fusion.151), channel_id=1, source_target_pairs={{0,32},{32,64},{64,96},{96,128},{128,160},{160,192},{192,224},{224... | collective-permute-start | bytes 82952 | tf_op jit(solution)/shard_map/ppermute | solution.py:16
  126.2 11.9 %collective-permute-start.6 = (bf16[2,6,6,192]{3,2,1,0:T(8,128)(2,1)S(1)}, bf16[2,6,6,192]{3,2,1,0:T(8,128)(2,1)S(1)}, u32[]{:S(2)}, u32[]{:S(2)}) collective-permute-start(bf16[2,6,6,192]{3,2,1,0:T(8,128)(2,1)S(1)} %get-tuple-element.28), channel_id=1, source_target_pairs={{0,480},{32,0},{64,32},{96,64},{128,96},{160,128},{192,160},{224,1... | collective-permute-start | bytes 82952 | tf_op jit(solution)/shard_map/ppermute | solution.py:16
  138.1 3.7 %collective-permute-start.7 = (bf16[2,3,12,192]{3,2,1,0:T(8,128)(2,1)S(1)}, bf16[2,3,12,192]{3,2,1,0:T(8,128)(2,1)S(1)}, u32[]{:S(2)}, u32[]{:S(2)}) collective-permute-start(bf16[2,3,12,192]{3,2,1,0:T(8,128)(2,1)S(1)} %get-tuple-element.26), channel_id=1, source_target_pairs={{0,28},{4,0},{8,4},{12,8},{16,12},{20,16},{24,20},{28,24},{1,29},{... | collective-permute-start | bytes 82952 | tf_op jit(solution)/shard_map/ppermute | solution.py:16
  141.8 23.0 %collective-permute-start.8 = (bf16[1,6,12,192]{3,2,1,0:T(8,128)(2,1)S(1)}, bf16[1,6,12,192]{3,2,1,0:T(8,128)(2,1)S(1)}, u32[]{:S(2)}, u32[]{:S(2)}) collective-permute-start(bf16[1,6,12,192]{3,2,1,0:T(8,128)(2,1)S(1)} %get-tuple-element.24), channel_id=1, source_target_pairs={{0,3},{1,0},{2,1},{3,2},{4,7},{5,4},{6,5},{7,6},{8,11},{9,8},{10,9... | collective-permute-start | bytes 82952 | tf_op jit(solution)/shard_map/ppermute | solution.py:16
  165.2 0.9 copy-start.6
  166.6 6.7 %collective-permute-start.9 = (bf16[1,6,12,192]{3,2,1,0:T(8,128)(2,1)S(1)}, bf16[1,6,12,192]{3,2,1,0:T(8,128)(2,1)S(1)}, u32[]{:S(2)}, u32[]{:S(2)}) collective-permute-start(bf16[1,6,12,192]{3,2,1,0:T(8,128)(2,1)S(1)} %slice.262), channel_id=1, source_target_pairs={{0,1},{1,2},{2,3},{3,0},{4,5},{5,6},{6,7},{7,4},{8,9},{9,10},{10,1... | collective-permute-start | bytes 82952 | tf_op jit(solution)/shard_map/ppermute | solution.py:16
  173.3 7.2 %collective-permute-start.10 = (bf16[2,3,12,192]{3,2,1,0:T(8,128)(2,1)S(1)}, bf16[2,3,12,192]{3,2,1,0:T(8,128)(2,1)S(1)}, u32[]{:S(2)}, u32[]{:S(2)}) collective-permute-start(bf16[2,3,12,192]{3,2,1,0:T(8,128)(2,1)S(1)} %get-tuple-element.21), channel_id=1, source_target_pairs={{0,4},{4,8},{8,12},{12,16},{16,20},{20,24},{24,28},{28,0},{1,5},{5... | collective-permute-start | bytes 82952 | tf_op jit(solution)/shard_map/ppermute | solution.py:16
  180.6 12.7 %collective-permute-start.11 = (bf16[2,6,6,192]{3,2,1,0:T(8,128)(2,1)S(1)}, bf16[2,6,6,192]{3,2,1,0:T(8,128)(2,1)S(1)}, u32[]{:S(2)}, u32[]{:S(2)}) collective-permute-start(bf16[2,6,6,192]{3,2,1,0:T(8,128)(2,1)S(1)} %fusion.148), channel_id=1, source_target_pairs={{0,32},{32,64},{64,96},{96,128},{128,160},{160,192},{192,224},{224... | collective-permute-start | bytes 82952 | tf_op jit(solution)/shard_map/ppermute | solution.py:16
  193.8 4.1 %copy-start.1 = (s32[8,6,12]{2,0,1:T(8,128)S(1)}, s32[8,6,12]{2,0,1:T(8,128)}, u32[]{:S(2)}) copy-start(s32[8,6,12]{2,0,1:T(8,128)} %param.15) | copy-start | bytes 6916
where the time goes:
time: 202 us; the launch traced here: 198 us
  local copies, waits for them, and re-layouts  72.4 us (36%)
  starting transfers between devices  52.9 us (26%)
  matrix products  37.5 us (19%)
  waiting for transfers between devices  30.2 us (15%)
  other arithmetic  3.95 us (2%)
    another operation x8, local copies, waits for them, and re-layouts, attend(): bias_full[:, None]  65.1 us
    ppermute x12, starting transfers between devices, shifted_2(): return lax.ppermute(value, axis, pairs)  52.9 us
    ppermute x12, waiting for transfers between devices, shifted_2(): return lax.ppermute(value, axis, pairs)  30.2 us
    dot_general x4, matrix products, expand_bias(): jnp.einsum('nhpqrsd,abd->nhpraqsb', shaped, selector, precision=lax.Preci...  16.3 us
    dot_general x4, matrix products, per_device(): jnp.dot(normed_two.reshape(-1, model_width), w_up[block_idx], preferred_e...  8.19 us
    dot_general x4, matrix products, per_device(): jnp.dot(hidden, w_down[block_idx], preferred_element_type=jnp.float32)  5.14 us
  transfers between devices with their start and end apart: 12, of which 9 were waited for; matrix products, arithmetic and copies ran while one was open for 32% of the time, Pallas kernels for 0%

commit v1 on v0

v1 whole, which is shorter than its diff:
```python
import functools

import jax
import jax.numpy as jnp
import numpy as np
from jax import lax
from jax.experimental import pallas as pl
from jax.experimental.pallas import tpu as pltpu
from jax.sharding import PartitionSpec as P

HEADS = 6
HD = 32
WZ = 2
WY = 6
WX = 12
BLOCKS = 4
D = 192
FF = 768
T = WZ * WY * WX
OFFS = 2 * WX - 1
POS = 3312
WIDE = 3328
SLOT = 32
QSLOT = 24
NEG = -1e30
MASK_AT = 192
BF = jnp.bfloat16
F32 = jnp.float32


def octant_maps():
    to_oct = np.zeros((8 * SLOT, T), np.float32)
    back = np.zeros((T, 8 * QSLOT), np.float32)
    for z in range(2):
        for y in range(6):
            for x in range(12):
                yh, yl, xh, xl = y // 3, y % 3, x // 6, x % 6
                tok = z * 72 + y * 12 + x
                slot = yl * 6 + xl
                to_oct[((xh * 2 + yh) * 2 + z) * SLOT + slot, tok] = 1.0
                back[tok, ((z * 2 + yh) * 2 + xh) * QSLOT + slot] = 1.0
    return to_oct, back


def selectors():
    regular = np.zeros((2, 256, 256), np.float32)
    for zq in range(2):
        for yq in range(6):
            for xq in range(12):
                regular[zq, yq * OFFS + 11 - xq, zq * 72 + yq * 12 + xq] = 1.0
    shifted = np.zeros((2, 256, 8 * SLOT), np.float32)
    pad = np.full((1, 8 * SLOT), NEG, np.float32)
    for zk in range(2):
        for yk in range(2):
            for xk in range(2):
                for yl in range(3):
                    for xl in range(6):
                        lane = ((zk * 2 + yk) * 2 + xk) * SLOT + yl * 6 + xl
                        yq, xq = yk * 3 + yl, xk * 6 + xl
                        shifted[zk, yq * OFFS + 11 - xq, lane] = 1.0
                        shifted[zk, MASK_AT + yq, lane] = 1.0
                        pad[0, lane] = 0.0
    return regular.reshape(512, 256), shifted.reshape(512, 8 * SLOT), pad


def dot(a, b):
    return jnp.dot(a, b, preferred_element_type=F32)


def dot_t(a, b):
    return lax.dot_general(a, b, (((1,), (1,)), ((), ())), preferred_element_type=F32)


def layer_norm(values, gain):
    center = values - jnp.mean(values, axis=-1, keepdims=True)
    spread = jnp.mean(center * center, axis=-1, keepdims=True)
    return (center * lax.rsqrt(spread + 1e-05) * gain).astype(BF)


def head_mask(rows):
    lane_head = lax.broadcasted_iota(jnp.int32, (rows, D), 1) // HD
    return [lane_head == h for h in range(HEADS)]


def spread_heads(q, masks):
    return jnp.concatenate([jnp.where(m, q, 0.0) for m in masks], axis=0).astype(BF)


def softmax_mix(scores, keys_v, rows, masks):
    top = jnp.max(scores, axis=-1, keepdims=True)
    terms = jnp.exp(scores - top)
    total = 1.0 / jnp.sum(terms, axis=-1, keepdims=True)
    mixed = dot(terms.astype(BF), keys_v) * total
    out = mixed[0:rows]
    for h in range(1, HEADS):
        out = jnp.where(masks[h], mixed[h * rows : (h + 1) * rows], out)
    return out


def feed_forward(middle, gain, w_up, w_down):
    normed = layer_norm(middle.astype(F32), gain)
    up = dot(normed, w_up)
    hidden = (0.5 * up * (1.0 + lax.erf(up * np.float32(0.5**0.5)))).astype(BF)
    return (middle.astype(F32) + dot(hidden, w_down)).astype(BF)


def regular_block(stream, gain0, gain1, w_qkv, w_out, w_up, w_down, bias):
    normed = layer_norm(stream.astype(F32), gain0)
    qkv = dot(normed, w_qkv)
    q = qkv[:, :D].astype(BF).astype(F32) * np.float32(HD**-0.5)
    k = qkv[:, D : 2 * D].astype(BF)
    v = qkv[:, 2 * D :].astype(BF)
    masks = head_mask(T)
    scores = dot_t(spread_heads(q, masks), k) + jnp.concatenate([bias[0], bias[1, :, : T - 128]], 1)
    heads_out = softmax_mix(scores, v, T, masks).astype(BF)
    attended = dot(heads_out, w_out).astype(BF)
    middle = (stream.astype(F32) + attended.astype(F32)).astype(BF)
    return feed_forward(middle, gain1, w_up, w_down)


def shifted_block(stream, slabs, gain1, w_qkv, w_out, w_up, w_down, bias_ref, back, k_ref, v_ref):
    for i, slab in enumerate(slabs):
        kv = dot(slab[...], w_qkv[:, D:])
        k_ref[i] = kv[:, :D].astype(BF).reshape(4, 4, SLOT, D)
        v_ref[i] = kv[:, D:].astype(BF).reshape(4, 4, SLOT, D)
    own = []
    for z in range(2):
        for yh in range(2):
            row = ((1 + yh) * 4 + 1) * SLOT
            own.append(slabs[1 + z][row : row + 2 * SLOT, :])
    q = dot(jnp.concatenate(own, axis=0), w_qkv[:, :D]).astype(BF).astype(F32) * np.float32(
        HD**-0.5
    )
    masks = head_mask(QSLOT)
    outs = []
    for z in range(2):
        for yh in range(2):
            for xh in range(2):
                w = (z * 2 + yh) * 2 + xh
                ks = k_ref[2 * z : 2 * z + 2, 2 * yh : 2 * yh + 2, 2 * xh : 2 * xh + 2]
                vs = v_ref[2 * z : 2 * z + 2, 2 * yh : 2 * yh + 2, 2 * xh : 2 * xh + 2]
                scores = dot_t(
                    spread_heads(q[w * SLOT : w * SLOT + QSLOT], masks),
                    ks.reshape(8 * SLOT, D),
                )
                rows = slice(w * 144, (w + 1) * 144)
                scores = scores + jnp.concatenate([bias_ref[0, rows], bias_ref[1, rows]], 1)
                outs.append(softmax_mix(scores, vs.reshape(8 * SLOT, D), QSLOT, masks))
    heads_out = jnp.concatenate(outs, axis=0).astype(BF)
    attended = dot(heads_out, w_out).astype(BF)
    attended = dot(back, attended)
    middle = (stream.astype(F32) + attended).astype(BF)
    return feed_forward(middle, gain1, w_up, w_down)


def bias_rolls(lhs_ref, sel):
    parts = [jnp.concatenate([lhs_ref[k, 0], lhs_ref[k, 1]], axis=1) for k in range(2)]
    lane = lax.broadcasted_iota(jnp.int32, parts[0].shape, 1)
    fixed = [jnp.where(lane >= MASK_AT, p, 0.0) for p in parts]
    moving = [jnp.where(lane < MASK_AT, p, 0.0) for p in parts]
    for xp in range(WX):
        rows = [
            (pltpu.roll(m, 256 - xp, 1) if xp else m) + f for m, f in zip(moving, fixed)
        ]
        yield xp, dot(jnp.concatenate(rows, axis=1).astype(BF), sel)


def put(ref, rows, value):
    for k in range(2):
        ref[k, rows, :] = value[:, k * 128 : (k + 1) * 128]


def widened(table, extra):
    wide = jnp.concatenate([table, jnp.zeros((HEADS, 256 - 6 * OFFS), F32)], axis=1)
    return wide if extra is None else wide + extra


def bias_regular_kernel(at, table_ref, sel_ref, out_ref, table, lhs):
    table[...] = table_ref[at].astype(F32)
    for zp in range(2):
        for zq in range(2):
            for yp in range(6):
                start = ((zp * 2 + zq) * 6 + yp) * 6 * OFFS
                part = widened(table[:, start : start + 6 * OFFS], None)
                put(lhs.at[zq], pl.ds(zp * 6 + yp, HEADS, stride=12), part)
    for xp, rows in bias_rolls(lhs, sel_ref[...]):
        put(out_ref, pl.ds(xp, 72, stride=WX), rows)


def bias_shifted_kernel(at, own_ref, south_ref, sel_ref, pad_ref, out_ref, table, lhs):
    lane = lax.broadcasted_iota(jnp.int32, (1, 128), 1)
    in_mask = (lane >= MASK_AT - 128) & (lane < MASK_AT - 122)
    lhs[...] = jnp.zeros_like(lhs)
    for z in range(2):
        for yh in range(2):
            source = own_ref if yh else south_ref
            table[...] = source[at, z].astype(F32)
            tags = table[0:1, WIDE - 128 : WIDE]
            first = POS - (WIDE - 128)
            zp = 1 - z
            for zq in range(2):
                turn = (MASK_AT - 128 - first - zq * 6) % 128
                keys = pltpu.roll(tags, turn, 1)
                for yl in range(3):
                    yp = yl if yh else yl + 3
                    mine = jnp.sum(
                        jnp.where(lane == first + zp * 6 + yp, tags, 0.0), axis=1, keepdims=True
                    )
                    mask = jnp.where(in_mask & (keys != mine), NEG, 0.0)
                    mask = jnp.concatenate([jnp.zeros((1, 128), F32), mask], axis=1)
                    start = ((zp * 2 + zq) * 6 + yp) * 6 * OFFS
                    part = widened(table[:, start : start + 6 * OFFS], mask)
                    put(lhs.at[zq], pl.ds((z * 2 + yh) * QSLOT + yl, HEADS, stride=4), part)
    for xp, rows in bias_rolls(lhs, sel_ref[...]):
        rows = rows + pad_ref[...]
        x = (xp + 6) % 12
        xh, xl = x // 6, x % 6
        for zy in range(4):
            base = (zy * 2 + xh) * 144 + xl
            put(out_ref, pl.ds(base, QSLOT, stride=6), rows[zy * QSLOT : (zy + 1) * QSLOT])


def first_kernel(x, gains, w_qkv, w_out, w_up, w_down, bias, to_oct, stream_out, west, east):
    stream = regular_block(
        x[...], gains[0, 0:1], gains[0, 1:2], w_qkv[0], w_out[0], w_up[0], w_down[0], bias
    )
    stream_out[...] = stream
    normed = layer_norm(stream.astype(F32), gains[1, 0:1])
    octs = dot(to_oct[...], normed).astype(BF)
    west[...] = octs[: 4 * SLOT]
    east[...] = octs[4 * SLOT :]


def middle_kernel(
    stream_in, z0, z1, z2, z3, gains, w_qkv, w_out, w_up, w_down, bias1, bias2, to_oct, back,
    stream_out, west, east, k_ref, v_ref,
):
    stream = shifted_block(
        stream_in[...], (z0, z1, z2, z3), gains[1, 1:2], w_qkv[1], w_out[1], w_up[1], w_down[1],
        bias1, back[...], k_ref, v_ref,
    )
    stream = regular_block(
        stream, gains[2, 0:1], gains[2, 1:2], w_qkv[2], w_out[2], w_up[2], w_down[2], bias2
    )
    stream_out[...] = stream
    normed = layer_norm(stream.astype(F32), gains[3, 0:1])
    octs = dot(to_oct[...], normed).astype(BF)
    west[...] = octs[: 4 * SLOT]
    east[...] = octs[4 * SLOT :]


def last_kernel(
    stream_in, z0, z1, z2, z3, gains, w_qkv, w_out, w_up, w_down, bias3, back, out, k_ref, v_ref
):
    out[...] = shifted_block(
        stream_in[...], (z0, z1, z2, z3), gains[3, 1:2], w_qkv[3], w_out[3], w_up[3], w_down[3],
        bias3, back[...], k_ref, v_ref,
    )


def lat_pack_kernel(recv_w, own_w, own_e, recv_e, south, north):
    for xk, ref in enumerate((recv_w, own_w, own_e, recv_e)):
        half = 2 * SLOT
        south[xk * half : (xk + 1) * half] = ref[:half]
        north[xk * half : (xk + 1) * half] = ref[half:]


def lev_pack_kernel(recv_s, south, north, recv_n, down, up):
    for yk, ref in enumerate((recv_s, south, north, recv_n)):
        for xk in range(4):
            at = (yk * 4 + xk) * SLOT
            down[at : at + SLOT] = ref[2 * xk * SLOT : (2 * xk + 1) * SLOT]
            up[at : at + SLOT] = ref[(2 * xk + 1) * SLOT : (2 * xk + 2) * SLOT]


def call(kernel, outs, *args, scratch=(), flops=0, limit=20):
    return pl.pallas_call(
        kernel,
        out_shape=outs,
        scratch_shapes=list(scratch),
        compiler_params=pltpu.CompilerParams(vmem_limit_bytes=limit << 20),
        cost_estimate=pl.CostEstimate(flops=flops, bytes_accessed=1 << 20, transcendentals=0),
    )(*args)


def shape(*dims, dtype=BF):
    return jax.ShapeDtypeStruct(dims, dtype)


def move(value, axis, steps):
    count = lax.axis_size(axis)
    return lax.ppermute(value, axis, [(i, (i + steps) % count) for i in range(count)])


def halo(west, east):
    recv_e = move(west, "lon", -1)
    recv_w = move(east, "lon", 1)
    south, north = call(
        lat_pack_kernel, [shape(8 * SLOT, D)] * 2, recv_w, west, east, recv_e, limit=4
    )
    recv_n = move(south, "lat", -1)
    recv_s = move(north, "lat", 1)
    down, up = call(
        lev_pack_kernel, [shape(16 * SLOT, D)] * 2, recv_s, south, north, recv_n, limit=4
    )
    recv_u = move(down, "lev", -1)
    recv_d = move(up, "lev", 1)
    return recv_d, down, up, recv_u


def per_device(fields, w_qkv, w_out, w_up, w_down, gains, bias_table, labels):
    level = lax.axis_index("lev")
    below = (level + 3) % 4
    to_oct_np, back_np = octant_maps()
    sel_reg, sel_shift, pad = selectors()
    to_oct = jnp.asarray(to_oct_np, BF)
    back = jnp.asarray(back_np, BF)
    sel_reg = jnp.asarray(sel_reg, BF)
    sel_shift = jnp.asarray(sel_shift, BF)
    pad = jnp.asarray(pad, F32)

    lab = labels[:, :, 0].astype(BF).reshape(4, 2 * WY)
    picked = []
    for window in (below, level):
        rows = lax.dynamic_index_in_dim(bias_table[:, :, 0], window, 1, keepdims=False)
        tags = lax.dynamic_index_in_dim(lab, window, 0, keepdims=False)
        tags = jnp.broadcast_to(tags, (BLOCKS, HEADS, 2 * WY))
        rows = jnp.concatenate([rows, tags], axis=-1)
        picked.append(jnp.pad(rows, ((0, 0), (0, 0), (0, WIDE - POS - 2 * WY))))
    own = picked[1]
    shifted_own = jnp.stack([jnp.stack([p[b] for p in picked]) for b in (1, 3)])
    shifted_south = move(shifted_own, "lat", 1)

    table_scratch = pltpu.VMEM((HEADS, WIDE), F32)

    def regular_bias(block):
        return call(
            functools.partial(bias_regular_kernel, block),
            shape(2, HEADS * T, 128, dtype=F32), own, sel_reg,
            scratch=[table_scratch, pltpu.VMEM((2, 2, 72, 128), F32)], flops=1 << 30,
        )

    def shifted_bias(at):
        return call(
            functools.partial(bias_shifted_kernel, at),
            shape(2, 8 * 144, 128, dtype=F32), shifted_own, shifted_south, sel_shift, pad,
            scratch=[table_scratch, pltpu.VMEM((2, 2, 96, 128), F32)], flops=1 << 30,
        )

    kv_scratch = [pltpu.VMEM((4, 4, 4, SLOT, D), BF)] * 2
    weights = (gains, w_qkv, w_out, w_up, w_down)
    stream, west, east = call(
        first_kernel, [shape(T, D), shape(4 * SLOT, D), shape(4 * SLOT, D)],
        fields.reshape(T, D), *weights, regular_bias(0), to_oct, flops=1 << 31,
    )
    slabs = halo(west, east)
    stream, west, east = call(
        middle_kernel, [shape(T, D), shape(4 * SLOT, D), shape(4 * SLOT, D)],
        stream, *slabs, *weights, shifted_bias(0), regular_bias(2), to_oct, back,
        scratch=kv_scratch, flops=1 << 31,
    )
    slabs = halo(west, east)
    stream = call(
        last_kernel, shape(T, D), stream, *slabs, *weights, shifted_bias(1), back,
        scratch=kv_scratch, flops=1 << 31,
    )
    return stream.reshape(2, 6, 12, D)


def solution(mesh):
    in_specs = (
        P("lev", "lat", "lon", None),
        P(),
        P(),
        P(),
        P(),
        P(),
        P(None, None, "lat", None, None),
        P(None, "lat", "lon"),
    )
    return jax.shard_map(
        per_device,
        mesh=mesh,
        in_specs=in_specs,
        out_specs=P("lev", "lat", "lon", None),
        check_vma=False,
    )
```

time: 202 us -> 101 us (0.50)
  the two profiles are of different devices: /device:TPU:6 before, /device:TPU:255 now
where the time goes in v1:
time: 101 us; the launch traced here: 100 us
  starting transfers between devices  48.9 us (48%)
  waiting for transfers between devices  30.2 us (30%)
  Pallas kernels  14.4 us (14%)
  local copies, waits for them, and re-layouts  6 us (6%)
    ppermute x13, starting transfers between devices, move(): lax.ppermute(value, axis, [(i, (i + steps) % count) for i in range(count)])  48.9 us
    ppermute x13, waiting for transfers between devices, move(): lax.ppermute(value, axis, [(i, (i + steps) % count) for i in range(count)])  30.2 us
    pallas_call x11, Pallas kernels, call(): pl.pallas_call(kernel, out_shape=outs, scratch_shapes=list(scratch), comp...  14.4 us
    unnamed x24, local copies, waits for them, and re-layouts  3.85 us
  transfers between devices with their start and end apart: 13, of which 10 were waited for; matrix products, arithmetic and copies ran while one was open for 0% of the time, Pallas kernels for 3%

profile of v1, /device:TPU:255, one launch (start us, length us, event | category | flops | bytes accessed | tf_op | source)
XLA Modules:
  0.0 100.2 jit_solution(3708263568635649735)
XLA Ops:
  0.9 1.7 %copy.24.w_down = bf16[4,768,192]{2,1,0:T(8,128)(2,1)S(1)} copy(bf16[4,768,192]{1,2,0:T(8,128)(2,1)} %param.17) | data formatting | bytes 2359296 | tf_op args[4]
  6.0 2.0 %shard_map.128 = (bf16[144,192]{1,0:T(8,128)(2,1)S(1)}, bf16[128,192]{1,0:T(8,128)(2,1)S(1)}, bf16[128,192]{1,0:T(8,128)(2,1)S(1)}) custom-call(bf16[144,192]{1,0:T(8,128)(2,1)S(1)} %reshape.13.x, f32[4,2,192]{2,1,0:T(2,128)S(1)} %copy-done.3, bf16[4,192,576]{2,1,0:T(8,128)(2,1)S(1)} %copy-done.1, bf16[4,192,192]{2,1,0:T(8,128)(2,1)S(1)} %copy-done.2, ...), custom_call_target="tpu_custom_call" | custom-call | flops 2147483648 | bytes 1048576 | tf_op jit(solution)/shard_map/pallas_call | solution.py:277
  8.0 7.5 %collective-permute-start = (bf16[128,192]{1,0:T(8,128)(2,1)S(1)}, bf16[128,192]{1,0:T(8,128)(2,1)S(1)}, u32[]{:S(2)}, u32[]{:S(2)}) collective-permute-start(bf16[128,192]{1,0:T(8,128)(2,1)S(1)} %get-tuple-element.20.own_e), channel_id=1, source_target_pairs={{0,32},{32,64},{64,96},{96,128},{128,160},{160,192},{192,224},{224... | collective-permute-start | bytes 147464 | tf_op jit(solution)/shard_map/ppermute | solution.py:292
  15.4 1.9 %collective-permute-start.1 = (bf16[128,192]{1,0:T(8,128)(2,1)S(1)}, bf16[128,192]{1,0:T(8,128)(2,1)S(1)}, u32[]{:S(2)}, u32[]{:S(2)}) collective-permute-start(bf16[128,192]{1,0:T(8,128)(2,1)S(1)} %get-tuple-element.21.own_w), channel_id=1, source_target_pairs={{0,480},{32,0},{64,32},{96,64},{128,96},{160,128},{192,160},{224,1... | collective-permute-start | bytes 147464 | tf_op jit(solution)/shard_map/ppermute | solution.py:292
  17.7 9.1 %collective-permute-done.1.recv_e = bf16[128,192]{1,0:T(8,128)(2,1)S(1)} collective-permute-done((bf16[128,192]{1,0:T(8,128)(2,1)S(1)}, bf16[128,192]{1,0:T(8,128)(2,1)S(1)}, u32[]{:S(2)}, u32[]{:S(2)}) %collective-permute-start.1) | collective-permute-done | bytes 49184 | tf_op jit(solution)/shard_map/ppermute | solution.py:292
  26.8 4.2 %collective-permute-start.2 = (bf16[256,192]{1,0:T(8,128)(2,1)S(1)}, bf16[256,192]{1,0:T(8,128)(2,1)S(1)}, u32[]{:S(2)}, u32[]{:S(2)}) collective-permute-start(bf16[256,192]{1,0:T(8,128)(2,1)S(1)} %get-tuple-element.22.north), channel_id=1, source_target_pairs={{0,4},{4,8},{8,12},{12,16},{16,20},{20,24},{24,28},{28,0},{1,5},{5... | collective-permute-start | bytes 294920 | tf_op jit(solution)/shard_map/ppermute | solution.py:292
  31.0 1.9 %collective-permute-start.3 = (bf16[256,192]{1,0:T(8,128)(2,1)S(1)}, bf16[256,192]{1,0:T(8,128)(2,1)S(1)}, u32[]{:S(2)}, u32[]{:S(2)}) collective-permute-start(bf16[256,192]{1,0:T(8,128)(2,1)S(1)} %get-tuple-element.23.south), channel_id=1, source_target_pairs={{0,28},{4,0},{8,4},{12,8},{16,12},{20,16},{24,20},{28,24},{1,29},{... | collective-permute-start | bytes 294920 | tf_op jit(solution)/shard_map/ppermute | solution.py:292
  33.0 5.4 %collective-permute-start.6 = (bf16[2,2,6,3328]{3,2,1,0:T(8,128)(2,1)S(1)}, bf16[2,2,6,3328]{3,2,1,0:T(8,128)(2,1)S(1)}, u32[]{:S(2)}, u32[]{:S(2)}) collective-permute-start(bf16[2,2,6,3328]{3,2,1,0:T(8,128)(2,1)S(1)} %pad_maximum_fusion.2.own_ref), channel_id=1, source_target_pairs={{0,4},{4,8},{8,12},{12,16},{16,20},{20,24},{24,28},{28,0},{1,5},{5... | collective-permute-start | bytes 479240 | tf_op jit(solution)/shard_map/ppermute | solution.py:292
  38.5 1.7 %collective-permute-done.3.recv_n = bf16[256,192]{1,0:T(8,128)(2,1)S(1)} collective-permute-done((bf16[256,192]{1,0:T(8,128)(2,1)S(1)}, bf16[256,192]{1,0:T(8,128)(2,1)S(1)}, u32[]{:S(2)}, u32[]{:S(2)}) %collective-permute-start.3) | collective-permute-done | bytes 98336 | tf_op jit(solution)/shard_map/ppermute | solution.py:292
  40.2 2.1 %collective-permute-start.4 = (bf16[512,192]{1,0:T(8,128)(2,1)S(1)}, bf16[512,192]{1,0:T(8,128)(2,1)S(1)}, u32[]{:S(2)}, u32[]{:S(2)}) collective-permute-start(bf16[512,192]{1,0:T(8,128)(2,1)S(1)} %get-tuple-element.24.z2), channel_id=1, source_target_pairs={{0,1},{1,2},{2,3},{3,0},{4,5},{5,6},{6,7},{7,4},{8,9},{9,10},{10,1... | collective-permute-start | bytes 589832 | tf_op jit(solution)/shard_map/ppermute | solution.py:292
  42.3 3.3 %collective-permute-start.5 = (bf16[512,192]{1,0:T(8,128)(2,1)S(1)}, bf16[512,192]{1,0:T(8,128)(2,1)S(1)}, u32[]{:S(2)}, u32[]{:S(2)}) collective-permute-start(bf16[512,192]{1,0:T(8,128)(2,1)S(1)} %get-tuple-element.25.z1), channel_id=1, source_target_pairs={{0,3},{1,0},{2,1},{3,2},{4,7},{5,4},{6,5},{7,6},{8,11},{9,8},{10,9... | collective-permute-start | bytes 589832 | tf_op jit(solution)/shard_map/ppermute | solution.py:292
  47.9 3.5 %collective-permute-done.5.z3 = bf16[512,192]{1,0:T(8,128)(2,1)S(1)} collective-permute-done((bf16[512,192]{1,0:T(8,128)(2,1)S(1)}, bf16[512,192]{1,0:T(8,128)(2,1)S(1)}, u32[]{:S(2)}, u32[]{:S(2)}) %collective-permute-start.5) | collective-permute-done | bytes 196640 | tf_op jit(solution)/shard_map/ppermute | solution.py:292
  51.4 5.4 %shard_map.133 = (bf16[144,192]{1,0:T(8,128)(2,1)S(1)}, bf16[128,192]{1,0:T(8,128)(2,1)S(1)}, bf16[128,192]{1,0:T(8,128)(2,1)S(1)}) custom-call(bf16[144,192]{1,0:T(8,128)(2,1)S(1)} %get-tuple-element.19.stream_in, bf16[512,192]{1,0:T(8,128)(2,1)S(1)} %collective-permute-done.4.z0, bf16[512,192]{1,0:T(8,128)(2,1)S(1)} %get-tuple-element.25.z1, ...), custom_call_target="tpu_custom_call" | custom-call | flops 2147483648 | bytes 1048576 | tf_op jit(solution)/shard_map/pallas_call | solution.py:277
  56.8 3.5 %collective-permute-start.7 = (bf16[128,192]{1,0:T(8,128)(2,1)S(1)}, bf16[128,192]{1,0:T(8,128)(2,1)S(1)}, u32[]{:S(2)}, u32[]{:S(2)}) collective-permute-start(bf16[128,192]{1,0:T(8,128)(2,1)S(1)} %get-tuple-element.27.own_e), channel_id=1, source_target_pairs={{0,32},{32,64},{64,96},{96,128},{128,160},{160,192},{192,224},{224... | collective-permute-start | bytes 147464 | tf_op jit(solution)/shard_map/ppermute | solution.py:292
  60.3 5.7 %collective-permute-start.8 = (bf16[128,192]{1,0:T(8,128)(2,1)S(1)}, bf16[128,192]{1,0:T(8,128)(2,1)S(1)}, u32[]{:S(2)}, u32[]{:S(2)}) collective-permute-start(bf16[128,192]{1,0:T(8,128)(2,1)S(1)} %get-tuple-element.28.own_w), channel_id=1, source_target_pairs={{0,480},{32,0},{64,32},{96,64},{128,96},{160,128},{192,160},{224,1... | collective-permute-start | bytes 147464 | tf_op jit(solution)/shard_map/ppermute | solution.py:292
  66.0 1.2 %collective-permute-done.7.recv_w = bf16[128,192]{1,0:T(8,128)(2,1)S(1)} collective-permute-done((bf16[128,192]{1,0:T(8,128)(2,1)S(1)}, bf16[128,192]{1,0:T(8,128)(2,1)S(1)}, u32[]{:S(2)}, u32[]{:S(2)}) %collective-permute-start.7) | collective-permute-done | bytes 49184 | tf_op jit(solution)/shard_map/ppermute | solution.py:292
  67.2 4.4 %collective-permute-done.8.recv_e = bf16[128,192]{1,0:T(8,128)(2,1)S(1)} collective-permute-done((bf16[128,192]{1,0:T(8,128)(2,1)S(1)}, bf16[128,192]{1,0:T(8,128)(2,1)S(1)}, u32[]{:S(2)}, u32[]{:S(2)}) %collective-permute-start.8) | collective-permute-done | bytes 49184 | tf_op jit(solution)/shard_map/ppermute | solution.py:292
  71.6 6.0 %collective-permute-start.9 = (bf16[256,192]{1,0:T(8,128)(2,1)S(1)}, bf16[256,192]{1,0:T(8,128)(2,1)S(1)}, u32[]{:S(2)}, u32[]{:S(2)}) collective-permute-start(bf16[256,192]{1,0:T(8,128)(2,1)S(1)} %get-tuple-element.29.north), channel_id=1, source_target_pairs={{0,4},{4,8},{8,12},{12,16},{16,20},{20,24},{24,28},{28,0},{1,5},{5... | collective-permute-start | bytes 294920 | tf_op jit(solution)/shard_map/ppermute | solution.py:292
  77.6 1.9 %collective-permute-start.10 = (bf16[256,192]{1,0:T(8,128)(2,1)S(1)}, bf16[256,192]{1,0:T(8,128)(2,1)S(1)}, u32[]{:S(2)}, u32[]{:S(2)}) collective-permute-start(bf16[256,192]{1,0:T(8,128)(2,1)S(1)} %get-tuple-element.30.south), channel_id=1, source_target_pairs={{0,28},{4,0},{8,4},{12,8},{16,12},{20,16},{24,20},{28,24},{1,29},{... | collective-permute-start | bytes 294920 | tf_op jit(solution)/shard_map/ppermute | solution.py:292
  80.6 5.1 %collective-permute-done.10.recv_n = bf16[256,192]{1,0:T(8,128)(2,1)S(1)} collective-permute-done((bf16[256,192]{1,0:T(8,128)(2,1)S(1)}, bf16[256,192]{1,0:T(8,128)(2,1)S(1)}, u32[]{:S(2)}, u32[]{:S(2)}) %collective-permute-start.10) | collective-permute-done | bytes 98336 | tf_op jit(solution)/shard_map/ppermute | solution.py:292
  85.7 1.9 %collective-permute-start.11 = (bf16[512,192]{1,0:T(8,128)(2,1)S(1)}, bf16[512,192]{1,0:T(8,128)(2,1)S(1)}, u32[]{:S(2)}, u32[]{:S(2)}) collective-permute-start(bf16[512,192]{1,0:T(8,128)(2,1)S(1)} %get-tuple-element.31.z2), channel_id=1, source_target_pairs={{0,1},{1,2},{2,3},{3,0},{4,5},{5,6},{6,7},{7,4},{8,9},{9,10},{10,1... | collective-permute-start | bytes 589832 | tf_op jit(solution)/shard_map/ppermute | solution.py:292
  87.6 3.5 %collective-permute-start.12 = (bf16[512,192]{1,0:T(8,128)(2,1)S(1)}, bf16[512,192]{1,0:T(8,128)(2,1)S(1)}, u32[]{:S(2)}, u32[]{:S(2)}) collective-permute-start(bf16[512,192]{1,0:T(8,128)(2,1)S(1)} %get-tuple-element.32.z1), channel_id=1, source_target_pairs={{0,3},{1,0},{2,1},{3,2},{4,7},{5,4},{6,5},{7,6},{8,11},{9,8},{10,9... | collective-permute-start | bytes 589832 | tf_op jit(solution)/shard_map/ppermute | solution.py:292
  92.8 3.1 %collective-permute-done.12.z3 = bf16[512,192]{1,0:T(8,128)(2,1)S(1)} collective-permute-done((bf16[512,192]{1,0:T(8,128)(2,1)S(1)}, bf16[512,192]{1,0:T(8,128)(2,1)S(1)}, u32[]{:S(2)}, u32[]{:S(2)}) %collective-permute-start.12) | collective-permute-done | bytes 196640 | tf_op jit(solution)/shard_map/ppermute | solution.py:292
  95.9 3.5 %shard_map.137 = bf16[144,192]{1,0:T(8,128)(2,1)S(1)} custom-call(bf16[144,192]{1,0:T(8,128)(2,1)S(1)} %get-tuple-element.26.stream_in, bf16[512,192]{1,0:T(8,128)(2,1)S(1)} %collective-permute-done.11.z0, bf16[512,192]{1,0:T(8,128)(2,1)S(1)} %get-tuple-element.32.z1, bf16[512,192]{1,0:T(8,128)(2,1)S(1)} %get-tuple-element.31.z2, ...), custom_call_target="tpu_custom_call" | custom-call | flops 2147483648 | bytes 1048576 | tf_op jit(solution)/shard_map/pallas_call | solution.py:277
  (58 shorter events, 10.3 us)
Async XLA Ops:
  0.9 1.7 %copy-start.9 = (bf16[4,4,1,6,3312]{4,1,3,2,0:T(4,128)(2,1)S(1)}, bf16[4,4,1,6,3312]{4,1,3,2,0:T(4,128)(2,1)}, u32[]{:S(2)}) copy-start(bf16[4,4,1,6,3312]{4,1,3,2,0:T(4,128)(2,1)} %param.19) | copy-start | bytes 1907716
  2.7 0.9 copy-start.10
  3.4 1.0 copy-start.5
  4.3 1.3 %copy-start = (bf16[4,192,768]{2,1,0:T(8,128)(2,1)S(1)}, bf16[4,192,768]{2,1,0:T(8,128)(2,1)}, u32[]{:S(2)}) copy-start(bf16[4,192,768]{2,1,0:T(8,128)(2,1)} %w_up.5) | copy-start | bytes 3538948
  4.3 1.6 %copy-start.1 = (bf16[4,192,576]{2,1,0:T(8,128)(2,1)S(1)}, bf16[4,192,576]{2,1,0:T(8,128)(2,1)}, u32[]{:S(2)}) copy-start(bf16[4,192,576]{2,1,0:T(8,128)(2,1)} %w_qkv.5) | copy-start | bytes 2654212
  4.3 1.6 %copy-start.2 = (bf16[4,192,192]{2,1,0:T(8,128)(2,1)S(1)}, bf16[4,192,192]{2,1,0:T(8,128)(2,1)}, u32[]{:S(2)}) copy-start(bf16[4,192,192]{2,1,0:T(8,128)(2,1)} %w_out.5) | copy-start | bytes 884740
  4.3 1.6 %copy-start.3 = (f32[4,2,192]{2,1,0:T(2,128)S(1)}, f32[4,2,192]{2,1,0:T(2,128)}, u32[]{:S(2)}) copy-start(f32[4,2,192]{2,1,0:T(2,128)} %gains.5) | copy-start | bytes 18436
  4.3 1.7 %copy-start.6 = (bf16[256,144]{1,0:T(8,128)(2,1)S(1)}, bf16[256,144]{1,0:T(8,128)(2,1)}, u32[]{:S(2)}) copy-start(bf16[256,144]{1,0:T(8,128)(2,1)} %constant.45.clone.to_oct) | copy-start | bytes 221188
  8.0 9.7 %collective-permute-start = (bf16[128,192]{1,0:T(8,128)(2,1)S(1)}, bf16[128,192]{1,0:T(8,128)(2,1)S(1)}, u32[]{:S(2)}, u32[]{:S(2)}) collective-permute-start(bf16[128,192]{1,0:T(8,128)(2,1)S(1)} %get-tuple-element.20.own_e), channel_id=1, source_target_pairs={{0,32},{32,64},{64,96},{96,128},{128,160},{160,192},{192,224},{224... | collective-permute-start | bytes 147464 | tf_op jit(solution)/shard_map/ppermute | solution.py:292
  15.4 11.4 %collective-permute-start.1 = (bf16[128,192]{1,0:T(8,128)(2,1)S(1)}, bf16[128,192]{1,0:T(8,128)(2,1)S(1)}, u32[]{:S(2)}, u32[]{:S(2)}) collective-permute-start(bf16[128,192]{1,0:T(8,128)(2,1)S(1)} %get-tuple-element.21.own_w), channel_id=1, source_target_pairs={{0,480},{32,0},{64,32},{96,64},{128,96},{160,128},{192,160},{224,1... | collective-permute-start | bytes 147464 | tf_op jit(solution)/shard_map/ppermute | solution.py:292
  26.8 11.7 %collective-permute-start.2 = (bf16[256,192]{1,0:T(8,128)(2,1)S(1)}, bf16[256,192]{1,0:T(8,128)(2,1)S(1)}, u32[]{:S(2)}, u32[]{:S(2)}) collective-permute-start(bf16[256,192]{1,0:T(8,128)(2,1)S(1)} %get-tuple-element.22.north), channel_id=1, source_target_pairs={{0,4},{4,8},{8,12},{12,16},{16,20},{20,24},{24,28},{28,0},{1,5},{5... | collective-permute-start | bytes 294920 | tf_op jit(solution)/shard_map/ppermute | solution.py:292
  31.0 9.1 %collective-permute-start.3 = (bf16[256,192]{1,0:T(8,128)(2,1)S(1)}, bf16[256,192]{1,0:T(8,128)(2,1)S(1)}, u32[]{:S(2)}, u32[]{:S(2)}) collective-permute-start(bf16[256,192]{1,0:T(8,128)(2,1)S(1)} %get-tuple-element.23.south), channel_id=1, source_target_pairs={{0,28},{4,0},{8,4},{12,8},{16,12},{20,16},{24,20},{28,24},{1,29},{... | collective-permute-start | bytes 294920 | tf_op jit(solution)/shard_map/ppermute | solution.py:292
  33.0 13.4 %collective-permute-start.6 = (bf16[2,2,6,3328]{3,2,1,0:T(8,128)(2,1)S(1)}, bf16[2,2,6,3328]{3,2,1,0:T(8,128)(2,1)S(1)}, u32[]{:S(2)}, u32[]{:S(2)}) collective-permute-start(bf16[2,2,6,3328]{3,2,1,0:T(8,128)(2,1)S(1)} %pad_maximum_fusion.2.own_ref), channel_id=1, source_target_pairs={{0,4},{4,8},{8,12},{12,16},{16,20},{20,24},{24,28},{28,0},{1,5},{5... | collective-permute-start | bytes 479240 | tf_op jit(solution)/shard_map/ppermute | solution.py:292
  40.2 7.7 %collective-permute-start.4 = (bf16[512,192]{1,0:T(8,128)(2,1)S(1)}, bf16[512,192]{1,0:T(8,128)(2,1)S(1)}, u32[]{:S(2)}, u32[]{:S(2)}) collective-permute-start(bf16[512,192]{1,0:T(8,128)(2,1)S(1)} %get-tuple-element.24.z2), channel_id=1, source_target_pairs={{0,1},{1,2},{2,3},{3,0},{4,5},{5,6},{6,7},{7,4},{8,9},{9,10},{10,1... | collective-permute-start | bytes 589832 | tf_op jit(solution)/shard_map/ppermute | solution.py:292
  42.3 4.1 %copy-start.4 = (bf16[512,256]{1,0:T(8,128)(2,1)S(1)}, bf16[512,256]{1,0:T(8,128)(2,1)}, u32[]{:S(2)}) copy-start(bf16[512,256]{1,0:T(8,128)(2,1)} %constant.48.clone.sel_ref) | copy-start | bytes 786436
  42.3 4.1 %copy-start.8 = (f32[1,256]{1,0:T(1,128)S(1)}, f32[1,256]{1,0:T(1,128)}, u32[]{:S(2)}) copy-start(f32[1,256]{1,0:T(1,128)} %constant.49.clone.pad_ref) | copy-start | bytes 3076
  42.3 9.1 %collective-permute-start.5 = (bf16[512,192]{1,0:T(8,128)(2,1)S(1)}, bf16[512,192]{1,0:T(8,128)(2,1)S(1)}, u32[]{:S(2)}, u32[]{:S(2)}) collective-permute-start(bf16[512,192]{1,0:T(8,128)(2,1)S(1)} %get-tuple-element.25.z1), channel_id=1, source_target_pairs={{0,3},{1,0},{2,1},{3,2},{4,7},{5,4},{6,5},{7,6},{8,11},{9,8},{10,9... | collective-permute-start | bytes 589832 | tf_op jit(solution)/shard_map/ppermute | solution.py:292
  46.4 5.0 %copy-start.7 = (bf16[144,192]{1,0:T(8,128)(2,1)S(1)}, bf16[144,192]{1,0:T(8,128)(2,1)}, u32[]{:S(2)}) copy-start(bf16[144,192]{1,0:T(8,128)(2,1)} %constant.46.clone.back) | copy-start | bytes 165892
  56.8 10.4 %collective-permute-start.7 = (bf16[128,192]{1,0:T(8,128)(2,1)S(1)}, bf16[128,192]{1,0:T(8,128)(2,1)S(1)}, u32[]{:S(2)}, u32[]{:S(2)}) collective-permute-start(bf16[128,192]{1,0:T(8,128)(2,1)S(1)} %get-tuple-element.27.own_e), channel_id=1, source_target_pairs={{0,32},{32,64},{64,96},{96,128},{128,160},{160,192},{192,224},{224... | collective-permute-start | bytes 147464 | tf_op jit(solution)/shard_map/ppermute | solution.py:292
  60.3 11.3 %collective-permute-start.8 = (bf16[128,192]{1,0:T(8,128)(2,1)S(1)}, bf16[128,192]{1,0:T(8,128)(2,1)S(1)}, u32[]{:S(2)}, u32[]{:S(2)}) collective-permute-start(bf16[128,192]{1,0:T(8,128)(2,1)S(1)} %get-tuple-element.28.own_w), channel_id=1, source_target_pairs={{0,480},{32,0},{64,32},{96,64},{128,96},{160,128},{192,160},{224,1... | collective-permute-start | bytes 147464 | tf_op jit(solution)/shard_map/ppermute | solution.py:292
  71.6 9.0 %collective-permute-start.9 = (bf16[256,192]{1,0:T(8,128)(2,1)S(1)}, bf16[256,192]{1,0:T(8,128)(2,1)S(1)}, u32[]{:S(2)}, u32[]{:S(2)}) collective-permute-start(bf16[256,192]{1,0:T(8,128)(2,1)S(1)} %get-tuple-element.29.north), channel_id=1, source_target_pairs={{0,4},{4,8},{8,12},{12,16},{16,20},{20,24},{24,28},{28,0},{1,5},{5... | collective-permute-start | bytes 294920 | tf_op jit(solution)/shard_map/ppermute | solution.py:292
  77.6 8.1 %collective-permute-start.10 = (bf16[256,192]{1,0:T(8,128)(2,1)S(1)}, bf16[256,192]{1,0:T(8,128)(2,1)S(1)}, u32[]{:S(2)}, u32[]{:S(2)}) collective-permute-start(bf16[256,192]{1,0:T(8,128)(2,1)S(1)} %get-tuple-element.30.south), channel_id=1, source_target_pairs={{0,28},{4,0},{8,4},{12,8},{16,12},{20,16},{24,20},{28,24},{1,29},{... | collective-permute-start | bytes 294920 | tf_op jit(solution)/shard_map/ppermute | solution.py:292
  85.7 7.1 %collective-permute-start.11 = (bf16[512,192]{1,0:T(8,128)(2,1)S(1)}, bf16[512,192]{1,0:T(8,128)(2,1)S(1)}, u32[]{:S(2)}, u32[]{:S(2)}) collective-permute-start(bf16[512,192]{1,0:T(8,128)(2,1)S(1)} %get-tuple-element.31.z2), channel_id=1, source_target_pairs={{0,1},{1,2},{2,3},{3,0},{4,5},{5,6},{6,7},{7,4},{8,9},{9,10},{10,1... | collective-permute-start | bytes 589832 | tf_op jit(solution)/shard_map/ppermute | solution.py:292
  87.6 8.3 %collective-permute-start.12 = (bf16[512,192]{1,0:T(8,128)(2,1)S(1)}, bf16[512,192]{1,0:T(8,128)(2,1)S(1)}, u32[]{:S(2)}, u32[]{:S(2)}) collective-permute-start(bf16[512,192]{1,0:T(8,128)(2,1)S(1)} %get-tuple-element.32.z1), channel_id=1, source_target_pairs={{0,3},{1,0},{2,1},{3,2},{4,7},{5,4},{6,5},{7,6},{8,11},{9,8},{10,9... | collective-permute-start | bytes 589832 | tf_op jit(solution)/shard_map/ppermute | solution.py:292

commit v2 on v1

v2 whole, which is shorter than its diff:
```python
import functools

import jax
import jax.numpy as jnp
import numpy as np
from jax import lax
from jax.experimental import pallas as pl
from jax.experimental.pallas import tpu as pltpu
from jax.sharding import PartitionSpec as P

HEADS = 6
HD = 32
WZ = 2
WY = 6
WX = 12
BLOCKS = 4
D = 192
FF = 768
T = WZ * WY * WX
OFFS = 2 * WX - 1
POS = 3312
SLOT = 24
PAIR = 2 * SLOT
NEG = -1e30
MASK_AT = 192
BF = jnp.bfloat16
F32 = jnp.float32


def octant_maps():
    to_oct = np.zeros((8 * SLOT, T), np.float32)
    back = np.zeros((T, 8 * SLOT), np.float32)
    for z in range(2):
        for y in range(6):
            for x in range(12):
                yh, yl, xh, xl = y // 3, y % 3, x // 6, x % 6
                tok = z * 72 + y * 12 + x
                slot = yl * 6 + xl
                to_oct[((xh * 2 + yh) * 2 + z) * SLOT + slot, tok] = 1.0
                back[tok, ((z * 2 + yh) * 2 + xh) * SLOT + slot] = 1.0
    return to_oct, back


def selectors():
    regular = np.zeros((2, 256, 256), np.float32)
    for zq in range(2):
        for yq in range(6):
            for xq in range(12):
                regular[zq, yq * OFFS + 11 - xq, zq * 72 + yq * 12 + xq] = 1.0
    shifted = np.zeros((2, 256, 256), np.float32)
    pad = np.full((1, 256), NEG, np.float32)
    for zk in range(2):
        for yk in range(2):
            for xk in range(2):
                for yl in range(3):
                    for xl in range(6):
                        lane = ((zk * 2 + yk) * 2 + xk) * SLOT + yl * 6 + xl
                        yq, xq = yk * 3 + yl, xk * 6 + xl
                        shifted[zk, yq * OFFS + 11 - xq, lane] = 1.0
                        shifted[zk, MASK_AT + yq, lane] = 1.0
                        pad[0, lane] = 0.0
    return regular.reshape(512, 256), shifted.reshape(512, 256), pad


def dot(a, b):
    return jnp.dot(a, b, preferred_element_type=F32)


def dot_t(a, b):
    return lax.dot_general(a, b, (((1,), (1,)), ((), ())), preferred_element_type=F32)


def layer_norm(values, gain):
    center = values - jnp.mean(values, axis=-1, keepdims=True)
    spread = jnp.mean(center * center, axis=-1, keepdims=True)
    return (center * lax.rsqrt(spread + 1e-05) * gain).astype(BF)


def head_mask(rows):
    lane_head = lax.broadcasted_iota(jnp.int32, (rows, D), 1) // HD
    return [lane_head == h for h in range(HEADS)]


def spread_heads(q, masks):
    return jnp.concatenate([jnp.where(m, q, 0.0) for m in masks], axis=0).astype(BF)


def softmax_mix(scores, keys_v, rows, masks):
    top = jnp.max(scores, axis=-1, keepdims=True)
    terms = jnp.exp(scores - top)
    total = 1.0 / jnp.sum(terms, axis=-1, keepdims=True)
    mixed = dot(terms.astype(BF), keys_v) * total
    out = mixed[0:rows]
    for h in range(1, HEADS):
        out = jnp.where(masks[h], mixed[h * rows : (h + 1) * rows], out)
    return out


def feed_forward(middle, gain, w_up, w_down):
    normed = layer_norm(middle.astype(F32), gain)
    up = dot(normed, w_up)
    hidden = (0.5 * up * (1.0 + lax.erf(up * np.float32(0.5**0.5)))).astype(BF)
    return (middle.astype(F32) + dot_t(hidden, w_down)).astype(BF)


def regular_block(stream, gain0, gain1, w_qkv, w_out, w_up, w_down, bias):
    normed = layer_norm(stream.astype(F32), gain0)
    qkv = dot(normed, w_qkv)
    q = qkv[:, :D].astype(BF).astype(F32) * np.float32(HD**-0.5)
    k = qkv[:, D : 2 * D].astype(BF)
    v = qkv[:, 2 * D :].astype(BF)
    masks = head_mask(T)
    bias = jnp.concatenate([bias[0], bias[1, :, : T - 128]], axis=1)
    scores = dot_t(spread_heads(q, masks), k) + bias
    heads_out = softmax_mix(scores, v, T, masks).astype(BF)
    attended = dot(heads_out, w_out).astype(BF)
    middle = (stream.astype(F32) + attended.astype(F32)).astype(BF)
    return feed_forward(middle, gain1, w_up, w_down)


def pack(tokens):
    half = tokens.shape[0] // 2
    tails = jnp.concatenate([tokens[:half, 128:], tokens[half:, 128:]], axis=1)
    return jnp.concatenate([tokens[:, :128], tails], axis=0).astype(BF)


def unpack(packed):
    values = packed.astype(F32)
    rows = values.shape[0] // 3 * 2
    tails = jnp.concatenate([values[rows:, :64], values[rows:, 64:]], axis=0)
    return jnp.concatenate([values[:rows], tails], axis=1)


def keys_values(tokens, w_qkv, k_ref, v_ref):
    kv = dot(tokens.astype(BF), w_qkv[:, D:])
    k_ref[...] = kv[:, :D].astype(BF).reshape(k_ref.shape)
    v_ref[...] = kv[:, D:].astype(BF).reshape(v_ref.shape)


def own_keys_kernel(block, down, up, w_qkv, q_ref, k_ref, v_ref):
    own = []
    for z, ref in enumerate((down, up)):
        tokens = unpack(ref[...])
        keys_values(tokens, w_qkv[block], k_ref.at[z], v_ref.at[z])
        for yh in range(2):
            row = (1 + yh) * 4 * SLOT + SLOT
            own.append(tokens[row : row + PAIR])
    q = dot(jnp.concatenate(own, axis=0).astype(BF), w_qkv[block, :, :D]).astype(BF)
    q_ref[...] = q.astype(F32) * np.float32(HD**-0.5)


def shifted_block(
    stream, below, above, q_ref, k_own, v_own, gain1, w_qkv, w_out, w_up, w_down, bias, back,
    k_ref, v_ref,
):
    for i, ref in enumerate((below, above)):
        keys_values(unpack(ref[...]), w_qkv, k_ref.at[i], v_ref.at[i])
    masks = head_mask(SLOT)
    outs = []
    for z in range(2):
        for yh in range(2):
            for xh in range(2):
                w = (z * 2 + yh) * 2 + xh
                sides = ((k_ref, v_ref, 0), (k_own, v_own, 0))
                if z:
                    sides = ((k_own, v_own, 1), (k_ref, v_ref, 1))
                ks, vs = [
                    jnp.concatenate(
                        [s[i][s[2], 2 * yh : 2 * yh + 2, xh].reshape(2 * PAIR, D) for s in sides],
                        axis=0,
                    )
                    for i in range(2)
                ]
                q = spread_heads(q_ref[w * SLOT : (w + 1) * SLOT], masks)
                rows = slice(w * 144, (w + 1) * 144)
                scores = dot_t(q, ks) + jnp.concatenate([bias[0, rows], bias[1, rows, :64]], 1)
                outs.append(softmax_mix(scores, vs, SLOT, masks))
    heads_out = jnp.concatenate(outs, axis=0).astype(BF)
    attended = dot(back, dot(heads_out, w_out).astype(BF))
    middle = (stream.astype(F32) + attended).astype(BF)
    return feed_forward(middle, gain1, w_up, w_down)


def pick_table(table_ref, block, window, table):
    rows = table_ref[block].astype(F32)
    at = lax.broadcasted_iota(jnp.int32, rows.shape, 1)
    table[...] = jnp.sum(jnp.where(at == window, rows, 0.0), axis=1)


def put(ref, rows, value):
    for k in range(2):
        ref[k, rows, :] = value[:, k * 128 : (k + 1) * 128]


def widened(table, start, extra):
    part = table[:, start : start + 6 * OFFS]
    wide = jnp.concatenate([part, jnp.zeros((HEADS, 256 - 6 * OFFS), F32)], axis=1)
    return wide if extra is None else wide + extra


def bias_rolls(parts, sel):
    lane = lax.broadcasted_iota(jnp.int32, parts[0].shape, 1)
    fixed = [jnp.where(lane >= MASK_AT, p, 0.0) for p in parts]
    moving = [jnp.where(lane < MASK_AT, p, 0.0) for p in parts]
    for xp in range(WX):
        rows = [
            (pltpu.roll(m, 256 - xp, 1) if xp else m) + f for m, f in zip(moving, fixed)
        ]
        yield xp, dot(jnp.concatenate(rows, axis=1).astype(BF), sel)


def bias_regular(table, sel, lhs, out_ref):
    for zp in range(2):
        for zq in range(2):
            for yp in range(6):
                start = ((zp * 2 + zq) * 6 + yp) * 6 * OFFS
                rows = pl.ds(zp * 6 + yp, HEADS, stride=12)
                put(lhs.at[zq], rows, widened(table, start, None))
    parts = [jnp.concatenate([lhs[k, 0], lhs[k, 1]], axis=1) for k in range(2)]
    for xp, rows in bias_rolls(parts, sel):
        put(out_ref, pl.ds(xp, 72, stride=WX), rows)


def tables_kernel(
    lev_ref, table_ref, label_ref, sel_ref, bias2, keep1, send1, keep3, send3, table, lhs, half
):
    pick_table(table_ref, 2, lev_ref[1], table)
    bias_regular(table, sel_ref[...], lhs, bias2)
    lane = lax.broadcasted_iota(jnp.int32, (8, 128), 1)
    level = lax.broadcasted_iota(jnp.int32, (8, 128), 0)
    first = MASK_AT - 128
    tags = jnp.zeros((8, 128), F32)
    for y in range(6):
        column = label_ref[y].astype(F32)[:, 0:1]
        tags = jnp.where(lane == first + y, column, tags)
    in_mask = (lane[0:1] >= first) & (lane[0:1] < first + 6)
    half[...] = jnp.zeros_like(half)
    for block, keep, send in ((1, keep1, send1), (3, keep3, send3)):
        for z in range(2):
            window = lev_ref[z]
            pick_table(table_ref, block, window, table)
            keys = [
                jnp.sum(jnp.where(level == window * 2 + zq, tags, 0.0), axis=0, keepdims=True)
                for zq in range(2)
            ]
            zp = 1 - z
            for yp in range(6):
                mine = jnp.sum(
                    jnp.where(lane[0:1] == first + yp, keys[zp], 0.0), axis=1, keepdims=True
                )
                for zq in range(2):
                    mask = jnp.where(in_mask & (keys[zq] != mine), NEG, 0.0)
                    mask = jnp.concatenate([jnp.zeros((1, 128), F32), mask], axis=1)
                    start = ((zp * 2 + zq) * 6 + yp) * 6 * OFFS
                    rows = pl.ds(z * 24 + yp % 3, HEADS, stride=4)
                    put(half.at[yp // 3, zq], rows, widened(table, start, mask))
        keep[...] = half[0].astype(BF)
        send[...] = half[1].astype(BF).reshape(192, 128)


def bias_shifted_kernel(keep, south, sel_ref, pad_ref, out_ref):
    moved = south[288:].reshape(2, 2, 48, 128)
    parts = []
    for zq in range(2):
        rows = [jnp.concatenate([src[zq, 0], src[zq, 1]], axis=1) for src in (moved, keep)]
        parts.append(jnp.concatenate(rows, axis=0).astype(F32))
    for xp, rows in bias_rolls(parts, sel_ref[...]):
        rows = rows + pad_ref[...]
        x = (xp + 6) % 12
        xh, xl = x // 6, x % 6
        for yh in range(2):
            for z in range(2):
                base = ((z * 2 + yh) * 2 + xh) * 144 + xl
                at = (yh * 2 + z) * 24
                put(out_ref, pl.ds(base, 24, stride=6), rows[at : at + 24])


def halves(stream, gain, to_oct, west, east):
    octs = dot(to_oct, layer_norm(stream.astype(F32), gain))
    west[...] = pack(octs[: 4 * SLOT])
    east[...] = pack(octs[4 * SLOT :])


def first_kernel(
    lev_ref, x, gains, w_qkv, w_out, w_up, w_down, table_ref, sel_ref, to_oct,
    stream_out, west, east, table, lhs, bias,
):
    pick_table(table_ref, 0, lev_ref[1], table)
    bias_regular(table, sel_ref[...], lhs, bias)
    stream = regular_block(
        x[...], gains[0, 0:1], gains[0, 1:2], w_qkv[0], w_out[0], w_up[0], w_down[0], bias
    )
    stream_out[...] = stream
    halves(stream, gains[1, 0:1], to_oct[...], west, east)


def middle_kernel(
    stream_in, below, above, q, k_own, v_own, gains, w_qkv, w_out, w_up, w_down, bias1, bias2,
    to_oct, back, stream_out, west, east, k_ref, v_ref,
):
    stream = shifted_block(
        stream_in[...], below, above, q, k_own, v_own, gains[1, 1:2], w_qkv[1], w_out[1], w_up[1],
        w_down[1], bias1, back[...], k_ref, v_ref,
    )
    stream = regular_block(
        stream, gains[2, 0:1], gains[2, 1:2], w_qkv[2], w_out[2], w_up[2], w_down[2], bias2
    )
    stream_out[...] = stream
    halves(stream, gains[3, 0:1], to_oct[...], west, east)


def last_kernel(
    stream_in, below, above, q, k_own, v_own, gains, w_qkv, w_out, w_up, w_down, bias3, back, out,
    k_ref, v_ref,
):
    out[...] = shifted_block(
        stream_in[...], below, above, q, k_own, v_own, gains[3, 1:2], w_qkv[3], w_out[3], w_up[3],
        w_down[3], bias3, back[...], k_ref, v_ref,
    )


def lat_pack_kernel(recv_w, own_w, own_e, recv_e, table_rows, south, north):
    parts = [unpack(ref[...]) for ref in (recv_w, own_w, own_e, recv_e)]
    for yh, ref in ((0, south), (1, north)):
        rows = [
            part[(yh * 2 + z) * SLOT : (yh * 2 + z + 1) * SLOT] for z in range(2) for part in parts
        ]
        ref[:288] = pack(jnp.concatenate(rows, axis=0))
    north[288:] = table_rows[...]


def lev_pack_kernel(recv_s, south, north, recv_n, down, up):
    parts = [unpack(ref[:288]) for ref in (recv_s, south, north, recv_n)]
    for z, ref in ((0, down), (1, up)):
        rows = [part[z * 4 * SLOT : (z + 1) * 4 * SLOT] for part in parts]
        ref[...] = pack(jnp.concatenate(rows, axis=0))


def call(kernel, outs, *args, scratch=(), flops=0, limit=20, scalars=0):
    specs = [pl.BlockSpec(memory_space=pltpu.SMEM)] * scalars
    specs += [pl.BlockSpec(memory_space=pltpu.VMEM)] * (len(args) - scalars)
    return pl.pallas_call(
        kernel,
        out_shape=outs,
        in_specs=specs,
        scratch_shapes=list(scratch),
        compiler_params=pltpu.CompilerParams(vmem_limit_bytes=limit << 20),
        cost_estimate=pl.CostEstimate(flops=flops, bytes_accessed=1 << 20, transcendentals=0),
    )(*args)


def shape(*dims, dtype=BF):
    return jax.ShapeDtypeStruct(dims, dtype)


def move(value, axis, steps):
    count = lax.axis_size(axis)
    return lax.ppermute(value, axis, [(i, (i + steps) % count) for i in range(count)])


def halo(block, west, east, keep, send, w_qkv, sel_shift, pad):
    recv_e = move(west, "lon", -1)
    recv_w = move(east, "lon", 1)
    south, north = call(
        lat_pack_kernel, [shape(288, 128), shape(480, 128)], recv_w, west, east, recv_e, send,
        limit=4,
    )
    recv_n = move(south, "lat", -1)
    recv_s = move(north, "lat", 1)
    down, up = call(
        lev_pack_kernel, [shape(576, 128)] * 2, recv_s, south, north, recv_n, limit=4
    )
    above = move(down, "lev", -1)
    below = move(up, "lev", 1)
    q, k, v = call(
        functools.partial(own_keys_kernel, block),
        [shape(8 * SLOT, D, dtype=F32), shape(2, 4, 2, PAIR, D), shape(2, 4, 2, PAIR, D)],
        down, up, w_qkv, flops=1 << 30, limit=8,
    )
    bias = call(
        bias_shifted_kernel, shape(2, 8 * 144, 128, dtype=F32), keep, recv_s, sel_shift, pad,
        flops=1 << 30, limit=8,
    )
    return below, above, q, k, v, bias


def per_device(fields, w_qkv, w_out, w_up, w_down, gains, bias_table, labels):
    level = lax.axis_index("lev")
    levels = jnp.stack([(level + 3) % 4, level]).astype(jnp.int32)
    to_oct, back = [jnp.asarray(m, BF) for m in octant_maps()]
    sel_reg, sel_shift, pad = selectors()
    sel_reg, sel_shift = jnp.asarray(sel_reg, BF), jnp.asarray(sel_shift, BF)
    pad = jnp.asarray(pad, F32)
    tables = bias_table[:, :, 0].transpose(0, 2, 1, 3)
    tags = labels.transpose(1, 0, 2)
    weights = (gains, w_qkv, w_out, w_up, w_down.transpose(0, 2, 1))

    bias_shape = (2, HEADS * T, 128)
    table_scratch = [pltpu.VMEM((HEADS, POS), F32), pltpu.VMEM((2, 2, 72, 128), F32)]
    kv_scratch = [pltpu.VMEM((2, 4, 2, PAIR, D), BF)] * 2
    streams = [shape(T, D), shape(144, 128), shape(144, 128)]
    stream, west, east = call(
        first_kernel, streams, levels, fields.reshape(T, D), *weights, tables, sel_reg, to_oct,
        scratch=[*table_scratch, pltpu.VMEM(bias_shape, F32)], flops=1 << 31, scalars=1,
    )
    rows = [shape(2, 2, 48, 128), shape(192, 128)]
    bias2, keep1, send1, keep3, send3 = call(
        tables_kernel, [shape(*bias_shape, dtype=F32), *rows, *rows], levels, tables, tags, sel_reg,
        scratch=[*table_scratch, pltpu.VMEM((2, 2, 2, 48, 128), F32)], flops=1 << 31, scalars=1,
    )
    *ready, bias1 = halo(1, west, east, keep1, send1, w_qkv, sel_shift, pad)
    stream, west, east = call(
        middle_kernel, streams, stream, *ready, *weights, bias1, bias2, to_oct, back,
        scratch=kv_scratch, flops=1 << 31,
    )
    *ready, bias3 = halo(3, west, east, keep3, send3, w_qkv, sel_shift, pad)
    stream = call(
        last_kernel, shape(T, D), stream, *ready, *weights, bias3, back,
        scratch=kv_scratch, flops=1 << 31,
    )
    return stream.reshape(2, 6, 12, D)


def solution(mesh):
    in_specs = (
        P("lev", "lat", "lon", None),
        P(),
        P(),
        P(),
        P(),
        P(),
        P(None, None, "lat", None, None),
        P(None, "lat", "lon"),
    )
    return jax.shard_map(
        per_device,
        mesh=mesh,
        in_specs=in_specs,
        out_specs=P("lev", "lat", "lon", None),
        check_vma=False,
    )
```

time: 101 us -> 99.8 us (0.988)
  starting transfers between devices: 48.9 us -> 42 us
  local copies, waits for them, and re-layouts: 6 us -> 10.1 us
  Pallas kernels: 14.4 us -> 17.5 us
  waiting for transfers between devices: 30.2 us -> 29 us
    ppermute x13 -> x12, starting transfers between devices: 48.9 us -> 42 us  [move(): lax.ppermute(value, axis, [(i, (i + steps) % count) for i in range(count)])]
    unnamed x24 -> x37, local copies, waits for them, and re-layouts: 3.85 us -> 9.31 us
    pallas_call x11 -> x12, Pallas kernels: 14.4 us -> 17.5 us  [call(): pl.pallas_call(kernel, out_shape=outs, in_specs=specs, scratch_shapes=lis...]
    ppermute x13 -> x12, waiting for transfers between devices: 30.2 us -> 29 us  [move(): lax.ppermute(value, axis, [(i, (i + steps) % count) for i in range(count)])]
  transfers between devices with their start and end apart: 13 -> 12, of which waited for: 10 -> 7; matrix products, arithmetic and copies ran while one was open for 0% -> 0% of each run, Pallas kernels for 3% -> 5%
where the time goes in v2:
time: 99.8 us; the launch traced here: 99 us
  starting transfers between devices  42 us (42%)
  waiting for transfers between devices  29 us (29%)
  Pallas kernels  17.5 us (18%)
  local copies, waits for them, and re-layouts  10.1 us (10%)
    ppermute x12, starting transfers between devices, move(): lax.ppermute(value, axis, [(i, (i + steps) % count) for i in range(count)])  42 us
    ppermute x12, waiting for transfers between devices, move(): lax.ppermute(value, axis, [(i, (i + steps) % count) for i in range(count)])  29 us
    pallas_call x12, Pallas kernels, call(): pl.pallas_call(kernel, out_shape=outs, in_specs=specs, scratch_shapes=lis...  17.5 us
    unnamed x37, local copies, waits for them, and re-layouts  9.31 us
  transfers between devices with their start and end apart: 12, of which 7 were waited for; matrix products, arithmetic and copies ran while one was open for 0% of the time, Pallas kernels for 5%

profile of v2, /device:TPU:255, one launch (start us, length us, event | category | flops | bytes accessed | tf_op | source)
XLA Modules:
  0.0 99.0 jit_solution(17734097274197598699)
XLA Ops:
  1.0 1.3 %copy-done = bf16[4,192,768]{2,1,0:T(8,128)(2,1)S(1)} copy-done((bf16[4,192,768]{2,1,0:T(8,128)(2,1)S(1)}, bf16[4,192,768]{2,1,0:T(8,128)(2,1)}, u32[]{:S(2)}) %copy-start) | copy-done | bytes 1179672
  2.3 1.3 %copy-done.2 = bf16[4,768,192]{1,2,0:T(8,128)(2,1)S(1)} copy-done((bf16[4,768,192]{1,2,0:T(8,128)(2,1)S(1)}, bf16[4,768,192]{1,2,0:T(8,128)(2,1)}, u32[]{:S(2)}) %copy-start.2) | copy-done | bytes 1179672
  9.4 3.5 %shard_map.127 = (bf16[144,192]{1,0:T(8,128)(2,1)S(1)}, bf16[144,128]{1,0:T(8,128)(2,1)S(1)}, bf16[144,128]{1,0:T(8,128)(2,1)S(1)}) custom-call(s32[2]{0:T(128)S(1)} %pad_add_fusion.lev_ref, bf16[144,192]{1,0:T(8,128)(2,1)S(1)} %reshape.6.x, f32[4,2,192]{2,1,0:T(2,128)S(1)} %copy-done.10, bf16[4,192,576]{2,1,0:T(8,128)(2,1)S(1)} %copy-done.4, ...), custom_call_target="tpu_custom_call" | custom-call | flops 2147483648 | bytes 1048576 | tf_op jit(solution)/shard_map/pallas_call | solution.py:342
  12.9 7.4 %collective-permute-start = (bf16[144,128]{1,0:T(8,128)(2,1)S(1)}, bf16[144,128]{1,0:T(8,128)(2,1)S(1)}, u32[]{:S(2)}, u32[]{:S(2)}) collective-permute-start(bf16[144,128]{1,0:T(8,128)(2,1)S(1)} %get-tuple-element.31.own_e), channel_id=1, source_target_pairs={{0,32},{32,64},{64,96},{96,128},{128,160},{160,192},{192,224},{224... | collective-permute-start | bytes 110600 | tf_op jit(solution)/shard_map/ppermute | solution.py:358
  20.4 1.9 %collective-permute-start.1 = (bf16[144,128]{1,0:T(8,128)(2,1)S(1)}, bf16[144,128]{1,0:T(8,128)(2,1)S(1)}, u32[]{:S(2)}, u32[]{:S(2)}) collective-permute-start(bf16[144,128]{1,0:T(8,128)(2,1)S(1)} %get-tuple-element.32.own_w), channel_id=1, source_target_pairs={{0,480},{32,0},{64,32},{96,64},{128,96},{160,128},{192,160},{224,1... | collective-permute-start | bytes 110600 | tf_op jit(solution)/shard_map/ppermute | solution.py:358
  22.3 2.4 %shard_map.128 = (f32[2,864,128]{2,1,0:T(8,128)S(1)}, bf16[2,2,48,128]{3,2,1,0:T(8,128)(2,1)S(1)}, bf16[192,128]{1,0:T(8,128)(2,1)S(1)}, bf16[2,2,48,128]{3,2,1,0:T(8,128)(2,1)S(1)}, bf16[192,128]{1,0:T(8,128)(2,1)S(1)}) custom-call(s32[2]{0:T(128)S(1)} %pad_add_fusion.lev_ref, bf16[4,6,4,3312]{3,2,1,0:T(4,128)(2,1)S(1)} %bitcast.11, ...), custom_call_target="tpu_custom_call" | custom-call | flops 2147483648 | bytes 1048576 | tf_op jit(solution)/shard_map/pallas_call | solution.py:342
  24.7 6.7 %collective-permute-done.1.recv_e = bf16[144,128]{1,0:T(8,128)(2,1)S(1)} collective-permute-done((bf16[144,128]{1,0:T(8,128)(2,1)S(1)}, bf16[144,128]{1,0:T(8,128)(2,1)S(1)}, u32[]{:S(2)}, u32[]{:S(2)}) %collective-permute-start.1) | collective-permute-done | bytes 36896 | tf_op jit(solution)/shard_map/ppermute | solution.py:358
  31.6 3.9 %collective-permute-start.2 = (bf16[480,128]{1,0:T(8,128)(2,1)S(1)}, bf16[480,128]{1,0:T(8,128)(2,1)S(1)}, u32[]{:S(2)}, u32[]{:S(2)}) collective-permute-start(bf16[480,128]{1,0:T(8,128)(2,1)S(1)} %get-tuple-element.34.north), channel_id=1, source_target_pairs={{0,4},{4,8},{8,12},{12,16},{16,20},{20,24},{24,28},{28,0},{1,5},{5... | collective-permute-start | bytes 368648 | tf_op jit(solution)/shard_map/ppermute | solution.py:358
  35.5 2.0 %collective-permute-start.3 = (bf16[288,128]{1,0:T(8,128)(2,1)S(1)}, bf16[288,128]{1,0:T(8,128)(2,1)S(1)}, u32[]{:S(2)}, u32[]{:S(2)}) collective-permute-start(bf16[288,128]{1,0:T(8,128)(2,1)S(1)} %get-tuple-element.35.south), channel_id=1, source_target_pairs={{0,28},{4,0},{8,4},{12,8},{16,12},{20,16},{24,20},{28,24},{1,29},{... | collective-permute-start | bytes 221192 | tf_op jit(solution)/shard_map/ppermute | solution.py:358
  37.5 5.4 %collective-permute-done.3.recv_n = bf16[288,128]{1,0:T(8,128)(2,1)S(1)} collective-permute-done((bf16[288,128]{1,0:T(8,128)(2,1)S(1)}, bf16[288,128]{1,0:T(8,128)(2,1)S(1)}, u32[]{:S(2)}, u32[]{:S(2)}) %collective-permute-start.3) | collective-permute-done | bytes 73760 | tf_op jit(solution)/shard_map/ppermute | solution.py:358
  43.1 2.1 %collective-permute-start.4 = (bf16[576,128]{1,0:T(8,128)(2,1)S(1)}, bf16[576,128]{1,0:T(8,128)(2,1)S(1)}, u32[]{:S(2)}, u32[]{:S(2)}) collective-permute-start(bf16[576,128]{1,0:T(8,128)(2,1)S(1)} %get-tuple-element.36.up), channel_id=1, source_target_pairs={{0,1},{1,2},{2,3},{3,0},{4,5},{5,6},{6,7},{7,4},{8,9},{9,10},{10,1... | collective-permute-start | bytes 442376 | tf_op jit(solution)/shard_map/ppermute | solution.py:358
  45.3 3.3 %collective-permute-start.5 = (bf16[576,128]{1,0:T(8,128)(2,1)S(1)}, bf16[576,128]{1,0:T(8,128)(2,1)S(1)}, u32[]{:S(2)}, u32[]{:S(2)}) collective-permute-start(bf16[576,128]{1,0:T(8,128)(2,1)S(1)} %get-tuple-element.37.down), channel_id=1, source_target_pairs={{0,3},{1,0},{2,1},{3,2},{4,7},{5,4},{6,5},{7,6},{8,11},{9,8},{10,9... | collective-permute-start | bytes 442376 | tf_op jit(solution)/shard_map/ppermute | solution.py:358
  50.0 3.1 %collective-permute-done.5.above = bf16[576,128]{1,0:T(8,128)(2,1)S(1)} collective-permute-done((bf16[576,128]{1,0:T(8,128)(2,1)S(1)}, bf16[576,128]{1,0:T(8,128)(2,1)S(1)}, u32[]{:S(2)}, u32[]{:S(2)}) %collective-permute-start.5) | collective-permute-done | bytes 147488 | tf_op jit(solution)/shard_map/ppermute | solution.py:358
  53.1 5.2 %shard_map.133 = (bf16[144,192]{1,0:T(8,128)(2,1)S(1)}, bf16[144,128]{1,0:T(8,128)(2,1)S(1)}, bf16[144,128]{1,0:T(8,128)(2,1)S(1)}) custom-call(bf16[144,192]{1,0:T(8,128)(2,1)S(1)} %get-tuple-element.30.stream_in, bf16[576,128]{1,0:T(8,128)(2,1)S(1)} %collective-permute-done.4.below, bf16[576,128]{1,0:T(8,128)(2,1)S(1)} %collective-permute-done.5.above, ...), custom_call_target="tpu_custom_call" | custom-call | flops 2147483648 | bytes 1048576 | tf_op jit(solution)/shard_map/pallas_call | solution.py:342
  58.4 4.4 %collective-permute-start.6 = (bf16[144,128]{1,0:T(8,128)(2,1)S(1)}, bf16[144,128]{1,0:T(8,128)(2,1)S(1)}, u32[]{:S(2)}, u32[]{:S(2)}) collective-permute-start(bf16[144,128]{1,0:T(8,128)(2,1)S(1)} %get-tuple-element.44.own_e), channel_id=1, source_target_pairs={{0,32},{32,64},{64,96},{96,128},{128,160},{160,192},{192,224},{224... | collective-permute-start | bytes 110600 | tf_op jit(solution)/shard_map/ppermute | solution.py:358
  62.7 4.8 %collective-permute-start.7 = (bf16[144,128]{1,0:T(8,128)(2,1)S(1)}, bf16[144,128]{1,0:T(8,128)(2,1)S(1)}, u32[]{:S(2)}, u32[]{:S(2)}) collective-permute-start(bf16[144,128]{1,0:T(8,128)(2,1)S(1)} %get-tuple-element.45.own_w), channel_id=1, source_target_pairs={{0,480},{32,0},{64,32},{96,64},{128,96},{160,128},{192,160},{224,1... | collective-permute-start | bytes 110600 | tf_op jit(solution)/shard_map/ppermute | solution.py:358
  67.9 5.6 %collective-permute-done.7.recv_e = bf16[144,128]{1,0:T(8,128)(2,1)S(1)} collective-permute-done((bf16[144,128]{1,0:T(8,128)(2,1)S(1)}, bf16[144,128]{1,0:T(8,128)(2,1)S(1)}, u32[]{:S(2)}, u32[]{:S(2)}) %collective-permute-start.7) | collective-permute-done | bytes 36896 | tf_op jit(solution)/shard_map/ppermute | solution.py:358
  73.6 4.7 %collective-permute-start.8 = (bf16[480,128]{1,0:T(8,128)(2,1)S(1)}, bf16[480,128]{1,0:T(8,128)(2,1)S(1)}, u32[]{:S(2)}, u32[]{:S(2)}) collective-permute-start(bf16[480,128]{1,0:T(8,128)(2,1)S(1)} %get-tuple-element.47.north), channel_id=1, source_target_pairs={{0,4},{4,8},{8,12},{12,16},{16,20},{20,24},{24,28},{28,0},{1,5},{5... | collective-permute-start | bytes 368648 | tf_op jit(solution)/shard_map/ppermute | solution.py:358
  78.3 1.9 %collective-permute-start.9 = (bf16[288,128]{1,0:T(8,128)(2,1)S(1)}, bf16[288,128]{1,0:T(8,128)(2,1)S(1)}, u32[]{:S(2)}, u32[]{:S(2)}) collective-permute-start(bf16[288,128]{1,0:T(8,128)(2,1)S(1)} %get-tuple-element.48.south), channel_id=1, source_target_pairs={{0,28},{4,0},{8,4},{12,8},{16,12},{20,16},{24,20},{28,24},{1,29},{... | collective-permute-start | bytes 221192 | tf_op jit(solution)/shard_map/ppermute | solution.py:358
  80.3 5.5 %collective-permute-done.9.recv_n = bf16[288,128]{1,0:T(8,128)(2,1)S(1)} collective-permute-done((bf16[288,128]{1,0:T(8,128)(2,1)S(1)}, bf16[288,128]{1,0:T(8,128)(2,1)S(1)}, u32[]{:S(2)}, u32[]{:S(2)}) %collective-permute-start.9) | collective-permute-done | bytes 73760 | tf_op jit(solution)/shard_map/ppermute | solution.py:358
  86.0 1.9 %collective-permute-start.10 = (bf16[576,128]{1,0:T(8,128)(2,1)S(1)}, bf16[576,128]{1,0:T(8,128)(2,1)S(1)}, u32[]{:S(2)}, u32[]{:S(2)}) collective-permute-start(bf16[576,128]{1,0:T(8,128)(2,1)S(1)} %get-tuple-element.49.up), channel_id=1, source_target_pairs={{0,1},{1,2},{2,3},{3,0},{4,5},{5,6},{6,7},{7,4},{8,9},{9,10},{10,1... | collective-permute-start | bytes 442376 | tf_op jit(solution)/shard_map/ppermute | solution.py:358
  87.9 3.5 %collective-permute-start.11 = (bf16[576,128]{1,0:T(8,128)(2,1)S(1)}, bf16[576,128]{1,0:T(8,128)(2,1)S(1)}, u32[]{:S(2)}, u32[]{:S(2)}) collective-permute-start(bf16[576,128]{1,0:T(8,128)(2,1)S(1)} %get-tuple-element.50.down), channel_id=1, source_target_pairs={{0,3},{1,0},{2,1},{3,2},{4,7},{5,4},{6,5},{7,6},{8,11},{9,8},{10,9... | collective-permute-start | bytes 442376 | tf_op jit(solution)/shard_map/ppermute | solution.py:358
  92.7 2.3 %collective-permute-done.11.above = bf16[576,128]{1,0:T(8,128)(2,1)S(1)} collective-permute-done((bf16[576,128]{1,0:T(8,128)(2,1)S(1)}, bf16[576,128]{1,0:T(8,128)(2,1)S(1)}, u32[]{:S(2)}, u32[]{:S(2)}) %collective-permute-start.11) | collective-permute-done | bytes 147488 | tf_op jit(solution)/shard_map/ppermute | solution.py:358
  95.0 3.2 %shard_map.138 = bf16[144,192]{1,0:T(8,128)(2,1)S(1)} custom-call(bf16[144,192]{1,0:T(8,128)(2,1)S(1)} %get-tuple-element.43.stream_in, bf16[576,128]{1,0:T(8,128)(2,1)S(1)} %collective-permute-done.10.below, bf16[576,128]{1,0:T(8,128)(2,1)S(1)} %collective-permute-done.11.above, f32[192,192]{1,0:T(8,128)S(1)} %get-tuple-element.51.q, ...), custom_call_target="tpu_custom_call" | custom-call | flops 2147483648 | bytes 1048576 | tf_op jit(solution)/shard_map/pallas_call | solution.py:342
  (53 shorter events, 11.1 us)
Async XLA Ops:
  1.0 1.3 %copy-start = (bf16[4,192,768]{2,1,0:T(8,128)(2,1)S(1)}, bf16[4,192,768]{2,1,0:T(8,128)(2,1)}, u32[]{:S(2)}) copy-start(bf16[4,192,768]{2,1,0:T(8,128)(2,1)} %w_up.5) | copy-start | bytes 3538948
  2.3 1.3 %copy-start.2 = (bf16[4,768,192]{1,2,0:T(8,128)(2,1)S(1)}, bf16[4,768,192]{1,2,0:T(8,128)(2,1)}, u32[]{:S(2)}) copy-start(bf16[4,768,192]{1,2,0:T(8,128)(2,1)} %param.17) | copy-start | bytes 3538948
  9.4 12.9 %copy-start.9 = (s32[8,6,12]{2,0,1:T(8,128)S(1)}, s32[8,6,12]{2,0,1:T(8,128)}, u32[]{:S(2)}) copy-start(s32[8,6,12]{2,0,1:T(8,128)} %param.20) | copy-start | bytes 6916
  12.9 11.8 %collective-permute-start = (bf16[144,128]{1,0:T(8,128)(2,1)S(1)}, bf16[144,128]{1,0:T(8,128)(2,1)S(1)}, u32[]{:S(2)}, u32[]{:S(2)}) collective-permute-start(bf16[144,128]{1,0:T(8,128)(2,1)S(1)} %get-tuple-element.31.own_e), channel_id=1, source_target_pairs={{0,32},{32,64},{64,96},{96,128},{128,160},{160,192},{192,224},{224... | collective-permute-start | bytes 110600 | tf_op jit(solution)/shard_map/ppermute | solution.py:358
  20.4 11.1 %collective-permute-start.1 = (bf16[144,128]{1,0:T(8,128)(2,1)S(1)}, bf16[144,128]{1,0:T(8,128)(2,1)S(1)}, u32[]{:S(2)}, u32[]{:S(2)}) collective-permute-start(bf16[144,128]{1,0:T(8,128)(2,1)S(1)} %get-tuple-element.32.own_w), channel_id=1, source_target_pairs={{0,480},{32,0},{64,32},{96,64},{128,96},{160,128},{192,160},{224,1... | collective-permute-start | bytes 110600 | tf_op jit(solution)/shard_map/ppermute | solution.py:358
  22.3 26.3 %copy-start.5 = (bf16[4,192,576]{2,1,0:T(8,128)(2,1)S(1)}, bf16[4,192,576]{2,1,0:T(8,128)(2,1)}, u32[]{:S(2)}) copy-start(bf16[4,192,576]{2,1,0:T(8,128)(2,1)} %w_qkv.9) | copy-start | bytes 2654212
  31.6 11.4 %collective-permute-start.2 = (bf16[480,128]{1,0:T(8,128)(2,1)S(1)}, bf16[480,128]{1,0:T(8,128)(2,1)S(1)}, u32[]{:S(2)}, u32[]{:S(2)}) collective-permute-start(bf16[480,128]{1,0:T(8,128)(2,1)S(1)} %get-tuple-element.34.north), channel_id=1, source_target_pairs={{0,4},{4,8},{8,12},{12,16},{16,20},{20,24},{24,28},{28,0},{1,5},{5... | collective-permute-start | bytes 368648 | tf_op jit(solution)/shard_map/ppermute | solution.py:358
  35.5 7.5 %collective-permute-start.3 = (bf16[288,128]{1,0:T(8,128)(2,1)S(1)}, bf16[288,128]{1,0:T(8,128)(2,1)S(1)}, u32[]{:S(2)}, u32[]{:S(2)}) collective-permute-start(bf16[288,128]{1,0:T(8,128)(2,1)S(1)} %get-tuple-element.35.south), channel_id=1, source_target_pairs={{0,28},{4,0},{8,4},{12,8},{16,12},{20,16},{24,20},{28,24},{1,29},{... | collective-permute-start | bytes 221192 | tf_op jit(solution)/shard_map/ppermute | solution.py:358
  43.1 6.8 %collective-permute-start.4 = (bf16[576,128]{1,0:T(8,128)(2,1)S(1)}, bf16[576,128]{1,0:T(8,128)(2,1)S(1)}, u32[]{:S(2)}, u32[]{:S(2)}) collective-permute-start(bf16[576,128]{1,0:T(8,128)(2,1)S(1)} %get-tuple-element.36.up), channel_id=1, source_target_pairs={{0,1},{1,2},{2,3},{3,0},{4,5},{5,6},{6,7},{7,4},{8,9},{9,10},{10,1... | collective-permute-start | bytes 442376 | tf_op jit(solution)/shard_map/ppermute | solution.py:358
  45.2 3.9 %copy-start.12 = (bf16[512,256]{1,0:T(8,128)(2,1)S(1)}, bf16[512,256]{1,0:T(8,128)(2,1)}, u32[]{:S(2)}) copy-start(bf16[512,256]{1,0:T(8,128)(2,1)} %constant.31.clone.sel_ref) | copy-start | bytes 786436
  45.3 3.9 %copy-start.17 = (f32[1,256]{1,0:T(1,128)S(1)}, f32[1,256]{1,0:T(1,128)}, u32[]{:S(2)}) copy-start(f32[1,256]{1,0:T(1,128)} %constant.32.clone.pad_ref) | copy-start | bytes 3076
  45.3 7.8 %collective-permute-start.5 = (bf16[576,128]{1,0:T(8,128)(2,1)S(1)}, bf16[576,128]{1,0:T(8,128)(2,1)S(1)}, u32[]{:S(2)}, u32[]{:S(2)}) collective-permute-start(bf16[576,128]{1,0:T(8,128)(2,1)S(1)} %get-tuple-element.37.down), channel_id=1, source_target_pairs={{0,3},{1,0},{2,1},{3,2},{4,7},{5,4},{6,5},{7,6},{8,11},{9,8},{10,9... | collective-permute-start | bytes 442376 | tf_op jit(solution)/shard_map/ppermute | solution.py:358
  49.2 3.9 %copy-start.1 = (bf16[4,192,768]{2,1,0:T(8,128)(2,1)S(1)}, bf16[4,192,768]{2,1,0:T(8,128)(2,1)}, u32[]{:S(2)}) copy-start(bf16[4,192,768]{2,1,0:T(8,128)(2,1)} %w_up.5) | copy-start | bytes 3538948
  49.2 3.9 %copy-start.3 = (bf16[4,768,192]{1,2,0:T(8,128)(2,1)S(1)}, bf16[4,768,192]{1,2,0:T(8,128)(2,1)}, u32[]{:S(2)}) copy-start(bf16[4,768,192]{1,2,0:T(8,128)(2,1)} %param.17) | copy-start | bytes 3538948
  49.2 3.9 %copy-start.8 = (bf16[4,192,192]{2,1,0:T(8,128)(2,1)S(1)}, bf16[4,192,192]{2,1,0:T(8,128)(2,1)}, u32[]{:S(2)}) copy-start(bf16[4,192,192]{2,1,0:T(8,128)(2,1)} %w_out.5) | copy-start | bytes 884740
  49.2 3.9 %copy-start.11 = (f32[4,2,192]{2,1,0:T(2,128)S(1)}, f32[4,2,192]{2,1,0:T(2,128)}, u32[]{:S(2)}) copy-start(f32[4,2,192]{2,1,0:T(2,128)} %gains.5) | copy-start | bytes 18436
  49.2 3.9 %copy-start.15 = (bf16[192,144]{1,0:T(8,128)(2,1)S(1)}, bf16[192,144]{1,0:T(8,128)(2,1)}, u32[]{:S(2)}) copy-start(bf16[192,144]{1,0:T(8,128)(2,1)} %constant.28.clone.to_oct) | copy-start | bytes 165892
  49.2 3.9 %copy-start.16 = (bf16[144,192]{1,0:T(8,128)(2,1)S(1)}, bf16[144,192]{1,0:T(8,128)(2,1)}, u32[]{:S(2)}) copy-start(bf16[144,192]{1,0:T(8,128)(2,1)} %constant.29.clone.back) | copy-start | bytes 165892
  58.4 9.5 %collective-permute-start.6 = (bf16[144,128]{1,0:T(8,128)(2,1)S(1)}, bf16[144,128]{1,0:T(8,128)(2,1)S(1)}, u32[]{:S(2)}, u32[]{:S(2)}) collective-permute-start(bf16[144,128]{1,0:T(8,128)(2,1)S(1)} %get-tuple-element.44.own_e), channel_id=1, source_target_pairs={{0,32},{32,64},{64,96},{96,128},{128,160},{160,192},{192,224},{224... | collective-permute-start | bytes 110600 | tf_op jit(solution)/shard_map/ppermute | solution.py:358
  62.7 10.7 %collective-permute-start.7 = (bf16[144,128]{1,0:T(8,128)(2,1)S(1)}, bf16[144,128]{1,0:T(8,128)(2,1)S(1)}, u32[]{:S(2)}, u32[]{:S(2)}) collective-permute-start(bf16[144,128]{1,0:T(8,128)(2,1)S(1)} %get-tuple-element.45.own_w), channel_id=1, source_target_pairs={{0,480},{32,0},{64,32},{96,64},{128,96},{160,128},{192,160},{224,1... | collective-permute-start | bytes 110600 | tf_op jit(solution)/shard_map/ppermute | solution.py:358
  73.6 12.2 %collective-permute-start.8 = (bf16[480,128]{1,0:T(8,128)(2,1)S(1)}, bf16[480,128]{1,0:T(8,128)(2,1)S(1)}, u32[]{:S(2)}, u32[]{:S(2)}) collective-permute-start(bf16[480,128]{1,0:T(8,128)(2,1)S(1)} %get-tuple-element.47.north), channel_id=1, source_target_pairs={{0,4},{4,8},{8,12},{12,16},{16,20},{20,24},{24,28},{28,0},{1,5},{5... | collective-permute-start | bytes 368648 | tf_op jit(solution)/shard_map/ppermute | solution.py:358
  78.3 7.5 %collective-permute-start.9 = (bf16[288,128]{1,0:T(8,128)(2,1)S(1)}, bf16[288,128]{1,0:T(8,128)(2,1)S(1)}, u32[]{:S(2)}, u32[]{:S(2)}) collective-permute-start(bf16[288,128]{1,0:T(8,128)(2,1)S(1)} %get-tuple-element.48.south), channel_id=1, source_target_pairs={{0,28},{4,0},{8,4},{12,8},{16,12},{20,16},{24,20},{28,24},{1,29},{... | collective-permute-start | bytes 221192 | tf_op jit(solution)/shard_map/ppermute | solution.py:358
  86.0 6.7 %collective-permute-start.10 = (bf16[576,128]{1,0:T(8,128)(2,1)S(1)}, bf16[576,128]{1,0:T(8,128)(2,1)S(1)}, u32[]{:S(2)}, u32[]{:S(2)}) collective-permute-start(bf16[576,128]{1,0:T(8,128)(2,1)S(1)} %get-tuple-element.49.up), channel_id=1, source_target_pairs={{0,1},{1,2},{2,3},{3,0},{4,5},{5,6},{6,7},{7,4},{8,9},{9,10},{10,1... | collective-permute-start | bytes 442376 | tf_op jit(solution)/shard_map/ppermute | solution.py:358
  87.9 7.1 %collective-permute-start.11 = (bf16[576,128]{1,0:T(8,128)(2,1)S(1)}, bf16[576,128]{1,0:T(8,128)(2,1)S(1)}, u32[]{:S(2)}, u32[]{:S(2)}) collective-permute-start(bf16[576,128]{1,0:T(8,128)(2,1)S(1)} %get-tuple-element.50.down), channel_id=1, source_target_pairs={{0,3},{1,0},{2,1},{3,2},{4,7},{5,4},{6,5},{7,6},{8,11},{9,8},{10,9... | collective-permute-start | bytes 442376 | tf_op jit(solution)/shard_map/ppermute | solution.py:358
  (6 other events, 5.8 us)

commit v3 on v2

--- a/solution.py
+++ b/solution.py
@@ -21,6 +21,7 @@
 POS = 3312
 SLOT = 24
 PAIR = 2 * SLOT
+FIRST_LIMIT = 62.0
 NEG = -1e30
 MASK_AT = 192
 BF = jnp.bfloat16
@@ -34,7 +35,7 @@
         for y in range(6):
             for x in range(12):
                 yh, yl, xh, xl = y // 3, y % 3, x // 6, x % 6
-                tok = z * 72 + y * 12 + x
+                tok = (y * 12 + x) * 2 + z
                 slot = yl * 6 + xl
                 to_oct[((xh * 2 + yh) * 2 + z) * SLOT + slot, tok] = 1.0
                 back[tok, ((z * 2 + yh) * 2 + xh) * SLOT + slot] = 1.0
@@ -46,7 +47,7 @@
     for zq in range(2):
         for yq in range(6):
             for xq in range(12):
-                regular[zq, yq * OFFS + 11 - xq, zq * 72 + yq * 12 + xq] = 1.0
+                regular[zq, yq * OFFS + 11 - xq, (yq * 12 + xq) * 2 + zq] = 1.0
     shifted = np.zeros((2, 256, 256), np.float32)
     pad = np.full((1, 256), NEG, np.float32)
     for zk in range(2):
@@ -214,17 +215,19 @@
         for zq in range(2):
             for yp in range(6):
                 start = ((zp * 2 + zq) * 6 + yp) * 6 * OFFS
-                rows = pl.ds(zp * 6 + yp, HEADS, stride=12)
+                rows = pl.ds(zp * 40 + yp, HEADS, stride=6)
                 put(lhs.at[zq], rows, widened(table, start, None))
     parts = [jnp.concatenate([lhs[k, 0], lhs[k, 1]], axis=1) for k in range(2)]
     for xp, rows in bias_rolls(parts, sel):
-        put(out_ref, pl.ds(xp, 72, stride=WX), rows)
+        for zp in range(2):
+            put(out_ref, pl.ds(2 * xp + zp, 36, stride=24), rows[zp * 40 : zp * 40 + 36])
 
 
 def tables_kernel(
     lev_ref, table_ref, label_ref, sel_ref, bias2, keep1, send1, keep3, send3, table, lhs, half
 ):
     pick_table(table_ref, 2, lev_ref[1], table)
+    lhs[...] = jnp.zeros_like(lhs)
     bias_regular(table, sel_ref[...], lhs, bias2)
     lane = lax.broadcasted_iota(jnp.int32, (8, 128), 1)
     level = lax.broadcasted_iota(jnp.int32, (8, 128), 0)
@@ -282,13 +285,28 @@
 
 
 def first_kernel(
-    lev_ref, x, gains, w_qkv, w_out, w_up, w_down, table_ref, sel_ref, to_oct,
-    stream_out, west, east, table, lhs, bias,
+    lev_ref, x_hbm, gains_hbm, w_qkv_hbm, w_out_hbm, w_up_hbm, w_down_hbm, table_hbm, sel_hbm,
+    oct_hbm, stream_out, west, east, table, lhs, bias, x, gains, w_qkv, w_out, w_up, w_down,
+    rows, sel, to_oct, sems,
 ):
-    pick_table(table_ref, 0, lev_ref[1], table)
-    bias_regular(table, sel_ref[...], lhs, bias)
+    pairs = (
+        (table_hbm.at[pl.ds(0, 1)], rows), (sel_hbm, sel), (x_hbm, x), (gains_hbm, gains),
+        (w_qkv_hbm.at[0], w_qkv), (w_out_hbm.at[0], w_out), (w_up_hbm.at[0], w_up),
+        (w_down_hbm.at[0], w_down), (oct_hbm, to_oct),
+    )
+    copies = [pltpu.make_async_copy(a, b, sems.at[i]) for i, (a, b) in enumerate(pairs)]
+    for copy in copies:
+        copy.start()
+    copies[0].wait()
+    pick_table(rows, 0, lev_ref[1], table)
+    lhs[...] = jnp.zeros_like(lhs)
+    copies[1].wait()
+    bias_regular(table, sel[...], lhs, bias)
+    for copy in copies[2:]:
+        copy.wait()
     stream = regular_block(
-        x[...], gains[0, 0:1], gains[0, 1:2], w_qkv[0], w_out[0], w_up[0], w_down[0], bias
+        x[...].astype(F32).reshape(T, D).astype(BF), gains[0, 0:1], gains[0, 1:2], w_qkv[...],
+        w_out[...], w_up[...], w_down[...], bias,
     )
     stream_out[...] = stream
     halves(stream, gains[1, 0:1], to_oct[...], west, east)
@@ -313,10 +331,11 @@
     stream_in, below, above, q, k_own, v_own, gains, w_qkv, w_out, w_up, w_down, bias3, back, out,
     k_ref, v_ref,
 ):
-    out[...] = shifted_block(
+    stream = shifted_block(
         stream_in[...], below, above, q, k_own, v_own, gains[3, 1:2], w_qkv[3], w_out[3], w_up[3],
         w_down[3], bias3, back[...], k_ref, v_ref,
     )
+    out[...] = stream.astype(F32).reshape(T // 2, 2, D).astype(BF)
 
 
 def lat_pack_kernel(recv_w, own_w, own_e, recv_e, table_rows, south, north):
@@ -336,15 +355,15 @@
         ref[...] = pack(jnp.concatenate(rows, axis=0))
 
 
-def call(kernel, outs, *args, scratch=(), flops=0, limit=20, scalars=0):
+def call(kernel, outs, *args, scratch=(), flops=0, limit=20, scalars=0, place=pltpu.VMEM):
     specs = [pl.BlockSpec(memory_space=pltpu.SMEM)] * scalars
-    specs += [pl.BlockSpec(memory_space=pltpu.VMEM)] * (len(args) - scalars)
+    specs += [pl.BlockSpec(memory_space=place)] * (len(args) - scalars)
     return pl.pallas_call(
         kernel,
         out_shape=outs,
         in_specs=specs,
         scratch_shapes=list(scratch),
-        compiler_params=pltpu.CompilerParams(vmem_limit_bytes=limit << 20),
+        compiler_params=pltpu.CompilerParams(vmem_limit_bytes=int(limit * (1 << 20))),
         cost_estimate=pl.CostEstimate(flops=flops, bytes_accessed=1 << 20, transcendentals=0),
     )(*args)
 
@@ -396,12 +415,19 @@
     weights = (gains, w_qkv, w_out, w_up, w_down.transpose(0, 2, 1))
 
     bias_shape = (2, HEADS * T, 128)
-    table_scratch = [pltpu.VMEM((HEADS, POS), F32), pltpu.VMEM((2, 2, 72, 128), F32)]
+    table_scratch = [pltpu.VMEM((HEADS, POS), F32), pltpu.VMEM((2, 2, 80, 128), F32)]
     kv_scratch = [pltpu.VMEM((2, 4, 2, PAIR, D), BF)] * 2
     streams = [shape(T, D), shape(144, 128), shape(144, 128)]
     stream, west, east = call(
-        first_kernel, streams, levels, fields.reshape(T, D), *weights, tables, sel_reg, to_oct,
-        scratch=[*table_scratch, pltpu.VMEM(bias_shape, F32)], flops=1 << 31, scalars=1,
+        first_kernel, streams, levels, fields.transpose(1, 2, 0, 3).reshape(T // 2, 2, D), *weights,
+        tables, sel_reg, to_oct,
+        scratch=[
+            *table_scratch, pltpu.VMEM(bias_shape, F32), pltpu.VMEM((T // 2, 2, D), BF),
+            pltpu.VMEM((BLOCKS, 2, D), F32), pltpu.VMEM((D, 3 * D), BF), pltpu.VMEM((D, D), BF),
+            pltpu.VMEM((D, FF), BF), pltpu.VMEM((D, FF), BF), pltpu.VMEM((1, HEADS, 4, POS), BF),
+            pltpu.VMEM((512, 256), BF), pltpu.VMEM((8 * SLOT, T), BF), pltpu.SemaphoreType.DMA((9,)),
+        ],
+        flops=1 << 31, scalars=1, place=pltpu.HBM, limit=FIRST_LIMIT,
     )
     rows = [shape(2, 2, 48, 128), shape(192, 128)]
     bias2, keep1, send1, keep3, send3 = call(
@@ -415,10 +441,10 @@
     )
     *ready, bias3 = halo(3, west, east, keep3, send3, w_qkv, sel_shift, pad)
     stream = call(
-        last_kernel, shape(T, D), stream, *ready, *weights, bias3, back,
+        last_kernel, shape(T // 2, 2, D), stream, *ready, *weights, bias3, back,
         scratch=kv_scratch, flops=1 << 31,
     )
-    return stream.reshape(2, 6, 12, D)
+    return stream.reshape(6, 12, 2, D).transpose(2, 0, 1, 3)
 
 
 def solution(mesh):

time: 99.8 us -> 92.8 us (0.930)
  local copies, waits for them, and re-layouts: 10.1 us -> 0.09 us
  Pallas kernels: 17.5 us -> 20.3 us
    unnamed x37 -> x32, local copies, waits for them, and re-layouts: 9.31 us -> 0.09 us
    pallas_call x12, Pallas kernels: 17.5 us -> 20.3 us  [call(): pl.pallas_call(kernel, out_shape=outs, in_specs=specs, scratch_shapes=lis...]
where the time goes in v3:
time: 92.8 us; the launch traced here: 92.3 us
  starting transfers between devices  42 us (45%)
  waiting for transfers between devices  29 us (31%)
  Pallas kernels  20.3 us (22%)
    ppermute x12, starting transfers between devices, move(): lax.ppermute(value, axis, [(i, (i + steps) % count) for i in range(count)])  42 us
    ppermute x12, waiting for transfers between devices, move(): lax.ppermute(value, axis, [(i, (i + steps) % count) for i in range(count)])  29 us
    pallas_call x12, Pallas kernels, call(): pl.pallas_call(kernel, out_shape=outs, in_specs=specs, scratch_shapes=lis...  20.3 us
  transfers between devices with their start and end apart: 12, of which 7 were waited for; matrix products, arithmetic and copies ran while one was open for 0% of the time, Pallas kernels for 5%

profile of v3, /device:TPU:255, one launch (start us, length us, event | category | flops | bytes accessed | tf_op | source)
XLA Modules:
  0.0 92.3 jit_solution(7460959455109993285)
XLA Ops:
  0.6 5.5 %shard_map.127 = (bf16[144,192]{1,0:T(8,128)(2,1)}, bf16[144,128]{1,0:T(8,128)(2,1)}, bf16[144,128]{1,0:T(8,128)(2,1)}) custom-call(s32[2]{0:T(128)} %pad_add_fusion.lev_ref, bf16[72,2,192]{2,1,0:T(2,128)(2,1)} %bitcast.19, f32[4,2,192]{2,1,0:T(2,128)} %gains.3, bf16[4,192,576]{2,1,0:T(8,128)(2,1)} %w_qkv.7, bf16[4,192,192]{2,1,0:T(8,128)(2,1)} %w_out.3, ...), custom_call_target="tpu_custom_call" | custom-call | flops 2147483648 | bytes 1048576 | tf_op jit(solution)/shard_map/pallas_call | solution.py:361
  6.1 7.5 %collective-permute-start = (bf16[144,128]{1,0:T(8,128)(2,1)}, bf16[144,128]{1,0:T(8,128)(2,1)S(1)}, u32[]{:S(2)}, u32[]{:S(2)}) collective-permute-start(bf16[144,128]{1,0:T(8,128)(2,1)} %get-tuple-element.31.own_e), channel_id=1, source_target_pairs={{0,32},{32,64},{64,96},{96,128},{128,160},{160,192},{192,224},{224... | collective-permute-start | bytes 110600 | tf_op jit(solution)/shard_map/ppermute | solution.py:377
  13.5 1.9 %collective-permute-start.1 = (bf16[144,128]{1,0:T(8,128)(2,1)}, bf16[144,128]{1,0:T(8,128)(2,1)S(1)}, u32[]{:S(2)}, u32[]{:S(2)}) collective-permute-start(bf16[144,128]{1,0:T(8,128)(2,1)} %get-tuple-element.32.own_w), channel_id=1, source_target_pairs={{0,480},{32,0},{64,32},{96,64},{128,96},{160,128},{192,160},{224,1... | collective-permute-start | bytes 110600 | tf_op jit(solution)/shard_map/ppermute | solution.py:377
  15.5 2.5 %shard_map.128 = (f32[2,864,128]{2,1,0:T(8,128)S(1)}, bf16[2,2,48,128]{3,2,1,0:T(8,128)(2,1)S(1)}, bf16[192,128]{1,0:T(8,128)(2,1)S(1)}, bf16[2,2,48,128]{3,2,1,0:T(8,128)(2,1)S(1)}, bf16[192,128]{1,0:T(8,128)(2,1)S(1)}) custom-call(s32[2]{0:T(128)S(1)} %copy-done.13, bf16[4,6,4,3312]{3,2,1,0:T(4,128)(2,1)S(1)} %bitcast.17, s32[6,8,12]{2,1,0:T(8,128)S(1)} %bitcast.18, ...), custom_call_target="tpu_custom_call" | custom-call | flops 2147483648 | bytes 1048576 | tf_op jit(solution)/shard_map/pallas_call | solution.py:361
  18.1 6.7 %collective-permute-done.1.recv_e = bf16[144,128]{1,0:T(8,128)(2,1)S(1)} collective-permute-done((bf16[144,128]{1,0:T(8,128)(2,1)}, bf16[144,128]{1,0:T(8,128)(2,1)S(1)}, u32[]{:S(2)}, u32[]{:S(2)}) %collective-permute-start.1) | collective-permute-done | bytes 36896 | tf_op jit(solution)/shard_map/ppermute | solution.py:377
  25.0 3.9 %collective-permute-start.2 = (bf16[480,128]{1,0:T(8,128)(2,1)S(1)}, bf16[480,128]{1,0:T(8,128)(2,1)S(1)}, u32[]{:S(2)}, u32[]{:S(2)}) collective-permute-start(bf16[480,128]{1,0:T(8,128)(2,1)S(1)} %get-tuple-element.34.north), channel_id=1, source_target_pairs={{0,4},{4,8},{8,12},{12,16},{16,20},{20,24},{24,28},{28,0},{1,5},{5... | collective-permute-start | bytes 368648 | tf_op jit(solution)/shard_map/ppermute | solution.py:377
  28.9 2.0 %collective-permute-start.3 = (bf16[288,128]{1,0:T(8,128)(2,1)S(1)}, bf16[288,128]{1,0:T(8,128)(2,1)S(1)}, u32[]{:S(2)}, u32[]{:S(2)}) collective-permute-start(bf16[288,128]{1,0:T(8,128)(2,1)S(1)} %get-tuple-element.35.south), channel_id=1, source_target_pairs={{0,28},{4,0},{8,4},{12,8},{16,12},{20,16},{24,20},{28,24},{1,29},{... | collective-permute-start | bytes 221192 | tf_op jit(solution)/shard_map/ppermute | solution.py:377
  30.9 5.4 %collective-permute-done.3.recv_n = bf16[288,128]{1,0:T(8,128)(2,1)S(1)} collective-permute-done((bf16[288,128]{1,0:T(8,128)(2,1)S(1)}, bf16[288,128]{1,0:T(8,128)(2,1)S(1)}, u32[]{:S(2)}, u32[]{:S(2)}) %collective-permute-start.3) | collective-permute-done | bytes 73760 | tf_op jit(solution)/shard_map/ppermute | solution.py:377
  36.5 2.1 %collective-permute-start.4 = (bf16[576,128]{1,0:T(8,128)(2,1)S(1)}, bf16[576,128]{1,0:T(8,128)(2,1)S(1)}, u32[]{:S(2)}, u32[]{:S(2)}) collective-permute-start(bf16[576,128]{1,0:T(8,128)(2,1)S(1)} %get-tuple-element.36.up), channel_id=1, source_target_pairs={{0,1},{1,2},{2,3},{3,0},{4,5},{5,6},{6,7},{7,4},{8,9},{9,10},{10,1... | collective-permute-start | bytes 442376 | tf_op jit(solution)/shard_map/ppermute | solution.py:377
  38.7 3.3 %collective-permute-start.5 = (bf16[576,128]{1,0:T(8,128)(2,1)S(1)}, bf16[576,128]{1,0:T(8,128)(2,1)S(1)}, u32[]{:S(2)}, u32[]{:S(2)}) collective-permute-start(bf16[576,128]{1,0:T(8,128)(2,1)S(1)} %get-tuple-element.37.down), channel_id=1, source_target_pairs={{0,3},{1,0},{2,1},{3,2},{4,7},{5,4},{6,5},{7,6},{8,11},{9,8},{10,9... | collective-permute-start | bytes 442376 | tf_op jit(solution)/shard_map/ppermute | solution.py:377
  43.3 3.1 %collective-permute-done.5.above = bf16[576,128]{1,0:T(8,128)(2,1)S(1)} collective-permute-done((bf16[576,128]{1,0:T(8,128)(2,1)S(1)}, bf16[576,128]{1,0:T(8,128)(2,1)S(1)}, u32[]{:S(2)}, u32[]{:S(2)}) %collective-permute-start.5) | collective-permute-done | bytes 147488 | tf_op jit(solution)/shard_map/ppermute | solution.py:377
  46.5 5.2 %shard_map.133 = (bf16[144,192]{1,0:T(8,128)(2,1)S(1)}, bf16[144,128]{1,0:T(8,128)(2,1)S(1)}, bf16[144,128]{1,0:T(8,128)(2,1)S(1)}) custom-call(bf16[144,192]{1,0:T(8,128)(2,1)S(1)} %copy-done.15, bf16[576,128]{1,0:T(8,128)(2,1)S(1)} %collective-permute-done.4.below, bf16[576,128]{1,0:T(8,128)(2,1)S(1)} %collective-permute-done.5.above, ...), custom_call_target="tpu_custom_call" | custom-call | flops 2147483648 | bytes 1048576 | tf_op jit(solution)/shard_map/pallas_call | solution.py:361
  51.8 4.4 %collective-permute-start.6 = (bf16[144,128]{1,0:T(8,128)(2,1)S(1)}, bf16[144,128]{1,0:T(8,128)(2,1)S(1)}, u32[]{:S(2)}, u32[]{:S(2)}) collective-permute-start(bf16[144,128]{1,0:T(8,128)(2,1)S(1)} %get-tuple-element.44.own_e), channel_id=1, source_target_pairs={{0,32},{32,64},{64,96},{96,128},{128,160},{160,192},{192,224},{224... | collective-permute-start | bytes 110600 | tf_op jit(solution)/shard_map/ppermute | solution.py:377
  56.1 4.8 %collective-permute-start.7 = (bf16[144,128]{1,0:T(8,128)(2,1)S(1)}, bf16[144,128]{1,0:T(8,128)(2,1)S(1)}, u32[]{:S(2)}, u32[]{:S(2)}) collective-permute-start(bf16[144,128]{1,0:T(8,128)(2,1)S(1)} %get-tuple-element.45.own_w), channel_id=1, source_target_pairs={{0,480},{32,0},{64,32},{96,64},{128,96},{160,128},{192,160},{224,1... | collective-permute-start | bytes 110600 | tf_op jit(solution)/shard_map/ppermute | solution.py:377
  61.0 0.7 collective-permute-done.6.recv_w
  61.7 5.1 %collective-permute-done.7.recv_e = bf16[144,128]{1,0:T(8,128)(2,1)S(1)} collective-permute-done((bf16[144,128]{1,0:T(8,128)(2,1)S(1)}, bf16[144,128]{1,0:T(8,128)(2,1)S(1)}, u32[]{:S(2)}, u32[]{:S(2)}) %collective-permute-start.7) | collective-permute-done | bytes 36896 | tf_op jit(solution)/shard_map/ppermute | solution.py:377
  67.0 4.7 %collective-permute-start.8 = (bf16[480,128]{1,0:T(8,128)(2,1)S(1)}, bf16[480,128]{1,0:T(8,128)(2,1)S(1)}, u32[]{:S(2)}, u32[]{:S(2)}) collective-permute-start(bf16[480,128]{1,0:T(8,128)(2,1)S(1)} %get-tuple-element.47.north), channel_id=1, source_target_pairs={{0,4},{4,8},{8,12},{12,16},{16,20},{20,24},{24,28},{28,0},{1,5},{5... | collective-permute-start | bytes 368648 | tf_op jit(solution)/shard_map/ppermute | solution.py:377
  71.7 1.9 %collective-permute-start.9 = (bf16[288,128]{1,0:T(8,128)(2,1)S(1)}, bf16[288,128]{1,0:T(8,128)(2,1)S(1)}, u32[]{:S(2)}, u32[]{:S(2)}) collective-permute-start(bf16[288,128]{1,0:T(8,128)(2,1)S(1)} %get-tuple-element.48.south), channel_id=1, source_target_pairs={{0,28},{4,0},{8,4},{12,8},{16,12},{20,16},{24,20},{28,24},{1,29},{... | collective-permute-start | bytes 221192 | tf_op jit(solution)/shard_map/ppermute | solution.py:377
  73.6 5.5 %collective-permute-done.9.recv_n = bf16[288,128]{1,0:T(8,128)(2,1)S(1)} collective-permute-done((bf16[288,128]{1,0:T(8,128)(2,1)S(1)}, bf16[288,128]{1,0:T(8,128)(2,1)S(1)}, u32[]{:S(2)}, u32[]{:S(2)}) %collective-permute-start.9) | collective-permute-done | bytes 73760 | tf_op jit(solution)/shard_map/ppermute | solution.py:377
  79.4 1.9 %collective-permute-start.10 = (bf16[576,128]{1,0:T(8,128)(2,1)S(1)}, bf16[576,128]{1,0:T(8,128)(2,1)S(1)}, u32[]{:S(2)}, u32[]{:S(2)}) collective-permute-start(bf16[576,128]{1,0:T(8,128)(2,1)S(1)} %get-tuple-element.49.up), channel_id=1, source_target_pairs={{0,1},{1,2},{2,3},{3,0},{4,5},{5,6},{6,7},{7,4},{8,9},{9,10},{10,1... | collective-permute-start | bytes 442376 | tf_op jit(solution)/shard_map/ppermute | solution.py:377
  81.3 3.5 %collective-permute-start.11 = (bf16[576,128]{1,0:T(8,128)(2,1)S(1)}, bf16[576,128]{1,0:T(8,128)(2,1)S(1)}, u32[]{:S(2)}, u32[]{:S(2)}) collective-permute-start(bf16[576,128]{1,0:T(8,128)(2,1)S(1)} %get-tuple-element.50.down), channel_id=1, source_target_pairs={{0,3},{1,0},{2,1},{3,2},{4,7},{5,4},{6,5},{7,6},{8,11},{9,8},{10,9... | collective-permute-start | bytes 442376 | tf_op jit(solution)/shard_map/ppermute | solution.py:377
  85.4 0.7 shard_map.137.bias3
  86.1 2.3 %collective-permute-done.11.above = bf16[576,128]{1,0:T(8,128)(2,1)S(1)} collective-permute-done((bf16[576,128]{1,0:T(8,128)(2,1)S(1)}, bf16[576,128]{1,0:T(8,128)(2,1)S(1)}, u32[]{:S(2)}, u32[]{:S(2)}) %collective-permute-start.11) | collective-permute-done | bytes 147488 | tf_op jit(solution)/shard_map/ppermute | solution.py:377
  88.4 3.9 %shard_map.138 = bf16[72,2,192]{2,1,0:T(2,128)(2,1)} custom-call(bf16[144,192]{1,0:T(8,128)(2,1)S(1)} %get-tuple-element.43.stream_in, bf16[576,128]{1,0:T(8,128)(2,1)S(1)} %collective-permute-done.10.below, bf16[576,128]{1,0:T(8,128)(2,1)S(1)} %collective-permute-done.11.above, f32[192,192]{1,0:T(8,128)S(1)} %get-tuple-element.51.q, ...), custom_call_target="tpu_custom_call" | custom-call | flops 2147483648 | bytes 1048576 | tf_op jit(solution)/shard_map/pallas_call | solution.py:361
  (45 shorter events, 3.1 us)
Async XLA Ops:
  0.6 14.9 %copy-start.5 = (bf16[4,4,1,6,3312]{4,1,3,2,0:T(4,128)(2,1)S(1)}, bf16[4,4,1,6,3312]{4,1,3,2,0:T(4,128)(2,1)}, u32[]{:S(2)}) copy-start(bf16[4,4,1,6,3312]{4,1,3,2,0:T(4,128)(2,1)} %param.19) | copy-start | bytes 1907716
  0.6 14.9 %copy-start.7 = (s32[8,6,12]{2,0,1:T(8,128)S(1)}, s32[8,6,12]{2,0,1:T(8,128)}, u32[]{:S(2)}) copy-start(s32[8,6,12]{2,0,1:T(8,128)} %param.20) | copy-start | bytes 6916
  0.6 14.9 %copy-start.10 = (bf16[512,256]{1,0:T(8,128)(2,1)S(1)}, bf16[512,256]{1,0:T(8,128)(2,1)}, u32[]{:S(2)}) copy-start(bf16[512,256]{1,0:T(8,128)(2,1)} %constant.30.clone.sel_hbm.sel_ref) | copy-start | bytes 786436
  0.6 14.9 %copy-start.13 = (s32[2]{0:T(128)S(1)}, s32[2]{0:T(128)}, u32[]{:S(2)}) copy-start(s32[2]{0:T(128)} %pad_add_fusion.lev_ref) | copy-start | bytes 28
  6.1 12.0 %collective-permute-start = (bf16[144,128]{1,0:T(8,128)(2,1)}, bf16[144,128]{1,0:T(8,128)(2,1)S(1)}, u32[]{:S(2)}, u32[]{:S(2)}) collective-permute-start(bf16[144,128]{1,0:T(8,128)(2,1)} %get-tuple-element.31.own_e), channel_id=1, source_target_pairs={{0,32},{32,64},{64,96},{96,128},{128,160},{160,192},{192,224},{224... | collective-permute-start | bytes 110600 | tf_op jit(solution)/shard_map/ppermute | solution.py:377
  13.5 11.3 %collective-permute-start.1 = (bf16[144,128]{1,0:T(8,128)(2,1)}, bf16[144,128]{1,0:T(8,128)(2,1)S(1)}, u32[]{:S(2)}, u32[]{:S(2)}) collective-permute-start(bf16[144,128]{1,0:T(8,128)(2,1)} %get-tuple-element.32.own_w), channel_id=1, source_target_pairs={{0,480},{32,0},{64,32},{96,64},{128,96},{160,128},{192,160},{224,1... | collective-permute-start | bytes 110600 | tf_op jit(solution)/shard_map/ppermute | solution.py:377
  15.5 9.3 %copy-start = (bf16[144,128]{1,0:T(8,128)(2,1)S(1)}, bf16[144,128]{1,0:T(8,128)(2,1)}, u32[]{:S(2)}) copy-start(bf16[144,128]{1,0:T(8,128)(2,1)} %get-tuple-element.32.own_w) | copy-start | bytes 110596
  15.5 9.3 %copy-start.1 = (bf16[144,128]{1,0:T(8,128)(2,1)S(1)}, bf16[144,128]{1,0:T(8,128)(2,1)}, u32[]{:S(2)}) copy-start(bf16[144,128]{1,0:T(8,128)(2,1)} %get-tuple-element.31.own_e) | copy-start | bytes 110596
  15.5 26.5 %copy-start.4 = (bf16[4,192,576]{2,1,0:T(8,128)(2,1)S(1)}, bf16[4,192,576]{2,1,0:T(8,128)(2,1)}, u32[]{:S(2)}) copy-start(bf16[4,192,576]{2,1,0:T(8,128)(2,1)} %w_qkv.7) | copy-start | bytes 2654212
  25.0 11.4 %collective-permute-start.2 = (bf16[480,128]{1,0:T(8,128)(2,1)S(1)}, bf16[480,128]{1,0:T(8,128)(2,1)S(1)}, u32[]{:S(2)}, u32[]{:S(2)}) collective-permute-start(bf16[480,128]{1,0:T(8,128)(2,1)S(1)} %get-tuple-element.34.north), channel_id=1, source_target_pairs={{0,4},{4,8},{8,12},{12,16},{16,20},{20,24},{24,28},{28,0},{1,5},{5... | collective-permute-start | bytes 368648 | tf_op jit(solution)/shard_map/ppermute | solution.py:377
  28.9 7.5 %collective-permute-start.3 = (bf16[288,128]{1,0:T(8,128)(2,1)S(1)}, bf16[288,128]{1,0:T(8,128)(2,1)S(1)}, u32[]{:S(2)}, u32[]{:S(2)}) collective-permute-start(bf16[288,128]{1,0:T(8,128)(2,1)S(1)} %get-tuple-element.35.south), channel_id=1, source_target_pairs={{0,28},{4,0},{8,4},{12,8},{16,12},{20,16},{24,20},{28,24},{1,29},{... | collective-permute-start | bytes 221192 | tf_op jit(solution)/shard_map/ppermute | solution.py:377
  36.5 6.8 %collective-permute-start.4 = (bf16[576,128]{1,0:T(8,128)(2,1)S(1)}, bf16[576,128]{1,0:T(8,128)(2,1)S(1)}, u32[]{:S(2)}, u32[]{:S(2)}) collective-permute-start(bf16[576,128]{1,0:T(8,128)(2,1)S(1)} %get-tuple-element.36.up), channel_id=1, source_target_pairs={{0,1},{1,2},{2,3},{3,0},{4,5},{5,6},{6,7},{7,4},{8,9},{9,10},{10,1... | collective-permute-start | bytes 442376 | tf_op jit(solution)/shard_map/ppermute | solution.py:377
  38.6 3.9 %copy-start.9 = (bf16[512,256]{1,0:T(8,128)(2,1)S(1)}, bf16[512,256]{1,0:T(8,128)(2,1)}, u32[]{:S(2)}) copy-start(bf16[512,256]{1,0:T(8,128)(2,1)} %constant.31.clone.sel_ref) | copy-start | bytes 786436
  38.6 3.9 %copy-start.14 = (f32[1,256]{1,0:T(1,128)S(1)}, f32[1,256]{1,0:T(1,128)}, u32[]{:S(2)}) copy-start(f32[1,256]{1,0:T(1,128)} %constant.32.clone.pad_ref) | copy-start | bytes 3076
  38.7 7.8 %collective-permute-start.5 = (bf16[576,128]{1,0:T(8,128)(2,1)S(1)}, bf16[576,128]{1,0:T(8,128)(2,1)S(1)}, u32[]{:S(2)}, u32[]{:S(2)}) collective-permute-start(bf16[576,128]{1,0:T(8,128)(2,1)S(1)} %get-tuple-element.37.down), channel_id=1, source_target_pairs={{0,3},{1,0},{2,1},{3,2},{4,7},{5,4},{6,5},{7,6},{8,11},{9,8},{10,9... | collective-permute-start | bytes 442376 | tf_op jit(solution)/shard_map/ppermute | solution.py:377
  42.6 3.9 %copy-start.2 = (bf16[4,192,768]{2,1,0:T(8,128)(2,1)S(1)}, bf16[4,192,768]{2,1,0:T(8,128)(2,1)}, u32[]{:S(2)}) copy-start(bf16[4,192,768]{2,1,0:T(8,128)(2,1)} %w_up.3) | copy-start | bytes 3538948
  42.6 3.9 %copy-start.3 = (bf16[4,768,192]{1,2,0:T(8,128)(2,1)S(1)}, bf16[4,768,192]{1,2,0:T(8,128)(2,1)}, u32[]{:S(2)}) copy-start(bf16[4,768,192]{1,2,0:T(8,128)(2,1)} %param.17) | copy-start | bytes 3538948
  42.6 3.9 %copy-start.6 = (bf16[4,192,192]{2,1,0:T(8,128)(2,1)S(1)}, bf16[4,192,192]{2,1,0:T(8,128)(2,1)}, u32[]{:S(2)}) copy-start(bf16[4,192,192]{2,1,0:T(8,128)(2,1)} %w_out.3) | copy-start | bytes 884740
  51.8 9.9 %collective-permute-start.6 = (bf16[144,128]{1,0:T(8,128)(2,1)S(1)}, bf16[144,128]{1,0:T(8,128)(2,1)S(1)}, u32[]{:S(2)}, u32[]{:S(2)}) collective-permute-start(bf16[144,128]{1,0:T(8,128)(2,1)S(1)} %get-tuple-element.44.own_e), channel_id=1, source_target_pairs={{0,32},{32,64},{64,96},{96,128},{128,160},{160,192},{192,224},{224... | collective-permute-start | bytes 110600 | tf_op jit(solution)/shard_map/ppermute | solution.py:377
  56.1 10.7 %collective-permute-start.7 = (bf16[144,128]{1,0:T(8,128)(2,1)S(1)}, bf16[144,128]{1,0:T(8,128)(2,1)S(1)}, u32[]{:S(2)}, u32[]{:S(2)}) collective-permute-start(bf16[144,128]{1,0:T(8,128)(2,1)S(1)} %get-tuple-element.45.own_w), channel_id=1, source_target_pairs={{0,480},{32,0},{64,32},{96,64},{128,96},{160,128},{192,160},{224,1... | collective-permute-start | bytes 110600 | tf_op jit(solution)/shard_map/ppermute | solution.py:377
  67.0 12.2 %collective-permute-start.8 = (bf16[480,128]{1,0:T(8,128)(2,1)S(1)}, bf16[480,128]{1,0:T(8,128)(2,1)S(1)}, u32[]{:S(2)}, u32[]{:S(2)}) collective-permute-start(bf16[480,128]{1,0:T(8,128)(2,1)S(1)} %get-tuple-element.47.north), channel_id=1, source_target_pairs={{0,4},{4,8},{8,12},{12,16},{16,20},{20,24},{24,28},{28,0},{1,5},{5... | collective-permute-start | bytes 368648 | tf_op jit(solution)/shard_map/ppermute | solution.py:377
  71.7 7.5 %collective-permute-start.9 = (bf16[288,128]{1,0:T(8,128)(2,1)S(1)}, bf16[288,128]{1,0:T(8,128)(2,1)S(1)}, u32[]{:S(2)}, u32[]{:S(2)}) collective-permute-start(bf16[288,128]{1,0:T(8,128)(2,1)S(1)} %get-tuple-element.48.south), channel_id=1, source_target_pairs={{0,28},{4,0},{8,4},{12,8},{16,12},{20,16},{24,20},{28,24},{1,29},{... | collective-permute-start | bytes 221192 | tf_op jit(solution)/shard_map/ppermute | solution.py:377
  79.4 6.7 %collective-permute-start.10 = (bf16[576,128]{1,0:T(8,128)(2,1)S(1)}, bf16[576,128]{1,0:T(8,128)(2,1)S(1)}, u32[]{:S(2)}, u32[]{:S(2)}) collective-permute-start(bf16[576,128]{1,0:T(8,128)(2,1)S(1)} %get-tuple-element.49.up), channel_id=1, source_target_pairs={{0,1},{1,2},{2,3},{3,0},{4,5},{5,6},{6,7},{7,4},{8,9},{9,10},{10,1... | collective-permute-start | bytes 442376 | tf_op jit(solution)/shard_map/ppermute | solution.py:377
  81.3 7.1 %collective-permute-start.11 = (bf16[576,128]{1,0:T(8,128)(2,1)S(1)}, bf16[576,128]{1,0:T(8,128)(2,1)S(1)}, u32[]{:S(2)}, u32[]{:S(2)}) collective-permute-start(bf16[576,128]{1,0:T(8,128)(2,1)S(1)} %get-tuple-element.50.down), channel_id=1, source_target_pairs={{0,3},{1,0},{2,1},{3,2},{4,7},{5,4},{6,5},{7,6},{8,11},{9,8},{10,9... | collective-permute-start | bytes 442376 | tf_op jit(solution)/shard_map/ppermute | solution.py:377
  (4 other events, 15.5 us)

commit v4 on v3

--- a/solution.py
+++ b/solution.py
@@ -261,8 +261,8 @@
         send[...] = half[1].astype(BF).reshape(192, 128)
 
 
-def bias_shifted_kernel(keep, south, sel_ref, pad_ref, out_ref):
-    moved = south[288:].reshape(2, 2, 48, 128)
+def bias_shifted_kernel(lev_ref, keep, far, near, sel_ref, pad_ref, out_ref):
+    moved = choose(lev_ref[2], near[288:], far[288:]).reshape(2, 2, 48, 128)
     parts = []
     for zq in range(2):
         rows = [jnp.concatenate([src[zq, 0], src[zq, 1]], axis=1) for src in (moved, keep)]
@@ -278,15 +278,20 @@
                 put(out_ref, pl.ds(base, 24, stride=6), rows[at : at + 24])
 
 
-def halves(stream, gain, to_oct, west, east):
+def choose(odd, value_odd, value_even):
+    return jnp.where(odd == 1, value_odd, value_even)
+
+
+def halves(lev_ref, stream, gain, to_oct, far, near):
     octs = dot(to_oct, layer_norm(stream.astype(F32), gain))
-    west[...] = pack(octs[: 4 * SLOT])
-    east[...] = pack(octs[4 * SLOT :])
+    west, east = pack(octs[: 4 * SLOT]), pack(octs[4 * SLOT :])
+    far[...] = choose(lev_ref[3], east, west)
+    near[...] = choose(lev_ref[3], west, east)
 
 
 def first_kernel(
     lev_ref, x_hbm, gains_hbm, w_qkv_hbm, w_out_hbm, w_up_hbm, w_down_hbm, table_hbm, sel_hbm,
-    oct_hbm, stream_out, west, east, table, lhs, bias, x, gains, w_qkv, w_out, w_up, w_down,
+    oct_hbm, stream_out, far, near, table, lhs, bias, x, gains, w_qkv, w_out, w_up, w_down,
     rows, sel, to_oct, sems,
 ):
     pairs = (
@@ -309,12 +314,12 @@
         w_out[...], w_up[...], w_down[...], bias,
     )
     stream_out[...] = stream
-    halves(stream, gains[1, 0:1], to_oct[...], west, east)
+    halves(lev_ref, stream, gains[1, 0:1], to_oct[...], far, near)
 
 
 def middle_kernel(
-    stream_in, below, above, q, k_own, v_own, gains, w_qkv, w_out, w_up, w_down, bias1, bias2,
-    to_oct, back, stream_out, west, east, k_ref, v_ref,
+    lev_ref, stream_in, below, above, q, k_own, v_own, gains, w_qkv, w_out, w_up, w_down, bias1,
+    bias2, to_oct, back, stream_out, far, near, k_ref, v_ref,
 ):
     stream = shifted_block(
         stream_in[...], below, above, q, k_own, v_own, gains[1, 1:2], w_qkv[1], w_out[1], w_up[1],
@@ -324,7 +329,7 @@
         stream, gains[2, 0:1], gains[2, 1:2], w_qkv[2], w_out[2], w_up[2], w_down[2], bias2
     )
     stream_out[...] = stream
-    halves(stream, gains[3, 0:1], to_oct[...], west, east)
+    halves(lev_ref, stream, gains[3, 0:1], to_oct[...], far, near)
 
 
 def last_kernel(
@@ -338,18 +343,24 @@
     out[...] = stream.astype(F32).reshape(T // 2, 2, D).astype(BF)
 
 
-def lat_pack_kernel(recv_w, own_w, own_e, recv_e, table_rows, south, north):
-    parts = [unpack(ref[...]) for ref in (recv_w, own_w, own_e, recv_e)]
-    for yh, ref in ((0, south), (1, north)):
+def lat_pack_kernel(lev_ref, recv_far, own_far, own_near, recv_near, table_rows, far, near):
+    parts = [unpack(ref[...]) for ref in (recv_far, own_far, own_near, recv_near)]
+    parts = [choose(lev_ref[3], parts[3 - i], parts[i]) for i in range(4)]
+    packed = []
+    for yh in range(2):
         rows = [
             part[(yh * 2 + z) * SLOT : (yh * 2 + z + 1) * SLOT] for z in range(2) for part in parts
         ]
-        ref[:288] = pack(jnp.concatenate(rows, axis=0))
-    north[288:] = table_rows[...]
-
-
-def lev_pack_kernel(recv_s, south, north, recv_n, down, up):
-    parts = [unpack(ref[:288]) for ref in (recv_s, south, north, recv_n)]
+        packed.append(pack(jnp.concatenate(rows, axis=0)))
+    far[:288] = choose(lev_ref[2], packed[1], packed[0])
+    near[:288] = choose(lev_ref[2], packed[0], packed[1])
+    far[288:] = table_rows[...]
+    near[288:] = table_rows[...]
+
+
+def lev_pack_kernel(lev_ref, recv_far, own_far, own_near, recv_near, down, up):
+    parts = [unpack(ref[:288]) for ref in (recv_far, own_far, own_near, recv_near)]
+    parts = [choose(lev_ref[2], parts[3 - i], parts[i]) for i in range(4)]
     for z, ref in ((0, down), (1, up)):
         rows = [part[z * 4 * SLOT : (z + 1) * 4 * SLOT] for part in parts]
         ref[...] = pack(jnp.concatenate(rows, axis=0))
@@ -377,17 +388,24 @@
     return lax.ppermute(value, axis, [(i, (i + steps) % count) for i in range(count)])
 
 
-def halo(block, west, east, keep, send, w_qkv, sel_shift, pad):
-    recv_e = move(west, "lon", -1)
-    recv_w = move(east, "lon", 1)
-    south, north = call(
-        lat_pack_kernel, [shape(288, 128), shape(480, 128)], recv_w, west, east, recv_e, send,
-        limit=4,
-    )
-    recv_n = move(south, "lat", -1)
-    recv_s = move(north, "lat", 1)
+def swap(value, axis, far):
+    count = lax.axis_size(axis)
+    steps = (-1, 1) if far else (1, -1)
+    return lax.ppermute(value, axis, [(i, (i + steps[i % 2]) % count) for i in range(count)])
+
+
+def halo(block, levels, far, near, keep, send, w_qkv, sel_shift, pad):
+    recv_far = swap(far, "lon", True)
+    recv_near = swap(near, "lon", False)
+    far, near = call(
+        lat_pack_kernel, [shape(480, 128)] * 2, levels, recv_far, far, near, recv_near, send,
+        limit=4, scalars=1,
+    )
+    recv_far = swap(far, "lat", True)
+    recv_near = swap(near, "lat", False)
     down, up = call(
-        lev_pack_kernel, [shape(576, 128)] * 2, recv_s, south, north, recv_n, limit=4
+        lev_pack_kernel, [shape(576, 128)] * 2, levels, recv_far, far, near, recv_near,
+        limit=4, scalars=1,
     )
     above = move(down, "lev", -1)
     below = move(up, "lev", 1)
@@ -397,15 +415,16 @@
         down, up, w_qkv, flops=1 << 30, limit=8,
     )
     bias = call(
-        bias_shifted_kernel, shape(2, 8 * 144, 128, dtype=F32), keep, recv_s, sel_shift, pad,
-        flops=1 << 30, limit=8,
+        bias_shifted_kernel, shape(2, 8 * 144, 128, dtype=F32), levels, keep, recv_far, recv_near,
+        sel_shift, pad, flops=1 << 30, limit=8, scalars=1,
     )
     return below, above, q, k, v, bias
 
 
 def per_device(fields, w_qkv, w_out, w_up, w_down, gains, bias_table, labels):
     level = lax.axis_index("lev")
-    levels = jnp.stack([(level + 3) % 4, level]).astype(jnp.int32)
+    odd = [lax.axis_index(axis) % 2 for axis in ("lat", "lon")]
+    levels = jnp.stack([(level + 3) % 4, level, *odd]).astype(jnp.int32)
     to_oct, back = [jnp.asarray(m, BF) for m in octant_maps()]
     sel_reg, sel_shift, pad = selectors()
     sel_reg, sel_shift = jnp.asarray(sel_reg, BF), jnp.asarray(sel_shift, BF)
@@ -418,7 +437,7 @@
     table_scratch = [pltpu.VMEM((HEADS, POS), F32), pltpu.VMEM((2, 2, 80, 128), F32)]
     kv_scratch = [pltpu.VMEM((2, 4, 2, PAIR, D), BF)] * 2
     streams = [shape(T, D), shape(144, 128), shape(144, 128)]
-    stream, west, east = call(
+    stream, far, near = call(
         first_kernel, streams, levels, fields.transpose(1, 2, 0, 3).reshape(T // 2, 2, D), *weights,
         tables, sel_reg, to_oct,
         scratch=[
@@ -434,12 +453,12 @@
         tables_kernel, [shape(*bias_shape, dtype=F32), *rows, *rows], levels, tables, tags, sel_reg,
         scratch=[*table_scratch, pltpu.VMEM((2, 2, 2, 48, 128), F32)], flops=1 << 31, scalars=1,
     )
-    *ready, bias1 = halo(1, west, east, keep1, send1, w_qkv, sel_shift, pad)
-    stream, west, east = call(
-        middle_kernel, streams, stream, *ready, *weights, bias1, bias2, to_oct, back,
-        scratch=kv_scratch, flops=1 << 31,
-    )
-    *ready, bias3 = halo(3, west, east, keep3, send3, w_qkv, sel_shift, pad)
+    *ready, bias1 = halo(1, levels, far, near, keep1, send1, w_qkv, sel_shift, pad)
+    stream, far, near = call(
+        middle_kernel, streams, levels, stream, *ready, *weights, bias1, bias2, to_oct, back,
+        scratch=kv_scratch, flops=1 << 31, scalars=1,
+    )
+    *ready, bias3 = halo(3, levels, far, near, keep3, send3, w_qkv, sel_shift, pad)
     stream = call(
         last_kernel, shape(T // 2, 2, D), stream, *ready, *weights, bias3, back,
         scratch=kv_scratch, flops=1 << 31,

time: 92.8 us -> 94.8 us (1.022)
  the two profiles are of different devices: /device:TPU:255 before, /device:TPU:6 now
where the time goes in v4:
time: 94.8 us; the launch traced here: 94.3 us
  starting transfers between devices  43.9 us (46%)
  waiting for transfers between devices  25.3 us (27%)
  Pallas kernels  24 us (25%)
    ppermute x8, starting transfers between devices, swap(): lax.ppermute(value, axis, [(i, (i + steps[i % 2]) % count) for i in range...  31.9 us
    pallas_call x12, Pallas kernels, call(): pl.pallas_call(kernel, out_shape=outs, in_specs=specs, scratch_shapes=lis...  24 us
    ppermute x8, waiting for transfers between devices, swap(): lax.ppermute(value, axis, [(i, (i + steps[i % 2]) % count) for i in range...  19.8 us
    ppermute x4, starting transfers between devices, move(): lax.ppermute(value, axis, [(i, (i + steps) % count) for i in range(count)])  12 us
    ppermute x4, waiting for transfers between devices, move(): lax.ppermute(value, axis, [(i, (i + steps) % count) for i in range(count)])  5.5 us
  transfers between devices with their start and end apart: 12, of which 7 were waited for; matrix products, arithmetic and copies ran while one was open for 0% of the time, Pallas kernels for 6%

profile of v4, /device:TPU:6, one launch (start us, length us, event | category | flops | bytes accessed | tf_op | source)
XLA Modules:
  0.0 94.3 jit_solution(2441663897810105270)
XLA Ops:
  0.6 5.5 %shard_map.127 = (bf16[144,192]{1,0:T(8,128)(2,1)}, bf16[144,128]{1,0:T(8,128)(2,1)}, bf16[144,128]{1,0:T(8,128)(2,1)}) custom-call(s32[4]{0:T(128)} %pad_add_fusion.lev_ref, bf16[72,2,192]{2,1,0:T(2,128)(2,1)} %bitcast.21, f32[4,2,192]{2,1,0:T(2,128)} %gains.3, bf16[4,192,576]{2,1,0:T(8,128)(2,1)} %w_qkv.7, bf16[4,192,192]{2,1,0:T(8,128)(2,1)} %w_out.3, ...), custom_call_target="tpu_custom_call" | custom-call | flops 2147483648 | bytes 1048576 | tf_op jit(solution)/shard_map/pallas_call | solution.py:372
  6.1 16.2 %collective-permute-start = (bf16[144,128]{1,0:T(8,128)(2,1)}, bf16[144,128]{1,0:T(8,128)(2,1)S(1)}, u32[]{:S(2)}, u32[]{:S(2)}) collective-permute-start(bf16[144,128]{1,0:T(8,128)(2,1)} %get-tuple-element.31.own_far), channel_id=1, source_target_pairs={{0,480},{32,64},{64,32},{96,128},{128,96},{160,192},{192,160},{224... | collective-permute-start | bytes 110600 | tf_op jit(solution)/shard_map/ppermute | solution.py:394
  22.3 1.9 %collective-permute-start.1 = (bf16[144,128]{1,0:T(8,128)(2,1)}, bf16[144,128]{1,0:T(8,128)(2,1)S(1)}, u32[]{:S(2)}, u32[]{:S(2)}) collective-permute-start(bf16[144,128]{1,0:T(8,128)(2,1)} %get-tuple-element.32.own_near), channel_id=1, source_target_pairs={{0,32},{32,0},{64,96},{96,64},{128,160},{160,128},{192,224},{224,1... | collective-permute-start | bytes 110600 | tf_op jit(solution)/shard_map/ppermute | solution.py:394
  24.3 2.5 %shard_map.128 = (f32[2,864,128]{2,1,0:T(8,128)S(1)}, bf16[2,2,48,128]{3,2,1,0:T(8,128)(2,1)S(1)}, bf16[192,128]{1,0:T(8,128)(2,1)S(1)}, bf16[2,2,48,128]{3,2,1,0:T(8,128)(2,1)S(1)}, bf16[192,128]{1,0:T(8,128)(2,1)S(1)}) custom-call(s32[4]{0:T(128)S(1)} %copy-done.2, bf16[4,6,4,3312]{3,2,1,0:T(4,128)(2,1)S(1)} %bitcast.19, s32[6,8,12]{2,1,0:T(8,128)S(1)} %bitcast.20, ...), custom_call_target="tpu_custom_call" | custom-call | flops 2147483648 | bytes 1048576 | tf_op jit(solution)/shard_map/pallas_call | solution.py:372
  26.8 5.4 %collective-permute-done.1.recv_near = bf16[144,128]{1,0:T(8,128)(2,1)S(1)} collective-permute-done((bf16[144,128]{1,0:T(8,128)(2,1)}, bf16[144,128]{1,0:T(8,128)(2,1)S(1)}, u32[]{:S(2)}, u32[]{:S(2)}) %collective-permute-start.1) | collective-permute-done | bytes 36896 | tf_op jit(solution)/shard_map/ppermute | solution.py:394
  33.0 1.9 %collective-permute-start.2 = (bf16[480,128]{1,0:T(8,128)(2,1)S(1)}, bf16[480,128]{1,0:T(8,128)(2,1)S(1)}, u32[]{:S(2)}, u32[]{:S(2)}) collective-permute-start(bf16[480,128]{1,0:T(8,128)(2,1)S(1)} %get-tuple-element.34.own_far), channel_id=1, source_target_pairs={{0,28},{4,8},{8,4},{12,16},{16,12},{20,24},{24,20},{28,0},{1,29},{... | collective-permute-start | bytes 368648 | tf_op jit(solution)/shard_map/ppermute | solution.py:394
  34.9 3.1 %collective-permute-start.3 = (bf16[480,128]{1,0:T(8,128)(2,1)S(1)}, bf16[480,128]{1,0:T(8,128)(2,1)S(1)}, u32[]{:S(2)}, u32[]{:S(2)}) collective-permute-start(bf16[480,128]{1,0:T(8,128)(2,1)S(1)} %get-tuple-element.35.own_near), channel_id=1, source_target_pairs={{0,4},{4,0},{8,12},{12,8},{16,20},{20,16},{24,28},{28,24},{1,5},{5... | collective-permute-start | bytes 368648 | tf_op jit(solution)/shard_map/ppermute | solution.py:394
  38.0 3.0 %collective-permute-done.2.recv_far.far = bf16[480,128]{1,0:T(8,128)(2,1)S(1)} collective-permute-done((bf16[480,128]{1,0:T(8,128)(2,1)S(1)}, bf16[480,128]{1,0:T(8,128)(2,1)S(1)}, u32[]{:S(2)}, u32[]{:S(2)}) %collective-permute-start.2) | collective-permute-done | bytes 122912 | tf_op jit(solution)/shard_map/ppermute | solution.py:394
  41.7 2.4 %collective-permute-start.4 = (bf16[576,128]{1,0:T(8,128)(2,1)S(1)}, bf16[576,128]{1,0:T(8,128)(2,1)S(1)}, u32[]{:S(2)}, u32[]{:S(2)}) collective-permute-start(bf16[576,128]{1,0:T(8,128)(2,1)S(1)} %get-tuple-element.36.up), channel_id=1, source_target_pairs={{0,1},{1,2},{2,3},{3,0},{4,5},{5,6},{6,7},{7,4},{8,9},{9,10},{10,1... | collective-permute-start | bytes 442376 | tf_op jit(solution)/shard_map/ppermute | solution.py:388
  44.1 3.6 %collective-permute-start.5 = (bf16[576,128]{1,0:T(8,128)(2,1)S(1)}, bf16[576,128]{1,0:T(8,128)(2,1)S(1)}, u32[]{:S(2)}, u32[]{:S(2)}) collective-permute-start(bf16[576,128]{1,0:T(8,128)(2,1)S(1)} %get-tuple-element.37.down), channel_id=1, source_target_pairs={{0,3},{1,0},{2,1},{3,2},{4,7},{5,4},{6,5},{7,6},{8,11},{9,8},{10,9... | collective-permute-start | bytes 442376 | tf_op jit(solution)/shard_map/ppermute | solution.py:388
  48.4 1.2 %shard_map.132.bias1 = f32[2,1152,128]{2,1,0:T(8,128)S(1)} custom-call(s32[4]{0:T(128)S(1)} %copy-done.2, bf16[2,2,48,128]{3,2,1,0:T(8,128)(2,1)S(1)} %get-tuple-element.41.keep, bf16[480,128]{1,0:T(8,128)(2,1)S(1)} %collective-permute-done.2.recv_far.far, bf16[480,128]{1,0:T(8,128)(2,1)S(1)} %collective-permute-done.3.recv_near.near, ...), custom_call_target="tpu_custom_call" | custom-call | flops 1073741824 | bytes 1048576 | tf_op jit(solution)/shard_map/pallas_call | solution.py:372
  49.6 2.9 %collective-permute-done.5.above = bf16[576,128]{1,0:T(8,128)(2,1)S(1)} collective-permute-done((bf16[576,128]{1,0:T(8,128)(2,1)S(1)}, bf16[576,128]{1,0:T(8,128)(2,1)S(1)}, u32[]{:S(2)}, u32[]{:S(2)}) %collective-permute-start.5) | collective-permute-done | bytes 147488 | tf_op jit(solution)/shard_map/ppermute | solution.py:388
  52.6 5.8 %shard_map.133 = (bf16[144,192]{1,0:T(8,128)(2,1)S(1)}, bf16[144,128]{1,0:T(8,128)(2,1)S(1)}, bf16[144,128]{1,0:T(8,128)(2,1)S(1)}) custom-call(s32[4]{0:T(128)S(1)} %copy-done.2, bf16[144,192]{1,0:T(8,128)(2,1)S(1)} %copy-done.15, bf16[576,128]{1,0:T(8,128)(2,1)S(1)} %collective-permute-done.4.below, bf16[576,128]{1,0:T(8,128)(2,1)S(1)} %collective-permute-done.5.above, ...), custom_call_target="tpu_custom_call" | custom-call | flops 2147483648 | bytes 1048576 | tf_op jit(solution)/shard_map/pallas_call | solution.py:372
  58.3 2.4 %collective-permute-start.6 = (bf16[144,128]{1,0:T(8,128)(2,1)S(1)}, bf16[144,128]{1,0:T(8,128)(2,1)S(1)}, u32[]{:S(2)}, u32[]{:S(2)}) collective-permute-start(bf16[144,128]{1,0:T(8,128)(2,1)S(1)} %get-tuple-element.44.own_far), channel_id=1, source_target_pairs={{0,480},{32,64},{64,32},{96,128},{128,96},{160,192},{192,160},{224... | collective-permute-start | bytes 110600 | tf_op jit(solution)/shard_map/ppermute | solution.py:394
  60.8 1.9 %collective-permute-start.7 = (bf16[144,128]{1,0:T(8,128)(2,1)S(1)}, bf16[144,128]{1,0:T(8,128)(2,1)S(1)}, u32[]{:S(2)}, u32[]{:S(2)}) collective-permute-start(bf16[144,128]{1,0:T(8,128)(2,1)S(1)} %get-tuple-element.45.own_near), channel_id=1, source_target_pairs={{0,32},{32,0},{64,96},{96,64},{128,160},{160,128},{192,224},{224,1... | collective-permute-start | bytes 110600 | tf_op jit(solution)/shard_map/ppermute | solution.py:394
  62.7 7.5 %collective-permute-done.6.recv_far = bf16[144,128]{1,0:T(8,128)(2,1)S(1)} collective-permute-done((bf16[144,128]{1,0:T(8,128)(2,1)S(1)}, bf16[144,128]{1,0:T(8,128)(2,1)S(1)}, u32[]{:S(2)}, u32[]{:S(2)}) %collective-permute-start.6) | collective-permute-done | bytes 36896 | tf_op jit(solution)/shard_map/ppermute | solution.py:394
  71.2 2.0 %collective-permute-start.8 = (bf16[480,128]{1,0:T(8,128)(2,1)S(1)}, bf16[480,128]{1,0:T(8,128)(2,1)S(1)}, u32[]{:S(2)}, u32[]{:S(2)}) collective-permute-start(bf16[480,128]{1,0:T(8,128)(2,1)S(1)} %get-tuple-element.47.own_far), channel_id=1, source_target_pairs={{0,28},{4,8},{8,4},{12,16},{16,12},{20,24},{24,20},{28,0},{1,29},{... | collective-permute-start | bytes 368648 | tf_op jit(solution)/shard_map/ppermute | solution.py:394
  73.2 2.4 %collective-permute-start.9 = (bf16[480,128]{1,0:T(8,128)(2,1)S(1)}, bf16[480,128]{1,0:T(8,128)(2,1)S(1)}, u32[]{:S(2)}, u32[]{:S(2)}) collective-permute-start(bf16[480,128]{1,0:T(8,128)(2,1)S(1)} %get-tuple-element.48.own_near), channel_id=1, source_target_pairs={{0,4},{4,0},{8,12},{12,8},{16,20},{20,16},{24,28},{28,24},{1,5},{5... | collective-permute-start | bytes 368648 | tf_op jit(solution)/shard_map/ppermute | solution.py:394
  75.7 3.6 %collective-permute-done.8.recv_far.far = bf16[480,128]{1,0:T(8,128)(2,1)S(1)} collective-permute-done((bf16[480,128]{1,0:T(8,128)(2,1)S(1)}, bf16[480,128]{1,0:T(8,128)(2,1)S(1)}, u32[]{:S(2)}, u32[]{:S(2)}) %collective-permute-start.8) | collective-permute-done | bytes 122912 | tf_op jit(solution)/shard_map/ppermute | solution.py:394
  79.9 2.2 %collective-permute-start.10 = (bf16[576,128]{1,0:T(8,128)(2,1)S(1)}, bf16[576,128]{1,0:T(8,128)(2,1)S(1)}, u32[]{:S(2)}, u32[]{:S(2)}) collective-permute-start(bf16[576,128]{1,0:T(8,128)(2,1)S(1)} %get-tuple-element.49.up), channel_id=1, source_target_pairs={{0,1},{1,2},{2,3},{3,0},{4,5},{5,6},{6,7},{7,4},{8,9},{9,10},{10,1... | collective-permute-start | bytes 442376 | tf_op jit(solution)/shard_map/ppermute | solution.py:388
  82.1 3.8 %collective-permute-start.11 = (bf16[576,128]{1,0:T(8,128)(2,1)S(1)}, bf16[576,128]{1,0:T(8,128)(2,1)S(1)}, u32[]{:S(2)}, u32[]{:S(2)}) collective-permute-start(bf16[576,128]{1,0:T(8,128)(2,1)S(1)} %get-tuple-element.50.down), channel_id=1, source_target_pairs={{0,3},{1,0},{2,1},{3,2},{4,7},{5,4},{6,5},{7,6},{8,11},{9,8},{10,9... | collective-permute-start | bytes 442376 | tf_op jit(solution)/shard_map/ppermute | solution.py:388
  86.5 1.2 %shard_map.137.bias3 = f32[2,1152,128]{2,1,0:T(8,128)S(1)} custom-call(s32[4]{0:T(128)S(1)} %copy-done.2, bf16[2,2,48,128]{3,2,1,0:T(8,128)(2,1)S(1)} %get-tuple-element.54.keep, bf16[480,128]{1,0:T(8,128)(2,1)S(1)} %collective-permute-done.8.recv_far.far, bf16[480,128]{1,0:T(8,128)(2,1)S(1)} %collective-permute-done.9.recv_near.near, ...), custom_call_target="tpu_custom_call" | custom-call | flops 1073741824 | bytes 1048576 | tf_op jit(solution)/shard_map/pallas_call | solution.py:372
  87.8 2.6 %collective-permute-done.11.above = bf16[576,128]{1,0:T(8,128)(2,1)S(1)} collective-permute-done((bf16[576,128]{1,0:T(8,128)(2,1)S(1)}, bf16[576,128]{1,0:T(8,128)(2,1)S(1)}, u32[]{:S(2)}, u32[]{:S(2)}) %collective-permute-start.11) | collective-permute-done | bytes 147488 | tf_op jit(solution)/shard_map/ppermute | solution.py:388
  90.4 3.9 %shard_map.138 = bf16[72,2,192]{2,1,0:T(2,128)(2,1)} custom-call(bf16[144,192]{1,0:T(8,128)(2,1)S(1)} %get-tuple-element.43.stream_in, bf16[576,128]{1,0:T(8,128)(2,1)S(1)} %collective-permute-done.10.below, bf16[576,128]{1,0:T(8,128)(2,1)S(1)} %collective-permute-done.11.above, f32[192,192]{1,0:T(8,128)S(1)} %get-tuple-element.51.q, ...), custom_call_target="tpu_custom_call" | custom-call | flops 2147483648 | bytes 1048576 | tf_op jit(solution)/shard_map/pallas_call | solution.py:372
  (45 shorter events, 4.9 us)
Async XLA Ops:
  0.6 23.6 %copy-start.2 = (s32[4]{0:T(128)S(1)}, s32[4]{0:T(128)}, u32[]{:S(2)}) copy-start(s32[4]{0:T(128)} %pad_add_fusion.lev_ref) | copy-start | bytes 52
  0.6 23.6 %copy-start.6 = (bf16[4,4,1,6,3312]{4,1,3,2,0:T(4,128)(2,1)S(1)}, bf16[4,4,1,6,3312]{4,1,3,2,0:T(4,128)(2,1)}, u32[]{:S(2)}) copy-start(bf16[4,4,1,6,3312]{4,1,3,2,0:T(4,128)(2,1)} %param.19) | copy-start | bytes 1907716
  0.6 23.7 %copy-start.8 = (s32[8,6,12]{2,0,1:T(8,128)S(1)}, s32[8,6,12]{2,0,1:T(8,128)}, u32[]{:S(2)}) copy-start(s32[8,6,12]{2,0,1:T(8,128)} %param.20) | copy-start | bytes 6916
  0.6 23.7 %copy-start.11 = (bf16[512,256]{1,0:T(8,128)(2,1)S(1)}, bf16[512,256]{1,0:T(8,128)(2,1)}, u32[]{:S(2)}) copy-start(bf16[512,256]{1,0:T(8,128)(2,1)} %constant.55.clone.sel_hbm.sel_ref) | copy-start | bytes 786436
  6.1 20.7 %collective-permute-start = (bf16[144,128]{1,0:T(8,128)(2,1)}, bf16[144,128]{1,0:T(8,128)(2,1)S(1)}, u32[]{:S(2)}, u32[]{:S(2)}) collective-permute-start(bf16[144,128]{1,0:T(8,128)(2,1)} %get-tuple-element.31.own_far), channel_id=1, source_target_pairs={{0,480},{32,64},{64,32},{96,128},{128,96},{160,192},{192,160},{224... | collective-permute-start | bytes 110600 | tf_op jit(solution)/shard_map/ppermute | solution.py:394
  22.3 10.0 %collective-permute-start.1 = (bf16[144,128]{1,0:T(8,128)(2,1)}, bf16[144,128]{1,0:T(8,128)(2,1)S(1)}, u32[]{:S(2)}, u32[]{:S(2)}) collective-permute-start(bf16[144,128]{1,0:T(8,128)(2,1)} %get-tuple-element.32.own_near), channel_id=1, source_target_pairs={{0,32},{32,0},{64,96},{96,64},{128,160},{160,128},{192,224},{224,1... | collective-permute-start | bytes 110600 | tf_op jit(solution)/shard_map/ppermute | solution.py:394
  24.3 8.0 %copy-start = (bf16[144,128]{1,0:T(8,128)(2,1)S(1)}, bf16[144,128]{1,0:T(8,128)(2,1)}, u32[]{:S(2)}) copy-start(bf16[144,128]{1,0:T(8,128)(2,1)} %get-tuple-element.31.own_far) | copy-start | bytes 110596
  24.3 8.0 %copy-start.1 = (bf16[144,128]{1,0:T(8,128)(2,1)S(1)}, bf16[144,128]{1,0:T(8,128)(2,1)}, u32[]{:S(2)}) copy-start(bf16[144,128]{1,0:T(8,128)(2,1)} %get-tuple-element.32.own_near) | copy-start | bytes 110596
  24.3 23.4 %copy-start.5 = (bf16[4,192,576]{2,1,0:T(8,128)(2,1)S(1)}, bf16[4,192,576]{2,1,0:T(8,128)(2,1)}, u32[]{:S(2)}) copy-start(bf16[4,192,576]{2,1,0:T(8,128)(2,1)} %w_qkv.7) | copy-start | bytes 2654212
  33.0 8.0 %collective-permute-start.2 = (bf16[480,128]{1,0:T(8,128)(2,1)S(1)}, bf16[480,128]{1,0:T(8,128)(2,1)S(1)}, u32[]{:S(2)}, u32[]{:S(2)}) collective-permute-start(bf16[480,128]{1,0:T(8,128)(2,1)S(1)} %get-tuple-element.34.own_far), channel_id=1, source_target_pairs={{0,28},{4,8},{8,4},{12,16},{16,12},{20,24},{24,20},{28,0},{1,29},{... | collective-permute-start | bytes 368648 | tf_op jit(solution)/shard_map/ppermute | solution.py:394
  34.9 6.1 %collective-permute-start.3 = (bf16[480,128]{1,0:T(8,128)(2,1)S(1)}, bf16[480,128]{1,0:T(8,128)(2,1)S(1)}, u32[]{:S(2)}, u32[]{:S(2)}) collective-permute-start(bf16[480,128]{1,0:T(8,128)(2,1)S(1)} %get-tuple-element.35.own_near), channel_id=1, source_target_pairs={{0,4},{4,0},{8,12},{12,8},{16,20},{20,16},{24,28},{28,24},{1,5},{5... | collective-permute-start | bytes 368648 | tf_op jit(solution)/shard_map/ppermute | solution.py:394
  41.7 7.9 %collective-permute-start.4 = (bf16[576,128]{1,0:T(8,128)(2,1)S(1)}, bf16[576,128]{1,0:T(8,128)(2,1)S(1)}, u32[]{:S(2)}, u32[]{:S(2)}) collective-permute-start(bf16[576,128]{1,0:T(8,128)(2,1)S(1)} %get-tuple-element.36.up), channel_id=1, source_target_pairs={{0,1},{1,2},{2,3},{3,0},{4,5},{5,6},{6,7},{7,4},{8,9},{9,10},{10,1... | collective-permute-start | bytes 442376 | tf_op jit(solution)/shard_map/ppermute | solution.py:388
  44.1 4.2 %copy-start.10 = (bf16[512,256]{1,0:T(8,128)(2,1)S(1)}, bf16[512,256]{1,0:T(8,128)(2,1)}, u32[]{:S(2)}) copy-start(bf16[512,256]{1,0:T(8,128)(2,1)} %constant.56.clone.sel_ref) | copy-start | bytes 786436
  44.1 4.2 %copy-start.14 = (f32[1,256]{1,0:T(1,128)S(1)}, f32[1,256]{1,0:T(1,128)}, u32[]{:S(2)}) copy-start(f32[1,256]{1,0:T(1,128)} %constant.57.clone.pad_ref) | copy-start | bytes 3076
  44.1 8.4 %collective-permute-start.5 = (bf16[576,128]{1,0:T(8,128)(2,1)S(1)}, bf16[576,128]{1,0:T(8,128)(2,1)S(1)}, u32[]{:S(2)}, u32[]{:S(2)}) collective-permute-start(bf16[576,128]{1,0:T(8,128)(2,1)S(1)} %get-tuple-element.37.down), channel_id=1, source_target_pairs={{0,3},{1,0},{2,1},{3,2},{4,7},{5,4},{6,5},{7,6},{8,11},{9,8},{10,9... | collective-permute-start | bytes 442376 | tf_op jit(solution)/shard_map/ppermute | solution.py:388
  48.3 4.2 %copy-start.3 = (bf16[4,192,768]{2,1,0:T(8,128)(2,1)S(1)}, bf16[4,192,768]{2,1,0:T(8,128)(2,1)}, u32[]{:S(2)}) copy-start(bf16[4,192,768]{2,1,0:T(8,128)(2,1)} %w_up.3) | copy-start | bytes 3538948
  48.3 4.2 %copy-start.4 = (bf16[4,768,192]{1,2,0:T(8,128)(2,1)S(1)}, bf16[4,768,192]{1,2,0:T(8,128)(2,1)}, u32[]{:S(2)}) copy-start(bf16[4,768,192]{1,2,0:T(8,128)(2,1)} %param.17) | copy-start | bytes 3538948
  48.3 4.2 %copy-start.7 = (bf16[4,192,192]{2,1,0:T(8,128)(2,1)S(1)}, bf16[4,192,192]{2,1,0:T(8,128)(2,1)}, u32[]{:S(2)}) copy-start(bf16[4,192,192]{2,1,0:T(8,128)(2,1)} %w_out.3) | copy-start | bytes 884740
  58.3 11.9 %collective-permute-start.6 = (bf16[144,128]{1,0:T(8,128)(2,1)S(1)}, bf16[144,128]{1,0:T(8,128)(2,1)S(1)}, u32[]{:S(2)}, u32[]{:S(2)}) collective-permute-start(bf16[144,128]{1,0:T(8,128)(2,1)S(1)} %get-tuple-element.44.own_far), channel_id=1, source_target_pairs={{0,480},{32,64},{64,32},{96,128},{128,96},{160,192},{192,160},{224... | collective-permute-start | bytes 110600 | tf_op jit(solution)/shard_map/ppermute | solution.py:394
  60.8 9.8 %collective-permute-start.7 = (bf16[144,128]{1,0:T(8,128)(2,1)S(1)}, bf16[144,128]{1,0:T(8,128)(2,1)S(1)}, u32[]{:S(2)}, u32[]{:S(2)}) collective-permute-start(bf16[144,128]{1,0:T(8,128)(2,1)S(1)} %get-tuple-element.45.own_near), channel_id=1, source_target_pairs={{0,32},{32,0},{64,96},{96,64},{128,160},{160,128},{192,224},{224,1... | collective-permute-start | bytes 110600 | tf_op jit(solution)/shard_map/ppermute | solution.py:394
  71.2 8.0 %collective-permute-start.8 = (bf16[480,128]{1,0:T(8,128)(2,1)S(1)}, bf16[480,128]{1,0:T(8,128)(2,1)S(1)}, u32[]{:S(2)}, u32[]{:S(2)}) collective-permute-start(bf16[480,128]{1,0:T(8,128)(2,1)S(1)} %get-tuple-element.47.own_far), channel_id=1, source_target_pairs={{0,28},{4,8},{8,4},{12,16},{16,12},{20,24},{24,20},{28,0},{1,29},{... | collective-permute-start | bytes 368648 | tf_op jit(solution)/shard_map/ppermute | solution.py:394
  73.2 6.0 %collective-permute-start.9 = (bf16[480,128]{1,0:T(8,128)(2,1)S(1)}, bf16[480,128]{1,0:T(8,128)(2,1)S(1)}, u32[]{:S(2)}, u32[]{:S(2)}) collective-permute-start(bf16[480,128]{1,0:T(8,128)(2,1)S(1)} %get-tuple-element.48.own_near), channel_id=1, source_target_pairs={{0,4},{4,0},{8,12},{12,8},{16,20},{20,16},{24,28},{28,24},{1,5},{5... | collective-permute-start | bytes 368648 | tf_op jit(solution)/shard_map/ppermute | solution.py:394
  79.9 7.8 %collective-permute-start.10 = (bf16[576,128]{1,0:T(8,128)(2,1)S(1)}, bf16[576,128]{1,0:T(8,128)(2,1)S(1)}, u32[]{:S(2)}, u32[]{:S(2)}) collective-permute-start(bf16[576,128]{1,0:T(8,128)(2,1)S(1)} %get-tuple-element.49.up), channel_id=1, source_target_pairs={{0,1},{1,2},{2,3},{3,0},{4,5},{5,6},{6,7},{7,4},{8,9},{9,10},{10,1... | collective-permute-start | bytes 442376 | tf_op jit(solution)/shard_map/ppermute | solution.py:388
  82.1 8.2 %collective-permute-start.11 = (bf16[576,128]{1,0:T(8,128)(2,1)S(1)}, bf16[576,128]{1,0:T(8,128)(2,1)S(1)}, u32[]{:S(2)}, u32[]{:S(2)}) collective-permute-start(bf16[576,128]{1,0:T(8,128)(2,1)S(1)} %get-tuple-element.50.down), channel_id=1, source_target_pairs={{0,3},{1,0},{2,1},{3,2},{4,7},{5,4},{6,5},{7,6},{8,11},{9,8},{10,9... | collective-permute-start | bytes 442376 | tf_op jit(solution)/shard_map/ppermute | solution.py:388
  (4 other events, 16.7 us)

commit v5 on v4

--- a/solution.py
+++ b/solution.py
@@ -224,9 +224,9 @@
 
 
 def tables_kernel(
-    lev_ref, table_ref, label_ref, sel_ref, bias2, keep1, send1, keep3, send3, table, lhs, half
+    table_ref, label_ref, sel_ref, bias2, keep1, send1, keep3, send3, table, lhs, half
 ):
-    pick_table(table_ref, 2, lev_ref[1], table)
+    pick_table(table_ref, 2, level_at(0), table)
     lhs[...] = jnp.zeros_like(lhs)
     bias_regular(table, sel_ref[...], lhs, bias2)
     lane = lax.broadcasted_iota(jnp.int32, (8, 128), 1)
@@ -240,7 +240,7 @@
     half[...] = jnp.zeros_like(half)
     for block, keep, send in ((1, keep1, send1), (3, keep3, send3)):
         for z in range(2):
-            window = lev_ref[z]
+            window = level_at(z - 1)
             pick_table(table_ref, block, window, table)
             keys = [
                 jnp.sum(jnp.where(level == window * 2 + zq, tags, 0.0), axis=0, keepdims=True)
@@ -261,8 +261,8 @@
         send[...] = half[1].astype(BF).reshape(192, 128)
 
 
-def bias_shifted_kernel(lev_ref, keep, far, near, sel_ref, pad_ref, out_ref):
-    moved = choose(lev_ref[2], near[288:], far[288:]).reshape(2, 2, 48, 128)
+def bias_shifted_kernel(keep, far, near, sel_ref, pad_ref, out_ref):
+    moved = choose(parity("lat"), near[288:], far[288:]).reshape(2, 2, 48, 128)
     parts = []
     for zq in range(2):
         rows = [jnp.concatenate([src[zq, 0], src[zq, 1]], axis=1) for src in (moved, keep)]
@@ -278,19 +278,27 @@
                 put(out_ref, pl.ds(base, 24, stride=6), rows[at : at + 24])
 
 
+def parity(axis):
+    return lax.rem(lax.axis_index(axis), 2)
+
+
+def level_at(steps):
+    return lax.rem(lax.axis_index("lev") + 4 + steps, 4)
+
+
 def choose(odd, value_odd, value_even):
     return jnp.where(odd == 1, value_odd, value_even)
 
 
-def halves(lev_ref, stream, gain, to_oct, far, near):
+def halves(stream, gain, to_oct, far, near):
     octs = dot(to_oct, layer_norm(stream.astype(F32), gain))
     west, east = pack(octs[: 4 * SLOT]), pack(octs[4 * SLOT :])
-    far[...] = choose(lev_ref[3], east, west)
-    near[...] = choose(lev_ref[3], west, east)
+    far[...] = choose(parity("lon"), east, west)
+    near[...] = choose(parity("lon"), west, east)
 
 
 def first_kernel(
-    lev_ref, x_hbm, gains_hbm, w_qkv_hbm, w_out_hbm, w_up_hbm, w_down_hbm, table_hbm, sel_hbm,
+    x_hbm, gains_hbm, w_qkv_hbm, w_out_hbm, w_up_hbm, w_down_hbm, table_hbm, sel_hbm,
     oct_hbm, stream_out, far, near, table, lhs, bias, x, gains, w_qkv, w_out, w_up, w_down,
     rows, sel, to_oct, sems,
 ):
@@ -303,7 +311,7 @@
     for copy in copies:
         copy.start()
     copies[0].wait()
-    pick_table(rows, 0, lev_ref[1], table)
+    pick_table(rows, 0, level_at(0), table)
     lhs[...] = jnp.zeros_like(lhs)
     copies[1].wait()
     bias_regular(table, sel[...], lhs, bias)
@@ -314,11 +322,11 @@
         w_out[...], w_up[...], w_down[...], bias,
     )
     stream_out[...] = stream
-    halves(lev_ref, stream, gains[1, 0:1], to_oct[...], far, near)
+    halves(stream, gains[1, 0:1], to_oct[...], far, near)
 
 
 def middle_kernel(
-    lev_ref, stream_in, below, above, q, k_own, v_own, gains, w_qkv, w_out, w_up, w_down, bias1,
+    stream_in, below, above, q, k_own, v_own, gains, w_qkv, w_out, w_up, w_down, bias1,
     bias2, to_oct, back, stream_out, far, near, k_ref, v_ref,
 ):
     stream = shifted_block(
@@ -329,7 +337,7 @@
         stream, gains[2, 0:1], gains[2, 1:2], w_qkv[2], w_out[2], w_up[2], w_down[2], bias2
     )
     stream_out[...] = stream
-    halves(lev_ref, stream, gains[3, 0:1], to_oct[...], far, near)
+    halves(stream, gains[3, 0:1], to_oct[...], far, near)
 
 
 def last_kernel(
@@ -343,32 +351,31 @@
     out[...] = stream.astype(F32).reshape(T // 2, 2, D).astype(BF)
 
 
-def lat_pack_kernel(lev_ref, recv_far, own_far, own_near, recv_near, table_rows, far, near):
+def lat_pack_kernel(recv_far, own_far, own_near, recv_near, table_rows, far, near):
     parts = [unpack(ref[...]) for ref in (recv_far, own_far, own_near, recv_near)]
-    parts = [choose(lev_ref[3], parts[3 - i], parts[i]) for i in range(4)]
+    parts = [choose(parity("lon"), parts[3 - i], parts[i]) for i in range(4)]
     packed = []
     for yh in range(2):
         rows = [
             part[(yh * 2 + z) * SLOT : (yh * 2 + z + 1) * SLOT] for z in range(2) for part in parts
         ]
         packed.append(pack(jnp.concatenate(rows, axis=0)))
-    far[:288] = choose(lev_ref[2], packed[1], packed[0])
-    near[:288] = choose(lev_ref[2], packed[0], packed[1])
+    far[:288] = choose(parity("lat"), packed[1], packed[0])
+    near[:288] = choose(parity("lat"), packed[0], packed[1])
     far[288:] = table_rows[...]
     near[288:] = table_rows[...]
 
 
-def lev_pack_kernel(lev_ref, recv_far, own_far, own_near, recv_near, down, up):
+def lev_pack_kernel(recv_far, own_far, own_near, recv_near, down, up):
     parts = [unpack(ref[:288]) for ref in (recv_far, own_far, own_near, recv_near)]
-    parts = [choose(lev_ref[2], parts[3 - i], parts[i]) for i in range(4)]
+    parts = [choose(parity("lat"), parts[3 - i], parts[i]) for i in range(4)]
     for z, ref in ((0, down), (1, up)):
         rows = [part[z * 4 * SLOT : (z + 1) * 4 * SLOT] for part in parts]
         ref[...] = pack(jnp.concatenate(rows, axis=0))
 
 
-def call(kernel, outs, *args, scratch=(), flops=0, limit=20, scalars=0, place=pltpu.VMEM):
-    specs = [pl.BlockSpec(memory_space=pltpu.SMEM)] * scalars
-    specs += [pl.BlockSpec(memory_space=place)] * (len(args) - scalars)
+def call(kernel, outs, *args, scratch=(), flops=0, limit=20, place=pltpu.VMEM):
+    specs = [pl.BlockSpec(memory_space=place)] * len(args)
     return pl.pallas_call(
         kernel,
         out_shape=outs,
@@ -394,18 +401,18 @@
     return lax.ppermute(value, axis, [(i, (i + steps[i % 2]) % count) for i in range(count)])
 
 
-def halo(block, levels, far, near, keep, send, w_qkv, sel_shift, pad):
+def halo(block, far, near, keep, send, w_qkv, sel_shift, pad):
     recv_far = swap(far, "lon", True)
     recv_near = swap(near, "lon", False)
     far, near = call(
-        lat_pack_kernel, [shape(480, 128)] * 2, levels, recv_far, far, near, recv_near, send,
-        limit=4, scalars=1,
+        lat_pack_kernel, [shape(480, 128)] * 2, recv_far, far, near, recv_near, send,
+        limit=4,
     )
     recv_far = swap(far, "lat", True)
     recv_near = swap(near, "lat", False)
     down, up = call(
-        lev_pack_kernel, [shape(576, 128)] * 2, levels, recv_far, far, near, recv_near,
-        limit=4, scalars=1,
+        lev_pack_kernel, [shape(576, 128)] * 2, recv_far, far, near, recv_near,
+        limit=4,
     )
     above = move(down, "lev", -1)
     below = move(up, "lev", 1)
@@ -415,16 +422,13 @@
         down, up, w_qkv, flops=1 << 30, limit=8,
     )
     bias = call(
-        bias_shifted_kernel, shape(2, 8 * 144, 128, dtype=F32), levels, keep, recv_far, recv_near,
-        sel_shift, pad, flops=1 << 30, limit=8, scalars=1,
+        bias_shifted_kernel, shape(2, 8 * 144, 128, dtype=F32), keep, recv_far, recv_near,
+        sel_shift, pad, flops=1 << 30, limit=8,
     )
     return below, above, q, k, v, bias
 
 
 def per_device(fields, w_qkv, w_out, w_up, w_down, gains, bias_table, labels):
-    level = lax.axis_index("lev")
-    odd = [lax.axis_index(axis) % 2 for axis in ("lat", "lon")]
-    levels = jnp.stack([(level + 3) % 4, level, *odd]).astype(jnp.int32)
     to_oct, back = [jnp.asarray(m, BF) for m in octant_maps()]
     sel_reg, sel_shift, pad = selectors()
     sel_reg, sel_shift = jnp.asarray(sel_reg, BF), jnp.asarray(sel_shift, BF)
@@ -438,7 +442,7 @@
     kv_scratch = [pltpu.VMEM((2, 4, 2, PAIR, D), BF)] * 2
     streams = [shape(T, D), shape(144, 128), shape(144, 128)]
     stream, far, near = call(
-        first_kernel, streams, levels, fields.transpose(1, 2, 0, 3).reshape(T // 2, 2, D), *weights,
+        first_kernel, streams, fields.transpose(1, 2, 0, 3).reshape(T // 2, 2, D), *weights,
         tables, sel_reg, to_oct,
         scratch=[
             *table_scratch, pltpu.VMEM(bias_shape, F32), pltpu.VMEM((T // 2, 2, D), BF),
@@ -446,19 +450,19 @@
             pltpu.VMEM((D, FF), BF), pltpu.VMEM((D, FF), BF), pltpu.VMEM((1, HEADS, 4, POS), BF),
             pltpu.VMEM((512, 256), BF), pltpu.VMEM((8 * SLOT, T), BF), pltpu.SemaphoreType.DMA((9,)),
         ],
-        flops=1 << 31, scalars=1, place=pltpu.HBM, limit=FIRST_LIMIT,
+        flops=1 << 31, place=pltpu.HBM, limit=FIRST_LIMIT,
     )
     rows = [shape(2, 2, 48, 128), shape(192, 128)]
     bias2, keep1, send1, keep3, send3 = call(
-        tables_kernel, [shape(*bias_shape, dtype=F32), *rows, *rows], levels, tables, tags, sel_reg,
-        scratch=[*table_scratch, pltpu.VMEM((2, 2, 2, 48, 128), F32)], flops=1 << 31, scalars=1,
-    )
-    *ready, bias1 = halo(1, levels, far, near, keep1, send1, w_qkv, sel_shift, pad)
+        tables_kernel, [shape(*bias_shape, dtype=F32), *rows, *rows], tables, tags, sel_reg,
+        scratch=[*table_scratch, pltpu.VMEM((2, 2, 2, 48, 128), F32)], flops=1 << 31,
+    )
+    *ready, bias1 = halo(1, far, near, keep1, send1, w_qkv, sel_shift, pad)
     stream, far, near = call(
-        middle_kernel, streams, levels, stream, *ready, *weights, bias1, bias2, to_oct, back,
-        scratch=kv_scratch, flops=1 << 31, scalars=1,
-    )
-    *ready, bias3 = halo(3, levels, far, near, keep3, send3, w_qkv, sel_shift, pad)
+        middle_kernel, streams, stream, *ready, *weights, bias1, bias2, to_oct, back,
+        scratch=kv_scratch, flops=1 << 31,
+    )
+    *ready, bias3 = halo(3, far, near, keep3, send3, w_qkv, sel_shift, pad)
     stream = call(
         last_kernel, shape(T // 2, 2, D), stream, *ready, *weights, bias3, back,
         scratch=kv_scratch, flops=1 << 31,

time: 94.8 us -> 90.5 us (0.955)
  Pallas kernels: 24 us -> 19 us
  waiting for transfers between devices: 25.3 us -> 26.9 us
    pallas_call x12, Pallas kernels: 24 us -> 19 us  [call(): pl.pallas_call(kernel, out_shape=outs, in_specs=specs, scratch_shapes=lis...]
    ppermute x4, waiting for transfers between devices: 5.5 us -> 6.53 us  [move(): lax.ppermute(value, axis, [(i, (i + steps) % count) for i in range(count)])]
  transfers between devices with their start and end apart: 12 -> 12, of which waited for: 7 -> 6; matrix products, arithmetic and copies ran while one was open for 0% -> 0% of each run, Pallas kernels for 6% -> 5%
where the time goes in v5:
time: 90.5 us; the launch traced here: 90 us
  starting transfers between devices  43.7 us (48%)
  waiting for transfers between devices  26.9 us (30%)
  Pallas kernels  19 us (21%)
    ppermute x8, starting transfers between devices, swap(): lax.ppermute(value, axis, [(i, (i + steps[i % 2]) % count) for i in range...  31.7 us
    ppermute x8, waiting for transfers between devices, swap(): lax.ppermute(value, axis, [(i, (i + steps[i % 2]) % count) for i in range...  20.4 us
    pallas_call x12, Pallas kernels, call(): pl.pallas_call(kernel, out_shape=outs, in_specs=specs, scratch_shapes=lis...  19 us
    ppermute x4, starting transfers between devices, move(): lax.ppermute(value, axis, [(i, (i + steps) % count) for i in range(count)])  12 us
    ppermute x4, waiting for transfers between devices, move(): lax.ppermute(value, axis, [(i, (i + steps) % count) for i in range(count)])  6.53 us
  transfers between devices with their start and end apart: 12, of which 6 were waited for; matrix products, arithmetic and copies ran while one was open for 0% of the time, Pallas kernels for 5%

profile of v5, /device:TPU:6, one launch (start us, length us, event | category | flops | bytes accessed | tf_op | source)
XLA Modules:
  0.0 90.0 jit_solution(15092711133568681497)
XLA Ops:
  0.0 4.8 %shard_map.127 = (bf16[144,192]{1,0:T(8,128)(2,1)}, bf16[144,128]{1,0:T(8,128)(2,1)}, bf16[144,128]{1,0:T(8,128)(2,1)}) custom-call(bf16[72,2,192]{2,1,0:T(2,128)(2,1)} %bitcast.17, f32[4,2,192]{2,1,0:T(2,128)} %gains.3, bf16[4,192,576]{2,1,0:T(8,128)(2,1)} %w_qkv.7, bf16[4,192,192]{2,1,0:T(8,128)(2,1)} %w_out.3, bf16[4,192,768]{2,1,0:T(8,128)(2,1)} %w_up.3, ...), custom_call_target="tpu_custom_call" | custom-call | flops 2147483648 | bytes 1048576 | tf_op jit(solution)/shard_map/pallas_call | solution.py:379
  4.8 16.2 %collective-permute-start = (bf16[144,128]{1,0:T(8,128)(2,1)}, bf16[144,128]{1,0:T(8,128)(2,1)S(1)}, u32[]{:S(2)}, u32[]{:S(2)}) collective-permute-start(bf16[144,128]{1,0:T(8,128)(2,1)} %get-tuple-element.31.own_far), channel_id=1, source_target_pairs={{0,480},{32,64},{64,32},{96,128},{128,96},{160,192},{192,160},{224... | collective-permute-start | bytes 110600 | tf_op jit(solution)/shard_map/ppermute | solution.py:401
  21.0 1.9 %collective-permute-start.1 = (bf16[144,128]{1,0:T(8,128)(2,1)}, bf16[144,128]{1,0:T(8,128)(2,1)S(1)}, u32[]{:S(2)}, u32[]{:S(2)}) collective-permute-start(bf16[144,128]{1,0:T(8,128)(2,1)} %get-tuple-element.32.own_near), channel_id=1, source_target_pairs={{0,32},{32,0},{64,96},{96,64},{128,160},{160,128},{192,224},{224,1... | collective-permute-start | bytes 110600 | tf_op jit(solution)/shard_map/ppermute | solution.py:401
  23.0 1.9 %shard_map.128 = (f32[2,864,128]{2,1,0:T(8,128)S(1)}, bf16[2,2,48,128]{3,2,1,0:T(8,128)(2,1)S(1)}, bf16[192,128]{1,0:T(8,128)(2,1)S(1)}, bf16[2,2,48,128]{3,2,1,0:T(8,128)(2,1)S(1)}, bf16[192,128]{1,0:T(8,128)(2,1)S(1)}) custom-call(bf16[4,6,4,3312]{3,2,1,0:T(4,128)(2,1)S(1)} %bitcast.15, s32[6,8,12]{2,1,0:T(8,128)S(1)} %bitcast.16, ...), custom_call_target="tpu_custom_call" | custom-call | flops 2147483648 | bytes 1048576 | tf_op jit(solution)/shard_map/pallas_call | solution.py:379
  24.9 6.1 %collective-permute-done.1.recv_near = bf16[144,128]{1,0:T(8,128)(2,1)S(1)} collective-permute-done((bf16[144,128]{1,0:T(8,128)(2,1)}, bf16[144,128]{1,0:T(8,128)(2,1)S(1)}, u32[]{:S(2)}, u32[]{:S(2)}) %collective-permute-start.1) | collective-permute-done | bytes 36896 | tf_op jit(solution)/shard_map/ppermute | solution.py:401
  31.1 1.9 %collective-permute-start.2 = (bf16[480,128]{1,0:T(8,128)(2,1)S(1)}, bf16[480,128]{1,0:T(8,128)(2,1)S(1)}, u32[]{:S(2)}, u32[]{:S(2)}) collective-permute-start(bf16[480,128]{1,0:T(8,128)(2,1)S(1)} %get-tuple-element.34.own_far), channel_id=1, source_target_pairs={{0,28},{4,8},{8,4},{12,16},{16,12},{20,24},{24,20},{28,0},{1,29},{... | collective-permute-start | bytes 368648 | tf_op jit(solution)/shard_map/ppermute | solution.py:401
  33.1 3.1 %collective-permute-start.3 = (bf16[480,128]{1,0:T(8,128)(2,1)S(1)}, bf16[480,128]{1,0:T(8,128)(2,1)S(1)}, u32[]{:S(2)}, u32[]{:S(2)}) collective-permute-start(bf16[480,128]{1,0:T(8,128)(2,1)S(1)} %get-tuple-element.35.own_near), channel_id=1, source_target_pairs={{0,4},{4,0},{8,12},{12,8},{16,20},{20,16},{24,28},{28,24},{1,5},{5... | collective-permute-start | bytes 368648 | tf_op jit(solution)/shard_map/ppermute | solution.py:401
  36.2 3.0 %collective-permute-done.2.recv_far.far = bf16[480,128]{1,0:T(8,128)(2,1)S(1)} collective-permute-done((bf16[480,128]{1,0:T(8,128)(2,1)S(1)}, bf16[480,128]{1,0:T(8,128)(2,1)S(1)}, u32[]{:S(2)}, u32[]{:S(2)}) %collective-permute-start.2) | collective-permute-done | bytes 122912 | tf_op jit(solution)/shard_map/ppermute | solution.py:401
  39.3 2.4 %collective-permute-start.4 = (bf16[576,128]{1,0:T(8,128)(2,1)S(1)}, bf16[576,128]{1,0:T(8,128)(2,1)S(1)}, u32[]{:S(2)}, u32[]{:S(2)}) collective-permute-start(bf16[576,128]{1,0:T(8,128)(2,1)S(1)} %get-tuple-element.36.up), channel_id=1, source_target_pairs={{0,1},{1,2},{2,3},{3,0},{4,5},{5,6},{6,7},{7,4},{8,9},{9,10},{10,1... | collective-permute-start | bytes 442376 | tf_op jit(solution)/shard_map/ppermute | solution.py:395
  41.8 3.6 %collective-permute-start.5 = (bf16[576,128]{1,0:T(8,128)(2,1)S(1)}, bf16[576,128]{1,0:T(8,128)(2,1)S(1)}, u32[]{:S(2)}, u32[]{:S(2)}) collective-permute-start(bf16[576,128]{1,0:T(8,128)(2,1)S(1)} %get-tuple-element.37.down), channel_id=1, source_target_pairs={{0,3},{1,0},{2,1},{3,2},{4,7},{5,4},{6,5},{7,6},{8,11},{9,8},{10,9... | collective-permute-start | bytes 442376 | tf_op jit(solution)/shard_map/ppermute | solution.py:395
  46.0 0.7 shard_map.132.bias1
  46.7 3.4 %collective-permute-done.5.above = bf16[576,128]{1,0:T(8,128)(2,1)S(1)} collective-permute-done((bf16[576,128]{1,0:T(8,128)(2,1)S(1)}, bf16[576,128]{1,0:T(8,128)(2,1)S(1)}, u32[]{:S(2)}, u32[]{:S(2)}) %collective-permute-start.5) | collective-permute-done | bytes 147488 | tf_op jit(solution)/shard_map/ppermute | solution.py:395
  50.2 5.2 %shard_map.133 = (bf16[144,192]{1,0:T(8,128)(2,1)S(1)}, bf16[144,128]{1,0:T(8,128)(2,1)S(1)}, bf16[144,128]{1,0:T(8,128)(2,1)S(1)}) custom-call(bf16[144,192]{1,0:T(8,128)(2,1)S(1)} %copy-done.14, bf16[576,128]{1,0:T(8,128)(2,1)S(1)} %collective-permute-done.4.below, bf16[576,128]{1,0:T(8,128)(2,1)S(1)} %collective-permute-done.5.above, ...), custom_call_target="tpu_custom_call" | custom-call | flops 2147483648 | bytes 1048576 | tf_op jit(solution)/shard_map/pallas_call | solution.py:379
  55.4 2.1 %collective-permute-start.6 = (bf16[144,128]{1,0:T(8,128)(2,1)S(1)}, bf16[144,128]{1,0:T(8,128)(2,1)S(1)}, u32[]{:S(2)}, u32[]{:S(2)}) collective-permute-start(bf16[144,128]{1,0:T(8,128)(2,1)S(1)} %get-tuple-element.44.own_far), channel_id=1, source_target_pairs={{0,480},{32,64},{64,32},{96,128},{128,96},{160,192},{192,160},{224... | collective-permute-start | bytes 110600 | tf_op jit(solution)/shard_map/ppermute | solution.py:401
  57.5 1.9 %collective-permute-start.7 = (bf16[144,128]{1,0:T(8,128)(2,1)S(1)}, bf16[144,128]{1,0:T(8,128)(2,1)S(1)}, u32[]{:S(2)}, u32[]{:S(2)}) collective-permute-start(bf16[144,128]{1,0:T(8,128)(2,1)S(1)} %get-tuple-element.45.own_near), channel_id=1, source_target_pairs={{0,32},{32,0},{64,96},{96,64},{128,160},{160,128},{192,224},{224,1... | collective-permute-start | bytes 110600 | tf_op jit(solution)/shard_map/ppermute | solution.py:401
  59.5 7.8 %collective-permute-done.6.recv_far = bf16[144,128]{1,0:T(8,128)(2,1)S(1)} collective-permute-done((bf16[144,128]{1,0:T(8,128)(2,1)S(1)}, bf16[144,128]{1,0:T(8,128)(2,1)S(1)}, u32[]{:S(2)}, u32[]{:S(2)}) %collective-permute-start.6) | collective-permute-done | bytes 36896 | tf_op jit(solution)/shard_map/ppermute | solution.py:401
  67.5 1.9 %collective-permute-start.8 = (bf16[480,128]{1,0:T(8,128)(2,1)S(1)}, bf16[480,128]{1,0:T(8,128)(2,1)S(1)}, u32[]{:S(2)}, u32[]{:S(2)}) collective-permute-start(bf16[480,128]{1,0:T(8,128)(2,1)S(1)} %get-tuple-element.47.own_far), channel_id=1, source_target_pairs={{0,28},{4,8},{8,4},{12,16},{16,12},{20,24},{24,20},{28,0},{1,29},{... | collective-permute-start | bytes 368648 | tf_op jit(solution)/shard_map/ppermute | solution.py:401
  69.4 2.6 %collective-permute-start.9 = (bf16[480,128]{1,0:T(8,128)(2,1)S(1)}, bf16[480,128]{1,0:T(8,128)(2,1)S(1)}, u32[]{:S(2)}, u32[]{:S(2)}) collective-permute-start(bf16[480,128]{1,0:T(8,128)(2,1)S(1)} %get-tuple-element.48.own_near), channel_id=1, source_target_pairs={{0,4},{4,0},{8,12},{12,8},{16,20},{20,16},{24,28},{28,24},{1,5},{5... | collective-permute-start | bytes 368648 | tf_op jit(solution)/shard_map/ppermute | solution.py:401
  72.0 3.5 %collective-permute-done.8.recv_far.far = bf16[480,128]{1,0:T(8,128)(2,1)S(1)} collective-permute-done((bf16[480,128]{1,0:T(8,128)(2,1)S(1)}, bf16[480,128]{1,0:T(8,128)(2,1)S(1)}, u32[]{:S(2)}, u32[]{:S(2)}) %collective-permute-start.8) | collective-permute-done | bytes 122912 | tf_op jit(solution)/shard_map/ppermute | solution.py:401
  75.7 2.2 %collective-permute-start.10 = (bf16[576,128]{1,0:T(8,128)(2,1)S(1)}, bf16[576,128]{1,0:T(8,128)(2,1)S(1)}, u32[]{:S(2)}, u32[]{:S(2)}) collective-permute-start(bf16[576,128]{1,0:T(8,128)(2,1)S(1)} %get-tuple-element.49.up), channel_id=1, source_target_pairs={{0,1},{1,2},{2,3},{3,0},{4,5},{5,6},{6,7},{7,4},{8,9},{9,10},{10,1... | collective-permute-start | bytes 442376 | tf_op jit(solution)/shard_map/ppermute | solution.py:395
  77.9 3.8 %collective-permute-start.11 = (bf16[576,128]{1,0:T(8,128)(2,1)S(1)}, bf16[576,128]{1,0:T(8,128)(2,1)S(1)}, u32[]{:S(2)}, u32[]{:S(2)}) collective-permute-start(bf16[576,128]{1,0:T(8,128)(2,1)S(1)} %get-tuple-element.50.down), channel_id=1, source_target_pairs={{0,3},{1,0},{2,1},{3,2},{4,7},{5,4},{6,5},{7,6},{8,11},{9,8},{10,9... | collective-permute-start | bytes 442376 | tf_op jit(solution)/shard_map/ppermute | solution.py:395
  82.3 0.7 shard_map.137.bias3
  83.0 3.1 %collective-permute-done.11.above = bf16[576,128]{1,0:T(8,128)(2,1)S(1)} collective-permute-done((bf16[576,128]{1,0:T(8,128)(2,1)S(1)}, bf16[576,128]{1,0:T(8,128)(2,1)S(1)}, u32[]{:S(2)}, u32[]{:S(2)}) %collective-permute-start.11) | collective-permute-done | bytes 147488 | tf_op jit(solution)/shard_map/ppermute | solution.py:395
  86.1 3.9 %shard_map.138 = bf16[72,2,192]{2,1,0:T(2,128)(2,1)} custom-call(bf16[144,192]{1,0:T(8,128)(2,1)S(1)} %get-tuple-element.43.stream_in, bf16[576,128]{1,0:T(8,128)(2,1)S(1)} %collective-permute-done.10.below, bf16[576,128]{1,0:T(8,128)(2,1)S(1)} %collective-permute-done.11.above, f32[192,192]{1,0:T(8,128)S(1)} %get-tuple-element.51.q, ...), custom_call_target="tpu_custom_call" | custom-call | flops 2147483648 | bytes 1048576 | tf_op jit(solution)/shard_map/pallas_call | solution.py:379
  (42 shorter events, 1.9 us)
Async XLA Ops:
  0.0 22.9 %copy-start.5 = (bf16[4,4,1,6,3312]{4,1,3,2,0:T(4,128)(2,1)S(1)}, bf16[4,4,1,6,3312]{4,1,3,2,0:T(4,128)(2,1)}, u32[]{:S(2)}) copy-start(bf16[4,4,1,6,3312]{4,1,3,2,0:T(4,128)(2,1)} %param.19) | copy-start | bytes 1907716
  0.0 22.9 %copy-start.7 = (s32[8,6,12]{2,0,1:T(8,128)S(1)}, s32[8,6,12]{2,0,1:T(8,128)}, u32[]{:S(2)}) copy-start(s32[8,6,12]{2,0,1:T(8,128)} %param.20) | copy-start | bytes 6916
  0.0 22.9 %copy-start.10 = (bf16[512,256]{1,0:T(8,128)(2,1)S(1)}, bf16[512,256]{1,0:T(8,128)(2,1)}, u32[]{:S(2)}) copy-start(bf16[512,256]{1,0:T(8,128)(2,1)} %constant.12.clone.sel_hbm.sel_ref) | copy-start | bytes 786436
  4.8 20.1 %collective-permute-start = (bf16[144,128]{1,0:T(8,128)(2,1)}, bf16[144,128]{1,0:T(8,128)(2,1)S(1)}, u32[]{:S(2)}, u32[]{:S(2)}) collective-permute-start(bf16[144,128]{1,0:T(8,128)(2,1)} %get-tuple-element.31.own_far), channel_id=1, source_target_pairs={{0,480},{32,64},{64,32},{96,128},{128,96},{160,192},{192,160},{224... | collective-permute-start | bytes 110600 | tf_op jit(solution)/shard_map/ppermute | solution.py:401
  21.0 10.0 %collective-permute-start.1 = (bf16[144,128]{1,0:T(8,128)(2,1)}, bf16[144,128]{1,0:T(8,128)(2,1)S(1)}, u32[]{:S(2)}, u32[]{:S(2)}) collective-permute-start(bf16[144,128]{1,0:T(8,128)(2,1)} %get-tuple-element.32.own_near), channel_id=1, source_target_pairs={{0,32},{32,0},{64,96},{96,64},{128,160},{160,128},{192,224},{224,1... | collective-permute-start | bytes 110600 | tf_op jit(solution)/shard_map/ppermute | solution.py:401
  23.0 8.0 %copy-start = (bf16[144,128]{1,0:T(8,128)(2,1)S(1)}, bf16[144,128]{1,0:T(8,128)(2,1)}, u32[]{:S(2)}) copy-start(bf16[144,128]{1,0:T(8,128)(2,1)} %get-tuple-element.31.own_far) | copy-start | bytes 110596
  23.0 8.0 %copy-start.1 = (bf16[144,128]{1,0:T(8,128)(2,1)S(1)}, bf16[144,128]{1,0:T(8,128)(2,1)}, u32[]{:S(2)}) copy-start(bf16[144,128]{1,0:T(8,128)(2,1)} %get-tuple-element.32.own_near) | copy-start | bytes 110596
  23.0 22.4 %copy-start.4 = (bf16[4,192,576]{2,1,0:T(8,128)(2,1)S(1)}, bf16[4,192,576]{2,1,0:T(8,128)(2,1)}, u32[]{:S(2)}) copy-start(bf16[4,192,576]{2,1,0:T(8,128)(2,1)} %w_qkv.7) | copy-start | bytes 2654212
  31.1 8.0 %collective-permute-start.2 = (bf16[480,128]{1,0:T(8,128)(2,1)S(1)}, bf16[480,128]{1,0:T(8,128)(2,1)S(1)}, u32[]{:S(2)}, u32[]{:S(2)}) collective-permute-start(bf16[480,128]{1,0:T(8,128)(2,1)S(1)} %get-tuple-element.34.own_far), channel_id=1, source_target_pairs={{0,28},{4,8},{8,4},{12,16},{16,12},{20,24},{24,20},{28,0},{1,29},{... | collective-permute-start | bytes 368648 | tf_op jit(solution)/shard_map/ppermute | solution.py:401
  33.1 6.1 %collective-permute-start.3 = (bf16[480,128]{1,0:T(8,128)(2,1)S(1)}, bf16[480,128]{1,0:T(8,128)(2,1)S(1)}, u32[]{:S(2)}, u32[]{:S(2)}) collective-permute-start(bf16[480,128]{1,0:T(8,128)(2,1)S(1)} %get-tuple-element.35.own_near), channel_id=1, source_target_pairs={{0,4},{4,0},{8,12},{12,8},{16,20},{20,16},{24,28},{28,24},{1,5},{5... | collective-permute-start | bytes 368648 | tf_op jit(solution)/shard_map/ppermute | solution.py:401
  39.3 7.4 %collective-permute-start.4 = (bf16[576,128]{1,0:T(8,128)(2,1)S(1)}, bf16[576,128]{1,0:T(8,128)(2,1)S(1)}, u32[]{:S(2)}, u32[]{:S(2)}) collective-permute-start(bf16[576,128]{1,0:T(8,128)(2,1)S(1)} %get-tuple-element.36.up), channel_id=1, source_target_pairs={{0,1},{1,2},{2,3},{3,0},{4,5},{5,6},{6,7},{7,4},{8,9},{9,10},{10,1... | collective-permute-start | bytes 442376 | tf_op jit(solution)/shard_map/ppermute | solution.py:395
  41.7 4.2 %copy-start.9 = (bf16[512,256]{1,0:T(8,128)(2,1)S(1)}, bf16[512,256]{1,0:T(8,128)(2,1)}, u32[]{:S(2)}) copy-start(bf16[512,256]{1,0:T(8,128)(2,1)} %constant.13.clone.sel_ref) | copy-start | bytes 786436
  41.7 4.2 %copy-start.13 = (f32[1,256]{1,0:T(1,128)S(1)}, f32[1,256]{1,0:T(1,128)}, u32[]{:S(2)}) copy-start(f32[1,256]{1,0:T(1,128)} %constant.14.clone.pad_ref) | copy-start | bytes 3076
  41.8 8.4 %collective-permute-start.5 = (bf16[576,128]{1,0:T(8,128)(2,1)S(1)}, bf16[576,128]{1,0:T(8,128)(2,1)S(1)}, u32[]{:S(2)}, u32[]{:S(2)}) collective-permute-start(bf16[576,128]{1,0:T(8,128)(2,1)S(1)} %get-tuple-element.37.down), channel_id=1, source_target_pairs={{0,3},{1,0},{2,1},{3,2},{4,7},{5,4},{6,5},{7,6},{8,11},{9,8},{10,9... | collective-permute-start | bytes 442376 | tf_op jit(solution)/shard_map/ppermute | solution.py:395
  45.9 4.2 %copy-start.2 = (bf16[4,192,768]{2,1,0:T(8,128)(2,1)S(1)}, bf16[4,192,768]{2,1,0:T(8,128)(2,1)}, u32[]{:S(2)}) copy-start(bf16[4,192,768]{2,1,0:T(8,128)(2,1)} %w_up.3) | copy-start | bytes 3538948
  46.0 4.2 %copy-start.3 = (bf16[4,768,192]{1,2,0:T(8,128)(2,1)S(1)}, bf16[4,768,192]{1,2,0:T(8,128)(2,1)}, u32[]{:S(2)}) copy-start(bf16[4,768,192]{1,2,0:T(8,128)(2,1)} %param.17) | copy-start | bytes 3538948
  46.0 4.2 %copy-start.6 = (bf16[4,192,192]{2,1,0:T(8,128)(2,1)S(1)}, bf16[4,192,192]{2,1,0:T(8,128)(2,1)}, u32[]{:S(2)}) copy-start(bf16[4,192,192]{2,1,0:T(8,128)(2,1)} %w_out.3) | copy-start | bytes 884740
  46.0 4.2 %copy-start.8 = (f32[4,2,192]{2,1,0:T(2,128)S(1)}, f32[4,2,192]{2,1,0:T(2,128)}, u32[]{:S(2)}) copy-start(f32[4,2,192]{2,1,0:T(2,128)} %gains.3) | copy-start | bytes 18436
  55.4 11.9 %collective-permute-start.6 = (bf16[144,128]{1,0:T(8,128)(2,1)S(1)}, bf16[144,128]{1,0:T(8,128)(2,1)S(1)}, u32[]{:S(2)}, u32[]{:S(2)}) collective-permute-start(bf16[144,128]{1,0:T(8,128)(2,1)S(1)} %get-tuple-element.44.own_far), channel_id=1, source_target_pairs={{0,480},{32,64},{64,32},{96,128},{128,96},{160,192},{192,160},{224... | collective-permute-start | bytes 110600 | tf_op jit(solution)/shard_map/ppermute | solution.py:401
  57.5 9.8 %collective-permute-start.7 = (bf16[144,128]{1,0:T(8,128)(2,1)S(1)}, bf16[144,128]{1,0:T(8,128)(2,1)S(1)}, u32[]{:S(2)}, u32[]{:S(2)}) collective-permute-start(bf16[144,128]{1,0:T(8,128)(2,1)S(1)} %get-tuple-element.45.own_near), channel_id=1, source_target_pairs={{0,32},{32,0},{64,96},{96,64},{128,160},{160,128},{192,224},{224,1... | collective-permute-start | bytes 110600 | tf_op jit(solution)/shard_map/ppermute | solution.py:401
  67.5 8.0 %collective-permute-start.8 = (bf16[480,128]{1,0:T(8,128)(2,1)S(1)}, bf16[480,128]{1,0:T(8,128)(2,1)S(1)}, u32[]{:S(2)}, u32[]{:S(2)}) collective-permute-start(bf16[480,128]{1,0:T(8,128)(2,1)S(1)} %get-tuple-element.47.own_far), channel_id=1, source_target_pairs={{0,28},{4,8},{8,4},{12,16},{16,12},{20,24},{24,20},{28,0},{1,29},{... | collective-permute-start | bytes 368648 | tf_op jit(solution)/shard_map/ppermute | solution.py:401
  69.4 6.1 %collective-permute-start.9 = (bf16[480,128]{1,0:T(8,128)(2,1)S(1)}, bf16[480,128]{1,0:T(8,128)(2,1)S(1)}, u32[]{:S(2)}, u32[]{:S(2)}) collective-permute-start(bf16[480,128]{1,0:T(8,128)(2,1)S(1)} %get-tuple-element.48.own_near), channel_id=1, source_target_pairs={{0,4},{4,0},{8,12},{12,8},{16,20},{20,16},{24,28},{28,24},{1,5},{5... | collective-permute-start | bytes 368648 | tf_op jit(solution)/shard_map/ppermute | solution.py:401
  75.7 7.3 %collective-permute-start.10 = (bf16[576,128]{1,0:T(8,128)(2,1)S(1)}, bf16[576,128]{1,0:T(8,128)(2,1)S(1)}, u32[]{:S(2)}, u32[]{:S(2)}) collective-permute-start(bf16[576,128]{1,0:T(8,128)(2,1)S(1)} %get-tuple-element.49.up), channel_id=1, source_target_pairs={{0,1},{1,2},{2,3},{3,0},{4,5},{5,6},{6,7},{7,4},{8,9},{9,10},{10,1... | collective-permute-start | bytes 442376 | tf_op jit(solution)/shard_map/ppermute | solution.py:395
  77.9 8.2 %collective-permute-start.11 = (bf16[576,128]{1,0:T(8,128)(2,1)S(1)}, bf16[576,128]{1,0:T(8,128)(2,1)S(1)}, u32[]{:S(2)}, u32[]{:S(2)}) collective-permute-start(bf16[576,128]{1,0:T(8,128)(2,1)S(1)} %get-tuple-element.50.down), channel_id=1, source_target_pairs={{0,3},{1,0},{2,1},{3,2},{4,7},{5,4},{6,5},{7,6},{8,11},{9,8},{10,9... | collective-permute-start | bytes 442376 | tf_op jit(solution)/shard_map/ppermute | solution.py:395
  (3 other events, 12.5 us)

commit v6 on v5

--- a/solution.py
+++ b/solution.py
@@ -21,7 +21,6 @@
 POS = 3312
 SLOT = 24
 PAIR = 2 * SLOT
-FIRST_LIMIT = 62.0
 NEG = -1e30
 MASK_AT = 192
 BF = jnp.bfloat16
@@ -150,33 +149,39 @@
     q_ref[...] = q.astype(F32) * np.float32(HD**-0.5)
 
 
+def level_windows(z, halo, q_ref, k_own, v_own, w_qkv, bias, k_ref, v_ref):
+    keys_values(unpack(halo[...]), w_qkv, k_ref, v_ref)
+    masks = head_mask(SLOT)
+    outs = []
+    for yh in range(2):
+        for xh in range(2):
+            sides = ((k_ref, v_ref), (k_own.at[z], v_own.at[z]))
+            if z:
+                sides = sides[::-1]
+            ks, vs = [
+                jnp.concatenate(
+                    [side[i][2 * yh : 2 * yh + 2, xh].reshape(2 * PAIR, D) for side in sides], axis=0
+                )
+                for i in range(2)
+            ]
+            w = (z * 2 + yh) * 2 + xh
+            q = spread_heads(q_ref[w * SLOT : (w + 1) * SLOT], masks)
+            rows = slice(w * 144, (w + 1) * 144)
+            scores = dot_t(q, ks) + jnp.concatenate([bias[0, rows], bias[1, rows, :64]], 1)
+            outs.append(softmax_mix(scores, vs, SLOT, masks))
+    return jnp.concatenate(outs, axis=0).astype(BF)
+
+
+def lower_kernel(block, below, q, k_own, v_own, w_qkv, bias, out, k_ref, v_ref):
+    out[...] = level_windows(0, below, q, k_own, v_own, w_qkv[block], bias, k_ref, v_ref)
+
+
 def shifted_block(
-    stream, below, above, q_ref, k_own, v_own, gain1, w_qkv, w_out, w_up, w_down, bias, back,
+    stream, lower, above, q, k_own, v_own, gain1, w_qkv, w_out, w_up, w_down, bias, back,
     k_ref, v_ref,
 ):
-    for i, ref in enumerate((below, above)):
-        keys_values(unpack(ref[...]), w_qkv, k_ref.at[i], v_ref.at[i])
-    masks = head_mask(SLOT)
-    outs = []
-    for z in range(2):
-        for yh in range(2):
-            for xh in range(2):
-                w = (z * 2 + yh) * 2 + xh
-                sides = ((k_ref, v_ref, 0), (k_own, v_own, 0))
-                if z:
-                    sides = ((k_own, v_own, 1), (k_ref, v_ref, 1))
-                ks, vs = [
-                    jnp.concatenate(
-                        [s[i][s[2], 2 * yh : 2 * yh + 2, xh].reshape(2 * PAIR, D) for s in sides],
-                        axis=0,
-                    )
-                    for i in range(2)
-                ]
-                q = spread_heads(q_ref[w * SLOT : (w + 1) * SLOT], masks)
-                rows = slice(w * 144, (w + 1) * 144)
-                scores = dot_t(q, ks) + jnp.concatenate([bias[0, rows], bias[1, rows, :64]], 1)
-                outs.append(softmax_mix(scores, vs, SLOT, masks))
-    heads_out = jnp.concatenate(outs, axis=0).astype(BF)
+    upper = level_windows(1, above, q, k_own, v_own, w_qkv, bias, k_ref, v_ref)
+    heads_out = jnp.concatenate([lower, upper], axis=0)
     attended = dot(back, dot(heads_out, w_out).astype(BF))
     middle = (stream.astype(F32) + attended).astype(BF)
     return feed_forward(middle, gain1, w_up, w_down)
@@ -318,7 +323,7 @@
     for copy in copies[2:]:
         copy.wait()
     stream = regular_block(
-        x[...].astype(F32).reshape(T, D).astype(BF), gains[0, 0:1], gains[0, 1:2], w_qkv[...],
+        x[...].reshape(T, D), gains[0, 0:1], gains[0, 1:2], w_qkv[...],
         w_out[...], w_up[...], w_down[...], bias,
     )
     stream_out[...] = stream
@@ -326,11 +331,11 @@
 
 
 def middle_kernel(
-    stream_in, below, above, q, k_own, v_own, gains, w_qkv, w_out, w_up, w_down, bias1,
+    stream_in, lower, above, q, k_own, v_own, gains, w_qkv, w_out, w_up, w_down, bias1,
     bias2, to_oct, back, stream_out, far, near, k_ref, v_ref,
 ):
     stream = shifted_block(
-        stream_in[...], below, above, q, k_own, v_own, gains[1, 1:2], w_qkv[1], w_out[1], w_up[1],
+        stream_in[...], lower[...], above, q, k_own, v_own, gains[1, 1:2], w_qkv[1], w_out[1], w_up[1],
         w_down[1], bias1, back[...], k_ref, v_ref,
     )
     stream = regular_block(
@@ -341,14 +346,14 @@
 
 
 def last_kernel(
-    stream_in, below, above, q, k_own, v_own, gains, w_qkv, w_out, w_up, w_down, bias3, back, out,
+    stream_in, lower, above, q, k_own, v_own, gains, w_qkv, w_out, w_up, w_down, bias3, back, out,
     k_ref, v_ref,
 ):
     stream = shifted_block(
-        stream_in[...], below, above, q, k_own, v_own, gains[3, 1:2], w_qkv[3], w_out[3], w_up[3],
+        stream_in[...], lower[...], above, q, k_own, v_own, gains[3, 1:2], w_qkv[3], w_out[3], w_up[3],
         w_down[3], bias3, back[...], k_ref, v_ref,
     )
-    out[...] = stream.astype(F32).reshape(T // 2, 2, D).astype(BF)
+    out[...] = stream.reshape(T // 2, 2, D)
 
 
 def lat_pack_kernel(recv_far, own_far, own_near, recv_near, table_rows, far, near):
@@ -376,6 +381,8 @@
 
 def call(kernel, outs, *args, scratch=(), flops=0, limit=20, place=pltpu.VMEM):
     specs = [pl.BlockSpec(memory_space=place)] * len(args)
+    if place == pltpu.HBM:
+        args = [pltpu.with_memory_space_constraint(arg, place) for arg in args]
     return pl.pallas_call(
         kernel,
         out_shape=outs,
@@ -401,6 +408,10 @@
     return lax.ppermute(value, axis, [(i, (i + steps[i % 2]) % count) for i in range(count)])
 
 
+def kv_scratch():
+    return [pltpu.VMEM((4, 2, PAIR, D), BF)] * 2
+
+
 def halo(block, far, near, keep, send, w_qkv, sel_shift, pad):
     recv_far = swap(far, "lon", True)
     recv_near = swap(near, "lon", False)
@@ -425,7 +436,11 @@
         bias_shifted_kernel, shape(2, 8 * 144, 128, dtype=F32), keep, recv_far, recv_near,
         sel_shift, pad, flops=1 << 30, limit=8,
     )
-    return below, above, q, k, v, bias
+    lower = call(
+        functools.partial(lower_kernel, block), shape(4 * SLOT, D), below, q, k, v, w_qkv, bias,
+        scratch=kv_scratch(), flops=1 << 30, limit=8,
+    )
+    return lower, above, q, k, v, bias
 
 
 def per_device(fields, w_qkv, w_out, w_up, w_down, gains, bias_table, labels):
@@ -439,7 +454,6 @@
 
     bias_shape = (2, HEADS * T, 128)
     table_scratch = [pltpu.VMEM((HEADS, POS), F32), pltpu.VMEM((2, 2, 80, 128), F32)]
-    kv_scratch = [pltpu.VMEM((2, 4, 2, PAIR, D), BF)] * 2
     streams = [shape(T, D), shape(144, 128), shape(144, 128)]
     stream, far, near = call(
         first_kernel, streams, fields.transpose(1, 2, 0, 3).reshape(T // 2, 2, D), *weights,
@@ -450,7 +464,7 @@
             pltpu.VMEM((D, FF), BF), pltpu.VMEM((D, FF), BF), pltpu.VMEM((1, HEADS, 4, POS), BF),
             pltpu.VMEM((512, 256), BF), pltpu.VMEM((8 * SLOT, T), BF), pltpu.SemaphoreType.DMA((9,)),
         ],
-        flops=1 << 31, place=pltpu.HBM, limit=FIRST_LIMIT,
+        flops=1 << 31, place=pltpu.HBM,
     )
     rows = [shape(2, 2, 48, 128), shape(192, 128)]
     bias2, keep1, send1, keep3, send3 = call(
@@ -460,12 +474,12 @@
     *ready, bias1 = halo(1, far, near, keep1, send1, w_qkv, sel_shift, pad)
     stream, far, near = call(
         middle_kernel, streams, stream, *ready, *weights, bias1, bias2, to_oct, back,
-        scratch=kv_scratch, flops=1 << 31,
+        scratch=kv_scratch(), flops=1 << 31,
     )
     *ready, bias3 = halo(3, far, near, keep3, send3, w_qkv, sel_shift, pad)
     stream = call(
         last_kernel, shape(T // 2, 2, D), stream, *ready, *weights, bias3, back,
-        scratch=kv_scratch, flops=1 << 31,
+        scratch=kv_scratch(), flops=1 << 31,
     )
     return stream.reshape(6, 12, 2, D).transpose(2, 0, 1, 3)
 

time: 90.5 us -> 87.4 us (0.966)
  waiting for transfers between devices: 26.9 us -> 24.2 us
    ppermute x4, waiting for transfers between devices: 6.53 us -> 4 us  [move(): lax.ppermute(value, axis, [(i, (i + steps) % count) for i in range(count)])]
    pallas_call x12 -> x14, Pallas kernels: 19 us -> 18.7 us  [call(): pl.pallas_call(kernel, out_shape=outs, in_specs=specs, scratch_shapes=lis...]
  transfers between devices with their start and end apart: 12 -> 12, of which waited for: 6 -> 6; matrix products, arithmetic and copies ran while one was open for 0% -> 0% of each run, Pallas kernels for 5% -> 8%
where the time goes in v6:
time: 87.4 us; the launch traced here: 87 us
  starting transfers between devices  43.7 us (50%)
  waiting for transfers between devices  24.2 us (28%)
  Pallas kernels  18.7 us (21%)
    ppermute x8, starting transfers between devices, swap(): lax.ppermute(value, axis, [(i, (i + steps[i % 2]) % count) for i in range...  31.7 us
    ppermute x8, waiting for transfers between devices, swap(): lax.ppermute(value, axis, [(i, (i + steps[i % 2]) % count) for i in range...  20.2 us
    pallas_call x14, Pallas kernels, call(): pl.pallas_call(kernel, out_shape=outs, in_specs=specs, scratch_shapes=lis...  18.7 us
    ppermute x4, starting transfers between devices, move(): lax.ppermute(value, axis, [(i, (i + steps) % count) for i in range(count)])  12 us
    ppermute x4, waiting for transfers between devices, move(): lax.ppermute(value, axis, [(i, (i + steps) % count) for i in range(count)])  4 us
  transfers between devices with their start and end apart: 12, of which 6 were waited for; matrix products, arithmetic and copies ran while one was open for 0% of the time, Pallas kernels for 8%

profile of v6, /device:TPU:6, one launch (start us, length us, event | category | flops | bytes accessed | tf_op | source)
XLA Modules:
  0.0 87.0 jit_solution(12920484161098264037)
XLA Ops:
  0.0 4.2 %shard_map.127 = (bf16[144,192]{1,0:T(8,128)(2,1)S(1)}, bf16[144,128]{1,0:T(8,128)(2,1)S(1)}, bf16[144,128]{1,0:T(8,128)(2,1)S(1)}) custom-call(bf16[72,2,192]{2,1,0:T(2,128)(2,1)} %bitcast.17, f32[4,2,192]{2,1,0:T(2,128)} %gains.3, bf16[4,192,576]{2,1,0:T(8,128)(2,1)} %w_qkv.11, bf16[4,192,192]{2,1,0:T(8,128)(2,1)} %w_out.3, bf16[4,192,768]{2,1,0:T(8,128)(2,1)} %w_up.3, ...), custom_call_target="tpu_custom_call" | custom-call | flops 2147483648 | bytes 1048576 | tf_op jit(solution)/shard_map/pallas_call | solution.py:386
  4.2 16.2 %collective-permute-start = (bf16[144,128]{1,0:T(8,128)(2,1)S(1)}, bf16[144,128]{1,0:T(8,128)(2,1)S(1)}, u32[]{:S(2)}, u32[]{:S(2)}) collective-permute-start(bf16[144,128]{1,0:T(8,128)(2,1)S(1)} %get-tuple-element.31.own_far), channel_id=1, source_target_pairs={{0,480},{32,64},{64,32},{96,128},{128,96},{160,192},{192,160},{224... | collective-permute-start | bytes 110600 | tf_op jit(solution)/shard_map/ppermute | solution.py:408
  20.4 1.9 %collective-permute-start.1 = (bf16[144,128]{1,0:T(8,128)(2,1)S(1)}, bf16[144,128]{1,0:T(8,128)(2,1)S(1)}, u32[]{:S(2)}, u32[]{:S(2)}) collective-permute-start(bf16[144,128]{1,0:T(8,128)(2,1)S(1)} %get-tuple-element.32.own_near), channel_id=1, source_target_pairs={{0,32},{32,0},{64,96},{96,64},{128,160},{160,128},{192,224},{224,1... | collective-permute-start | bytes 110600 | tf_op jit(solution)/shard_map/ppermute | solution.py:408
  22.4 1.9 %shard_map.128 = (f32[2,864,128]{2,1,0:T(8,128)S(1)}, bf16[2,2,48,128]{3,2,1,0:T(8,128)(2,1)S(1)}, bf16[192,128]{1,0:T(8,128)(2,1)S(1)}, bf16[2,2,48,128]{3,2,1,0:T(8,128)(2,1)S(1)}, bf16[192,128]{1,0:T(8,128)(2,1)S(1)}) custom-call(bf16[4,6,4,3312]{3,2,1,0:T(4,128)(2,1)S(1)} %bitcast.15, s32[6,8,12]{2,1,0:T(8,128)S(1)} %bitcast.16, ...), custom_call_target="tpu_custom_call" | custom-call | flops 2147483648 | bytes 1048576 | tf_op jit(solution)/shard_map/pallas_call | solution.py:386
  24.3 5.9 %collective-permute-done.1.recv_near = bf16[144,128]{1,0:T(8,128)(2,1)S(1)} collective-permute-done((bf16[144,128]{1,0:T(8,128)(2,1)S(1)}, bf16[144,128]{1,0:T(8,128)(2,1)S(1)}, u32[]{:S(2)}, u32[]{:S(2)}) %collective-permute-start.1) | collective-permute-done | bytes 36896 | tf_op jit(solution)/shard_map/ppermute | solution.py:408
  30.3 1.9 %collective-permute-start.2 = (bf16[480,128]{1,0:T(8,128)(2,1)S(1)}, bf16[480,128]{1,0:T(8,128)(2,1)S(1)}, u32[]{:S(2)}, u32[]{:S(2)}) collective-permute-start(bf16[480,128]{1,0:T(8,128)(2,1)S(1)} %get-tuple-element.34.own_far), channel_id=1, source_target_pairs={{0,28},{4,8},{8,4},{12,16},{16,12},{20,24},{24,20},{28,0},{1,29},{... | collective-permute-start | bytes 368648 | tf_op jit(solution)/shard_map/ppermute | solution.py:408
  32.3 3.1 %collective-permute-start.3 = (bf16[480,128]{1,0:T(8,128)(2,1)S(1)}, bf16[480,128]{1,0:T(8,128)(2,1)S(1)}, u32[]{:S(2)}, u32[]{:S(2)}) collective-permute-start(bf16[480,128]{1,0:T(8,128)(2,1)S(1)} %get-tuple-element.35.own_near), channel_id=1, source_target_pairs={{0,4},{4,0},{8,12},{12,8},{16,20},{20,16},{24,28},{28,24},{1,5},{5... | collective-permute-start | bytes 368648 | tf_op jit(solution)/shard_map/ppermute | solution.py:408
  35.4 3.0 %collective-permute-done.2.recv_far.far = bf16[480,128]{1,0:T(8,128)(2,1)S(1)} collective-permute-done((bf16[480,128]{1,0:T(8,128)(2,1)S(1)}, bf16[480,128]{1,0:T(8,128)(2,1)S(1)}, u32[]{:S(2)}, u32[]{:S(2)}) %collective-permute-start.2) | collective-permute-done | bytes 122912 | tf_op jit(solution)/shard_map/ppermute | solution.py:408
  38.5 2.4 %collective-permute-start.4 = (bf16[576,128]{1,0:T(8,128)(2,1)S(1)}, bf16[576,128]{1,0:T(8,128)(2,1)S(1)}, u32[]{:S(2)}, u32[]{:S(2)}) collective-permute-start(bf16[576,128]{1,0:T(8,128)(2,1)S(1)} %get-tuple-element.36.up), channel_id=1, source_target_pairs={{0,1},{1,2},{2,3},{3,0},{4,5},{5,6},{6,7},{7,4},{8,9},{9,10},{10,1... | collective-permute-start | bytes 442376 | tf_op jit(solution)/shard_map/ppermute | solution.py:402
  41.0 3.6 %collective-permute-start.5 = (bf16[576,128]{1,0:T(8,128)(2,1)S(1)}, bf16[576,128]{1,0:T(8,128)(2,1)S(1)}, u32[]{:S(2)}, u32[]{:S(2)}) collective-permute-start(bf16[576,128]{1,0:T(8,128)(2,1)S(1)} %get-tuple-element.37.down), channel_id=1, source_target_pairs={{0,3},{1,0},{2,1},{3,2},{4,7},{5,4},{6,5},{7,6},{8,11},{9,8},{10,9... | collective-permute-start | bytes 442376 | tf_op jit(solution)/shard_map/ppermute | solution.py:402
  45.9 1.3 %shard_map.133.lower = bf16[96,192]{1,0:T(8,128)(2,1)S(1)} custom-call(bf16[576,128]{1,0:T(8,128)(2,1)S(1)} %collective-permute-done.4.below, f32[192,192]{1,0:T(8,128)S(1)} %get-tuple-element.38.q, bf16[2,4,2,48,192]{4,3,2,1,0:T(8,128)(2,1)S(1)} %get-tuple-element.39.k_own, bf16[2,4,2,48,192]{4,3,2,1,0:T(8,128)(2,1)S(1)} %get-tuple-element.40.v_own, ...), custom_call_target="tpu_custom_call" | custom-call | flops 1073741824 | bytes 1048576 | tf_op jit(solution)/shard_map/pallas_call | solution.py:386
  47.2 2.1 %collective-permute-done.5.above = bf16[576,128]{1,0:T(8,128)(2,1)S(1)} collective-permute-done((bf16[576,128]{1,0:T(8,128)(2,1)S(1)}, bf16[576,128]{1,0:T(8,128)(2,1)S(1)}, u32[]{:S(2)}, u32[]{:S(2)}) %collective-permute-start.5) | collective-permute-done | bytes 147488 | tf_op jit(solution)/shard_map/ppermute | solution.py:402
  49.4 4.2 %shard_map.134 = (bf16[144,192]{1,0:T(8,128)(2,1)S(1)}, bf16[144,128]{1,0:T(8,128)(2,1)S(1)}, bf16[144,128]{1,0:T(8,128)(2,1)S(1)}) custom-call(bf16[144,192]{1,0:T(8,128)(2,1)S(1)} %get-tuple-element.30.stream_in, bf16[96,192]{1,0:T(8,128)(2,1)S(1)} %shard_map.133.lower, bf16[576,128]{1,0:T(8,128)(2,1)S(1)} %collective-permute-done.5.above, ...), custom_call_target="tpu_custom_call" | custom-call | flops 2147483648 | bytes 1048576 | tf_op jit(solution)/shard_map/pallas_call | solution.py:386
  53.5 2.1 %collective-permute-start.6 = (bf16[144,128]{1,0:T(8,128)(2,1)S(1)}, bf16[144,128]{1,0:T(8,128)(2,1)S(1)}, u32[]{:S(2)}, u32[]{:S(2)}) collective-permute-start(bf16[144,128]{1,0:T(8,128)(2,1)S(1)} %get-tuple-element.44.own_far), channel_id=1, source_target_pairs={{0,480},{32,64},{64,32},{96,128},{128,96},{160,192},{192,160},{224... | collective-permute-start | bytes 110600 | tf_op jit(solution)/shard_map/ppermute | solution.py:408
  55.7 1.9 %collective-permute-start.7 = (bf16[144,128]{1,0:T(8,128)(2,1)S(1)}, bf16[144,128]{1,0:T(8,128)(2,1)S(1)}, u32[]{:S(2)}, u32[]{:S(2)}) collective-permute-start(bf16[144,128]{1,0:T(8,128)(2,1)S(1)} %get-tuple-element.45.own_near), channel_id=1, source_target_pairs={{0,32},{32,0},{64,96},{96,64},{128,160},{160,128},{192,224},{224,1... | collective-permute-start | bytes 110600 | tf_op jit(solution)/shard_map/ppermute | solution.py:408
  57.6 7.8 %collective-permute-done.6.recv_far = bf16[144,128]{1,0:T(8,128)(2,1)S(1)} collective-permute-done((bf16[144,128]{1,0:T(8,128)(2,1)S(1)}, bf16[144,128]{1,0:T(8,128)(2,1)S(1)}, u32[]{:S(2)}, u32[]{:S(2)}) %collective-permute-start.6) | collective-permute-done | bytes 36896 | tf_op jit(solution)/shard_map/ppermute | solution.py:408
  65.6 1.9 %collective-permute-start.8 = (bf16[480,128]{1,0:T(8,128)(2,1)S(1)}, bf16[480,128]{1,0:T(8,128)(2,1)S(1)}, u32[]{:S(2)}, u32[]{:S(2)}) collective-permute-start(bf16[480,128]{1,0:T(8,128)(2,1)S(1)} %get-tuple-element.47.own_far), channel_id=1, source_target_pairs={{0,28},{4,8},{8,4},{12,16},{16,12},{20,24},{24,20},{28,0},{1,29},{... | collective-permute-start | bytes 368648 | tf_op jit(solution)/shard_map/ppermute | solution.py:408
  67.5 2.6 %collective-permute-start.9 = (bf16[480,128]{1,0:T(8,128)(2,1)S(1)}, bf16[480,128]{1,0:T(8,128)(2,1)S(1)}, u32[]{:S(2)}, u32[]{:S(2)}) collective-permute-start(bf16[480,128]{1,0:T(8,128)(2,1)S(1)} %get-tuple-element.48.own_near), channel_id=1, source_target_pairs={{0,4},{4,0},{8,12},{12,8},{16,20},{20,16},{24,28},{28,24},{1,5},{5... | collective-permute-start | bytes 368648 | tf_op jit(solution)/shard_map/ppermute | solution.py:408
  70.1 3.4 %collective-permute-done.8.recv_far.far = bf16[480,128]{1,0:T(8,128)(2,1)S(1)} collective-permute-done((bf16[480,128]{1,0:T(8,128)(2,1)S(1)}, bf16[480,128]{1,0:T(8,128)(2,1)S(1)}, u32[]{:S(2)}, u32[]{:S(2)}) %collective-permute-start.8) | collective-permute-done | bytes 122912 | tf_op jit(solution)/shard_map/ppermute | solution.py:408
  73.8 2.2 %collective-permute-start.10 = (bf16[576,128]{1,0:T(8,128)(2,1)S(1)}, bf16[576,128]{1,0:T(8,128)(2,1)S(1)}, u32[]{:S(2)}, u32[]{:S(2)}) collective-permute-start(bf16[576,128]{1,0:T(8,128)(2,1)S(1)} %get-tuple-element.49.up), channel_id=1, source_target_pairs={{0,1},{1,2},{2,3},{3,0},{4,5},{5,6},{6,7},{7,4},{8,9},{9,10},{10,1... | collective-permute-start | bytes 442376 | tf_op jit(solution)/shard_map/ppermute | solution.py:402
  76.0 3.8 %collective-permute-start.11 = (bf16[576,128]{1,0:T(8,128)(2,1)S(1)}, bf16[576,128]{1,0:T(8,128)(2,1)S(1)}, u32[]{:S(2)}, u32[]{:S(2)}) collective-permute-start(bf16[576,128]{1,0:T(8,128)(2,1)S(1)} %get-tuple-element.50.down), channel_id=1, source_target_pairs={{0,3},{1,0},{2,1},{3,2},{4,7},{5,4},{6,5},{7,6},{8,11},{9,8},{10,9... | collective-permute-start | bytes 442376 | tf_op jit(solution)/shard_map/ppermute | solution.py:402
  81.1 1.3 %shard_map.139.lower = bf16[96,192]{1,0:T(8,128)(2,1)S(1)} custom-call(bf16[576,128]{1,0:T(8,128)(2,1)S(1)} %collective-permute-done.10.below, f32[192,192]{1,0:T(8,128)S(1)} %get-tuple-element.51.q, bf16[2,4,2,48,192]{4,3,2,1,0:T(8,128)(2,1)S(1)} %get-tuple-element.52.k_own, bf16[2,4,2,48,192]{4,3,2,1,0:T(8,128)(2,1)S(1)} %get-tuple-element.53.v_own, ...), custom_call_target="tpu_custom_call" | custom-call | flops 1073741824 | bytes 1048576 | tf_op jit(solution)/shard_map/pallas_call | solution.py:386
  82.4 1.9 %collective-permute-done.11.above = bf16[576,128]{1,0:T(8,128)(2,1)S(1)} collective-permute-done((bf16[576,128]{1,0:T(8,128)(2,1)S(1)}, bf16[576,128]{1,0:T(8,128)(2,1)S(1)}, u32[]{:S(2)}, u32[]{:S(2)}) %collective-permute-start.11) | collective-permute-done | bytes 147488 | tf_op jit(solution)/shard_map/ppermute | solution.py:402
  84.2 2.7 %shard_map.140 = bf16[72,2,192]{2,1,0:T(2,128)(2,1)} custom-call(bf16[144,192]{1,0:T(8,128)(2,1)S(1)} %get-tuple-element.43.stream_in, bf16[96,192]{1,0:T(8,128)(2,1)S(1)} %shard_map.139.lower, bf16[576,128]{1,0:T(8,128)(2,1)S(1)} %collective-permute-done.11.above, f32[192,192]{1,0:T(8,128)S(1)} %get-tuple-element.51.q, ...), custom_call_target="tpu_custom_call" | custom-call | flops 2147483648 | bytes 1048576 | tf_op jit(solution)/shard_map/pallas_call | solution.py:386
  (38 shorter events, 3.3 us)
Async XLA Ops:
  0.0 22.3 %copy-start.3 = (bf16[4,4,1,6,3312]{4,1,3,2,0:T(4,128)(2,1)S(1)}, bf16[4,4,1,6,3312]{4,1,3,2,0:T(4,128)(2,1)}, u32[]{:S(2)}) copy-start(bf16[4,4,1,6,3312]{4,1,3,2,0:T(4,128)(2,1)} %param.19) | copy-start | bytes 1907716
  0.0 22.4 %copy-start.5 = (s32[8,6,12]{2,0,1:T(8,128)S(1)}, s32[8,6,12]{2,0,1:T(8,128)}, u32[]{:S(2)}) copy-start(s32[8,6,12]{2,0,1:T(8,128)} %param.20) | copy-start | bytes 6916
  0.0 22.4 %copy-start.8 = (bf16[512,256]{1,0:T(8,128)(2,1)S(1)}, bf16[512,256]{1,0:T(8,128)(2,1)}, u32[]{:S(2)}) copy-start(bf16[512,256]{1,0:T(8,128)(2,1)} %constant.12.clone.sel_hbm.sel_ref) | copy-start | bytes 786436
  4.2 20.1 %collective-permute-start = (bf16[144,128]{1,0:T(8,128)(2,1)S(1)}, bf16[144,128]{1,0:T(8,128)(2,1)S(1)}, u32[]{:S(2)}, u32[]{:S(2)}) collective-permute-start(bf16[144,128]{1,0:T(8,128)(2,1)S(1)} %get-tuple-element.31.own_far), channel_id=1, source_target_pairs={{0,480},{32,64},{64,32},{96,128},{128,96},{160,192},{192,160},{224... | collective-permute-start | bytes 110600 | tf_op jit(solution)/shard_map/ppermute | solution.py:408
  20.4 9.8 %collective-permute-start.1 = (bf16[144,128]{1,0:T(8,128)(2,1)S(1)}, bf16[144,128]{1,0:T(8,128)(2,1)S(1)}, u32[]{:S(2)}, u32[]{:S(2)}) collective-permute-start(bf16[144,128]{1,0:T(8,128)(2,1)S(1)} %get-tuple-element.32.own_near), channel_id=1, source_target_pairs={{0,32},{32,0},{64,96},{96,64},{128,160},{160,128},{192,224},{224,1... | collective-permute-start | bytes 110600 | tf_op jit(solution)/shard_map/ppermute | solution.py:408
  22.4 22.2 %copy-start.2 = (bf16[4,192,576]{2,1,0:T(8,128)(2,1)S(1)}, bf16[4,192,576]{2,1,0:T(8,128)(2,1)}, u32[]{:S(2)}) copy-start(bf16[4,192,576]{2,1,0:T(8,128)(2,1)} %w_qkv.11) | copy-start | bytes 2654212
  30.3 8.0 %collective-permute-start.2 = (bf16[480,128]{1,0:T(8,128)(2,1)S(1)}, bf16[480,128]{1,0:T(8,128)(2,1)S(1)}, u32[]{:S(2)}, u32[]{:S(2)}) collective-permute-start(bf16[480,128]{1,0:T(8,128)(2,1)S(1)} %get-tuple-element.34.own_far), channel_id=1, source_target_pairs={{0,28},{4,8},{8,4},{12,16},{16,12},{20,24},{24,20},{28,0},{1,29},{... | collective-permute-start | bytes 368648 | tf_op jit(solution)/shard_map/ppermute | solution.py:408
  32.3 6.1 %collective-permute-start.3 = (bf16[480,128]{1,0:T(8,128)(2,1)S(1)}, bf16[480,128]{1,0:T(8,128)(2,1)S(1)}, u32[]{:S(2)}, u32[]{:S(2)}) collective-permute-start(bf16[480,128]{1,0:T(8,128)(2,1)S(1)} %get-tuple-element.35.own_near), channel_id=1, source_target_pairs={{0,4},{4,0},{8,12},{12,8},{16,20},{20,16},{24,28},{28,24},{1,5},{5... | collective-permute-start | bytes 368648 | tf_op jit(solution)/shard_map/ppermute | solution.py:408
  38.5 7.3 %collective-permute-start.4 = (bf16[576,128]{1,0:T(8,128)(2,1)S(1)}, bf16[576,128]{1,0:T(8,128)(2,1)S(1)}, u32[]{:S(2)}, u32[]{:S(2)}) collective-permute-start(bf16[576,128]{1,0:T(8,128)(2,1)S(1)} %get-tuple-element.36.up), channel_id=1, source_target_pairs={{0,1},{1,2},{2,3},{3,0},{4,5},{5,6},{6,7},{7,4},{8,9},{9,10},{10,1... | collective-permute-start | bytes 442376 | tf_op jit(solution)/shard_map/ppermute | solution.py:402
  40.9 4.2 %copy-start.7 = (bf16[512,256]{1,0:T(8,128)(2,1)S(1)}, bf16[512,256]{1,0:T(8,128)(2,1)}, u32[]{:S(2)}) copy-start(bf16[512,256]{1,0:T(8,128)(2,1)} %constant.13.clone.sel_ref) | copy-start | bytes 786436
  40.9 4.2 %copy-start.11 = (f32[1,256]{1,0:T(1,128)S(1)}, f32[1,256]{1,0:T(1,128)}, u32[]{:S(2)}) copy-start(f32[1,256]{1,0:T(1,128)} %constant.14.clone.pad_ref) | copy-start | bytes 3076
  41.0 8.4 %collective-permute-start.5 = (bf16[576,128]{1,0:T(8,128)(2,1)S(1)}, bf16[576,128]{1,0:T(8,128)(2,1)S(1)}, u32[]{:S(2)}, u32[]{:S(2)}) collective-permute-start(bf16[576,128]{1,0:T(8,128)(2,1)S(1)} %get-tuple-element.37.down), channel_id=1, source_target_pairs={{0,3},{1,0},{2,1},{3,2},{4,7},{5,4},{6,5},{7,6},{8,11},{9,8},{10,9... | collective-permute-start | bytes 442376 | tf_op jit(solution)/shard_map/ppermute | solution.py:402
  45.9 3.5 %copy-start = (bf16[4,192,768]{2,1,0:T(8,128)(2,1)S(1)}, bf16[4,192,768]{2,1,0:T(8,128)(2,1)}, u32[]{:S(2)}) copy-start(bf16[4,192,768]{2,1,0:T(8,128)(2,1)} %w_up.3) | copy-start | bytes 3538948
  45.9 3.5 %copy-start.1 = (bf16[4,768,192]{1,2,0:T(8,128)(2,1)S(1)}, bf16[4,768,192]{1,2,0:T(8,128)(2,1)}, u32[]{:S(2)}) copy-start(bf16[4,768,192]{1,2,0:T(8,128)(2,1)} %param.17) | copy-start | bytes 3538948
  45.9 3.5 %copy-start.4 = (bf16[4,192,192]{2,1,0:T(8,128)(2,1)S(1)}, bf16[4,192,192]{2,1,0:T(8,128)(2,1)}, u32[]{:S(2)}) copy-start(bf16[4,192,192]{2,1,0:T(8,128)(2,1)} %w_out.3) | copy-start | bytes 884740
  45.9 3.5 %copy-start.6 = (f32[4,2,192]{2,1,0:T(2,128)S(1)}, f32[4,2,192]{2,1,0:T(2,128)}, u32[]{:S(2)}) copy-start(f32[4,2,192]{2,1,0:T(2,128)} %gains.3) | copy-start | bytes 18436
  45.9 3.5 %copy-start.9 = (bf16[192,144]{1,0:T(8,128)(2,1)S(1)}, bf16[192,144]{1,0:T(8,128)(2,1)}, u32[]{:S(2)}) copy-start(bf16[192,144]{1,0:T(8,128)(2,1)} %constant.10.clone.oct_hbm.to_oct) | copy-start | bytes 165892
  45.9 3.5 %copy-start.10 = (bf16[144,192]{1,0:T(8,128)(2,1)S(1)}, bf16[144,192]{1,0:T(8,128)(2,1)}, u32[]{:S(2)}) copy-start(bf16[144,192]{1,0:T(8,128)(2,1)} %constant.11.clone.back) | copy-start | bytes 165892
  53.5 11.9 %collective-permute-start.6 = (bf16[144,128]{1,0:T(8,128)(2,1)S(1)}, bf16[144,128]{1,0:T(8,128)(2,1)S(1)}, u32[]{:S(2)}, u32[]{:S(2)}) collective-permute-start(bf16[144,128]{1,0:T(8,128)(2,1)S(1)} %get-tuple-element.44.own_far), channel_id=1, source_target_pairs={{0,480},{32,64},{64,32},{96,128},{128,96},{160,192},{192,160},{224... | collective-permute-start | bytes 110600 | tf_op jit(solution)/shard_map/ppermute | solution.py:408
  55.7 9.8 %collective-permute-start.7 = (bf16[144,128]{1,0:T(8,128)(2,1)S(1)}, bf16[144,128]{1,0:T(8,128)(2,1)S(1)}, u32[]{:S(2)}, u32[]{:S(2)}) collective-permute-start(bf16[144,128]{1,0:T(8,128)(2,1)S(1)} %get-tuple-element.45.own_near), channel_id=1, source_target_pairs={{0,32},{32,0},{64,96},{96,64},{128,160},{160,128},{192,224},{224,1... | collective-permute-start | bytes 110600 | tf_op jit(solution)/shard_map/ppermute | solution.py:408
  65.6 8.0 %collective-permute-start.8 = (bf16[480,128]{1,0:T(8,128)(2,1)S(1)}, bf16[480,128]{1,0:T(8,128)(2,1)S(1)}, u32[]{:S(2)}, u32[]{:S(2)}) collective-permute-start(bf16[480,128]{1,0:T(8,128)(2,1)S(1)} %get-tuple-element.47.own_far), channel_id=1, source_target_pairs={{0,28},{4,8},{8,4},{12,16},{16,12},{20,24},{24,20},{28,0},{1,29},{... | collective-permute-start | bytes 368648 | tf_op jit(solution)/shard_map/ppermute | solution.py:408
  67.5 6.1 %collective-permute-start.9 = (bf16[480,128]{1,0:T(8,128)(2,1)S(1)}, bf16[480,128]{1,0:T(8,128)(2,1)S(1)}, u32[]{:S(2)}, u32[]{:S(2)}) collective-permute-start(bf16[480,128]{1,0:T(8,128)(2,1)S(1)} %get-tuple-element.48.own_near), channel_id=1, source_target_pairs={{0,4},{4,0},{8,12},{12,8},{16,20},{20,16},{24,28},{28,24},{1,5},{5... | collective-permute-start | bytes 368648 | tf_op jit(solution)/shard_map/ppermute | solution.py:408
  73.8 7.3 %collective-permute-start.10 = (bf16[576,128]{1,0:T(8,128)(2,1)S(1)}, bf16[576,128]{1,0:T(8,128)(2,1)S(1)}, u32[]{:S(2)}, u32[]{:S(2)}) collective-permute-start(bf16[576,128]{1,0:T(8,128)(2,1)S(1)} %get-tuple-element.49.up), channel_id=1, source_target_pairs={{0,1},{1,2},{2,3},{3,0},{4,5},{5,6},{6,7},{7,4},{8,9},{9,10},{10,1... | collective-permute-start | bytes 442376 | tf_op jit(solution)/shard_map/ppermute | solution.py:402
  76.0 8.2 %collective-permute-start.11 = (bf16[576,128]{1,0:T(8,128)(2,1)S(1)}, bf16[576,128]{1,0:T(8,128)(2,1)S(1)}, u32[]{:S(2)}, u32[]{:S(2)}) collective-permute-start(bf16[576,128]{1,0:T(8,128)(2,1)S(1)} %get-tuple-element.50.down), channel_id=1, source_target_pairs={{0,3},{1,0},{2,1},{3,2},{4,7},{5,4},{6,5},{7,6},{8,11},{9,8},{10,9... | collective-permute-start | bytes 442376 | tf_op jit(solution)/shard_map/ppermute | solution.py:402

commit v7 on v6

--- a/solution.py
+++ b/solution.py
@@ -85,15 +85,19 @@
     return jnp.concatenate([jnp.where(m, q, 0.0) for m in masks], axis=0).astype(BF)
 
 
-def softmax_mix(scores, keys_v, rows, masks):
-    top = jnp.max(scores, axis=-1, keepdims=True)
-    terms = jnp.exp(scores - top)
-    total = 1.0 / jnp.sum(terms, axis=-1, keepdims=True)
-    mixed = dot(terms.astype(BF), keys_v) * total
-    out = mixed[0:rows]
-    for h in range(1, HEADS):
-        out = jnp.where(masks[h], mixed[h * rows : (h + 1) * rows], out)
-    return out
+def softmax_mix(scores, values, rows, masks):
+    tops = [jnp.max(score, axis=-1, keepdims=True) for score in scores]
+    terms = [jnp.exp(score - top) for score, top in zip(scores, tops)]
+    totals = [1.0 / jnp.sum(term, axis=-1, keepdims=True) for term in terms]
+    mixed = [dot(term.astype(BF), v) for term, v in zip(terms, values)]
+    outs = []
+    for part, total in zip(mixed, totals):
+        part = part * total
+        out = part[0:rows]
+        for h in range(1, HEADS):
+            out = jnp.where(masks[h], part[h * rows : (h + 1) * rows], out)
+        outs.append(out)
+    return outs
 
 
 def feed_forward(middle, gain, w_up, w_down):
@@ -107,12 +111,14 @@
     normed = layer_norm(stream.astype(F32), gain0)
     qkv = dot(normed, w_qkv)
     q = qkv[:, :D].astype(BF).astype(F32) * np.float32(HD**-0.5)
-    k = qkv[:, D : 2 * D].astype(BF)
-    v = qkv[:, 2 * D :].astype(BF)
     masks = head_mask(T)
     bias = jnp.concatenate([bias[0], bias[1, :, : T - 128]], axis=1)
-    scores = dot_t(spread_heads(q, masks), k) + bias
-    heads_out = softmax_mix(scores, v, T, masks).astype(BF)
+    scores, values = [], []
+    for at in range(0, stream.shape[0], T):
+        k = qkv[at : at + T, D : 2 * D].astype(BF)
+        values.append(qkv[at : at + T, 2 * D :].astype(BF))
+        scores.append(dot_t(spread_heads(q[at : at + T], masks), k) + bias)
+    heads_out = jnp.concatenate(softmax_mix(scores, values, T, masks), axis=0).astype(BF)
     attended = dot(heads_out, w_out).astype(BF)
     middle = (stream.astype(F32) + attended.astype(F32)).astype(BF)
     return feed_forward(middle, gain1, w_up, w_down)
@@ -138,38 +144,48 @@
 
 
 def own_keys_kernel(block, down, up, w_qkv, q_ref, k_ref, v_ref):
+    across = k_ref.shape[2] * 2
     own = []
     for z, ref in enumerate((down, up)):
         tokens = unpack(ref[...])
         keys_values(tokens, w_qkv[block], k_ref.at[z], v_ref.at[z])
         for yh in range(2):
-            row = (1 + yh) * 4 * SLOT + SLOT
-            own.append(tokens[row : row + PAIR])
+            row = ((1 + yh) * across + 1) * SLOT
+            own.append(tokens[row : row + (across - 2) * SLOT])
     q = dot(jnp.concatenate(own, axis=0).astype(BF), w_qkv[block, :, :D]).astype(BF)
     q_ref[...] = q.astype(F32) * np.float32(HD**-0.5)
 
 
 def level_windows(z, halo, q_ref, k_own, v_own, w_qkv, bias, k_ref, v_ref):
+    pairs = k_own.shape[2]
+    windows = pairs - 1
     keys_values(unpack(halo[...]), w_qkv, k_ref, v_ref)
     masks = head_mask(SLOT)
-    outs = []
+    sides = ((k_ref, v_ref), (k_own.at[z], v_own.at[z]))
+    if z:
+        sides = sides[::-1]
+    names, scores, values = [], [], []
     for yh in range(2):
-        for xh in range(2):
-            sides = ((k_ref, v_ref), (k_own.at[z], v_own.at[z]))
-            if z:
-                sides = sides[::-1]
+        for pair in range(pairs):
             ks, vs = [
                 jnp.concatenate(
-                    [side[i][2 * yh : 2 * yh + 2, xh].reshape(2 * PAIR, D) for side in sides], axis=0
+                    [side[i][2 * yh : 2 * yh + 2, pair].reshape(2 * PAIR, D) for side in sides],
+                    axis=0,
                 )
                 for i in range(2)
             ]
-            w = (z * 2 + yh) * 2 + xh
-            q = spread_heads(q_ref[w * SLOT : (w + 1) * SLOT], masks)
-            rows = slice(w * 144, (w + 1) * 144)
-            scores = dot_t(q, ks) + jnp.concatenate([bias[0, rows], bias[1, rows, :64]], 1)
-            outs.append(softmax_mix(scores, vs, SLOT, masks))
-    return jnp.concatenate(outs, axis=0).astype(BF)
+            for half in (2 * pair - 1, 2 * pair):
+                if half < 0 or half >= 2 * windows:
+                    continue
+                at = ((z * 2 + yh) * 2 * windows + half) * SLOT
+                q = spread_heads(q_ref[at : at + SLOT], masks)
+                at = ((z * 2 + yh) * 2 + half % 2) * 144
+                added = jnp.concatenate([bias[0, at : at + 144], bias[1, at : at + 144, :64]], 1)
+                names.append((half // 2, yh, half % 2))
+                scores.append(dot_t(q, ks) + added)
+                values.append(vs)
+    outs = dict(zip(names, softmax_mix(scores, values, SLOT, masks)))
+    return jnp.concatenate([outs[key] for key in sorted(outs)], axis=0).astype(BF)
 
 
 def lower_kernel(block, below, q, k_own, v_own, w_qkv, bias, out, k_ref, v_ref):
@@ -181,9 +197,12 @@
     k_ref, v_ref,
 ):
     upper = level_windows(1, above, q, k_own, v_own, w_qkv, bias, k_ref, v_ref)
-    heads_out = jnp.concatenate([lower, upper], axis=0)
-    attended = dot(back, dot(heads_out, w_out).astype(BF))
-    middle = (stream.astype(F32) + attended).astype(BF)
+    rows = 4 * SLOT
+    starts = range(0, upper.shape[0], rows)
+    heads_out = [half[at : at + rows] for at in starts for half in (lower, upper)]
+    projected = dot(jnp.concatenate(heads_out, axis=0), w_out).astype(BF)
+    attended = [dot(back, projected[2 * at : 2 * at + 2 * rows]) for at in starts]
+    middle = (stream.astype(F32) + jnp.concatenate(attended, axis=0)).astype(BF)
     return feed_forward(middle, gain1, w_up, w_down)
 
 
@@ -267,7 +286,7 @@
 
 
 def bias_shifted_kernel(keep, far, near, sel_ref, pad_ref, out_ref):
-    moved = choose(parity("lat"), near[288:], far[288:]).reshape(2, 2, 48, 128)
+    moved = choose(parity("lat"), near[-192:], far[-192:]).reshape(2, 2, 48, 128)
     parts = []
     for zq in range(2):
         rows = [jnp.concatenate([src[zq, 0], src[zq, 1]], axis=1) for src in (moved, keep)]
@@ -295,11 +314,11 @@
     return jnp.where(odd == 1, value_odd, value_even)
 
 
-def halves(stream, gain, to_oct, far, near):
+def halves(stream, gain, to_oct, odd, far, near):
     octs = dot(to_oct, layer_norm(stream.astype(F32), gain))
     west, east = pack(octs[: 4 * SLOT]), pack(octs[4 * SLOT :])
-    far[...] = choose(parity("lon"), east, west)
-    near[...] = choose(parity("lon"), west, east)
+    far[...] = choose(odd, east, west)
+    near[...] = choose(odd, west, east)
 
 
 def first_kernel(
@@ -326,23 +345,45 @@
         x[...].reshape(T, D), gains[0, 0:1], gains[0, 1:2], w_qkv[...],
         w_out[...], w_up[...], w_down[...], bias,
     )
-    stream_out[...] = stream
-    halves(stream, gains[1, 0:1], to_oct[...], far, near)
+    stream_out[...] = pack(stream.astype(F32))
+    halves(stream, gains[1, 0:1], to_oct[...], parity("lon"), far, near)
+
+
+def join_kernel(other, near, joined):
+    joined[:216] = other[...]
+    joined[216:] = near[...]
+
+
+def partner_kernel(other, gains, to_oct, far, near):
+    halves(unpack(other[...]), gains[1, 0:1], to_oct[...], 1 - parity("lon"), far, near)
+
+
+def third_kernel(third, gains, to_oct, far, near, beyond):
+    halves(unpack(third[:216]), gains[1, 0:1], to_oct[...], 1 - parity("lon"), far, near)
+    beyond[...] = third[216:]
 
 
 def middle_kernel(
-    stream_in, lower, above, q, k_own, v_own, gains, w_qkv, w_out, w_up, w_down, bias1,
-    bias2, to_oct, back, stream_out, far, near, k_ref, v_ref,
+    own_in, other_in, third_in, lower, above, q, k_own, v_own, gains, w_qkv, w_out, w_up, w_down,
+    bias1, bias2, to_oct, back, stream_out, beside_w, west, east, beside_e, k_ref, v_ref,
 ):
+    odd = parity("lon")
+    other, third = unpack(other_in[...]), unpack(third_in[:216])
+    stream = [choose(odd, other, third), unpack(own_in[...]), choose(odd, third, other)]
     stream = shifted_block(
-        stream_in[...], lower[...], above, q, k_own, v_own, gains[1, 1:2], w_qkv[1], w_out[1], w_up[1],
-        w_down[1], bias1, back[...], k_ref, v_ref,
+        jnp.concatenate(stream, axis=0).astype(BF), lower[...], above, q, k_own, v_own, gains[1, 1:2],
+        w_qkv[1], w_out[1], w_up[1], w_down[1], bias1, back[...], k_ref, v_ref,
     )
     stream = regular_block(
         stream, gains[2, 0:1], gains[2, 1:2], w_qkv[2], w_out[2], w_up[2], w_down[2], bias2
     )
-    stream_out[...] = stream
-    halves(stream, gains[3, 0:1], to_oct[...], far, near)
+    stream_out[...] = stream[T : 2 * T]
+    normed = layer_norm(stream.astype(F32), gains[3, 0:1])
+    beside_w[...] = pack(dot(to_oct[4 * SLOT :], normed[:T]))
+    octs = dot(to_oct[...], normed[T : 2 * T])
+    west[...] = pack(octs[: 4 * SLOT])
+    east[...] = pack(octs[4 * SLOT :])
+    beside_e[...] = pack(dot(to_oct[: 4 * SLOT], normed[2 * T :]))
 
 
 def last_kernel(
@@ -356,27 +397,31 @@
     out[...] = stream.reshape(T // 2, 2, D)
 
 
-def lat_pack_kernel(recv_far, own_far, own_near, recv_near, table_rows, far, near):
-    parts = [unpack(ref[...]) for ref in (recv_far, own_far, own_near, recv_near)]
-    parts = [choose(parity("lon"), parts[3 - i], parts[i]) for i in range(4)]
+def lat_pack_kernel(mirrored, *refs):
+    *columns, table_rows, far, near = refs
+    count = len(columns)
+    parts = [unpack(ref[...]) for ref in columns]
+    if mirrored:
+        parts = [choose(parity("lon"), parts[count - 1 - i], parts[i]) for i in range(count)]
     packed = []
     for yh in range(2):
         rows = [
             part[(yh * 2 + z) * SLOT : (yh * 2 + z + 1) * SLOT] for z in range(2) for part in parts
         ]
         packed.append(pack(jnp.concatenate(rows, axis=0)))
-    far[:288] = choose(parity("lat"), packed[1], packed[0])
-    near[:288] = choose(parity("lat"), packed[0], packed[1])
-    far[288:] = table_rows[...]
-    near[288:] = table_rows[...]
+    size = packed[0].shape[0]
+    far[:size] = choose(parity("lat"), packed[1], packed[0])
+    near[:size] = choose(parity("lat"), packed[0], packed[1])
+    far[size:] = table_rows[...]
+    near[size:] = table_rows[...]
 
 
 def lev_pack_kernel(recv_far, own_far, own_near, recv_near, down, up):
-    parts = [unpack(ref[:288]) for ref in (recv_far, own_far, own_near, recv_near)]
+    parts = [unpack(ref[:-192]) for ref in (recv_far, own_far, own_near, recv_near)]
     parts = [choose(parity("lat"), parts[3 - i], parts[i]) for i in range(4)]
+    half = parts[0].shape[0] // 2
     for z, ref in ((0, down), (1, up)):
-        rows = [part[z * 4 * SLOT : (z + 1) * 4 * SLOT] for part in parts]
-        ref[...] = pack(jnp.concatenate(rows, axis=0))
+        ref[...] = pack(jnp.concatenate([part[z * half : (z + 1) * half] for part in parts], axis=0))
 
 
 def call(kernel, outs, *args, scratch=(), flops=0, limit=20, place=pltpu.VMEM):
@@ -402,34 +447,33 @@
     return lax.ppermute(value, axis, [(i, (i + steps) % count) for i in range(count)])
 
 
-def swap(value, axis, far):
+def swap(value, axis, steps):
     count = lax.axis_size(axis)
-    steps = (-1, 1) if far else (1, -1)
-    return lax.ppermute(value, axis, [(i, (i + steps[i % 2]) % count) for i in range(count)])
-
-
-def kv_scratch():
-    return [pltpu.VMEM((4, 2, PAIR, D), BF)] * 2
-
-
-def halo(block, far, near, keep, send, w_qkv, sel_shift, pad):
-    recv_far = swap(far, "lon", True)
-    recv_near = swap(near, "lon", False)
+    pairs = [(i, (i + (-steps if i % 2 else steps)) % count) for i in range(count)]
+    return lax.ppermute(value, axis, pairs)
+
+
+def kv_scratch(pairs):
+    return [pltpu.VMEM((4, pairs, PAIR, D), BF)] * 2
+
+
+def halo(block, columns, keep, send, w_qkv, sel_shift, pad):
+    across = len(columns)
     far, near = call(
-        lat_pack_kernel, [shape(480, 128)] * 2, recv_far, far, near, recv_near, send,
-        limit=4,
-    )
-    recv_far = swap(far, "lat", True)
-    recv_near = swap(near, "lat", False)
+        functools.partial(lat_pack_kernel, block == 1), [shape(across * 72 + 192, 128)] * 2,
+        *columns, send, limit=4,
+    )
+    recv_far = swap(far, "lat", -1)
+    recv_near = swap(near, "lat", 1)
     down, up = call(
-        lev_pack_kernel, [shape(576, 128)] * 2, recv_far, far, near, recv_near,
-        limit=4,
+        lev_pack_kernel, [shape(across * 144, 128)] * 2, recv_far, far, near, recv_near, limit=4
     )
     above = move(down, "lev", -1)
     below = move(up, "lev", 1)
+    kv = shape(2, 4, across // 2, PAIR, D)
     q, k, v = call(
         functools.partial(own_keys_kernel, block),
-        [shape(8 * SLOT, D, dtype=F32), shape(2, 4, 2, PAIR, D), shape(2, 4, 2, PAIR, D)],
+        [shape((across - 2) * 4 * SLOT, D, dtype=F32), kv, kv],
         down, up, w_qkv, flops=1 << 30, limit=8,
     )
     bias = call(
@@ -437,8 +481,8 @@
         sel_shift, pad, flops=1 << 30, limit=8,
     )
     lower = call(
-        functools.partial(lower_kernel, block), shape(4 * SLOT, D), below, q, k, v, w_qkv, bias,
-        scratch=kv_scratch(), flops=1 << 30, limit=8,
+        functools.partial(lower_kernel, block), shape((across - 2) * 2 * SLOT, D), below, q, k, v,
+        w_qkv, bias, scratch=kv_scratch(across // 2), flops=1 << 30, limit=8,
     )
     return lower, above, q, k, v, bias
 
@@ -454,9 +498,9 @@
 
     bias_shape = (2, HEADS * T, 128)
     table_scratch = [pltpu.VMEM((HEADS, POS), F32), pltpu.VMEM((2, 2, 80, 128), F32)]
-    streams = [shape(T, D), shape(144, 128), shape(144, 128)]
+    half = shape(144, 128)
     stream, far, near = call(
-        first_kernel, streams, fields.transpose(1, 2, 0, 3).reshape(T // 2, 2, D), *weights,
+        first_kernel, [shape(216, 128), half, half], fields.transpose(1, 2, 0, 3).reshape(T // 2, 2, D), *weights,
         tables, sel_reg, to_oct,
         scratch=[
             *table_scratch, pltpu.VMEM(bias_shape, F32), pltpu.VMEM((T // 2, 2, D), BF),
@@ -466,20 +510,32 @@
         ],
         flops=1 << 31, place=pltpu.HBM,
     )
+    other = swap(stream, "lon", 1)
+    outer_own = swap(far, "lon", -2)
     rows = [shape(2, 2, 48, 128), shape(192, 128)]
     bias2, keep1, send1, keep3, send3 = call(
         tables_kernel, [shape(*bias_shape, dtype=F32), *rows, *rows], tables, tags, sel_reg,
         scratch=[*table_scratch, pltpu.VMEM((2, 2, 2, 48, 128), F32)], flops=1 << 31,
     )
-    *ready, bias1 = halo(1, far, near, keep1, send1, w_qkv, sel_shift, pad)
-    stream, far, near = call(
-        middle_kernel, streams, stream, *ready, *weights, bias1, bias2, to_oct, back,
-        scratch=kv_scratch(), flops=1 << 31,
-    )
-    *ready, bias3 = halo(3, far, near, keep3, send3, w_qkv, sel_shift, pad)
+    other, send1, outer_own = lax.optimization_barrier((other, send1, outer_own))
+    joined = call(join_kernel, shape(360, 128), other, near, limit=4)
+    third = swap(joined, "lon", 2)
+    other_far, other_near = call(
+        partner_kernel, [half, half], other, gains, to_oct, flops=1 << 28, limit=4
+    )
+    third_far, third_near, beyond = call(
+        third_kernel, [half, half, half], third, gains, to_oct, limit=4
+    )
+    columns = (beyond, third_near, third_far, far, near, other_near, other_far, outer_own)
+    *ready, bias1 = halo(1, columns, keep1, send1, w_qkv, sel_shift, pad)
+    stream, *columns = call(
+        middle_kernel, [shape(T, D), half, half, half, half], stream, other, third, *ready,
+        *weights, bias1, bias2, to_oct, back, scratch=kv_scratch(4), flops=1 << 31,
+    )
+    *ready, bias3 = halo(3, columns, keep3, send3, w_qkv, sel_shift, pad)
     stream = call(
         last_kernel, shape(T // 2, 2, D), stream, *ready, *weights, bias3, back,
-        scratch=kv_scratch(), flops=1 << 31,
+        scratch=kv_scratch(2), flops=1 << 31,
     )
     return stream.reshape(6, 12, 2, D).transpose(2, 0, 1, 3)
 

time: 87.4 us -> 83.2 us (0.952)
  waiting for transfers between devices: 24.2 us -> 18.4 us
  Pallas kernels: 18.7 us -> 20.7 us
    ppermute x8 -> x7, waiting for transfers between devices: 20.2 us -> 11.5 us  [swap(): return lax.ppermute(value, axis, pairs)]
    ppermute x4, waiting for transfers between devices: 4 us -> 6.94 us  [move(): lax.ppermute(value, axis, [(i, (i + steps) % count) for i in range(count)])]
    pallas_call x14 -> x17, Pallas kernels: 18.7 us -> 20.7 us  [call(): pl.pallas_call(kernel, out_shape=outs, in_specs=specs, scratch_shapes=lis...]
    ppermute x8 -> x7, starting transfers between devices: 31.7 us -> 31.3 us  [swap(): return lax.ppermute(value, axis, pairs)]
  transfers between devices with their start and end apart: 12 -> 11, of which waited for: 6 -> 6; matrix products, arithmetic and copies ran while one was open for 0% -> 0% of each run, Pallas kernels for 8% -> 9%
where the time goes in v7:
time: 83.2 us; the launch traced here: 82.8 us
  starting transfers between devices  43.2 us (52%)
  Pallas kernels  20.7 us (25%)
  waiting for transfers between devices  18.4 us (22%)
    ppermute x7, starting transfers between devices, swap(): return lax.ppermute(value, axis, pairs)  31.3 us
    pallas_call x17, Pallas kernels, call(): pl.pallas_call(kernel, out_shape=outs, in_specs=specs, scratch_shapes=lis...  20.7 us
    ppermute x4, starting transfers between devices, move(): lax.ppermute(value, axis, [(i, (i + steps) % count) for i in range(count)])  12 us
    ppermute x7, waiting for transfers between devices, swap(): return lax.ppermute(value, axis, pairs)  11.5 us
    ppermute x4, waiting for transfers between devices, move(): lax.ppermute(value, axis, [(i, (i + steps) % count) for i in range(count)])  6.94 us
  transfers between devices with their start and end apart: 11, of which 6 were waited for; matrix products, arithmetic and copies ran while one was open for 0% of the time, Pallas kernels for 9%

profile of v7, /device:TPU:6, one launch (start us, length us, event | category | flops | bytes accessed | tf_op | source)
XLA Modules:
  0.0 82.8 jit_solution(12955641608907449964)
XLA Ops:
  0.0 4.2 %shard_map.127 = (bf16[216,128]{1,0:T(8,128)(2,1)S(1)}, bf16[144,128]{1,0:T(8,128)(2,1)S(1)}, bf16[144,128]{1,0:T(8,128)(2,1)S(1)}) custom-call(bf16[72,2,192]{2,1,0:T(2,128)(2,1)} %bitcast.17, f32[4,2,192]{2,1,0:T(2,128)} %gains.7, bf16[4,192,576]{2,1,0:T(8,128)(2,1)} %w_qkv.11, bf16[4,192,192]{2,1,0:T(8,128)(2,1)} %w_out.3, bf16[4,192,768]{2,1,0:T(8,128)(2,1)} %w_up.3, ...), custom_call_target="tpu_custom_call" | custom-call | flops 2147483648 | bytes 1048576 | tf_op jit(solution)/shard_map/pallas_call | solution.py:431
  4.2 7.7 %collective-permute-start = (bf16[216,128]{1,0:T(8,128)(2,1)S(1)}, bf16[216,128]{1,0:T(8,128)(2,1)S(1)}, u32[]{:S(2)}, u32[]{:S(2)}) collective-permute-start(bf16[216,128]{1,0:T(8,128)(2,1)S(1)} %get-tuple-element.40.own_in), channel_id=1, source_target_pairs={{0,32},{32,0},{64,96},{96,64},{128,160},{160,128},{192,224},{224,1... | collective-permute-start | bytes 165896 | tf_op jit(solution)/shard_map/ppermute | solution.py:453
  11.9 10.9 %collective-permute-start.1 = (bf16[144,128]{1,0:T(8,128)(2,1)S(1)}, bf16[144,128]{1,0:T(8,128)(2,1)S(1)}, u32[]{:S(2)}, u32[]{:S(2)}) collective-permute-start(bf16[144,128]{1,0:T(8,128)(2,1)S(1)} %get-tuple-element.42.refs_3_), channel_id=1, source_target_pairs={{0,448},{32,96},{64,0},{96,160},{128,64},{160,224},{192,128},{224,... | collective-permute-start | bytes 110600 | tf_op jit(solution)/shard_map/ppermute | solution.py:453
  23.0 1.8 %shard_map.128 = (f32[2,864,128]{2,1,0:T(8,128)S(1)}, bf16[2,2,48,128]{3,2,1,0:T(8,128)(2,1)S(1)}, bf16[192,128]{1,0:T(8,128)(2,1)S(1)}, bf16[2,2,48,128]{3,2,1,0:T(8,128)(2,1)S(1)}, bf16[192,128]{1,0:T(8,128)(2,1)S(1)}) custom-call(bf16[4,6,4,3312]{3,2,1,0:T(4,128)(2,1)S(1)} %bitcast.15, s32[6,8,12]{2,1,0:T(8,128)S(1)} %bitcast.16, ...), custom_call_target="tpu_custom_call" | custom-call | flops 2147483648 | bytes 1048576 | tf_op jit(solution)/shard_map/pallas_call | solution.py:431
  24.8 2.1 %collective-permute-start.2 = (bf16[360,128]{1,0:T(8,128)(2,1)S(1)}, bf16[360,128]{1,0:T(8,128)(2,1)S(1)}, u32[]{:S(2)}, u32[]{:S(2)}) collective-permute-start(bf16[360,128]{1,0:T(8,128)(2,1)S(1)} %shard_map.129), channel_id=1, source_target_pairs={{0,64},{32,480},{64,128},{96,32},{128,192},{160,96},{192,256},{224... | collective-permute-start | bytes 276488 | tf_op jit(solution)/shard_map/ppermute | solution.py:453
  27.4 5.2 %collective-permute-done.2.third.third_in = bf16[360,128]{1,0:T(8,128)(2,1)S(1)} collective-permute-done((bf16[360,128]{1,0:T(8,128)(2,1)S(1)}, bf16[360,128]{1,0:T(8,128)(2,1)S(1)}, u32[]{:S(2)}, u32[]{:S(2)}) %collective-permute-start.2) | collective-permute-done | bytes 92192 | tf_op jit(solution)/shard_map/ppermute | solution.py:453
  33.4 1.9 %collective-permute-start.3 = (bf16[768,128]{1,0:T(8,128)(2,1)S(1)}, bf16[768,128]{1,0:T(8,128)(2,1)S(1)}, u32[]{:S(2)}, u32[]{:S(2)}) collective-permute-start(bf16[768,128]{1,0:T(8,128)(2,1)S(1)} %get-tuple-element.52.own_far), channel_id=1, source_target_pairs={{0,28},{4,8},{8,4},{12,16},{16,12},{20,24},{24,20},{28,0},{1,29},{... | collective-permute-start | bytes 589832 | tf_op jit(solution)/shard_map/ppermute | solution.py:453
  35.3 2.7 %collective-permute-start.4 = (bf16[768,128]{1,0:T(8,128)(2,1)S(1)}, bf16[768,128]{1,0:T(8,128)(2,1)S(1)}, u32[]{:S(2)}, u32[]{:S(2)}) collective-permute-start(bf16[768,128]{1,0:T(8,128)(2,1)S(1)} %get-tuple-element.53.own_near), channel_id=1, source_target_pairs={{0,4},{4,0},{8,12},{12,8},{16,20},{20,16},{24,28},{28,24},{1,5},{5... | collective-permute-start | bytes 589832 | tf_op jit(solution)/shard_map/ppermute | solution.py:453
  38.0 4.2 %collective-permute-done.3.recv_far.far = bf16[768,128]{1,0:T(8,128)(2,1)S(1)} collective-permute-done((bf16[768,128]{1,0:T(8,128)(2,1)S(1)}, bf16[768,128]{1,0:T(8,128)(2,1)S(1)}, u32[]{:S(2)}, u32[]{:S(2)}) %collective-permute-start.3) | collective-permute-done | bytes 196640 | tf_op jit(solution)/shard_map/ppermute | solution.py:453
  42.4 2.4 %collective-permute-start.5 = (bf16[1152,128]{1,0:T(8,128)(2,1)S(1)}, bf16[1152,128]{1,0:T(8,128)(2,1)S(1)}, u32[]{:S(2)}, u32[]{:S(2)}) collective-permute-start(bf16[1152,128]{1,0:T(8,128)(2,1)S(1)} %get-tuple-element.54.up), channel_id=1, source_target_pairs={{0,1},{1,2},{2,3},{3,0},{4,5},{5,6},{6,7},{7,4},{8,9},{9,10},{10,1... | collective-permute-start | bytes 884744 | tf_op jit(solution)/shard_map/ppermute | solution.py:447
  44.9 3.8 %collective-permute-start.6 = (bf16[1152,128]{1,0:T(8,128)(2,1)S(1)}, bf16[1152,128]{1,0:T(8,128)(2,1)S(1)}, u32[]{:S(2)}, u32[]{:S(2)}) collective-permute-start(bf16[1152,128]{1,0:T(8,128)(2,1)S(1)} %get-tuple-element.55.down), channel_id=1, source_target_pairs={{0,3},{1,0},{2,1},{3,2},{4,7},{5,4},{6,5},{7,6},{8,11},{9,8},{10,9... | collective-permute-start | bytes 884744 | tf_op jit(solution)/shard_map/ppermute | solution.py:447
  48.6 0.8 shard_map.134
  50.2 1.7 %collective-permute-done.5.below = bf16[1152,128]{1,0:T(8,128)(2,1)S(1)} collective-permute-done((bf16[1152,128]{1,0:T(8,128)(2,1)S(1)}, bf16[1152,128]{1,0:T(8,128)(2,1)S(1)}, u32[]{:S(2)}, u32[]{:S(2)}) %collective-permute-start.5) | collective-permute-done | bytes 294944 | tf_op jit(solution)/shard_map/ppermute | solution.py:447
  51.9 1.3 %shard_map.136.lower = bf16[288,192]{1,0:T(8,128)(2,1)S(1)} custom-call(bf16[1152,128]{1,0:T(8,128)(2,1)S(1)} %collective-permute-done.5.below, f32[576,192]{1,0:T(8,128)S(1)} %get-tuple-element.56.q, bf16[2,4,4,48,192]{4,3,2,1,0:T(8,128)(2,1)S(1)} %get-tuple-element.57.k_own, bf16[2,4,4,48,192]{4,3,2,1,0:T(8,128)(2,1)S(1)} %get-tuple-element.58.v_own, ...), custom_call_target="tpu_custom_call" | custom-call | flops 1073741824 | bytes 1048576 | tf_op jit(solution)/shard_map/pallas_call | solution.py:431
  53.2 2.1 %collective-permute-done.6.above = bf16[1152,128]{1,0:T(8,128)(2,1)S(1)} collective-permute-done((bf16[1152,128]{1,0:T(8,128)(2,1)S(1)}, bf16[1152,128]{1,0:T(8,128)(2,1)S(1)}, u32[]{:S(2)}, u32[]{:S(2)}) %collective-permute-start.6) | collective-permute-done | bytes 294944 | tf_op jit(solution)/shard_map/ppermute | solution.py:447
  55.4 5.8 %shard_map.137 = (bf16[144,192]{1,0:T(8,128)(2,1)S(1)}, bf16[144,128]{1,0:T(8,128)(2,1)S(1)}, bf16[144,128]{1,0:T(8,128)(2,1)S(1)}, bf16[144,128]{1,0:T(8,128)(2,1)S(1)}, bf16[144,128]{1,0:T(8,128)(2,1)S(1)}) custom-call(bf16[216,128]{1,0:T(8,128)(2,1)S(1)} %get-tuple-element.40.own_in, bf16[216,128]{1,0:T(8,128)(2,1)S(1)} %collective-permute-done.other.other_in, ...), custom_call_target="tpu_custom_call" | custom-call | flops 2147483648 | bytes 1048576 | tf_op jit(solution)/shard_map/pallas_call | solution.py:431
  61.3 4.0 %collective-permute-start.7 = (bf16[480,128]{1,0:T(8,128)(2,1)S(1)}, bf16[480,128]{1,0:T(8,128)(2,1)S(1)}, u32[]{:S(2)}, u32[]{:S(2)}) collective-permute-start(bf16[480,128]{1,0:T(8,128)(2,1)S(1)} %get-tuple-element.67.own_far), channel_id=1, source_target_pairs={{0,28},{4,8},{8,4},{12,16},{16,12},{20,24},{24,20},{28,0},{1,29},{... | collective-permute-start | bytes 368648 | tf_op jit(solution)/shard_map/ppermute | solution.py:453
  65.3 1.9 %collective-permute-start.8 = (bf16[480,128]{1,0:T(8,128)(2,1)S(1)}, bf16[480,128]{1,0:T(8,128)(2,1)S(1)}, u32[]{:S(2)}, u32[]{:S(2)}) collective-permute-start(bf16[480,128]{1,0:T(8,128)(2,1)S(1)} %get-tuple-element.68.own_near), channel_id=1, source_target_pairs={{0,4},{4,0},{8,12},{12,8},{16,20},{20,16},{24,28},{28,24},{1,5},{5... | collective-permute-start | bytes 368648 | tf_op jit(solution)/shard_map/ppermute | solution.py:453
  67.2 2.1 %collective-permute-done.7.recv_far.far = bf16[480,128]{1,0:T(8,128)(2,1)S(1)} collective-permute-done((bf16[480,128]{1,0:T(8,128)(2,1)S(1)}, bf16[480,128]{1,0:T(8,128)(2,1)S(1)}, u32[]{:S(2)}, u32[]{:S(2)}) %collective-permute-start.7) | collective-permute-done | bytes 122912 | tf_op jit(solution)/shard_map/ppermute | solution.py:453
  69.5 2.2 %collective-permute-start.9 = (bf16[576,128]{1,0:T(8,128)(2,1)S(1)}, bf16[576,128]{1,0:T(8,128)(2,1)S(1)}, u32[]{:S(2)}, u32[]{:S(2)}) collective-permute-start(bf16[576,128]{1,0:T(8,128)(2,1)S(1)} %get-tuple-element.69.up), channel_id=1, source_target_pairs={{0,1},{1,2},{2,3},{3,0},{4,5},{5,6},{6,7},{7,4},{8,9},{9,10},{10,1... | collective-permute-start | bytes 442376 | tf_op jit(solution)/shard_map/ppermute | solution.py:447
  72.3 3.7 %collective-permute-start.10 = (bf16[576,128]{1,0:T(8,128)(2,1)S(1)}, bf16[576,128]{1,0:T(8,128)(2,1)S(1)}, u32[]{:S(2)}, u32[]{:S(2)}) collective-permute-start(bf16[576,128]{1,0:T(8,128)(2,1)S(1)} %get-tuple-element.70.down), channel_id=1, source_target_pairs={{0,3},{1,0},{2,1},{3,2},{4,7},{5,4},{6,5},{7,6},{8,11},{9,8},{10,9... | collective-permute-start | bytes 442376 | tf_op jit(solution)/shard_map/ppermute | solution.py:447
  76.6 0.8 shard_map.142.lower
  77.4 3.1 %collective-permute-done.10.above = bf16[576,128]{1,0:T(8,128)(2,1)S(1)} collective-permute-done((bf16[576,128]{1,0:T(8,128)(2,1)S(1)}, bf16[576,128]{1,0:T(8,128)(2,1)S(1)}, u32[]{:S(2)}, u32[]{:S(2)}) %collective-permute-start.10) | collective-permute-done | bytes 147488 | tf_op jit(solution)/shard_map/ppermute | solution.py:447
  80.5 2.3 %shard_map.143 = bf16[72,2,192]{2,1,0:T(2,128)(2,1)} custom-call(bf16[144,192]{1,0:T(8,128)(2,1)S(1)} %get-tuple-element.61.stream_in, bf16[96,192]{1,0:T(8,128)(2,1)S(1)} %shard_map.142.lower, bf16[576,128]{1,0:T(8,128)(2,1)S(1)} %collective-permute-done.10.above, f32[192,192]{1,0:T(8,128)S(1)} %get-tuple-element.71.q, ...), custom_call_target="tpu_custom_call" | custom-call | flops 2147483648 | bytes 1048576 | tf_op jit(solution)/shard_map/pallas_call | solution.py:431
  (39 shorter events, 3.8 us)
Async XLA Ops:
  0.0 22.9 %copy-start.7 = (bf16[4,4,1,6,3312]{4,1,3,2,0:T(4,128)(2,1)S(1)}, bf16[4,4,1,6,3312]{4,1,3,2,0:T(4,128)(2,1)}, u32[]{:S(2)}) copy-start(bf16[4,4,1,6,3312]{4,1,3,2,0:T(4,128)(2,1)} %param.19) | copy-start | bytes 1907716
  0.0 22.9 %copy-start.8 = (s32[8,6,12]{2,0,1:T(8,128)S(1)}, s32[8,6,12]{2,0,1:T(8,128)}, u32[]{:S(2)}) copy-start(s32[8,6,12]{2,0,1:T(8,128)} %param.20) | copy-start | bytes 6916
  0.0 22.9 %copy-start.10 = (bf16[512,256]{1,0:T(8,128)(2,1)S(1)}, bf16[512,256]{1,0:T(8,128)(2,1)}, u32[]{:S(2)}) copy-start(bf16[512,256]{1,0:T(8,128)(2,1)} %constant.12.clone.sel_hbm.sel_ref) | copy-start | bytes 786436
  4.2 20.6 %collective-permute-start = (bf16[216,128]{1,0:T(8,128)(2,1)S(1)}, bf16[216,128]{1,0:T(8,128)(2,1)S(1)}, u32[]{:S(2)}, u32[]{:S(2)}) collective-permute-start(bf16[216,128]{1,0:T(8,128)(2,1)S(1)} %get-tuple-element.40.own_in), channel_id=1, source_target_pairs={{0,32},{32,0},{64,96},{96,64},{128,160},{160,128},{192,224},{224,1... | collective-permute-start | bytes 165896 | tf_op jit(solution)/shard_map/ppermute | solution.py:453
  11.9 12.9 %collective-permute-start.1 = (bf16[144,128]{1,0:T(8,128)(2,1)S(1)}, bf16[144,128]{1,0:T(8,128)(2,1)S(1)}, u32[]{:S(2)}, u32[]{:S(2)}) collective-permute-start(bf16[144,128]{1,0:T(8,128)(2,1)S(1)} %get-tuple-element.42.refs_3_), channel_id=1, source_target_pairs={{0,448},{32,96},{64,0},{96,160},{128,64},{160,224},{192,128},{224,... | collective-permute-start | bytes 110600 | tf_op jit(solution)/shard_map/ppermute | solution.py:453
  22.9 4.0 %copy-start.3 = (bf16[192,144]{1,0:T(8,128)(2,1)S(1)}, bf16[192,144]{1,0:T(8,128)(2,1)}, u32[]{:S(2)}) copy-start(bf16[192,144]{1,0:T(8,128)(2,1)} %constant.10.clone.oct_hbm.to_oct) | copy-start | bytes 165892
  22.9 4.0 %copy-start.6 = (f32[4,2,192]{2,1,0:T(2,128)S(1)}, f32[4,2,192]{2,1,0:T(2,128)}, u32[]{:S(2)}) copy-start(f32[4,2,192]{2,1,0:T(2,128)} %gains.7) | copy-start | bytes 18436
  24.8 23.8 %copy-start = (bf16[4,192,576]{2,1,0:T(8,128)(2,1)S(1)}, bf16[4,192,576]{2,1,0:T(8,128)(2,1)}, u32[]{:S(2)}) copy-start(bf16[4,192,576]{2,1,0:T(8,128)(2,1)} %w_qkv.11) | copy-start | bytes 2654212
  24.8 7.8 %collective-permute-start.2 = (bf16[360,128]{1,0:T(8,128)(2,1)S(1)}, bf16[360,128]{1,0:T(8,128)(2,1)S(1)}, u32[]{:S(2)}, u32[]{:S(2)}) collective-permute-start(bf16[360,128]{1,0:T(8,128)(2,1)S(1)} %shard_map.129), channel_id=1, source_target_pairs={{0,64},{32,480},{64,128},{96,32},{128,192},{160,96},{192,256},{224... | collective-permute-start | bytes 276488 | tf_op jit(solution)/shard_map/ppermute | solution.py:453
  33.4 8.8 %collective-permute-start.3 = (bf16[768,128]{1,0:T(8,128)(2,1)S(1)}, bf16[768,128]{1,0:T(8,128)(2,1)S(1)}, u32[]{:S(2)}, u32[]{:S(2)}) collective-permute-start(bf16[768,128]{1,0:T(8,128)(2,1)S(1)} %get-tuple-element.52.own_far), channel_id=1, source_target_pairs={{0,28},{4,8},{8,4},{12,16},{16,12},{20,24},{24,20},{28,0},{1,29},{... | collective-permute-start | bytes 589832 | tf_op jit(solution)/shard_map/ppermute | solution.py:453
  35.3 6.9 %collective-permute-start.4 = (bf16[768,128]{1,0:T(8,128)(2,1)S(1)}, bf16[768,128]{1,0:T(8,128)(2,1)S(1)}, u32[]{:S(2)}, u32[]{:S(2)}) collective-permute-start(bf16[768,128]{1,0:T(8,128)(2,1)S(1)} %get-tuple-element.53.own_near), channel_id=1, source_target_pairs={{0,4},{4,0},{8,12},{12,8},{16,20},{20,16},{24,28},{28,24},{1,5},{5... | collective-permute-start | bytes 589832 | tf_op jit(solution)/shard_map/ppermute | solution.py:453
  42.4 9.4 %collective-permute-start.5 = (bf16[1152,128]{1,0:T(8,128)(2,1)S(1)}, bf16[1152,128]{1,0:T(8,128)(2,1)S(1)}, u32[]{:S(2)}, u32[]{:S(2)}) collective-permute-start(bf16[1152,128]{1,0:T(8,128)(2,1)S(1)} %get-tuple-element.54.up), channel_id=1, source_target_pairs={{0,1},{1,2},{2,3},{3,0},{4,5},{5,6},{6,7},{7,4},{8,9},{9,10},{10,1... | collective-permute-start | bytes 884744 | tf_op jit(solution)/shard_map/ppermute | solution.py:447
  44.8 4.6 %copy-start.9 = (bf16[512,256]{1,0:T(8,128)(2,1)S(1)}, bf16[512,256]{1,0:T(8,128)(2,1)}, u32[]{:S(2)}) copy-start(bf16[512,256]{1,0:T(8,128)(2,1)} %constant.13.clone.sel_ref) | copy-start | bytes 786436
  44.9 4.6 %copy-start.11 = (f32[1,256]{1,0:T(1,128)S(1)}, f32[1,256]{1,0:T(1,128)}, u32[]{:S(2)}) copy-start(f32[1,256]{1,0:T(1,128)} %constant.14.clone.pad_ref) | copy-start | bytes 3076
  44.9 10.5 %collective-permute-start.6 = (bf16[1152,128]{1,0:T(8,128)(2,1)S(1)}, bf16[1152,128]{1,0:T(8,128)(2,1)S(1)}, u32[]{:S(2)}, u32[]{:S(2)}) collective-permute-start(bf16[1152,128]{1,0:T(8,128)(2,1)S(1)} %get-tuple-element.55.down), channel_id=1, source_target_pairs={{0,3},{1,0},{2,1},{3,2},{4,7},{5,4},{6,5},{7,6},{8,11},{9,8},{10,9... | collective-permute-start | bytes 884744 | tf_op jit(solution)/shard_map/ppermute | solution.py:447
  51.9 3.5 %copy-start.1 = (bf16[4,192,768]{2,1,0:T(8,128)(2,1)S(1)}, bf16[4,192,768]{2,1,0:T(8,128)(2,1)}, u32[]{:S(2)}) copy-start(bf16[4,192,768]{2,1,0:T(8,128)(2,1)} %w_up.3) | copy-start | bytes 3538948
  51.9 3.5 %copy-start.2 = (bf16[4,768,192]{1,2,0:T(8,128)(2,1)S(1)}, bf16[4,768,192]{1,2,0:T(8,128)(2,1)}, u32[]{:S(2)}) copy-start(bf16[4,768,192]{1,2,0:T(8,128)(2,1)} %param.17) | copy-start | bytes 3538948
  51.9 3.5 %copy-start.4 = (bf16[4,192,192]{2,1,0:T(8,128)(2,1)S(1)}, bf16[4,192,192]{2,1,0:T(8,128)(2,1)}, u32[]{:S(2)}) copy-start(bf16[4,192,192]{2,1,0:T(8,128)(2,1)} %w_out.3) | copy-start | bytes 884740
  51.9 3.5 %copy-start.5 = (bf16[144,192]{1,0:T(8,128)(2,1)S(1)}, bf16[144,192]{1,0:T(8,128)(2,1)}, u32[]{:S(2)}) copy-start(bf16[144,192]{1,0:T(8,128)(2,1)} %constant.11.clone.back) | copy-start | bytes 165892
  61.3 8.0 %collective-permute-start.7 = (bf16[480,128]{1,0:T(8,128)(2,1)S(1)}, bf16[480,128]{1,0:T(8,128)(2,1)S(1)}, u32[]{:S(2)}, u32[]{:S(2)}) collective-permute-start(bf16[480,128]{1,0:T(8,128)(2,1)S(1)} %get-tuple-element.67.own_far), channel_id=1, source_target_pairs={{0,28},{4,8},{8,4},{12,16},{16,12},{20,24},{24,20},{28,0},{1,29},{... | collective-permute-start | bytes 368648 | tf_op jit(solution)/shard_map/ppermute | solution.py:453
  65.3 4.0 %collective-permute-start.8 = (bf16[480,128]{1,0:T(8,128)(2,1)S(1)}, bf16[480,128]{1,0:T(8,128)(2,1)S(1)}, u32[]{:S(2)}, u32[]{:S(2)}) collective-permute-start(bf16[480,128]{1,0:T(8,128)(2,1)S(1)} %get-tuple-element.68.own_near), channel_id=1, source_target_pairs={{0,4},{4,0},{8,12},{12,8},{16,20},{20,16},{24,28},{28,24},{1,5},{5... | collective-permute-start | bytes 368648 | tf_op jit(solution)/shard_map/ppermute | solution.py:453
  69.5 7.1 %collective-permute-start.9 = (bf16[576,128]{1,0:T(8,128)(2,1)S(1)}, bf16[576,128]{1,0:T(8,128)(2,1)S(1)}, u32[]{:S(2)}, u32[]{:S(2)}) collective-permute-start(bf16[576,128]{1,0:T(8,128)(2,1)S(1)} %get-tuple-element.69.up), channel_id=1, source_target_pairs={{0,1},{1,2},{2,3},{3,0},{4,5},{5,6},{6,7},{7,4},{8,9},{9,10},{10,1... | collective-permute-start | bytes 442376 | tf_op jit(solution)/shard_map/ppermute | solution.py:447
  72.3 8.2 %collective-permute-start.10 = (bf16[576,128]{1,0:T(8,128)(2,1)S(1)}, bf16[576,128]{1,0:T(8,128)(2,1)S(1)}, u32[]{:S(2)}, u32[]{:S(2)}) collective-permute-start(bf16[576,128]{1,0:T(8,128)(2,1)S(1)} %get-tuple-element.70.down), channel_id=1, source_target_pairs={{0,3},{1,0},{2,1},{3,2},{4,7},{5,4},{6,5},{7,6},{8,11},{9,8},{10,9... | collective-permute-start | bytes 442376 | tf_op jit(solution)/shard_map/ppermute | solution.py:447

commit v8 on v7

--- a/solution.py
+++ b/solution.py
@@ -20,6 +20,7 @@
 OFFS = 2 * WX - 1
 POS = 3312
 SLOT = 24
+FILLED = 18
 PAIR = 2 * SLOT
 NEG = -1e30
 MASK_AT = 192
@@ -38,7 +39,16 @@
                 slot = yl * 6 + xl
                 to_oct[((xh * 2 + yh) * 2 + z) * SLOT + slot, tok] = 1.0
                 back[tok, ((z * 2 + yh) * 2 + xh) * SLOT + slot] = 1.0
-    return to_oct, back
+    side = np.zeros((2, T // 2, T), np.float32)
+    side_oct = np.zeros((4 * SLOT, T // 2), np.float32)
+    for z in range(2):
+        for y in range(6):
+            for x in range(12):
+                half = (y * 6 + x % 6) * 2 + z
+                side[x // 6, half, (y * 12 + x) * 2 + z] = 1.0
+                row = (y // 3 * 2 + z) * SLOT + y % 3 * 6 + x % 6
+                side_oct[row, half] = 1.0
+    return to_oct, back, side, side_oct
 
 
 def selectors():
@@ -85,13 +95,14 @@
     return jnp.concatenate([jnp.where(m, q, 0.0) for m in masks], axis=0).astype(BF)
 
 
-def softmax_mix(scores, values, rows, masks):
+def softmax_mix(scores, values, sizes):
     tops = [jnp.max(score, axis=-1, keepdims=True) for score in scores]
     terms = [jnp.exp(score - top) for score, top in zip(scores, tops)]
     totals = [1.0 / jnp.sum(term, axis=-1, keepdims=True) for term in terms]
     mixed = [dot(term.astype(BF), v) for term, v in zip(terms, values)]
     outs = []
-    for part, total in zip(mixed, totals):
+    for part, total, rows in zip(mixed, totals, sizes):
+        masks = head_mask(rows)
         part = part * total
         out = part[0:rows]
         for h in range(1, HEADS):
@@ -107,21 +118,29 @@
     return (middle.astype(F32) + dot_t(hidden, w_down)).astype(BF)
 
 
-def regular_block(stream, gain0, gain1, w_qkv, w_out, w_up, w_down, bias):
-    normed = layer_norm(stream.astype(F32), gain0)
-    qkv = dot(normed, w_qkv)
-    q = qkv[:, :D].astype(BF).astype(F32) * np.float32(HD**-0.5)
-    masks = head_mask(T)
-    bias = jnp.concatenate([bias[0], bias[1, :, : T - 128]], axis=1)
-    scores, values = [], []
-    for at in range(0, stream.shape[0], T):
-        k = qkv[at : at + T, D : 2 * D].astype(BF)
-        values.append(qkv[at : at + T, 2 * D :].astype(BF))
-        scores.append(dot_t(spread_heads(q[at : at + T], masks), k) + bias)
-    heads_out = jnp.concatenate(softmax_mix(scores, values, T, masks), axis=0).astype(BF)
-    attended = dot(heads_out, w_out).astype(BF)
-    middle = (stream.astype(F32) + attended.astype(F32)).astype(BF)
-    return feed_forward(middle, gain1, w_up, w_down)
+def regular_block(
+    stream, queries, normed_q, gain0, gain1, w_qkv, w_out, w_up, w_down, biases, arrive=lambda: None
+):
+    if normed_q is None:
+        normed_q = normed = layer_norm(stream.astype(F32), gain0)
+    else:
+        normed = layer_norm(stream.astype(F32), gain0)
+        normed_q = normed_q(normed)
+    q = dot(normed_q, w_qkv[:, :D]).astype(BF).astype(F32) * np.float32(HD**-0.5)
+    kv = dot(normed, w_qkv[:, D:])
+    scores, values, at = [], [], 0
+    sizes = [bias.shape[1] // HEADS for bias in biases]
+    for i, (bias, size) in enumerate(zip(biases, sizes)):
+        k = kv[i * T : (i + 1) * T, :D].astype(BF)
+        values.append(kv[i * T : (i + 1) * T, D:].astype(BF))
+        added = jnp.concatenate([bias[0], bias[1, :, : T - 128]], axis=1)
+        scores.append(dot_t(spread_heads(q[at : at + size], head_mask(size)), k) + added)
+        at += size
+    heads_out = jnp.concatenate(softmax_mix(scores, values, sizes), axis=0).astype(BF)
+    arrive()
+    attended = dot(heads_out, w_out[...]).astype(BF)
+    middle = (queries.astype(F32) + attended.astype(F32)).astype(BF)
+    return feed_forward(middle, gain1, w_up[...], w_down[...])
 
 
 def pack(tokens):
@@ -130,10 +149,11 @@
     return jnp.concatenate([tokens[:, :128], tails], axis=0).astype(BF)
 
 
-def unpack(packed):
+def unpack(packed, rows=None):
     values = packed.astype(F32)
-    rows = values.shape[0] // 3 * 2
-    tails = jnp.concatenate([values[rows:, :64], values[rows:, 64:]], axis=0)
+    rows = rows or values.shape[0] // 3 * 2
+    tails = values[rows : rows // 2 * 3]
+    tails = jnp.concatenate([tails[:, :64], tails[:, 64:]], axis=0)
     return jnp.concatenate([values[:rows], tails], axis=1)
 
 
@@ -147,7 +167,7 @@
     across = k_ref.shape[2] * 2
     own = []
     for z, ref in enumerate((down, up)):
-        tokens = unpack(ref[...])
+        tokens = ref[...].astype(F32)
         keys_values(tokens, w_qkv[block], k_ref.at[z], v_ref.at[z])
         for yh in range(2):
             row = ((1 + yh) * across + 1) * SLOT
@@ -159,7 +179,7 @@
 def level_windows(z, halo, q_ref, k_own, v_own, w_qkv, bias, k_ref, v_ref):
     pairs = k_own.shape[2]
     windows = pairs - 1
-    keys_values(unpack(halo[...]), w_qkv, k_ref, v_ref)
+    keys_values(spaced(unpack(halo[...])), w_qkv, k_ref, v_ref)
     masks = head_mask(SLOT)
     sides = ((k_ref, v_ref), (k_own.at[z], v_own.at[z]))
     if z:
@@ -184,7 +204,7 @@
                 names.append((half // 2, yh, half % 2))
                 scores.append(dot_t(q, ks) + added)
                 values.append(vs)
-    outs = dict(zip(names, softmax_mix(scores, values, SLOT, masks)))
+    outs = dict(zip(names, softmax_mix(scores, values, [SLOT] * len(scores))))
     return jnp.concatenate([outs[key] for key in sorted(outs)], axis=0).astype(BF)
 
 
@@ -234,7 +254,7 @@
         yield xp, dot(jnp.concatenate(rows, axis=1).astype(BF), sel)
 
 
-def bias_regular(table, sel, lhs, out_ref):
+def bias_regular(table, sel, lhs, out_ref, sides=None):
     for zp in range(2):
         for zq in range(2):
             for yp in range(6):
@@ -244,15 +264,18 @@
     parts = [jnp.concatenate([lhs[k, 0], lhs[k, 1]], axis=1) for k in range(2)]
     for xp, rows in bias_rolls(parts, sel):
         for zp in range(2):
-            put(out_ref, pl.ds(2 * xp + zp, 36, stride=24), rows[zp * 40 : zp * 40 + 36])
+            part = rows[zp * 40 : zp * 40 + 36]
+            put(out_ref, pl.ds(2 * xp + zp, 36, stride=24), part)
+            if sides is not None:
+                put(sides.at[xp // 6], pl.ds(2 * (xp % 6) + zp, 36, stride=12), part)
 
 
 def tables_kernel(
-    table_ref, label_ref, sel_ref, bias2, keep1, send1, keep3, send3, table, lhs, half
+    table_ref, label_ref, sel_ref, bias2, sides2, keep1, send1, keep3, send3, table, lhs, half
 ):
     pick_table(table_ref, 2, level_at(0), table)
     lhs[...] = jnp.zeros_like(lhs)
-    bias_regular(table, sel_ref[...], lhs, bias2)
+    bias_regular(table, sel_ref[...], lhs, bias2, sides2)
     lane = lax.broadcasted_iota(jnp.int32, (8, 128), 1)
     level = lax.broadcasted_iota(jnp.int32, (8, 128), 0)
     first = MASK_AT - 128
@@ -339,51 +362,61 @@
     lhs[...] = jnp.zeros_like(lhs)
     copies[1].wait()
     bias_regular(table, sel[...], lhs, bias)
-    for copy in copies[2:]:
+    for copy in copies[2:5]:
         copy.wait()
+
+    def arrive():
+        for copy in copies[5:]:
+            copy.wait()
+
+    tokens = x[...].reshape(T, D)
     stream = regular_block(
-        x[...].reshape(T, D), gains[0, 0:1], gains[0, 1:2], w_qkv[...],
-        w_out[...], w_up[...], w_down[...], bias,
-    )
-    stream_out[...] = pack(stream.astype(F32))
+        tokens, tokens, None, gains[0, 0:1], gains[0, 1:2], w_qkv[...],
+        w_out, w_up, w_down, [bias], arrive,
+    )
+    packed = pack(stream.astype(F32))
+    stream_out[...] = jnp.concatenate([packed, jnp.zeros((8, 128), BF)], axis=0)
     halves(stream, gains[1, 0:1], to_oct[...], parity("lon"), far, near)
 
 
 def join_kernel(other, near, joined):
-    joined[:216] = other[...]
-    joined[216:] = near[...]
+    joined[:144] = near[...]
+    joined[144:] = other[...]
 
 
 def partner_kernel(other, gains, to_oct, far, near):
-    halves(unpack(other[...]), gains[1, 0:1], to_oct[...], 1 - parity("lon"), far, near)
-
-
-def third_kernel(third, gains, to_oct, far, near, beyond):
-    halves(unpack(third[:216]), gains[1, 0:1], to_oct[...], 1 - parity("lon"), far, near)
-    beyond[...] = third[216:]
+    halves(unpack(other[...], T), gains[1, 0:1], to_oct[...], 1 - parity("lon"), far, near)
 
 
 def middle_kernel(
     own_in, other_in, third_in, lower, above, q, k_own, v_own, gains, w_qkv, w_out, w_up, w_down,
-    bias1, bias2, to_oct, back, stream_out, beside_w, west, east, beside_e, k_ref, v_ref,
+    bias1, bias2, sides2, to_oct, back, side, side_oct, stream_out, beside_w, west, east, beside_e, k_ref, v_ref,
 ):
     odd = parity("lon")
-    other, third = unpack(other_in[...]), unpack(third_in[:216])
-    stream = [choose(odd, other, third), unpack(own_in[...]), choose(odd, third, other)]
+    other, third = unpack(other_in[...], T), unpack(third_in[144:], T)
+    stream = [choose(odd, other, third), unpack(own_in[...], T), choose(odd, third, other)]
     stream = shifted_block(
         jnp.concatenate(stream, axis=0).astype(BF), lower[...], above, q, k_own, v_own, gains[1, 1:2],
         w_qkv[1], w_out[1], w_up[1], w_down[1], bias1, back[...], k_ref, v_ref,
     )
+
+    def worked(tokens):
+        left, right = dot(side[1], tokens[:T]), dot(side[0], tokens[2 * T :])
+        return jnp.concatenate([left, tokens[T : 2 * T].astype(F32), right], axis=0).astype(BF)
+
     stream = regular_block(
-        stream, gains[2, 0:1], gains[2, 1:2], w_qkv[2], w_out[2], w_up[2], w_down[2], bias2
-    )
-    stream_out[...] = stream[T : 2 * T]
-    normed = layer_norm(stream.astype(F32), gains[3, 0:1])
-    beside_w[...] = pack(dot(to_oct[4 * SLOT :], normed[:T]))
-    octs = dot(to_oct[...], normed[T : 2 * T])
+        stream, worked(stream), worked, gains[2, 0:1], gains[2, 1:2], w_qkv[2], w_out[2], w_up[2],
+        w_down[2], [sides2.at[1], bias2, sides2.at[0]],
+    )
+    stream = stream.astype(F32)
+    half = T // 2
+    stream_out[...] = stream[half : half + T].astype(BF)
+    normed = layer_norm(stream, gains[3, 0:1]).astype(F32)
+    beside_w[...] = pack(dot(side_oct[...], normed[:half].astype(BF)))
+    octs = dot(to_oct[...], normed[half : half + T].astype(BF))
     west[...] = pack(octs[: 4 * SLOT])
     east[...] = pack(octs[4 * SLOT :])
-    beside_e[...] = pack(dot(to_oct[: 4 * SLOT], normed[2 * T :]))
+    beside_e[...] = pack(dot(side_oct[...], normed[half + T :].astype(BF)))
 
 
 def last_kernel(
@@ -399,9 +432,16 @@
 
 def lat_pack_kernel(mirrored, *refs):
     *columns, table_rows, far, near = refs
-    count = len(columns)
+    if mirrored:
+        third, gains, to_oct, *columns = columns
     parts = [unpack(ref[...]) for ref in columns]
     if mirrored:
+        octs = dot(to_oct[...], layer_norm(unpack(third[144:], T), gains[1, 0:1]))
+        west, east = octs[: 4 * SLOT], octs[4 * SLOT :]
+        odd = parity("lon")
+        sides = [choose(odd, east, west), choose(odd, west, east)]
+        parts = [unpack(third[:144]), *sides, *parts]
+        count = len(parts)
         parts = [choose(parity("lon"), parts[count - 1 - i], parts[i]) for i in range(count)]
     packed = []
     for yh in range(2):
@@ -416,12 +456,22 @@
     near[size:] = table_rows[...]
 
 
-def lev_pack_kernel(recv_far, own_far, own_near, recv_near, down, up):
+def lev_pack_kernel(recv_far, own_far, own_near, recv_near, down, up, own_down, own_up):
     parts = [unpack(ref[:-192]) for ref in (recv_far, own_far, own_near, recv_near)]
     parts = [choose(parity("lat"), parts[3 - i], parts[i]) for i in range(4)]
     half = parts[0].shape[0] // 2
-    for z, ref in ((0, down), (1, up)):
-        ref[...] = pack(jnp.concatenate([part[z * half : (z + 1) * half] for part in parts], axis=0))
+    for z, ref, own in ((0, down, own_down), (1, up, own_up)):
+        tokens = jnp.concatenate([part[z * half : (z + 1) * half] for part in parts], axis=0)
+        own[...] = tokens.astype(BF)
+        starts = range(0, tokens.shape[0], SLOT)
+        ref[...] = pack(jnp.concatenate([tokens[at : at + FILLED] for at in starts], axis=0))
+
+
+def spaced(tokens):
+    starts = range(0, tokens.shape[0], FILLED)
+    gap = jnp.zeros((SLOT - FILLED, D), F32)
+    rows = [part for at in starts for part in (tokens[at : at + FILLED], gap)]
+    return jnp.concatenate(rows, axis=0)
 
 
 def call(kernel, outs, *args, scratch=(), flops=0, limit=20, place=pltpu.VMEM):
@@ -465,8 +515,9 @@
     )
     recv_far = swap(far, "lat", -1)
     recv_near = swap(near, "lat", 1)
-    down, up = call(
-        lev_pack_kernel, [shape(across * 144, 128)] * 2, recv_far, far, near, recv_near, limit=4
+    down, up, own_down, own_up = call(
+        lev_pack_kernel, [shape(across * 108, 128)] * 2 + [shape(across * 96, D)] * 2,
+        recv_far, far, near, recv_near, limit=4,
     )
     above = move(down, "lev", -1)
     below = move(up, "lev", 1)
@@ -474,7 +525,7 @@
     q, k, v = call(
         functools.partial(own_keys_kernel, block),
         [shape((across - 2) * 4 * SLOT, D, dtype=F32), kv, kv],
-        down, up, w_qkv, flops=1 << 30, limit=8,
+        own_down, own_up, w_qkv, flops=1 << 30, limit=8,
     )
     bias = call(
         bias_shifted_kernel, shape(2, 8 * 144, 128, dtype=F32), keep, recv_far, recv_near,
@@ -488,7 +539,7 @@
 
 
 def per_device(fields, w_qkv, w_out, w_up, w_down, gains, bias_table, labels):
-    to_oct, back = [jnp.asarray(m, BF) for m in octant_maps()]
+    to_oct, back, side, side_oct = [jnp.asarray(m, BF) for m in octant_maps()]
     sel_reg, sel_shift, pad = selectors()
     sel_reg, sel_shift = jnp.asarray(sel_reg, BF), jnp.asarray(sel_shift, BF)
     pad = jnp.asarray(pad, F32)
@@ -500,7 +551,7 @@
     table_scratch = [pltpu.VMEM((HEADS, POS), F32), pltpu.VMEM((2, 2, 80, 128), F32)]
     half = shape(144, 128)
     stream, far, near = call(
-        first_kernel, [shape(216, 128), half, half], fields.transpose(1, 2, 0, 3).reshape(T // 2, 2, D), *weights,
+        first_kernel, [shape(224, 128), half, half], fields.transpose(1, 2, 0, 3).reshape(T // 2, 2, D), *weights,
         tables, sel_reg, to_oct,
         scratch=[
             *table_scratch, pltpu.VMEM(bias_shape, F32), pltpu.VMEM((T // 2, 2, D), BF),
@@ -513,24 +564,23 @@
     other = swap(stream, "lon", 1)
     outer_own = swap(far, "lon", -2)
     rows = [shape(2, 2, 48, 128), shape(192, 128)]
-    bias2, keep1, send1, keep3, send3 = call(
-        tables_kernel, [shape(*bias_shape, dtype=F32), *rows, *rows], tables, tags, sel_reg,
+    bias2, sides2, keep1, send1, keep3, send3 = call(
+        tables_kernel,
+        [shape(*bias_shape, dtype=F32), shape(2, 2, HEADS * T // 2, 128, dtype=F32), *rows, *rows],
+        tables, tags, sel_reg,
         scratch=[*table_scratch, pltpu.VMEM((2, 2, 2, 48, 128), F32)], flops=1 << 31,
     )
     other, send1, outer_own = lax.optimization_barrier((other, send1, outer_own))
-    joined = call(join_kernel, shape(360, 128), other, near, limit=4)
+    joined = call(join_kernel, shape(368, 128), other, near, limit=4)
     third = swap(joined, "lon", 2)
     other_far, other_near = call(
         partner_kernel, [half, half], other, gains, to_oct, flops=1 << 28, limit=4
     )
-    third_far, third_near, beyond = call(
-        third_kernel, [half, half, half], third, gains, to_oct, limit=4
-    )
-    columns = (beyond, third_near, third_far, far, near, other_near, other_far, outer_own)
+    columns = (third, gains, to_oct, far, near, other_near, other_far, outer_own)
     *ready, bias1 = halo(1, columns, keep1, send1, w_qkv, sel_shift, pad)
     stream, *columns = call(
         middle_kernel, [shape(T, D), half, half, half, half], stream, other, third, *ready,
-        *weights, bias1, bias2, to_oct, back, scratch=kv_scratch(4), flops=1 << 31,
+        *weights, bias1, bias2, sides2, to_oct, back, side, side_oct, scratch=kv_scratch(4), flops=1 << 31,
     )
     *ready, bias3 = halo(3, columns, keep3, send3, w_qkv, sel_shift, pad)
     stream = call(

time: 83.2 us -> 80.5 us (0.968)
  waiting for transfers between devices: 18.4 us -> 16.3 us
    ppermute x4, waiting for transfers between devices: 6.94 us -> 4.51 us  [move(): lax.ppermute(value, axis, [(i, (i + steps) % count) for i in range(count)])]
    pallas_call x17 -> x16, Pallas kernels: 20.7 us -> 20.4 us  [call(): pl.pallas_call(kernel, out_shape=outs, in_specs=specs, scratch_shapes=lis...]
where the time goes in v8:
time: 80.5 us; the launch traced here: 80.1 us
  starting transfers between devices  42.9 us (53%)
  Pallas kernels  20.4 us (25%)
  waiting for transfers between devices  16.3 us (20%)
    ppermute x7, starting transfers between devices, swap(): return lax.ppermute(value, axis, pairs)  31 us
    pallas_call x16, Pallas kernels, call(): pl.pallas_call(kernel, out_shape=outs, in_specs=specs, scratch_shapes=lis...  20.4 us
    ppermute x4, starting transfers between devices, move(): lax.ppermute(value, axis, [(i, (i + steps) % count) for i in range(count)])  11.9 us
    ppermute x7, waiting for transfers between devices, swap(): return lax.ppermute(value, axis, pairs)  11.7 us
    ppermute x4, waiting for transfers between devices, move(): lax.ppermute(value, axis, [(i, (i + steps) % count) for i in range(count)])  4.51 us
  transfers between devices with their start and end apart: 11, of which 6 were waited for; matrix products, arithmetic and copies ran while one was open for 0% of the time, Pallas kernels for 9%

profile of v8, /device:TPU:6, one launch (start us, length us, event | category | flops | bytes accessed | tf_op | source)
XLA Modules:
  0.0 80.1 jit_solution(8647272013273536213)
XLA Ops:
  0.0 4.3 %shard_map.145 = (bf16[224,128]{1,0:T(8,128)(2,1)S(1)}, bf16[144,128]{1,0:T(8,128)(2,1)S(1)}, bf16[144,128]{1,0:T(8,128)(2,1)S(1)}) custom-call(bf16[72,2,192]{2,1,0:T(2,128)(2,1)} %bitcast.17, f32[4,2,192]{2,1,0:T(2,128)} %gains.5, bf16[4,192,576]{2,1,0:T(8,128)(2,1)} %w_qkv.11, bf16[4,192,192]{2,1,0:T(8,128)(2,1)} %w_out.3, bf16[4,192,768]{2,1,0:T(8,128)(2,1)} %w_up.3, ...), custom_call_target="tpu_custom_call" | custom-call | flops 2147483648 | bytes 1048576 | tf_op jit(solution)/shard_map/pallas_call | solution.py:481
  4.3 7.7 %collective-permute-start = (bf16[224,128]{1,0:T(8,128)(2,1)S(1)}, bf16[224,128]{1,0:T(8,128)(2,1)S(1)}, u32[]{:S(2)}, u32[]{:S(2)}) collective-permute-start(bf16[224,128]{1,0:T(8,128)(2,1)S(1)} %get-tuple-element.42.own_in), channel_id=1, source_target_pairs={{0,32},{32,0},{64,96},{96,64},{128,160},{160,128},{192,224},{224,1... | collective-permute-start | bytes 172040 | tf_op jit(solution)/shard_map/ppermute | solution.py:503
  12.1 10.9 %collective-permute-start.1 = (bf16[144,128]{1,0:T(8,128)(2,1)S(1)}, bf16[144,128]{1,0:T(8,128)(2,1)S(1)}, u32[]{:S(2)}, u32[]{:S(2)}) collective-permute-start(bf16[144,128]{1,0:T(8,128)(2,1)S(1)} %get-tuple-element.44.refs_3_), channel_id=1, source_target_pairs={{0,448},{32,96},{64,0},{96,160},{128,64},{160,224},{192,128},{224,... | collective-permute-start | bytes 110600 | tf_op jit(solution)/shard_map/ppermute | solution.py:503
  23.1 1.9 %shard_map.146 = (f32[2,864,128]{2,1,0:T(8,128)S(1)}, f32[2,2,432,128]{3,2,1,0:T(8,128)S(1)}, bf16[2,2,48,128]{3,2,1,0:T(8,128)(2,1)S(1)}, bf16[192,128]{1,0:T(8...) custom-call(bf16[4,6,4,3312]{3,2,1,0:T(4,128)(2,1)S(1)} %bitcast.15, ...), custom_call_target="tpu_custom_call" | custom-call | flops 2147483648 | bytes 1048576 | tf_op jit(solution)/shard_map/pallas_call | solution.py:481
  25.1 2.1 %collective-permute-start.2 = (bf16[368,128]{1,0:T(8,128)(2,1)S(1)}, bf16[368,128]{1,0:T(8,128)(2,1)S(1)}, u32[]{:S(2)}, u32[]{:S(2)}) collective-permute-start(bf16[368,128]{1,0:T(8,128)(2,1)S(1)} %shard_map.147), channel_id=1, source_target_pairs={{0,64},{32,480},{64,128},{96,32},{128,192},{160,96},{192,256},{224... | collective-permute-start | bytes 282632 | tf_op jit(solution)/shard_map/ppermute | solution.py:503
  27.6 5.3 %collective-permute-done.2.refs_0_.third_in = bf16[368,128]{1,0:T(8,128)(2,1)S(1)} collective-permute-done((bf16[368,128]{1,0:T(8,128)(2,1)S(1)}, bf16[368,128]{1,0:T(8,128)(2,1)S(1)}, u32[]{:S(2)}, u32[]{:S(2)}) %collective-permute-start.2) | collective-permute-done | bytes 94240 | tf_op jit(solution)/shard_map/ppermute | solution.py:503
  33.4 1.9 %collective-permute-start.3 = (bf16[768,128]{1,0:T(8,128)(2,1)S(1)}, bf16[768,128]{1,0:T(8,128)(2,1)S(1)}, u32[]{:S(2)}, u32[]{:S(2)}) collective-permute-start(bf16[768,128]{1,0:T(8,128)(2,1)S(1)} %get-tuple-element.51.own_far), channel_id=1, source_target_pairs={{0,28},{4,8},{8,4},{12,16},{16,12},{20,24},{24,20},{28,0},{1,29},{... | collective-permute-start | bytes 589832 | tf_op jit(solution)/shard_map/ppermute | solution.py:503
  35.3 2.7 %collective-permute-start.4 = (bf16[768,128]{1,0:T(8,128)(2,1)S(1)}, bf16[768,128]{1,0:T(8,128)(2,1)S(1)}, u32[]{:S(2)}, u32[]{:S(2)}) collective-permute-start(bf16[768,128]{1,0:T(8,128)(2,1)S(1)} %get-tuple-element.52.own_near), channel_id=1, source_target_pairs={{0,4},{4,0},{8,12},{12,8},{16,20},{20,16},{24,28},{28,24},{1,5},{5... | collective-permute-start | bytes 589832 | tf_op jit(solution)/shard_map/ppermute | solution.py:503
  38.0 4.2 %collective-permute-done.3.recv_far.far = bf16[768,128]{1,0:T(8,128)(2,1)S(1)} collective-permute-done((bf16[768,128]{1,0:T(8,128)(2,1)S(1)}, bf16[768,128]{1,0:T(8,128)(2,1)S(1)}, u32[]{:S(2)}, u32[]{:S(2)}) %collective-permute-start.3) | collective-permute-done | bytes 196640 | tf_op jit(solution)/shard_map/ppermute | solution.py:503
  42.5 2.4 %collective-permute-start.5 = (bf16[864,128]{1,0:T(8,128)(2,1)S(1)}, bf16[864,128]{1,0:T(8,128)(2,1)S(1)}, u32[]{:S(2)}, u32[]{:S(2)}) collective-permute-start(bf16[864,128]{1,0:T(8,128)(2,1)S(1)} %get-tuple-element.53), channel_id=1, source_target_pairs={{0,1},{1,2},{2,3},{3,0},{4,5},{5,6},{6,7},{7,4},{8,9},{9,10},{10,1... | collective-permute-start | bytes 663560 | tf_op jit(solution)/shard_map/ppermute | solution.py:497
  44.9 3.6 %collective-permute-start.6 = (bf16[864,128]{1,0:T(8,128)(2,1)S(1)}, bf16[864,128]{1,0:T(8,128)(2,1)S(1)}, u32[]{:S(2)}, u32[]{:S(2)}) collective-permute-start(bf16[864,128]{1,0:T(8,128)(2,1)S(1)} %get-tuple-element.60), channel_id=1, source_target_pairs={{0,3},{1,0},{2,1},{3,2},{4,7},{5,4},{6,5},{7,6},{8,11},{9,8},{10,9... | collective-permute-start | bytes 663560 | tf_op jit(solution)/shard_map/ppermute | solution.py:497
  48.5 0.8 shard_map.151
  50.4 1.3 %shard_map.153.lower = bf16[288,192]{1,0:T(8,128)(2,1)S(1)} custom-call(bf16[864,128]{1,0:T(8,128)(2,1)S(1)} %collective-permute-done.5.below, f32[576,192]{1,0:T(8,128)S(1)} %get-tuple-element.56.q, bf16[2,4,4,48,192]{4,3,2,1,0:T(8,128)(2,1)S(1)} %get-tuple-element.57.k_own, bf16[2,4,4,48,192]{4,3,2,1,0:T(8,128)(2,1)S(1)} %get-tuple-element.58.v_own, ...), custom_call_target="tpu_custom_call" | custom-call | flops 1073741824 | bytes 1048576 | tf_op jit(solution)/shard_map/pallas_call | solution.py:481
  51.7 2.2 %collective-permute-done.6.above = bf16[864,128]{1,0:T(8,128)(2,1)S(1)} collective-permute-done((bf16[864,128]{1,0:T(8,128)(2,1)S(1)}, bf16[864,128]{1,0:T(8,128)(2,1)S(1)}, u32[]{:S(2)}, u32[]{:S(2)}) %collective-permute-start.6) | collective-permute-done | bytes 221216 | tf_op jit(solution)/shard_map/ppermute | solution.py:497
  54.0 5.4 %shard_map.154 = (bf16[144,192]{1,0:T(8,128)(2,1)S(1)}, bf16[144,128]{1,0:T(8,128)(2,1)S(1)}, bf16[144,128]{1,0:T(8,128)(2,1)S(1)}, bf16[144,128]{1,0:T(8,128)(2,1)S(1)}, bf16[144,128]{1,0:T(8,128)(2,1)S(1)}) custom-call(bf16[224,128]{1,0:T(8,128)(2,1)S(1)} %get-tuple-element.42.own_in, bf16[224,128]{1,0:T(8,128)(2,1)S(1)} %collective-permute-done.other.other_in, ...), custom_call_target="tpu_custom_call" | custom-call | flops 2147483648 | bytes 1048576 | tf_op jit(solution)/shard_map/pallas_call | solution.py:481
  59.5 3.7 %collective-permute-start.7 = (bf16[480,128]{1,0:T(8,128)(2,1)S(1)}, bf16[480,128]{1,0:T(8,128)(2,1)S(1)}, u32[]{:S(2)}, u32[]{:S(2)}) collective-permute-start(bf16[480,128]{1,0:T(8,128)(2,1)S(1)} %get-tuple-element.69.own_far), channel_id=1, source_target_pairs={{0,28},{4,8},{8,4},{12,16},{16,12},{20,24},{24,20},{28,0},{1,29},{... | collective-permute-start | bytes 368648 | tf_op jit(solution)/shard_map/ppermute | solution.py:503
  63.3 1.9 %collective-permute-start.8 = (bf16[480,128]{1,0:T(8,128)(2,1)S(1)}, bf16[480,128]{1,0:T(8,128)(2,1)S(1)}, u32[]{:S(2)}, u32[]{:S(2)}) collective-permute-start(bf16[480,128]{1,0:T(8,128)(2,1)S(1)} %get-tuple-element.70.own_near), channel_id=1, source_target_pairs={{0,4},{4,0},{8,12},{12,8},{16,20},{20,16},{24,28},{28,24},{1,5},{5... | collective-permute-start | bytes 368648 | tf_op jit(solution)/shard_map/ppermute | solution.py:503
  65.2 2.3 %collective-permute-done.7.recv_far.far = bf16[480,128]{1,0:T(8,128)(2,1)S(1)} collective-permute-done((bf16[480,128]{1,0:T(8,128)(2,1)S(1)}, bf16[480,128]{1,0:T(8,128)(2,1)S(1)}, u32[]{:S(2)}, u32[]{:S(2)}) %collective-permute-start.7) | collective-permute-done | bytes 122912 | tf_op jit(solution)/shard_map/ppermute | solution.py:503
  67.7 2.2 %collective-permute-start.9 = (bf16[432,128]{1,0:T(8,128)(2,1)S(1)}, bf16[432,128]{1,0:T(8,128)(2,1)S(1)}, u32[]{:S(2)}, u32[]{:S(2)}) collective-permute-start(bf16[432,128]{1,0:T(8,128)(2,1)S(1)} %get-tuple-element.71), channel_id=1, source_target_pairs={{0,1},{1,2},{2,3},{3,0},{4,5},{5,6},{6,7},{7,4},{8,9},{9,10},{10,1... | collective-permute-start | bytes 331784 | tf_op jit(solution)/shard_map/ppermute | solution.py:497
  69.9 3.6 %collective-permute-start.10 = (bf16[432,128]{1,0:T(8,128)(2,1)S(1)}, bf16[432,128]{1,0:T(8,128)(2,1)S(1)}, u32[]{:S(2)}, u32[]{:S(2)}) collective-permute-start(bf16[432,128]{1,0:T(8,128)(2,1)S(1)} %get-tuple-element.78), channel_id=1, source_target_pairs={{0,3},{1,0},{2,1},{3,2},{4,7},{5,4},{6,5},{7,6},{8,11},{9,8},{10,9... | collective-permute-start | bytes 331784 | tf_op jit(solution)/shard_map/ppermute | solution.py:497
  74.1 0.7 shard_map.158.bias.bias3
  74.8 0.8 shard_map.159.lower
  75.6 2.2 %collective-permute-done.10.above = bf16[432,128]{1,0:T(8,128)(2,1)S(1)} collective-permute-done((bf16[432,128]{1,0:T(8,128)(2,1)S(1)}, bf16[432,128]{1,0:T(8,128)(2,1)S(1)}, u32[]{:S(2)}, u32[]{:S(2)}) %collective-permute-start.10) | collective-permute-done | bytes 110624 | tf_op jit(solution)/shard_map/ppermute | solution.py:497
  77.8 2.3 %shard_map.160 = bf16[72,2,192]{2,1,0:T(2,128)(2,1)} custom-call(bf16[144,192]{1,0:T(8,128)(2,1)S(1)} %get-tuple-element.63.stream_in, bf16[96,192]{1,0:T(8,128)(2,1)S(1)} %shard_map.159.lower, bf16[432,128]{1,0:T(8,128)(2,1)S(1)} %collective-permute-done.10.above, f32[192,192]{1,0:T(8,128)S(1)} %get-tuple-element.74.q, ...), custom_call_target="tpu_custom_call" | custom-call | flops 2147483648 | bytes 1048576 | tf_op jit(solution)/shard_map/pallas_call | solution.py:481
  (42 shorter events, 3.2 us)
Async XLA Ops:
  0.0 23.0 %copy-start.9 = (bf16[4,4,1,6,3312]{4,1,3,2,0:T(4,128)(2,1)S(1)}, bf16[4,4,1,6,3312]{4,1,3,2,0:T(4,128)(2,1)}, u32[]{:S(2)}) copy-start(bf16[4,4,1,6,3312]{4,1,3,2,0:T(4,128)(2,1)} %param.21) | copy-start | bytes 1907716
  0.0 23.0 %copy-start.10 = (s32[8,6,12]{2,0,1:T(8,128)S(1)}, s32[8,6,12]{2,0,1:T(8,128)}, u32[]{:S(2)}) copy-start(s32[8,6,12]{2,0,1:T(8,128)} %param.22) | copy-start | bytes 6916
  0.0 23.0 %copy-start.12 = (bf16[512,256]{1,0:T(8,128)(2,1)S(1)}, bf16[512,256]{1,0:T(8,128)(2,1)}, u32[]{:S(2)}) copy-start(bf16[512,256]{1,0:T(8,128)(2,1)} %constant.18.clone.sel_hbm.sel_ref) | copy-start | bytes 786436
  4.3 20.7 %collective-permute-start = (bf16[224,128]{1,0:T(8,128)(2,1)S(1)}, bf16[224,128]{1,0:T(8,128)(2,1)S(1)}, u32[]{:S(2)}, u32[]{:S(2)}) collective-permute-start(bf16[224,128]{1,0:T(8,128)(2,1)S(1)} %get-tuple-element.42.own_in), channel_id=1, source_target_pairs={{0,32},{32,0},{64,96},{96,64},{128,160},{160,128},{192,224},{224,1... | collective-permute-start | bytes 172040 | tf_op jit(solution)/shard_map/ppermute | solution.py:503
  12.1 13.0 %collective-permute-start.1 = (bf16[144,128]{1,0:T(8,128)(2,1)S(1)}, bf16[144,128]{1,0:T(8,128)(2,1)S(1)}, u32[]{:S(2)}, u32[]{:S(2)}) collective-permute-start(bf16[144,128]{1,0:T(8,128)(2,1)S(1)} %get-tuple-element.44.refs_3_), channel_id=1, source_target_pairs={{0,448},{32,96},{64,0},{96,160},{128,64},{160,224},{192,128},{224,... | collective-permute-start | bytes 110600 | tf_op jit(solution)/shard_map/ppermute | solution.py:503
  23.0 4.1 %copy-start.3 = (bf16[192,144]{1,0:T(8,128)(2,1)S(1)}, bf16[192,144]{1,0:T(8,128)(2,1)}, u32[]{:S(2)}) copy-start(bf16[192,144]{1,0:T(8,128)(2,1)} %constant.14.clone.oct_hbm.to_oct.refs_2_) | copy-start | bytes 165892
  23.0 4.1 %copy-start.7 = (f32[4,2,192]{2,1,0:T(2,128)S(1)}, f32[4,2,192]{2,1,0:T(2,128)}, u32[]{:S(2)}) copy-start(f32[4,2,192]{2,1,0:T(2,128)} %gains.5) | copy-start | bytes 18436
  25.0 23.5 %copy-start = (bf16[4,192,576]{2,1,0:T(8,128)(2,1)S(1)}, bf16[4,192,576]{2,1,0:T(8,128)(2,1)}, u32[]{:S(2)}) copy-start(bf16[4,192,576]{2,1,0:T(8,128)(2,1)} %w_qkv.11) | copy-start | bytes 2654212
  25.1 7.8 %collective-permute-start.2 = (bf16[368,128]{1,0:T(8,128)(2,1)S(1)}, bf16[368,128]{1,0:T(8,128)(2,1)S(1)}, u32[]{:S(2)}, u32[]{:S(2)}) collective-permute-start(bf16[368,128]{1,0:T(8,128)(2,1)S(1)} %shard_map.147), channel_id=1, source_target_pairs={{0,64},{32,480},{64,128},{96,32},{128,192},{160,96},{192,256},{224... | collective-permute-start | bytes 282632 | tf_op jit(solution)/shard_map/ppermute | solution.py:503
  33.4 8.8 %collective-permute-start.3 = (bf16[768,128]{1,0:T(8,128)(2,1)S(1)}, bf16[768,128]{1,0:T(8,128)(2,1)S(1)}, u32[]{:S(2)}, u32[]{:S(2)}) collective-permute-start(bf16[768,128]{1,0:T(8,128)(2,1)S(1)} %get-tuple-element.51.own_far), channel_id=1, source_target_pairs={{0,28},{4,8},{8,4},{12,16},{16,12},{20,24},{24,20},{28,0},{1,29},{... | collective-permute-start | bytes 589832 | tf_op jit(solution)/shard_map/ppermute | solution.py:503
  35.3 6.9 %collective-permute-start.4 = (bf16[768,128]{1,0:T(8,128)(2,1)S(1)}, bf16[768,128]{1,0:T(8,128)(2,1)S(1)}, u32[]{:S(2)}, u32[]{:S(2)}) collective-permute-start(bf16[768,128]{1,0:T(8,128)(2,1)S(1)} %get-tuple-element.52.own_near), channel_id=1, source_target_pairs={{0,4},{4,0},{8,12},{12,8},{16,20},{20,16},{24,28},{28,24},{1,5},{5... | collective-permute-start | bytes 589832 | tf_op jit(solution)/shard_map/ppermute | solution.py:503
  42.5 7.8 %collective-permute-start.5 = (bf16[864,128]{1,0:T(8,128)(2,1)S(1)}, bf16[864,128]{1,0:T(8,128)(2,1)S(1)}, u32[]{:S(2)}, u32[]{:S(2)}) collective-permute-start(bf16[864,128]{1,0:T(8,128)(2,1)S(1)} %get-tuple-element.53), channel_id=1, source_target_pairs={{0,1},{1,2},{2,3},{3,0},{4,5},{5,6},{6,7},{7,4},{8,9},{9,10},{10,1... | collective-permute-start | bytes 663560 | tf_op jit(solution)/shard_map/ppermute | solution.py:497
  44.9 9.0 %collective-permute-start.6 = (bf16[864,128]{1,0:T(8,128)(2,1)S(1)}, bf16[864,128]{1,0:T(8,128)(2,1)S(1)}, u32[]{:S(2)}, u32[]{:S(2)}) collective-permute-start(bf16[864,128]{1,0:T(8,128)(2,1)S(1)} %get-tuple-element.60), channel_id=1, source_target_pairs={{0,3},{1,0},{2,1},{3,2},{4,7},{5,4},{6,5},{7,6},{8,11},{9,8},{10,9... | collective-permute-start | bytes 663560 | tf_op jit(solution)/shard_map/ppermute | solution.py:497
  48.5 1.0 %copy-start.11 = (bf16[512,256]{1,0:T(8,128)(2,1)S(1)}, bf16[512,256]{1,0:T(8,128)(2,1)}, u32[]{:S(2)}) copy-start(bf16[512,256]{1,0:T(8,128)(2,1)} %constant.19.clone.sel_ref) | copy-start | bytes 786436
  50.3 3.6 %copy-start.1 = (bf16[4,192,768]{2,1,0:T(8,128)(2,1)S(1)}, bf16[4,192,768]{2,1,0:T(8,128)(2,1)}, u32[]{:S(2)}) copy-start(bf16[4,192,768]{2,1,0:T(8,128)(2,1)} %w_up.3) | copy-start | bytes 3538948
  50.3 3.6 %copy-start.2 = (bf16[4,768,192]{1,2,0:T(8,128)(2,1)S(1)}, bf16[4,768,192]{1,2,0:T(8,128)(2,1)}, u32[]{:S(2)}) copy-start(bf16[4,768,192]{1,2,0:T(8,128)(2,1)} %param.19) | copy-start | bytes 3538948
  50.3 3.6 %copy-start.4 = (bf16[4,192,192]{2,1,0:T(8,128)(2,1)S(1)}, bf16[4,192,192]{2,1,0:T(8,128)(2,1)}, u32[]{:S(2)}) copy-start(bf16[4,192,192]{2,1,0:T(8,128)(2,1)} %w_out.3) | copy-start | bytes 884740
  50.3 3.6 %copy-start.5 = (bf16[144,192]{1,0:T(8,128)(2,1)S(1)}, bf16[144,192]{1,0:T(8,128)(2,1)}, u32[]{:S(2)}) copy-start(bf16[144,192]{1,0:T(8,128)(2,1)} %constant.15.clone.back) | copy-start | bytes 165892
  50.3 3.6 %copy-start.6 = (bf16[2,72,144]{2,1,0:T(8,128)(2,1)S(1)}, bf16[2,72,144]{2,1,0:T(8,128)(2,1)}, u32[]{:S(2)}) copy-start(bf16[2,72,144]{2,1,0:T(8,128)(2,1)} %constant.16.clone.side) | copy-start | bytes 124420
  50.3 3.6 %copy-start.8 = (bf16[96,72]{1,0:T(8,128)(2,1)S(1)}, bf16[96,72]{1,0:T(8,128)(2,1)}, u32[]{:S(2)}) copy-start(bf16[96,72]{1,0:T(8,128)(2,1)} %constant.17.clone.side_oct) | copy-start | bytes 41476
  59.5 8.0 %collective-permute-start.7 = (bf16[480,128]{1,0:T(8,128)(2,1)S(1)}, bf16[480,128]{1,0:T(8,128)(2,1)S(1)}, u32[]{:S(2)}, u32[]{:S(2)}) collective-permute-start(bf16[480,128]{1,0:T(8,128)(2,1)S(1)} %get-tuple-element.69.own_far), channel_id=1, source_target_pairs={{0,28},{4,8},{8,4},{12,16},{16,12},{20,24},{24,20},{28,0},{1,29},{... | collective-permute-start | bytes 368648 | tf_op jit(solution)/shard_map/ppermute | solution.py:503
  63.3 4.3 %collective-permute-start.8 = (bf16[480,128]{1,0:T(8,128)(2,1)S(1)}, bf16[480,128]{1,0:T(8,128)(2,1)S(1)}, u32[]{:S(2)}, u32[]{:S(2)}) collective-permute-start(bf16[480,128]{1,0:T(8,128)(2,1)S(1)} %get-tuple-element.70.own_near), channel_id=1, source_target_pairs={{0,4},{4,0},{8,12},{12,8},{16,20},{20,16},{24,28},{28,24},{1,5},{5... | collective-permute-start | bytes 368648 | tf_op jit(solution)/shard_map/ppermute | solution.py:503
  67.7 7.1 %collective-permute-start.9 = (bf16[432,128]{1,0:T(8,128)(2,1)S(1)}, bf16[432,128]{1,0:T(8,128)(2,1)S(1)}, u32[]{:S(2)}, u32[]{:S(2)}) collective-permute-start(bf16[432,128]{1,0:T(8,128)(2,1)S(1)} %get-tuple-element.71), channel_id=1, source_target_pairs={{0,1},{1,2},{2,3},{3,0},{4,5},{5,6},{6,7},{7,4},{8,9},{9,10},{10,1... | collective-permute-start | bytes 331784 | tf_op jit(solution)/shard_map/ppermute | solution.py:497
  69.9 7.9 %collective-permute-start.10 = (bf16[432,128]{1,0:T(8,128)(2,1)S(1)}, bf16[432,128]{1,0:T(8,128)(2,1)S(1)}, u32[]{:S(2)}, u32[]{:S(2)}) collective-permute-start(bf16[432,128]{1,0:T(8,128)(2,1)S(1)} %get-tuple-element.78), channel_id=1, source_target_pairs={{0,3},{1,0},{2,1},{3,2},{4,7},{5,4},{6,5},{7,6},{8,11},{9,8},{10,9... | collective-permute-start | bytes 331784 | tf_op jit(solution)/shard_map/ppermute | solution.py:497
  (1 other events, 0.9 us)

commit v9 on v8

--- a/solution.py
+++ b/solution.py
@@ -430,6 +430,10 @@
     out[...] = stream.reshape(T // 2, 2, D)
 
 
+def lat_rows(across):
+    return -(-across * 3 * FILLED // 16) * 16
+
+
 def lat_pack_kernel(mirrored, *refs):
     *columns, table_rows, far, near = refs
     if mirrored:
@@ -446,25 +450,32 @@
     packed = []
     for yh in range(2):
         rows = [
-            part[(yh * 2 + z) * SLOT : (yh * 2 + z + 1) * SLOT] for z in range(2) for part in parts
+            part[(yh * 2 + z) * SLOT : (yh * 2 + z) * SLOT + FILLED]
+            for z in range(2)
+            for part in parts
         ]
         packed.append(pack(jnp.concatenate(rows, axis=0)))
-    size = packed[0].shape[0]
+    size = lat_rows(len(parts))
+    gap = size - packed[0].shape[0]
+    if gap:
+        packed = [jnp.concatenate([p, jnp.zeros((gap, 128), BF)], axis=0) for p in packed]
     far[:size] = choose(parity("lat"), packed[1], packed[0])
     near[:size] = choose(parity("lat"), packed[0], packed[1])
     far[size:] = table_rows[...]
     near[size:] = table_rows[...]
 
 
-def lev_pack_kernel(recv_far, own_far, own_near, recv_near, down, up, own_down, own_up):
-    parts = [unpack(ref[:-192]) for ref in (recv_far, own_far, own_near, recv_near)]
+def lev_pack_kernel(
+    across, recv_far, own_far, own_near, recv_near, down, up, own_down, own_up
+):
+    refs = (recv_far, own_far, own_near, recv_near)
+    parts = [unpack(ref[: lat_rows(across)], across * 2 * FILLED) for ref in refs]
     parts = [choose(parity("lat"), parts[3 - i], parts[i]) for i in range(4)]
-    half = parts[0].shape[0] // 2
+    half = across * FILLED
     for z, ref, own in ((0, down, own_down), (1, up, own_up)):
         tokens = jnp.concatenate([part[z * half : (z + 1) * half] for part in parts], axis=0)
-        own[...] = tokens.astype(BF)
-        starts = range(0, tokens.shape[0], SLOT)
-        ref[...] = pack(jnp.concatenate([tokens[at : at + FILLED] for at in starts], axis=0))
+        own[...] = spaced(tokens).astype(BF)
+        ref[...] = pack(tokens)
 
 
 def spaced(tokens):
@@ -510,13 +521,14 @@
 def halo(block, columns, keep, send, w_qkv, sel_shift, pad):
     across = len(columns)
     far, near = call(
-        functools.partial(lat_pack_kernel, block == 1), [shape(across * 72 + 192, 128)] * 2,
+        functools.partial(lat_pack_kernel, block == 1), [shape(lat_rows(across) + 192, 128)] * 2,
         *columns, send, limit=4,
     )
     recv_far = swap(far, "lat", -1)
     recv_near = swap(near, "lat", 1)
     down, up, own_down, own_up = call(
-        lev_pack_kernel, [shape(across * 108, 128)] * 2 + [shape(across * 96, D)] * 2,
+        functools.partial(lev_pack_kernel, across),
+        [shape(across * 108, 128)] * 2 + [shape(across * 96, D)] * 2,
         recv_far, far, near, recv_near, limit=4,
     )
     above = move(down, "lev", -1)

time: 80.5 us -> 80.3 us (level)
  no operation moved by 1% of the time
where the time goes in v9:
time: 80.3 us; the launch traced here: 79.8 us
  starting transfers between devices  43.2 us (54%)
  Pallas kernels  20.4 us (25%)
  waiting for transfers between devices  15.6 us (19%)
    ppermute x7, starting transfers between devices, swap(): return lax.ppermute(value, axis, pairs)  31.3 us
    pallas_call x16, Pallas kernels, call(): pl.pallas_call(kernel, out_shape=outs, in_specs=specs, scratch_shapes=lis...  20.4 us
    ppermute x4, starting transfers between devices, move(): lax.ppermute(value, axis, [(i, (i + steps) % count) for i in range(count)])  11.9 us
    ppermute x7, waiting for transfers between devices, swap(): return lax.ppermute(value, axis, pairs)  11.2 us
    ppermute x4, waiting for transfers between devices, move(): lax.ppermute(value, axis, [(i, (i + steps) % count) for i in range(count)])  4.47 us
  transfers between devices with their start and end apart: 11, of which 6 were waited for; matrix products, arithmetic and copies ran while one was open for 0% of the time, Pallas kernels for 9%

profile of v9, /device:TPU:6, one launch (start us, length us, event | category | flops | bytes accessed | tf_op | source)
XLA Modules:
  0.0 79.8 jit_solution(10080709584920480686)
XLA Ops:
  0.0 4.3 %shard_map.145 = (bf16[224,128]{1,0:T(8,128)(2,1)S(1)}, bf16[144,128]{1,0:T(8,128)(2,1)S(1)}, bf16[144,128]{1,0:T(8,128)(2,1)S(1)}) custom-call(bf16[72,2,192]{2,1,0:T(2,128)(2,1)} %bitcast.17, f32[4,2,192]{2,1,0:T(2,128)} %gains.5, bf16[4,192,576]{2,1,0:T(8,128)(2,1)} %w_qkv.11, bf16[4,192,192]{2,1,0:T(8,128)(2,1)} %w_out.3, bf16[4,192,768]{2,1,0:T(8,128)(2,1)} %w_up.3, ...), custom_call_target="tpu_custom_call" | custom-call | flops 2147483648 | bytes 1048576 | tf_op jit(solution)/shard_map/pallas_call | solution.py:492
  4.3 7.7 %collective-permute-start = (bf16[224,128]{1,0:T(8,128)(2,1)S(1)}, bf16[224,128]{1,0:T(8,128)(2,1)S(1)}, u32[]{:S(2)}, u32[]{:S(2)}) collective-permute-start(bf16[224,128]{1,0:T(8,128)(2,1)S(1)} %get-tuple-element.42.own_in), channel_id=1, source_target_pairs={{0,32},{32,0},{64,96},{96,64},{128,160},{160,128},{192,224},{224,1... | collective-permute-start | bytes 172040 | tf_op jit(solution)/shard_map/ppermute | solution.py:514
  12.1 10.9 %collective-permute-start.1 = (bf16[144,128]{1,0:T(8,128)(2,1)S(1)}, bf16[144,128]{1,0:T(8,128)(2,1)S(1)}, u32[]{:S(2)}, u32[]{:S(2)}) collective-permute-start(bf16[144,128]{1,0:T(8,128)(2,1)S(1)} %get-tuple-element.44.refs_3_), channel_id=1, source_target_pairs={{0,448},{32,96},{64,0},{96,160},{128,64},{160,224},{192,128},{224,... | collective-permute-start | bytes 110600 | tf_op jit(solution)/shard_map/ppermute | solution.py:514
  23.1 1.9 %shard_map.146 = (f32[2,864,128]{2,1,0:T(8,128)S(1)}, f32[2,2,432,128]{3,2,1,0:T(8,128)S(1)}, bf16[2,2,48,128]{3,2,1,0:T(8,128)(2,1)S(1)}, bf16[192,128]{1,0:T(8...) custom-call(bf16[4,6,4,3312]{3,2,1,0:T(4,128)(2,1)S(1)} %bitcast.15, ...), custom_call_target="tpu_custom_call" | custom-call | flops 2147483648 | bytes 1048576 | tf_op jit(solution)/shard_map/pallas_call | solution.py:492
  25.1 2.1 %collective-permute-start.2 = (bf16[368,128]{1,0:T(8,128)(2,1)S(1)}, bf16[368,128]{1,0:T(8,128)(2,1)S(1)}, u32[]{:S(2)}, u32[]{:S(2)}) collective-permute-start(bf16[368,128]{1,0:T(8,128)(2,1)S(1)} %shard_map.147), channel_id=1, source_target_pairs={{0,64},{32,480},{64,128},{96,32},{128,192},{160,96},{192,256},{224... | collective-permute-start | bytes 282632 | tf_op jit(solution)/shard_map/ppermute | solution.py:514
  27.6 5.3 %collective-permute-done.2.refs_0_.third_in = bf16[368,128]{1,0:T(8,128)(2,1)S(1)} collective-permute-done((bf16[368,128]{1,0:T(8,128)(2,1)S(1)}, bf16[368,128]{1,0:T(8,128)(2,1)S(1)}, u32[]{:S(2)}, u32[]{:S(2)}) %collective-permute-start.2) | collective-permute-done | bytes 94240 | tf_op jit(solution)/shard_map/ppermute | solution.py:514
  33.4 1.9 %collective-permute-start.3 = (bf16[624,128]{1,0:T(8,128)(2,1)S(1)}, bf16[624,128]{1,0:T(8,128)(2,1)S(1)}, u32[]{:S(2)}, u32[]{:S(2)}) collective-permute-start(bf16[624,128]{1,0:T(8,128)(2,1)S(1)} %get-tuple-element.51.own_far), channel_id=1, source_target_pairs={{0,28},{4,8},{8,4},{12,16},{16,12},{20,24},{24,20},{28,0},{1,29},{... | collective-permute-start | bytes 479240 | tf_op jit(solution)/shard_map/ppermute | solution.py:514
  35.3 2.7 %collective-permute-start.4 = (bf16[624,128]{1,0:T(8,128)(2,1)S(1)}, bf16[624,128]{1,0:T(8,128)(2,1)S(1)}, u32[]{:S(2)}, u32[]{:S(2)}) collective-permute-start(bf16[624,128]{1,0:T(8,128)(2,1)S(1)} %get-tuple-element.52.own_near), channel_id=1, source_target_pairs={{0,4},{4,0},{8,12},{12,8},{16,20},{20,16},{24,28},{28,24},{1,5},{5... | collective-permute-start | bytes 479240 | tf_op jit(solution)/shard_map/ppermute | solution.py:514
  38.0 3.8 %collective-permute-done.3.recv_far.far = bf16[624,128]{1,0:T(8,128)(2,1)S(1)} collective-permute-done((bf16[624,128]{1,0:T(8,128)(2,1)S(1)}, bf16[624,128]{1,0:T(8,128)(2,1)S(1)}, u32[]{:S(2)}, u32[]{:S(2)}) %collective-permute-start.3) | collective-permute-done | bytes 159776 | tf_op jit(solution)/shard_map/ppermute | solution.py:514
  42.1 2.4 %collective-permute-start.5 = (bf16[864,128]{1,0:T(8,128)(2,1)S(1)}, bf16[864,128]{1,0:T(8,128)(2,1)S(1)}, u32[]{:S(2)}, u32[]{:S(2)}) collective-permute-start(bf16[864,128]{1,0:T(8,128)(2,1)S(1)} %get-tuple-element.53), channel_id=1, source_target_pairs={{0,1},{1,2},{2,3},{3,0},{4,5},{5,6},{6,7},{7,4},{8,9},{9,10},{10,1... | collective-permute-start | bytes 663560 | tf_op jit(solution)/shard_map/ppermute | solution.py:508
  44.5 3.6 %collective-permute-start.6 = (bf16[864,128]{1,0:T(8,128)(2,1)S(1)}, bf16[864,128]{1,0:T(8,128)(2,1)S(1)}, u32[]{:S(2)}, u32[]{:S(2)}) collective-permute-start(bf16[864,128]{1,0:T(8,128)(2,1)S(1)} %get-tuple-element.60), channel_id=1, source_target_pairs={{0,3},{1,0},{2,1},{3,2},{4,7},{5,4},{6,5},{7,6},{8,11},{9,8},{10,9... | collective-permute-start | bytes 663560 | tf_op jit(solution)/shard_map/ppermute | solution.py:508
  48.1 0.8 shard_map.151
  49.1 0.7 shard_map.152.bias.bias1
  49.9 1.3 %shard_map.153.lower = bf16[288,192]{1,0:T(8,128)(2,1)S(1)} custom-call(bf16[864,128]{1,0:T(8,128)(2,1)S(1)} %collective-permute-done.5.below, f32[576,192]{1,0:T(8,128)S(1)} %get-tuple-element.56.q, bf16[2,4,4,48,192]{4,3,2,1,0:T(8,128)(2,1)S(1)} %get-tuple-element.57.k_own, bf16[2,4,4,48,192]{4,3,2,1,0:T(8,128)(2,1)S(1)} %get-tuple-element.58.v_own, ...), custom_call_target="tpu_custom_call" | custom-call | flops 1073741824 | bytes 1048576 | tf_op jit(solution)/shard_map/pallas_call | solution.py:492
  51.3 2.2 %collective-permute-done.6.above = bf16[864,128]{1,0:T(8,128)(2,1)S(1)} collective-permute-done((bf16[864,128]{1,0:T(8,128)(2,1)S(1)}, bf16[864,128]{1,0:T(8,128)(2,1)S(1)}, u32[]{:S(2)}, u32[]{:S(2)}) %collective-permute-start.6) | collective-permute-done | bytes 221216 | tf_op jit(solution)/shard_map/ppermute | solution.py:508
  53.5 5.4 %shard_map.154 = (bf16[144,192]{1,0:T(8,128)(2,1)S(1)}, bf16[144,128]{1,0:T(8,128)(2,1)S(1)}, bf16[144,128]{1,0:T(8,128)(2,1)S(1)}, bf16[144,128]{1,0:T(8,128)(2,1)S(1)}, bf16[144,128]{1,0:T(8,128)(2,1)S(1)}) custom-call(bf16[224,128]{1,0:T(8,128)(2,1)S(1)} %get-tuple-element.42.own_in, bf16[224,128]{1,0:T(8,128)(2,1)S(1)} %collective-permute-done.other.other_in, ...), custom_call_target="tpu_custom_call" | custom-call | flops 2147483648 | bytes 1048576 | tf_op jit(solution)/shard_map/pallas_call | solution.py:492
  59.1 4.1 %collective-permute-start.7 = (bf16[416,128]{1,0:T(8,128)(2,1)S(1)}, bf16[416,128]{1,0:T(8,128)(2,1)S(1)}, u32[]{:S(2)}, u32[]{:S(2)}) collective-permute-start(bf16[416,128]{1,0:T(8,128)(2,1)S(1)} %get-tuple-element.69.own_far), channel_id=1, source_target_pairs={{0,28},{4,8},{8,4},{12,16},{16,12},{20,24},{24,20},{28,0},{1,29},{... | collective-permute-start | bytes 319496 | tf_op jit(solution)/shard_map/ppermute | solution.py:514
  63.2 1.9 %collective-permute-start.8 = (bf16[416,128]{1,0:T(8,128)(2,1)S(1)}, bf16[416,128]{1,0:T(8,128)(2,1)S(1)}, u32[]{:S(2)}, u32[]{:S(2)}) collective-permute-start(bf16[416,128]{1,0:T(8,128)(2,1)S(1)} %get-tuple-element.70.own_near), channel_id=1, source_target_pairs={{0,4},{4,0},{8,12},{12,8},{16,20},{20,16},{24,28},{28,24},{1,5},{5... | collective-permute-start | bytes 319496 | tf_op jit(solution)/shard_map/ppermute | solution.py:514
  65.2 2.1 %collective-permute-done.7.recv_far.far = bf16[416,128]{1,0:T(8,128)(2,1)S(1)} collective-permute-done((bf16[416,128]{1,0:T(8,128)(2,1)S(1)}, bf16[416,128]{1,0:T(8,128)(2,1)S(1)}, u32[]{:S(2)}, u32[]{:S(2)}) %collective-permute-start.7) | collective-permute-done | bytes 106528 | tf_op jit(solution)/shard_map/ppermute | solution.py:514
  67.5 2.2 %collective-permute-start.9 = (bf16[432,128]{1,0:T(8,128)(2,1)S(1)}, bf16[432,128]{1,0:T(8,128)(2,1)S(1)}, u32[]{:S(2)}, u32[]{:S(2)}) collective-permute-start(bf16[432,128]{1,0:T(8,128)(2,1)S(1)} %get-tuple-element.71), channel_id=1, source_target_pairs={{0,1},{1,2},{2,3},{3,0},{4,5},{5,6},{6,7},{7,4},{8,9},{9,10},{10,1... | collective-permute-start | bytes 331784 | tf_op jit(solution)/shard_map/ppermute | solution.py:508
  69.7 3.7 %collective-permute-start.10 = (bf16[432,128]{1,0:T(8,128)(2,1)S(1)}, bf16[432,128]{1,0:T(8,128)(2,1)S(1)}, u32[]{:S(2)}, u32[]{:S(2)}) collective-permute-start(bf16[432,128]{1,0:T(8,128)(2,1)S(1)} %get-tuple-element.78), channel_id=1, source_target_pairs={{0,3},{1,0},{2,1},{3,2},{4,7},{5,4},{6,5},{7,6},{8,11},{9,8},{10,9... | collective-permute-start | bytes 331784 | tf_op jit(solution)/shard_map/ppermute | solution.py:508
  74.6 0.8 shard_map.159.lower
  75.4 2.1 %collective-permute-done.10.above = bf16[432,128]{1,0:T(8,128)(2,1)S(1)} collective-permute-done((bf16[432,128]{1,0:T(8,128)(2,1)S(1)}, bf16[432,128]{1,0:T(8,128)(2,1)S(1)}, u32[]{:S(2)}, u32[]{:S(2)}) %collective-permute-start.10) | collective-permute-done | bytes 110624 | tf_op jit(solution)/shard_map/ppermute | solution.py:508
  77.5 2.3 %shard_map.160 = bf16[72,2,192]{2,1,0:T(2,128)(2,1)} custom-call(bf16[144,192]{1,0:T(8,128)(2,1)S(1)} %get-tuple-element.63.stream_in, bf16[96,192]{1,0:T(8,128)(2,1)S(1)} %shard_map.159.lower, bf16[432,128]{1,0:T(8,128)(2,1)S(1)} %collective-permute-done.10.above, f32[192,192]{1,0:T(8,128)S(1)} %get-tuple-element.74.q, ...), custom_call_target="tpu_custom_call" | custom-call | flops 2147483648 | bytes 1048576 | tf_op jit(solution)/shard_map/pallas_call | solution.py:492
  (42 shorter events, 3.2 us)
Async XLA Ops:
  0.0 23.0 %copy-start.9 = (bf16[4,4,1,6,3312]{4,1,3,2,0:T(4,128)(2,1)S(1)}, bf16[4,4,1,6,3312]{4,1,3,2,0:T(4,128)(2,1)}, u32[]{:S(2)}) copy-start(bf16[4,4,1,6,3312]{4,1,3,2,0:T(4,128)(2,1)} %param.21) | copy-start | bytes 1907716
  0.0 23.0 %copy-start.10 = (s32[8,6,12]{2,0,1:T(8,128)S(1)}, s32[8,6,12]{2,0,1:T(8,128)}, u32[]{:S(2)}) copy-start(s32[8,6,12]{2,0,1:T(8,128)} %param.22) | copy-start | bytes 6916
  0.0 23.0 %copy-start.12 = (bf16[512,256]{1,0:T(8,128)(2,1)S(1)}, bf16[512,256]{1,0:T(8,128)(2,1)}, u32[]{:S(2)}) copy-start(bf16[512,256]{1,0:T(8,128)(2,1)} %constant.18.clone.sel_hbm.sel_ref) | copy-start | bytes 786436
  4.3 20.7 %collective-permute-start = (bf16[224,128]{1,0:T(8,128)(2,1)S(1)}, bf16[224,128]{1,0:T(8,128)(2,1)S(1)}, u32[]{:S(2)}, u32[]{:S(2)}) collective-permute-start(bf16[224,128]{1,0:T(8,128)(2,1)S(1)} %get-tuple-element.42.own_in), channel_id=1, source_target_pairs={{0,32},{32,0},{64,96},{96,64},{128,160},{160,128},{192,224},{224,1... | collective-permute-start | bytes 172040 | tf_op jit(solution)/shard_map/ppermute | solution.py:514
  12.1 13.0 %collective-permute-start.1 = (bf16[144,128]{1,0:T(8,128)(2,1)S(1)}, bf16[144,128]{1,0:T(8,128)(2,1)S(1)}, u32[]{:S(2)}, u32[]{:S(2)}) collective-permute-start(bf16[144,128]{1,0:T(8,128)(2,1)S(1)} %get-tuple-element.44.refs_3_), channel_id=1, source_target_pairs={{0,448},{32,96},{64,0},{96,160},{128,64},{160,224},{192,128},{224,... | collective-permute-start | bytes 110600 | tf_op jit(solution)/shard_map/ppermute | solution.py:514
  23.0 4.1 %copy-start.3 = (bf16[192,144]{1,0:T(8,128)(2,1)S(1)}, bf16[192,144]{1,0:T(8,128)(2,1)}, u32[]{:S(2)}) copy-start(bf16[192,144]{1,0:T(8,128)(2,1)} %constant.14.clone.oct_hbm.to_oct.refs_2_) | copy-start | bytes 165892
  23.0 4.1 %copy-start.7 = (f32[4,2,192]{2,1,0:T(2,128)S(1)}, f32[4,2,192]{2,1,0:T(2,128)}, u32[]{:S(2)}) copy-start(f32[4,2,192]{2,1,0:T(2,128)} %gains.5) | copy-start | bytes 18436
  25.0 23.1 %copy-start = (bf16[4,192,576]{2,1,0:T(8,128)(2,1)S(1)}, bf16[4,192,576]{2,1,0:T(8,128)(2,1)}, u32[]{:S(2)}) copy-start(bf16[4,192,576]{2,1,0:T(8,128)(2,1)} %w_qkv.11) | copy-start | bytes 2654212
  25.1 7.8 %collective-permute-start.2 = (bf16[368,128]{1,0:T(8,128)(2,1)S(1)}, bf16[368,128]{1,0:T(8,128)(2,1)S(1)}, u32[]{:S(2)}, u32[]{:S(2)}) collective-permute-start(bf16[368,128]{1,0:T(8,128)(2,1)S(1)} %shard_map.147), channel_id=1, source_target_pairs={{0,64},{32,480},{64,128},{96,32},{128,192},{160,96},{192,256},{224... | collective-permute-start | bytes 282632 | tf_op jit(solution)/shard_map/ppermute | solution.py:514
  33.4 8.4 %collective-permute-start.3 = (bf16[624,128]{1,0:T(8,128)(2,1)S(1)}, bf16[624,128]{1,0:T(8,128)(2,1)S(1)}, u32[]{:S(2)}, u32[]{:S(2)}) collective-permute-start(bf16[624,128]{1,0:T(8,128)(2,1)S(1)} %get-tuple-element.51.own_far), channel_id=1, source_target_pairs={{0,28},{4,8},{8,4},{12,16},{16,12},{20,24},{24,20},{28,0},{1,29},{... | collective-permute-start | bytes 479240 | tf_op jit(solution)/shard_map/ppermute | solution.py:514
  35.3 6.5 %collective-permute-start.4 = (bf16[624,128]{1,0:T(8,128)(2,1)S(1)}, bf16[624,128]{1,0:T(8,128)(2,1)S(1)}, u32[]{:S(2)}, u32[]{:S(2)}) collective-permute-start(bf16[624,128]{1,0:T(8,128)(2,1)S(1)} %get-tuple-element.52.own_near), channel_id=1, source_target_pairs={{0,4},{4,0},{8,12},{12,8},{16,20},{20,16},{24,28},{28,24},{1,5},{5... | collective-permute-start | bytes 479240 | tf_op jit(solution)/shard_map/ppermute | solution.py:514
  42.1 7.8 %collective-permute-start.5 = (bf16[864,128]{1,0:T(8,128)(2,1)S(1)}, bf16[864,128]{1,0:T(8,128)(2,1)S(1)}, u32[]{:S(2)}, u32[]{:S(2)}) collective-permute-start(bf16[864,128]{1,0:T(8,128)(2,1)S(1)} %get-tuple-element.53), channel_id=1, source_target_pairs={{0,1},{1,2},{2,3},{3,0},{4,5},{5,6},{6,7},{7,4},{8,9},{9,10},{10,1... | collective-permute-start | bytes 663560 | tf_op jit(solution)/shard_map/ppermute | solution.py:508
  44.5 9.0 %collective-permute-start.6 = (bf16[864,128]{1,0:T(8,128)(2,1)S(1)}, bf16[864,128]{1,0:T(8,128)(2,1)S(1)}, u32[]{:S(2)}, u32[]{:S(2)}) collective-permute-start(bf16[864,128]{1,0:T(8,128)(2,1)S(1)} %get-tuple-element.60), channel_id=1, source_target_pairs={{0,3},{1,0},{2,1},{3,2},{4,7},{5,4},{6,5},{7,6},{8,11},{9,8},{10,9... | collective-permute-start | bytes 663560 | tf_op jit(solution)/shard_map/ppermute | solution.py:508
  48.1 1.0 %copy-start.11 = (bf16[512,256]{1,0:T(8,128)(2,1)S(1)}, bf16[512,256]{1,0:T(8,128)(2,1)}, u32[]{:S(2)}) copy-start(bf16[512,256]{1,0:T(8,128)(2,1)} %constant.19.clone.sel_ref) | copy-start | bytes 786436
  49.9 3.6 %copy-start.1 = (bf16[4,192,768]{2,1,0:T(8,128)(2,1)S(1)}, bf16[4,192,768]{2,1,0:T(8,128)(2,1)}, u32[]{:S(2)}) copy-start(bf16[4,192,768]{2,1,0:T(8,128)(2,1)} %w_up.3) | copy-start | bytes 3538948
  49.9 3.6 %copy-start.2 = (bf16[4,768,192]{1,2,0:T(8,128)(2,1)S(1)}, bf16[4,768,192]{1,2,0:T(8,128)(2,1)}, u32[]{:S(2)}) copy-start(bf16[4,768,192]{1,2,0:T(8,128)(2,1)} %param.19) | copy-start | bytes 3538948
  49.9 3.6 %copy-start.4 = (bf16[4,192,192]{2,1,0:T(8,128)(2,1)S(1)}, bf16[4,192,192]{2,1,0:T(8,128)(2,1)}, u32[]{:S(2)}) copy-start(bf16[4,192,192]{2,1,0:T(8,128)(2,1)} %w_out.3) | copy-start | bytes 884740
  49.9 3.6 %copy-start.5 = (bf16[144,192]{1,0:T(8,128)(2,1)S(1)}, bf16[144,192]{1,0:T(8,128)(2,1)}, u32[]{:S(2)}) copy-start(bf16[144,192]{1,0:T(8,128)(2,1)} %constant.15.clone.back) | copy-start | bytes 165892
  49.9 3.6 %copy-start.6 = (bf16[2,72,144]{2,1,0:T(8,128)(2,1)S(1)}, bf16[2,72,144]{2,1,0:T(8,128)(2,1)}, u32[]{:S(2)}) copy-start(bf16[2,72,144]{2,1,0:T(8,128)(2,1)} %constant.16.clone.side) | copy-start | bytes 124420
  49.9 3.6 %copy-start.8 = (bf16[96,72]{1,0:T(8,128)(2,1)S(1)}, bf16[96,72]{1,0:T(8,128)(2,1)}, u32[]{:S(2)}) copy-start(bf16[96,72]{1,0:T(8,128)(2,1)} %constant.17.clone.side_oct) | copy-start | bytes 41476
  59.1 8.2 %collective-permute-start.7 = (bf16[416,128]{1,0:T(8,128)(2,1)S(1)}, bf16[416,128]{1,0:T(8,128)(2,1)S(1)}, u32[]{:S(2)}, u32[]{:S(2)}) collective-permute-start(bf16[416,128]{1,0:T(8,128)(2,1)S(1)} %get-tuple-element.69.own_far), channel_id=1, source_target_pairs={{0,28},{4,8},{8,4},{12,16},{16,12},{20,24},{24,20},{28,0},{1,29},{... | collective-permute-start | bytes 319496 | tf_op jit(solution)/shard_map/ppermute | solution.py:514
  63.2 4.1 %collective-permute-start.8 = (bf16[416,128]{1,0:T(8,128)(2,1)S(1)}, bf16[416,128]{1,0:T(8,128)(2,1)S(1)}, u32[]{:S(2)}, u32[]{:S(2)}) collective-permute-start(bf16[416,128]{1,0:T(8,128)(2,1)S(1)} %get-tuple-element.70.own_near), channel_id=1, source_target_pairs={{0,4},{4,0},{8,12},{12,8},{16,20},{20,16},{24,28},{28,24},{1,5},{5... | collective-permute-start | bytes 319496 | tf_op jit(solution)/shard_map/ppermute | solution.py:514
  67.5 7.1 %collective-permute-start.9 = (bf16[432,128]{1,0:T(8,128)(2,1)S(1)}, bf16[432,128]{1,0:T(8,128)(2,1)S(1)}, u32[]{:S(2)}, u32[]{:S(2)}) collective-permute-start(bf16[432,128]{1,0:T(8,128)(2,1)S(1)} %get-tuple-element.71), channel_id=1, source_target_pairs={{0,1},{1,2},{2,3},{3,0},{4,5},{5,6},{6,7},{7,4},{8,9},{9,10},{10,1... | collective-permute-start | bytes 331784 | tf_op jit(solution)/shard_map/ppermute | solution.py:508
  69.7 7.9 %collective-permute-start.10 = (bf16[432,128]{1,0:T(8,128)(2,1)S(1)}, bf16[432,128]{1,0:T(8,128)(2,1)S(1)}, u32[]{:S(2)}, u32[]{:S(2)}) collective-permute-start(bf16[432,128]{1,0:T(8,128)(2,1)S(1)} %get-tuple-element.78), channel_id=1, source_target_pairs={{0,3},{1,0},{2,1},{3,2},{4,7},{5,4},{6,5},{7,6},{8,11},{9,8},{10,9... | collective-permute-start | bytes 331784 | tf_op jit(solution)/shard_map/ppermute | solution.py:508
  (1 other events, 0.9 us)

commit v10 on v9

--- a/solution.py
+++ b/solution.py
@@ -173,14 +173,16 @@
             row = ((1 + yh) * across + 1) * SLOT
             own.append(tokens[row : row + (across - 2) * SLOT])
     q = dot(jnp.concatenate(own, axis=0).astype(BF), w_qkv[block, :, :D]).astype(BF)
-    q_ref[...] = q.astype(F32) * np.float32(HD**-0.5)
+    q = q.astype(F32) * np.float32(HD**-0.5)
+    masks = head_mask(SLOT)
+    for at in range(0, q.shape[0], SLOT):
+        q_ref[at * HEADS : (at + SLOT) * HEADS] = spread_heads(q[at : at + SLOT], masks)
 
 
 def level_windows(z, halo, q_ref, k_own, v_own, w_qkv, bias, k_ref, v_ref):
     pairs = k_own.shape[2]
     windows = pairs - 1
     keys_values(spaced(unpack(halo[...])), w_qkv, k_ref, v_ref)
-    masks = head_mask(SLOT)
     sides = ((k_ref, v_ref), (k_own.at[z], v_own.at[z]))
     if z:
         sides = sides[::-1]
@@ -198,7 +200,7 @@
                 if half < 0 or half >= 2 * windows:
                     continue
                 at = ((z * 2 + yh) * 2 * windows + half) * SLOT
-                q = spread_heads(q_ref[at : at + SLOT], masks)
+                q = q_ref[at * HEADS : (at + SLOT) * HEADS]
                 at = ((z * 2 + yh) * 2 + half % 2) * 144
                 added = jnp.concatenate([bias[0, at : at + 144], bias[1, at : at + 144, :64]], 1)
                 names.append((half // 2, yh, half % 2))
@@ -536,7 +538,7 @@
     kv = shape(2, 4, across // 2, PAIR, D)
     q, k, v = call(
         functools.partial(own_keys_kernel, block),
-        [shape((across - 2) * 4 * SLOT, D, dtype=F32), kv, kv],
+        [shape((across - 2) * 4 * SLOT * HEADS, D), kv, kv],
         own_down, own_up, w_qkv, flops=1 << 30, limit=8,
     )
     bias = call(

time: 80.3 us -> 80.3 us (level)
  no operation moved by 1% of the time
where the time goes in v10:
time: 80.3 us; the launch traced here: 79.8 us
  starting transfers between devices  43.2 us (54%)
  Pallas kernels  20.5 us (26%)
  waiting for transfers between devices  15.6 us (19%)
    ppermute x7, starting transfers between devices, swap(): return lax.ppermute(value, axis, pairs)  31.3 us
    pallas_call x16, Pallas kernels, call(): pl.pallas_call(kernel, out_shape=outs, in_specs=specs, scratch_shapes=lis...  20.5 us
    ppermute x4, starting transfers between devices, move(): lax.ppermute(value, axis, [(i, (i + steps) % count) for i in range(count)])  11.9 us
    ppermute x7, waiting for transfers between devices, swap(): return lax.ppermute(value, axis, pairs)  11.2 us
    ppermute x4, waiting for transfers between devices, move(): lax.ppermute(value, axis, [(i, (i + steps) % count) for i in range(count)])  4.45 us
  transfers between devices with their start and end apart: 11, of which 6 were waited for; matrix products, arithmetic and copies ran while one was open for 0% of the time, Pallas kernels for 9%

profile of v10, /device:TPU:6, one launch (start us, length us, event | category | flops | bytes accessed | tf_op | source)
XLA Modules:
  0.0 79.8 jit_solution(13499858158340224234)
XLA Ops:
  0.0 4.3 %shard_map.145 = (bf16[224,128]{1,0:T(8,128)(2,1)S(1)}, bf16[144,128]{1,0:T(8,128)(2,1)S(1)}, bf16[144,128]{1,0:T(8,128)(2,1)S(1)}) custom-call(bf16[72,2,192]{2,1,0:T(2,128)(2,1)} %bitcast.17, f32[4,2,192]{2,1,0:T(2,128)} %gains.5, bf16[4,192,576]{2,1,0:T(8,128)(2,1)} %w_qkv.11, bf16[4,192,192]{2,1,0:T(8,128)(2,1)} %w_out.3, bf16[4,192,768]{2,1,0:T(8,128)(2,1)} %w_up.3, ...), custom_call_target="tpu_custom_call" | custom-call | flops 2147483648 | bytes 1048576 | tf_op jit(solution)/shard_map/pallas_call | solution.py:494
  4.3 7.7 %collective-permute-start = (bf16[224,128]{1,0:T(8,128)(2,1)S(1)}, bf16[224,128]{1,0:T(8,128)(2,1)S(1)}, u32[]{:S(2)}, u32[]{:S(2)}) collective-permute-start(bf16[224,128]{1,0:T(8,128)(2,1)S(1)} %get-tuple-element.42.own_in), channel_id=1, source_target_pairs={{0,32},{32,0},{64,96},{96,64},{128,160},{160,128},{192,224},{224,1... | collective-permute-start | bytes 172040 | tf_op jit(solution)/shard_map/ppermute | solution.py:516
  12.1 10.9 %collective-permute-start.1 = (bf16[144,128]{1,0:T(8,128)(2,1)S(1)}, bf16[144,128]{1,0:T(8,128)(2,1)S(1)}, u32[]{:S(2)}, u32[]{:S(2)}) collective-permute-start(bf16[144,128]{1,0:T(8,128)(2,1)S(1)} %get-tuple-element.44.refs_3_), channel_id=1, source_target_pairs={{0,448},{32,96},{64,0},{96,160},{128,64},{160,224},{192,128},{224,... | collective-permute-start | bytes 110600 | tf_op jit(solution)/shard_map/ppermute | solution.py:516
  23.1 2.0 %shard_map.146 = (f32[2,864,128]{2,1,0:T(8,128)S(1)}, f32[2,2,432,128]{3,2,1,0:T(8,128)S(1)}, bf16[2,2,48,128]{3,2,1,0:T(8,128)(2,1)S(1)}, bf16[192,128]{1,0:T(8...) custom-call(bf16[4,6,4,3312]{3,2,1,0:T(4,128)(2,1)S(1)} %bitcast.15, ...), custom_call_target="tpu_custom_call" | custom-call | flops 2147483648 | bytes 1048576 | tf_op jit(solution)/shard_map/pallas_call | solution.py:494
  25.1 2.1 %collective-permute-start.2 = (bf16[368,128]{1,0:T(8,128)(2,1)S(1)}, bf16[368,128]{1,0:T(8,128)(2,1)S(1)}, u32[]{:S(2)}, u32[]{:S(2)}) collective-permute-start(bf16[368,128]{1,0:T(8,128)(2,1)S(1)} %shard_map.147), channel_id=1, source_target_pairs={{0,64},{32,480},{64,128},{96,32},{128,192},{160,96},{192,256},{224... | collective-permute-start | bytes 282632 | tf_op jit(solution)/shard_map/ppermute | solution.py:516
  27.6 5.3 %collective-permute-done.2.refs_0_.third_in = bf16[368,128]{1,0:T(8,128)(2,1)S(1)} collective-permute-done((bf16[368,128]{1,0:T(8,128)(2,1)S(1)}, bf16[368,128]{1,0:T(8,128)(2,1)S(1)}, u32[]{:S(2)}, u32[]{:S(2)}) %collective-permute-start.2) | collective-permute-done | bytes 94240 | tf_op jit(solution)/shard_map/ppermute | solution.py:516
  33.4 1.9 %collective-permute-start.3 = (bf16[624,128]{1,0:T(8,128)(2,1)S(1)}, bf16[624,128]{1,0:T(8,128)(2,1)S(1)}, u32[]{:S(2)}, u32[]{:S(2)}) collective-permute-start(bf16[624,128]{1,0:T(8,128)(2,1)S(1)} %get-tuple-element.51.own_far), channel_id=1, source_target_pairs={{0,28},{4,8},{8,4},{12,16},{16,12},{20,24},{24,20},{28,0},{1,29},{... | collective-permute-start | bytes 479240 | tf_op jit(solution)/shard_map/ppermute | solution.py:516
  35.3 2.7 %collective-permute-start.4 = (bf16[624,128]{1,0:T(8,128)(2,1)S(1)}, bf16[624,128]{1,0:T(8,128)(2,1)S(1)}, u32[]{:S(2)}, u32[]{:S(2)}) collective-permute-start(bf16[624,128]{1,0:T(8,128)(2,1)S(1)} %get-tuple-element.52.own_near), channel_id=1, source_target_pairs={{0,4},{4,0},{8,12},{12,8},{16,20},{20,16},{24,28},{28,24},{1,5},{5... | collective-permute-start | bytes 479240 | tf_op jit(solution)/shard_map/ppermute | solution.py:516
  38.0 3.8 %collective-permute-done.3.recv_far.far = bf16[624,128]{1,0:T(8,128)(2,1)S(1)} collective-permute-done((bf16[624,128]{1,0:T(8,128)(2,1)S(1)}, bf16[624,128]{1,0:T(8,128)(2,1)S(1)}, u32[]{:S(2)}, u32[]{:S(2)}) %collective-permute-start.3) | collective-permute-done | bytes 159776 | tf_op jit(solution)/shard_map/ppermute | solution.py:516
  42.1 2.4 %collective-permute-start.5 = (bf16[864,128]{1,0:T(8,128)(2,1)S(1)}, bf16[864,128]{1,0:T(8,128)(2,1)S(1)}, u32[]{:S(2)}, u32[]{:S(2)}) collective-permute-start(bf16[864,128]{1,0:T(8,128)(2,1)S(1)} %get-tuple-element.53), channel_id=1, source_target_pairs={{0,1},{1,2},{2,3},{3,0},{4,5},{5,6},{6,7},{7,4},{8,9},{9,10},{10,1... | collective-permute-start | bytes 663560 | tf_op jit(solution)/shard_map/ppermute | solution.py:510
  44.5 3.6 %collective-permute-start.6 = (bf16[864,128]{1,0:T(8,128)(2,1)S(1)}, bf16[864,128]{1,0:T(8,128)(2,1)S(1)}, u32[]{:S(2)}, u32[]{:S(2)}) collective-permute-start(bf16[864,128]{1,0:T(8,128)(2,1)S(1)} %get-tuple-element.60), channel_id=1, source_target_pairs={{0,3},{1,0},{2,1},{3,2},{4,7},{5,4},{6,5},{7,6},{8,11},{9,8},{10,9... | collective-permute-start | bytes 663560 | tf_op jit(solution)/shard_map/ppermute | solution.py:510
  48.2 0.8 %shard_map.151 = (bf16[3456,192]{1,0:T(8,128)(2,1)S(1)}, bf16[2,4,4,48,192]{4,3,2,1,0:T(8,128)(2,1)S(1)}, bf16[2,4,4,48,192]{4,3,2,1,0:T(8,128)(2,1)S(1)}) custom-call(bf16[768,192]{1,0:T(8,128)(2,1)S(1)} %get-tuple-element.54.down, bf16[768,192]{1,0:T(8,128)(2,1)S(1)} %get-tuple-element.55.up, bf16[4,192,576]{2,1,0:T(8,128)(2,1)S(1)} %copy-done), custom_call_target="tpu_custom_call" | custom-call | flops 1073741824 | bytes 1048576 | tf_op jit(solution)/shard_map/pallas_call | solution.py:494
  49.1 0.7 shard_map.152.bias.bias1
  49.9 1.4 %shard_map.153.lower = bf16[288,192]{1,0:T(8,128)(2,1)S(1)} custom-call(bf16[864,128]{1,0:T(8,128)(2,1)S(1)} %collective-permute-done.5.below, bf16[3456,192]{1,0:T(8,128)(2,1)S(1)} %get-tuple-element.56.q, bf16[2,4,4,48,192]{4,3,2,1,0:T(8,128)(2,1)S(1)} %get-tuple-element.57.k_own, bf16[2,4,4,48,192]{4,3,2,1,0:T(8,128)(2,1)S(1)} %get-tuple-element.58.v_own, ...), custom_call_target="tpu_custom_call" | custom-call | flops 1073741824 | bytes 1048576 | tf_op jit(solution)/shard_map/pallas_call | solution.py:494
  51.3 2.2 %collective-permute-done.6.above = bf16[864,128]{1,0:T(8,128)(2,1)S(1)} collective-permute-done((bf16[864,128]{1,0:T(8,128)(2,1)S(1)}, bf16[864,128]{1,0:T(8,128)(2,1)S(1)}, u32[]{:S(2)}, u32[]{:S(2)}) %collective-permute-start.6) | collective-permute-done | bytes 221216 | tf_op jit(solution)/shard_map/ppermute | solution.py:510
  53.6 5.4 %shard_map.154 = (bf16[144,192]{1,0:T(8,128)(2,1)S(1)}, bf16[144,128]{1,0:T(8,128)(2,1)S(1)}, bf16[144,128]{1,0:T(8,128)(2,1)S(1)}, bf16[144,128]{1,0:T(8,128)(2,1)S(1)}, bf16[144,128]{1,0:T(8,128)(2,1)S(1)}) custom-call(bf16[224,128]{1,0:T(8,128)(2,1)S(1)} %get-tuple-element.42.own_in, bf16[224,128]{1,0:T(8,128)(2,1)S(1)} %collective-permute-done.other.other_in, ...), custom_call_target="tpu_custom_call" | custom-call | flops 2147483648 | bytes 1048576 | tf_op jit(solution)/shard_map/pallas_call | solution.py:494
  59.1 4.1 %collective-permute-start.7 = (bf16[416,128]{1,0:T(8,128)(2,1)S(1)}, bf16[416,128]{1,0:T(8,128)(2,1)S(1)}, u32[]{:S(2)}, u32[]{:S(2)}) collective-permute-start(bf16[416,128]{1,0:T(8,128)(2,1)S(1)} %get-tuple-element.69.own_far), channel_id=1, source_target_pairs={{0,28},{4,8},{8,4},{12,16},{16,12},{20,24},{24,20},{28,0},{1,29},{... | collective-permute-start | bytes 319496 | tf_op jit(solution)/shard_map/ppermute | solution.py:516
  63.2 1.9 %collective-permute-start.8 = (bf16[416,128]{1,0:T(8,128)(2,1)S(1)}, bf16[416,128]{1,0:T(8,128)(2,1)S(1)}, u32[]{:S(2)}, u32[]{:S(2)}) collective-permute-start(bf16[416,128]{1,0:T(8,128)(2,1)S(1)} %get-tuple-element.70.own_near), channel_id=1, source_target_pairs={{0,4},{4,0},{8,12},{12,8},{16,20},{20,16},{24,28},{28,24},{1,5},{5... | collective-permute-start | bytes 319496 | tf_op jit(solution)/shard_map/ppermute | solution.py:516
  65.1 2.1 %collective-permute-done.7.recv_far.far = bf16[416,128]{1,0:T(8,128)(2,1)S(1)} collective-permute-done((bf16[416,128]{1,0:T(8,128)(2,1)S(1)}, bf16[416,128]{1,0:T(8,128)(2,1)S(1)}, u32[]{:S(2)}, u32[]{:S(2)}) %collective-permute-start.7) | collective-permute-done | bytes 106528 | tf_op jit(solution)/shard_map/ppermute | solution.py:516
  67.5 2.2 %collective-permute-start.9 = (bf16[432,128]{1,0:T(8,128)(2,1)S(1)}, bf16[432,128]{1,0:T(8,128)(2,1)S(1)}, u32[]{:S(2)}, u32[]{:S(2)}) collective-permute-start(bf16[432,128]{1,0:T(8,128)(2,1)S(1)} %get-tuple-element.71), channel_id=1, source_target_pairs={{0,1},{1,2},{2,3},{3,0},{4,5},{5,6},{6,7},{7,4},{8,9},{9,10},{10,1... | collective-permute-start | bytes 331784 | tf_op jit(solution)/shard_map/ppermute | solution.py:510
  69.7 3.6 %collective-permute-start.10 = (bf16[432,128]{1,0:T(8,128)(2,1)S(1)}, bf16[432,128]{1,0:T(8,128)(2,1)S(1)}, u32[]{:S(2)}, u32[]{:S(2)}) collective-permute-start(bf16[432,128]{1,0:T(8,128)(2,1)S(1)} %get-tuple-element.78), channel_id=1, source_target_pairs={{0,3},{1,0},{2,1},{3,2},{4,7},{5,4},{6,5},{7,6},{8,11},{9,8},{10,9... | collective-permute-start | bytes 331784 | tf_op jit(solution)/shard_map/ppermute | solution.py:510
  74.6 0.8 shard_map.159.lower
  75.4 2.1 %collective-permute-done.10.above = bf16[432,128]{1,0:T(8,128)(2,1)S(1)} collective-permute-done((bf16[432,128]{1,0:T(8,128)(2,1)S(1)}, bf16[432,128]{1,0:T(8,128)(2,1)S(1)}, u32[]{:S(2)}, u32[]{:S(2)}) %collective-permute-start.10) | collective-permute-done | bytes 110624 | tf_op jit(solution)/shard_map/ppermute | solution.py:510
  77.5 2.3 %shard_map.160 = bf16[72,2,192]{2,1,0:T(2,128)(2,1)} custom-call(bf16[144,192]{1,0:T(8,128)(2,1)S(1)} %get-tuple-element.63.stream_in, bf16[96,192]{1,0:T(8,128)(2,1)S(1)} %shard_map.159.lower, bf16[432,128]{1,0:T(8,128)(2,1)S(1)} %collective-permute-done.10.above, bf16[1152,192]{1,0:T(8,128)(2,1)S(1)} %get-tuple-element.74.q, ...), custom_call_target="tpu_custom_call" | custom-call | flops 2147483648 | bytes 1048576 | tf_op jit(solution)/shard_map/pallas_call | solution.py:494
  (42 shorter events, 3.2 us)
Async XLA Ops:
  0.0 23.0 %copy-start.9 = (bf16[4,4,1,6,3312]{4,1,3,2,0:T(4,128)(2,1)S(1)}, bf16[4,4,1,6,3312]{4,1,3,2,0:T(4,128)(2,1)}, u32[]{:S(2)}) copy-start(bf16[4,4,1,6,3312]{4,1,3,2,0:T(4,128)(2,1)} %param.21) | copy-start | bytes 1907716
  0.0 23.0 %copy-start.10 = (s32[8,6,12]{2,0,1:T(8,128)S(1)}, s32[8,6,12]{2,0,1:T(8,128)}, u32[]{:S(2)}) copy-start(s32[8,6,12]{2,0,1:T(8,128)} %param.22) | copy-start | bytes 6916
  0.0 23.0 %copy-start.12 = (bf16[512,256]{1,0:T(8,128)(2,1)S(1)}, bf16[512,256]{1,0:T(8,128)(2,1)}, u32[]{:S(2)}) copy-start(bf16[512,256]{1,0:T(8,128)(2,1)} %constant.18.clone.sel_hbm.sel_ref) | copy-start | bytes 786436
  4.3 20.7 %collective-permute-start = (bf16[224,128]{1,0:T(8,128)(2,1)S(1)}, bf16[224,128]{1,0:T(8,128)(2,1)S(1)}, u32[]{:S(2)}, u32[]{:S(2)}) collective-permute-start(bf16[224,128]{1,0:T(8,128)(2,1)S(1)} %get-tuple-element.42.own_in), channel_id=1, source_target_pairs={{0,32},{32,0},{64,96},{96,64},{128,160},{160,128},{192,224},{224,1... | collective-permute-start | bytes 172040 | tf_op jit(solution)/shard_map/ppermute | solution.py:516
  12.1 13.0 %collective-permute-start.1 = (bf16[144,128]{1,0:T(8,128)(2,1)S(1)}, bf16[144,128]{1,0:T(8,128)(2,1)S(1)}, u32[]{:S(2)}, u32[]{:S(2)}) collective-permute-start(bf16[144,128]{1,0:T(8,128)(2,1)S(1)} %get-tuple-element.44.refs_3_), channel_id=1, source_target_pairs={{0,448},{32,96},{64,0},{96,160},{128,64},{160,224},{192,128},{224,... | collective-permute-start | bytes 110600 | tf_op jit(solution)/shard_map/ppermute | solution.py:516
  23.0 4.1 %copy-start.3 = (bf16[192,144]{1,0:T(8,128)(2,1)S(1)}, bf16[192,144]{1,0:T(8,128)(2,1)}, u32[]{:S(2)}) copy-start(bf16[192,144]{1,0:T(8,128)(2,1)} %constant.14.clone.oct_hbm.to_oct.refs_2_) | copy-start | bytes 165892
  23.0 4.1 %copy-start.7 = (f32[4,2,192]{2,1,0:T(2,128)S(1)}, f32[4,2,192]{2,1,0:T(2,128)}, u32[]{:S(2)}) copy-start(f32[4,2,192]{2,1,0:T(2,128)} %gains.5) | copy-start | bytes 18436
  25.0 23.1 %copy-start = (bf16[4,192,576]{2,1,0:T(8,128)(2,1)S(1)}, bf16[4,192,576]{2,1,0:T(8,128)(2,1)}, u32[]{:S(2)}) copy-start(bf16[4,192,576]{2,1,0:T(8,128)(2,1)} %w_qkv.11) | copy-start | bytes 2654212
  25.1 7.8 %collective-permute-start.2 = (bf16[368,128]{1,0:T(8,128)(2,1)S(1)}, bf16[368,128]{1,0:T(8,128)(2,1)S(1)}, u32[]{:S(2)}, u32[]{:S(2)}) collective-permute-start(bf16[368,128]{1,0:T(8,128)(2,1)S(1)} %shard_map.147), channel_id=1, source_target_pairs={{0,64},{32,480},{64,128},{96,32},{128,192},{160,96},{192,256},{224... | collective-permute-start | bytes 282632 | tf_op jit(solution)/shard_map/ppermute | solution.py:516
  33.4 8.4 %collective-permute-start.3 = (bf16[624,128]{1,0:T(8,128)(2,1)S(1)}, bf16[624,128]{1,0:T(8,128)(2,1)S(1)}, u32[]{:S(2)}, u32[]{:S(2)}) collective-permute-start(bf16[624,128]{1,0:T(8,128)(2,1)S(1)} %get-tuple-element.51.own_far), channel_id=1, source_target_pairs={{0,28},{4,8},{8,4},{12,16},{16,12},{20,24},{24,20},{28,0},{1,29},{... | collective-permute-start | bytes 479240 | tf_op jit(solution)/shard_map/ppermute | solution.py:516
  35.3 6.5 %collective-permute-start.4 = (bf16[624,128]{1,0:T(8,128)(2,1)S(1)}, bf16[624,128]{1,0:T(8,128)(2,1)S(1)}, u32[]{:S(2)}, u32[]{:S(2)}) collective-permute-start(bf16[624,128]{1,0:T(8,128)(2,1)S(1)} %get-tuple-element.52.own_near), channel_id=1, source_target_pairs={{0,4},{4,0},{8,12},{12,8},{16,20},{20,16},{24,28},{28,24},{1,5},{5... | collective-permute-start | bytes 479240 | tf_op jit(solution)/shard_map/ppermute | solution.py:516
  42.1 7.8 %collective-permute-start.5 = (bf16[864,128]{1,0:T(8,128)(2,1)S(1)}, bf16[864,128]{1,0:T(8,128)(2,1)S(1)}, u32[]{:S(2)}, u32[]{:S(2)}) collective-permute-start(bf16[864,128]{1,0:T(8,128)(2,1)S(1)} %get-tuple-element.53), channel_id=1, source_target_pairs={{0,1},{1,2},{2,3},{3,0},{4,5},{5,6},{6,7},{7,4},{8,9},{9,10},{10,1... | collective-permute-start | bytes 663560 | tf_op jit(solution)/shard_map/ppermute | solution.py:510
  44.5 9.0 %collective-permute-start.6 = (bf16[864,128]{1,0:T(8,128)(2,1)S(1)}, bf16[864,128]{1,0:T(8,128)(2,1)S(1)}, u32[]{:S(2)}, u32[]{:S(2)}) collective-permute-start(bf16[864,128]{1,0:T(8,128)(2,1)S(1)} %get-tuple-element.60), channel_id=1, source_target_pairs={{0,3},{1,0},{2,1},{3,2},{4,7},{5,4},{6,5},{7,6},{8,11},{9,8},{10,9... | collective-permute-start | bytes 663560 | tf_op jit(solution)/shard_map/ppermute | solution.py:510
  48.1 1.0 %copy-start.11 = (bf16[512,256]{1,0:T(8,128)(2,1)S(1)}, bf16[512,256]{1,0:T(8,128)(2,1)}, u32[]{:S(2)}) copy-start(bf16[512,256]{1,0:T(8,128)(2,1)} %constant.19.clone.sel_ref) | copy-start | bytes 786436
  49.9 3.6 %copy-start.1 = (bf16[4,192,768]{2,1,0:T(8,128)(2,1)S(1)}, bf16[4,192,768]{2,1,0:T(8,128)(2,1)}, u32[]{:S(2)}) copy-start(bf16[4,192,768]{2,1,0:T(8,128)(2,1)} %w_up.3) | copy-start | bytes 3538948
  49.9 3.6 %copy-start.2 = (bf16[4,768,192]{1,2,0:T(8,128)(2,1)S(1)}, bf16[4,768,192]{1,2,0:T(8,128)(2,1)}, u32[]{:S(2)}) copy-start(bf16[4,768,192]{1,2,0:T(8,128)(2,1)} %param.19) | copy-start | bytes 3538948
  49.9 3.6 %copy-start.4 = (bf16[4,192,192]{2,1,0:T(8,128)(2,1)S(1)}, bf16[4,192,192]{2,1,0:T(8,128)(2,1)}, u32[]{:S(2)}) copy-start(bf16[4,192,192]{2,1,0:T(8,128)(2,1)} %w_out.3) | copy-start | bytes 884740
  49.9 3.6 %copy-start.5 = (bf16[144,192]{1,0:T(8,128)(2,1)S(1)}, bf16[144,192]{1,0:T(8,128)(2,1)}, u32[]{:S(2)}) copy-start(bf16[144,192]{1,0:T(8,128)(2,1)} %constant.15.clone.back) | copy-start | bytes 165892
  49.9 3.6 %copy-start.6 = (bf16[2,72,144]{2,1,0:T(8,128)(2,1)S(1)}, bf16[2,72,144]{2,1,0:T(8,128)(2,1)}, u32[]{:S(2)}) copy-start(bf16[2,72,144]{2,1,0:T(8,128)(2,1)} %constant.16.clone.side) | copy-start | bytes 124420
  49.9 3.6 %copy-start.8 = (bf16[96,72]{1,0:T(8,128)(2,1)S(1)}, bf16[96,72]{1,0:T(8,128)(2,1)}, u32[]{:S(2)}) copy-start(bf16[96,72]{1,0:T(8,128)(2,1)} %constant.17.clone.side_oct) | copy-start | bytes 41476
  59.1 8.2 %collective-permute-start.7 = (bf16[416,128]{1,0:T(8,128)(2,1)S(1)}, bf16[416,128]{1,0:T(8,128)(2,1)S(1)}, u32[]{:S(2)}, u32[]{:S(2)}) collective-permute-start(bf16[416,128]{1,0:T(8,128)(2,1)S(1)} %get-tuple-element.69.own_far), channel_id=1, source_target_pairs={{0,28},{4,8},{8,4},{12,16},{16,12},{20,24},{24,20},{28,0},{1,29},{... | collective-permute-start | bytes 319496 | tf_op jit(solution)/shard_map/ppermute | solution.py:516
  63.2 4.1 %collective-permute-start.8 = (bf16[416,128]{1,0:T(8,128)(2,1)S(1)}, bf16[416,128]{1,0:T(8,128)(2,1)S(1)}, u32[]{:S(2)}, u32[]{:S(2)}) collective-permute-start(bf16[416,128]{1,0:T(8,128)(2,1)S(1)} %get-tuple-element.70.own_near), channel_id=1, source_target_pairs={{0,4},{4,0},{8,12},{12,8},{16,20},{20,16},{24,28},{28,24},{1,5},{5... | collective-permute-start | bytes 319496 | tf_op jit(solution)/shard_map/ppermute | solution.py:516
  67.5 7.1 %collective-permute-start.9 = (bf16[432,128]{1,0:T(8,128)(2,1)S(1)}, bf16[432,128]{1,0:T(8,128)(2,1)S(1)}, u32[]{:S(2)}, u32[]{:S(2)}) collective-permute-start(bf16[432,128]{1,0:T(8,128)(2,1)S(1)} %get-tuple-element.71), channel_id=1, source_target_pairs={{0,1},{1,2},{2,3},{3,0},{4,5},{5,6},{6,7},{7,4},{8,9},{9,10},{10,1... | collective-permute-start | bytes 331784 | tf_op jit(solution)/shard_map/ppermute | solution.py:510
  69.7 7.9 %collective-permute-start.10 = (bf16[432,128]{1,0:T(8,128)(2,1)S(1)}, bf16[432,128]{1,0:T(8,128)(2,1)S(1)}, u32[]{:S(2)}, u32[]{:S(2)}) collective-permute-start(bf16[432,128]{1,0:T(8,128)(2,1)S(1)} %get-tuple-element.78), channel_id=1, source_target_pairs={{0,3},{1,0},{2,1},{3,2},{4,7},{5,4},{6,5},{7,6},{8,11},{9,8},{10,9... | collective-permute-start | bytes 331784 | tf_op jit(solution)/shard_map/ppermute | solution.py:510
  (1 other events, 0.9 us)
